TPU v7x, 32 devices: a whole 2x2x4 slice. The times are simulated.
32 devices in a mesh: prow: 8 (over z, y), pcol: 4 (over x, core).
Axes of the slice: x: 2, y: 2, z: 4, core: 2. Of those that a mesh axis runs over, the one named last changes fastest.
Arguments:
- right_side: bfloat16 [3, 8, 256, 128], P(None, 'prow'), may hold values from -6 to 6
- lower_blocks: bfloat16 [3, 8, 256, 2048], P(None, 'prow', None, 'pcol'), may hold values from -0.125 to 0.125
- upper_blocks: bfloat16 [3, 8, 256, 2048], P(None, 'prow', None, 'pcol'), may hold values from -0.125 to 0.125
- lower_inverse: bfloat16 [3, 8, 256, 256], P(None, 'prow'), as said below
- upper_inverse: bfloat16 [3, 8, 256, 256], P(None, 'prow'), as said below
- pattern: int32 [3, 8, 8], replicated, may hold values 0 or 1
Outputs:
- solution: bfloat16 [3, 8, 256, 128], P(None, 'prow')
Inputs may be any that keep to these rules, and one draw needn't show every extreme that they name: `lower_inverse`: each block is lower triangular with its diagonal between 0.6 and 1.4. `upper_inverse`: each block is upper triangular with its diagonal between 0.6 and 1.4.
All inputs are finite; a program needn't handle non-finite values.
Results may differ from a plain program's by a relative error of at most 0.007.
Values may be sent and summed in bfloat16 or wider, within the bound.
No kernel may reach another device: no remote copies, remote signals or barrier semaphores. Data moves between devices by JAX's collectives and lax.ppermute only.
A program may use at most 64 MiB of HBM per device.

v0:
```python
import functools

import jax
import jax.numpy as jnp
from jax import lax
from jax.experimental import pallas as pl
from jax.experimental.pallas import tpu as pltpu
from jax.sharding import PartitionSpec as P

CORES = 2
ROW, CHIP, CORE, DEPTH, LINE = range(5)
VMEM_BYTES = 40 * 1024 * 1024
FULL_BYTES = 58 * 1024 * 1024


def pair_index(later, earlier):
    return later * (later - 1) // 2 + earlier


def exact(left, right):
    return jnp.dot(left, right, preferred_element_type=jnp.float32)


def split(values, count):
    parts = []
    for _ in range(count):
        part = values.astype(jnp.bfloat16)
        parts.append(part)
        values = values - part.astype(jnp.float32)
    return parts


def level_of(array, level):
    shape = (1,) + array.shape[1:]
    return array, pl.BlockSpec(shape, lambda step: (level,) + (0,) * (len(shape) - 1))


def call(kernel, shapes, operands, scalars=0, scratch=(), room=VMEM_BYTES):
    arrays, specs = [], []
    for place, operand in enumerate(operands):
        if isinstance(operand, tuple):
            array, spec = operand
        else:
            array = operand
            space = pltpu.SMEM if place < scalars else pltpu.VMEM
            spec = pl.BlockSpec(memory_space=space)
        arrays.append(array)
        specs.append(spec)
    return pl.pallas_call(
        kernel,
        grid=(1,),
        out_shape=shapes,
        in_specs=specs,
        out_specs=jax.tree.map(lambda _: pl.BlockSpec(memory_space=pltpu.VMEM), shapes),
        scratch_shapes=list(scratch),
        compiler_params=pltpu.CompilerParams(vmem_limit_bytes=room),
    )(*arrays)


def share_of(values, turned, share, chip):
    turned[...] = values.T
    return turned[pl.ds(pl.multiple_of(chip * share, share), share), :]


def first_kernel(share, spot, rhs, inverse, out, turned):
    value = exact(inverse[0, 0], rhs[0, 0])
    out[...] = share_of(value, turned, share, spot[CHIP]).astype(out.dtype)


def panel_kernel(share, levels, spot, first, rhs, lower, upper, *rest):
    outs, turned = rest[:-1], rest[-1]
    chip = spot[CHIP]
    mine = spot[CORE] == 0
    value = lax.dot_general(
        first[...], upper[0, 0], (((1,), (1,)), ((), ())), preferred_element_type=jnp.float32
    )
    outs[0][...] = jnp.where(mine, value, 0.0)
    for level in range(1, levels):
        start = exact(lower[level, 0], rhs[level, 0])
        end = sum(exact(upper[level, 0], part) for part in split(start, 3))
        outs[level][...] = jnp.where(mine, share_of(end, turned, share, chip), 0.0)
        if level < levels - 1:
            value = share_of(start, turned, share, chip)
            outs[levels + level - 1][...] = jnp.where(mine, value, 0.0)


def fold_kernel(picks, left_count, spot, pattern, *refs):
    outs = refs[-len(picks) :]
    pieces = refs[left_count : -len(picks)]
    row, chip, core = spot[ROW], spot[CHIP], spot[CORE]
    depth, line = spot[DEPTH], spot[LINE]
    size = outs[0].shape[-1]
    group = pieces[0].shape[-1] // size
    if left_count == 1:
        sides = [refs[0][0, 0]]
    else:
        sides = split(exact(refs[0][0, 0], refs[1][0, 0]), 3)
    for index, piece in enumerate(pieces):
        deep = (chip ^ index) * CORES + core
        turn = (deep // CORES) ^ (depth // CORES)
        for across in range(group):
            block = deep * group + across
            slot = (across ^ line) * len(pieces) + turn
            columns = slice(across * size, (across + 1) * size)
            for pick, out in zip(picks, outs):
                pair, first, is_upper = pick
                keep = pattern[pair, block, row] if is_upper else pattern[pair, row, block]
                matrix = piece[pair - first if index else pair, 0, :, columns]
                matrix = jnp.where(keep > 0, matrix, jnp.zeros_like(matrix))
                folded = sum(exact(part, matrix) for part in sides).T
                for low, part in enumerate(split(folded, 2)):
                    out[slot, low] = part


def step_kernel(lines, base, *refs):
    out = refs[-1]
    refs = refs[:-1]
    total = base[...]
    share = total.shape[0]
    for term in range(len(refs) // (lines + 1)):
        stacks = refs[term * (lines + 1) :][:lines]
        matrix = refs[term * (lines + 1) + lines]
        each = matrix.shape[0] // lines
        for line in range(lines):
            for index in range(each):
                block = stacks[line][index * share : (index + 1) * share, :]
                for low in range(2):
                    total = total - exact(block, matrix[line * each + index, low])
    out[...] = total


def last_kernel(levels, chips, spot, *refs):
    out, turned = refs[-2], refs[-1]
    share = turned.shape[0] // chips
    chip = spot[CHIP]
    at = [pl.ds(pl.multiple_of((chip ^ b) * share, share), share) for b in range(chips)]
    for level in range(levels):
        for b in range(chips):
            if level > 0:
                part = refs[b][(level - 1) * share : level * share, :]
            else:
                part = refs[chips + b][...]
            turned[at[b], :] = part.astype(jnp.float32)
        out[level, 0] = turned[...].T.astype(out.dtype)


def make_body(rows, cols):
    chips = cols // CORES
    lines = chips
    depths = rows // lines
    near = depths // CORES
    assert near == chips

    def send(value, source_of):
        pairs = []
        for z in range(depths):
            for y in range(lines):
                for x in range(chips):
                    for core in range(CORES):
                        a, b, c, d = source_of(z, y, x, core)
                        pairs.append(
                            (
                                (a * lines + b) * cols + c * CORES + d,
                                (z * lines + y) * cols + x * CORES + core,
                            )
                        )
        return lax.ppermute(value, ("prow", "pcol"), pairs)

    def after(value, *signs):
        return lax.optimization_barrier((value,) + signs)[0]

    def body(right_side, lower_blocks, upper_blocks, lower_inverse, upper_inverse, pattern):
        levels, _, size, width = right_side.shape
        share = width // chips
        row = lax.axis_index("prow")
        col = lax.axis_index("pcol")
        line, core = row % lines, col % CORES
        spot = jnp.stack([row, col // CORES, core, row // lines, line]).astype(jnp.int32)
        top = levels - 1
        piece = jax.ShapeDtypeStruct((share, size), jnp.float32)
        chunk = jax.ShapeDtypeStruct((share, size), jnp.bfloat16)
        turned = pltpu.VMEM((width, size), jnp.float32)

        def relay(blocks):
            return [
                send(blocks, lambda z, y, x, core, b=b: (z, y, x ^ b, core))
                for b in range(1, chips)
            ]

        def fold(picks, inverses, pieces, sign):
            shape = jax.ShapeDtypeStruct((near * lines, 2, size, size), jnp.bfloat16)
            return call(
                functools.partial(fold_kernel, picks, len(inverses)),
                [shape] * len(picks),
                [after(spot, sign), pattern] + inverses + pieces,
                scalars=2,
            )

        def deep(value, work=None):
            found = [value]
            for m in range(1, depths):
                found.append(send(value, lambda z, y, x, core, m=m: (z ^ m, y, x, core)))
            parts = [
                jnp.where((row // lines) % CORES == core, found[m], found[m + 1])
                for m in range(0, depths, CORES)
            ]
            stack = jnp.concatenate(parts, axis=0)
            return after(stack, *work(found[1])) if work else stack

        def wide(stack):
            return [stack] + [
                send(stack, lambda z, y, x, core, e=e: (z, y ^ e, x, core)) for e in range(1, lines)
            ]

        def settle(partial_value):
            other = send(partial_value, lambda z, y, x, core: (z, y, x, 1 - core))
            return (partial_value + other).astype(jnp.bfloat16)

        def collect(value):
            return [value] + [
                send(value, lambda z, y, x, core, b=b: (z, y, x ^ b, core)) for b in range(1, chips)
            ]

        def step(base, terms):
            operands = [base]
            for stacks, matrix in terms:
                operands += stacks + [matrix]
            return call(functools.partial(step_kernel, lines), piece, operands)

        first = call(
            functools.partial(first_kernel, share),
            chunk,
            [spot, level_of(right_side, 0), level_of(lower_inverse, 0)],
            scalars=1,
            scratch=[turned],
            room=FULL_BYTES,
        )
        panels = call(
            functools.partial(panel_kernel, share, levels),
            [piece] * (2 * levels - 2),
            [spot, first, right_side, lower_inverse, upper_inverse],
            scalars=1,
            scratch=[turned],
        )
        ends, starts = panels[:levels], [None] + list(panels[levels:])

        low_all = relay(lower_blocks)
        last_pair = pair_index(top, top - 1)
        parts = (upper_blocks[last_pair:], upper_blocks[:last_pair])
        stack = deep(first, lambda sign: panels)
        stack, upper_one, upper_rest = lax.optimization_barrier((stack,) + parts)
        high_one = relay(upper_one)
        high_rest = relay(upper_rest)

        def fold_lower(later, both, sign):
            pairs = [pair_index(later, e) for e in range(later)]
            picks = tuple((pair, 0, False) for pair in pairs)
            inverses = [level_of(lower_inverse, later)]
            if both:
                inverses = [level_of(upper_inverse, later)] + inverses
            found = dict(zip(pairs, fold(picks, inverses, [lower_blocks] + low_all, sign)))
            (backward if both else forward).update(found)
            return list(found.values())

        def fold_upper(later, earlier, sign):
            pair = pair_index(later, earlier)
            picks = ((pair, pair if pair == last_pair else 0, True),)
            moved = high_one if pair == last_pair else high_rest
            inverses = [level_of(upper_inverse, earlier)]
            found = fold(picks, inverses, [upper_blocks] + moved, sign)[0]
            upward[later, earlier] = found
            return [found]

        fetched, back, solved = {}, {}, {}
        forward, backward, upward = {}, {}, {}
        fetched[0] = wide(stack)
        for level in range(1, top):
            fold_lower(level, False, stack)
            value = starts[level]
            for earlier in range(level):
                value = step(value, [(fetched[earlier], forward[pair_index(level, earlier)])])
            stack = deep(settle(value), lambda sign: fold_lower(level, True, sign))
            if level == top - 1:
                stack = after(stack, *high_one)
            fetched[level] = wide(stack)
        fold_lower(top, True, stack)

        for level in reversed(range(levels)):
            value = ends[level]
            if level == 0:
                results = collect(jnp.concatenate([solved[k] for k in range(1, levels)], axis=0))
                value = after(value, *results)
            for earlier in range(level):
                value = step(value, [(fetched[earlier], backward[pair_index(level, earlier)])])
            for later in reversed(range(level + 1, levels)):
                value = step(value, [(back[later], upward[later, level])])
            solved[level] = settle(value)
            if level > 0:
                work = None
                if level < top:
                    work = lambda sign: fold_upper(top, level - 1, sign)
                found = solved[level]
                if level == 1:
                    found = after(found, *high_rest)
                stack = deep(found, work)
                back[level] = wide(stack)
                for later in range(level, levels):
                    if (later, level - 1) not in upward:
                        fold_upper(later, level - 1, stack)
        results += collect(solved[0])
        return call(
            functools.partial(last_kernel, levels, chips),
            jax.ShapeDtypeStruct((levels, 1, size, width), jnp.bfloat16),
            [spot] + results,
            scalars=1,
            scratch=[turned],
        )

    return body


def solution(mesh):
    placed = (
        P(None, "prow", None, None),
        P(None, "prow", None, "pcol"),
        P(None, "prow", None, "pcol"),
        P(None, "prow", None, None),
        P(None, "prow", None, None),
        P(),
    )
    return jax.shard_map(
        make_body(mesh.shape["prow"], mesh.shape["pcol"]),
        mesh=mesh,
        in_specs=placed,
        out_specs=P(None, "prow", None, None),
        check_vma=False,
    )
```

profile of v0, /device:TPU:0, one launch (start us, length us, event | category | flops | bytes accessed | tf_op | source)
XLA Modules:
  0.0 75.7 jit_solution(11955432265891569069)
XLA Ops:
  0.0 2.9 %collective-permute-start.4 = (bf16[3,1,256,512]{3,2,1,0:T(8,128)(2,1)}, bf16[3,1,256,512]{3,2,1,0:T(8,128)(2,1)S(1)}, u32[]{:S(2)}, u32[]{:S(2)}) collective-permute-start(bf16[3,1,256,512]{3,2,1,0:T(8,128)(2,1)} %refs_2_.3), channel_id=1, source_target_pairs={{2,0},{3,1},{0,2},{1,3},{6,4},{7,5},{4,6},{5,7},{10,8},{11,9},{8,1... | collective-permute-start | bytes 2359304 | tf_op jit(solution)/shard_map/ppermute | solution.py:167
  2.9 0.6 stack.23.spot
  3.5 1.8 %shard_map.64.first = bf16[64,256]{1,0:T(8,128)(2,1)} custom-call(s32[5]{0:T(128)} %stack.23.spot, bf16[3,1,256,128]{3,2,1,0:T(8,128)(2,1)} %rhs.3, bf16[3,1,256,256]{3,2,1,0:T(8,128)(2,1)} %refs_1_.8), custom_call_target="tpu_custom_call" | custom-call | tf_op jit(solution)/shard_map/pallas_call | solution.py:49
  5.3 1.6 %collective-permute-start = (bf16[64,256]{1,0:T(8,128)(2,1)}, bf16[64,256]{1,0:T(8,128)(2,1)S(1)}, u32[]{:S(2)}, u32[]{:S(2)}) collective-permute-start(bf16[64,256]{1,0:T(8,128)(2,1)} %shard_map.64.first), channel_id=1, source_target_pairs={{8,0},{9,1},{10,2},{11,3},{12,4},{13,5},{14,6},{15,7},{0,8},{1,9},... | collective-permute-start | bytes 98312 | tf_op jit(solution)/shard_map/ppermute | solution.py:167
  6.9 2.5 %collective-permute-start.2 = (bf16[64,256]{1,0:T(8,128)(2,1)}, bf16[64,256]{1,0:T(8,128)(2,1)S(1)}, u32[]{:S(2)}, u32[]{:S(2)}) collective-permute-start(bf16[64,256]{1,0:T(8,128)(2,1)} %shard_map.64.first), channel_id=1, source_target_pairs={{24,0},{25,1},{26,2},{27,3},{28,4},{29,5},{30,6},{31,7},{16,8},{17... | collective-permute-start | bytes 98312 | tf_op jit(solution)/shard_map/ppermute | solution.py:167
  9.4 0.1 collective-permute-start.1
  9.5 1.7 %slice.6 = bf16[1,1,256,512]{3,2,1,0:T(8,128)(2,1)} slice(bf16[3,1,256,512]{3,2,1,0:T(8,128)(2,1)} %refs_1_.11), slice={[2:3], [0:1], [0:256], [0:512]} | slice | bytes 524288 | tf_op jit(solution)/shard_map/slice | solution.py:249
  11.2 0.0 copy-start.6
  11.2 0.8 %slice.7 = bf16[2,1,256,512]{3,2,1,0:T(8,128)(2,1)} slice(bf16[3,1,256,512]{3,2,1,0:T(8,128)(2,1)S(1)} %copy-done.1), slice={[0:2], [0:1], [0:256], [0:512]} | slice | bytes 1048576 | tf_op jit(solution)/shard_map/slice | solution.py:249
  12.0 0.2 copy-done
  12.2 0.2 copy-done.2
  12.5 0.0 copy-done.4
  12.5 1.4 %shard_map.65 = (f32[64,256]{1,0:T(8,128)S(1)}, f32[64,256]{1,0:T(8,128)S(1)}, f32[64,256]{1,0:T(8,128)S(1)}, f32[64,256]{1,0:T(8,128)S(1)}) custom-call(s32[5]{0:T(128)S(1)} %copy-done.7, bf16[64,256]{1,0:T(8,128)(2,1)S(1)} %copy-done.6, bf16[3,1,256,128]{3,2,1,0:T(8,128)(2,1)S(1)} %copy-done.4, bf16[3,1,256,256]{3,2,1,0:T(8,128)(2,1)S(1)} %copy-done.2, ...), custom_call_target="tpu_custom_call" | custom-call | tf_op jit(solution)/shard_map/pallas_call | solution.py:49
  14.0 0.8 %collective-permute-done.1 = bf16[64,256]{1,0:T(8,128)(2,1)S(1)} collective-permute-done((bf16[64,256]{1,0:T(8,128)(2,1)}, bf16[64,256]{1,0:T(8,128)(2,1)S(1)}, u32[]{:S(2)}, u32[]{:S(2)}) %collective-permute-start.1) | collective-permute-done | bytes 32800 | tf_op jit(solution)/shard_map/ppermute | solution.py:167
  14.8 1.6 %collective-permute-start.3 = (bf16[128,256]{1,0:T(8,128)(2,1)S(1)}, bf16[128,256]{1,0:T(8,128)(2,1)S(1)}, u32[]{:S(2)}, u32[]{:S(2)}) collective-permute-start(bf16[128,256]{1,0:T(8,128)(2,1)S(1)} %pad_maximum_fusion.refs_0_), channel_id=1, source_target_pairs={{4,0},{5,1},{6,2},{7,3},{0,4},{1,5},{2,6},{3,7},{12,8},{13,9},{14,... | collective-permute-start | bytes 196616 | tf_op jit(solution)/shard_map/ppermute | solution.py:167
  16.4 4.3 %collective-permute-done.4.refs_2_.refs_3_ = bf16[3,1,256,512]{3,2,1,0:T(8,128)(2,1)S(1)} collective-permute-done((bf16[3,1,256,512]{3,2,1,0:T(8,128)(2,1)}, bf16[3,1,256,512]{3,2,1,0:T(8,128)(2,1)S(1)}, u32[]{:S(2)}, u32[]{:S(2)}) %collective-permute-start.4) | collective-permute-done | bytes 786464 | tf_op jit(solution)/shard_map/ppermute | solution.py:167
  20.7 1.3 %shard_map.66.refs_2_ = bf16[4,2,256,256]{3,2,1,0:T(8,128)(2,1)S(1)} custom-call(s32[5]{0:T(128)S(1)} %copy-done.7, s32[3,8,8]{2,1,0:T(8,128)S(1)} %copy-done.5, bf16[3,1,256,256]{3,2,1,0:T(8,128)(2,1)S(1)} %copy-done.2, bf16[3,1,256,512]{3,2,1,0:T(8,128)(2,1)S(1)} %copy-done.3, bf16[3,1,256,512]{3,2,1,0:T(8,128)(2,1)S(1)} %collective-permute-done.4.refs_2_.refs_3_), custom_call_target="tpu_custom_call" | custom-call | tf_op jit(solution)/shard_map/pallas_call | solution.py:49
  22.0 0.3 shard_map.67
  22.3 0.1 collective-permute-start.5
  22.4 1.2 %collective-permute-done.5 = f32[64,256]{1,0:T(8,128)S(1)} collective-permute-done((f32[64,256]{1,0:T(8,128)S(1)}, f32[64,256]{1,0:T(8,128)S(1)}, u32[]{:S(2)}, u32[]{:S(2)}) %collective-permute-start.5) | collective-permute-done | bytes 65568 | tf_op jit(solution)/shard_map/ppermute | solution.py:167
  23.6 1.9 %collective-permute-start.6 = (bf16[64,256]{1,0:T(8,128)(2,1)S(1)}, bf16[64,256]{1,0:T(8,128)(2,1)S(1)}, u32[]{:S(2)}, u32[]{:S(2)}) collective-permute-start(bf16[64,256]{1,0:T(8,128)(2,1)S(1)} %add_convert_fusion.3), channel_id=1, source_target_pairs={{8,0},{9,1},{10,2},{11,3},{12,4},{13,5},{14,6},{15,7},{0,8},{1,9},... | collective-permute-start | bytes 98312 | tf_op jit(solution)/shard_map/ppermute | solution.py:167
  25.5 1.5 %collective-permute-start.9 = (bf16[1,1,256,512]{3,2,1,0:T(8,128)(2,1)S(1)}, bf16[1,1,256,512]{3,2,1,0:T(8,128)(2,1)S(1)}, u32[]{:S(2)}, u32[]{:S(2)}) collective-permute-start(bf16[1,1,256,512]{3,2,1,0:T(8,128)(2,1)S(1)} %copy-done.9), channel_id=1, source_target_pairs={{2,0},{3,1},{0,2},{1,3},{6,4},{7,5},{4,6},{5,7},{10,8},{11,9},{8,1... | collective-permute-start | bytes 786440 | tf_op jit(solution)/shard_map/ppermute | solution.py:167
  27.0 2.5 %collective-permute-start.8 = (bf16[64,256]{1,0:T(8,128)(2,1)S(1)}, bf16[64,256]{1,0:T(8,128)(2,1)S(1)}, u32[]{:S(2)}, u32[]{:S(2)}) collective-permute-start(bf16[64,256]{1,0:T(8,128)(2,1)S(1)} %add_convert_fusion.3), channel_id=1, source_target_pairs={{24,0},{25,1},{26,2},{27,3},{28,4},{29,5},{30,6},{31,7},{16,8},{17... | collective-permute-start | bytes 98312 | tf_op jit(solution)/shard_map/ppermute | solution.py:167
  29.5 0.1 collective-permute-start.7
  29.6 1.6 %shard_map.68.refs_2_ = bf16[4,2,256,256]{3,2,1,0:T(8,128)(2,1)S(1)} custom-call(s32[5]{0:T(128)S(1)} %copy-done.7, s32[3,8,8]{2,1,0:T(8,128)S(1)} %copy-done.5, bf16[3,1,256,256]{3,2,1,0:T(8,128)(2,1)S(1)} %copy-done, bf16[3,1,256,256]{3,2,1,0:T(8,128)(2,1)S(1)} %copy-done.2, bf16[3,1,256,512]{3,2,1,0:T(8,128)(2,1)S(1)} %copy-done.3, ...), custom_call_target="tpu_custom_call" | custom-call | tf_op jit(solution)/shard_map/pallas_call | solution.py:49
  31.2 1.9 %collective-permute-done.8 = bf16[64,256]{1,0:T(8,128)(2,1)S(1)} collective-permute-done((bf16[64,256]{1,0:T(8,128)(2,1)S(1)}, bf16[64,256]{1,0:T(8,128)(2,1)S(1)}, u32[]{:S(2)}, u32[]{:S(2)}) %collective-permute-start.8) | collective-permute-done | bytes 32800 | tf_op jit(solution)/shard_map/ppermute | solution.py:167
  33.2 1.5 %collective-permute-done.7 = bf16[64,256]{1,0:T(8,128)(2,1)S(1)} collective-permute-done((bf16[64,256]{1,0:T(8,128)(2,1)S(1)}, bf16[64,256]{1,0:T(8,128)(2,1)S(1)}, u32[]{:S(2)}, u32[]{:S(2)}) %collective-permute-start.7) | collective-permute-done | bytes 32800 | tf_op jit(solution)/shard_map/ppermute | solution.py:167
  34.7 1.6 %collective-permute-start.10 = (bf16[128,256]{1,0:T(8,128)(2,1)S(1)}, bf16[128,256]{1,0:T(8,128)(2,1)S(1)}, u32[]{:S(2)}, u32[]{:S(2)}) collective-permute-start(bf16[128,256]{1,0:T(8,128)(2,1)S(1)} %pad_maximum_fusion.1.refs_0_), channel_id=1, source_target_pairs={{4,0},{5,1},{6,2},{7,3},{0,4},{1,5},{2,6},{3,7},{12,8},{13,9},{14,... | collective-permute-start | bytes 196616 | tf_op jit(solution)/shard_map/ppermute | solution.py:167
  36.3 2.0 %shard_map.70 = (bf16[4,2,256,256]{3,2,1,0:T(8,128)(2,1)S(1)}, bf16[4,2,256,256]{3,2,1,0:T(8,128)(2,1)S(1)}) custom-call(s32[5]{0:T(128)S(1)} %copy-done.7, s32[3,8,8]{2,1,0:T(8,128)S(1)} %copy-done.5, bf16[3,1,256,256]{3,2,1,0:T(8,128)(2,1)S(1)} %copy-done, bf16[3,1,256,256]{3,2,1,0:T(8,128)(2,1)S(1)} %copy-done.2, bf16[3,1,256,512]{3,2,1,0:T(8,128)(2,1)S(1)} %copy-done.3, ...), custom_call_target="tpu_custom_call" | custom-call | tf_op jit(solution)/shard_map/pallas_call | solution.py:49
  38.3 0.3 shard_map.71.base
  38.6 0.4 collective-permute-done.10.refs_1_
  39.0 0.3 shard_map.72
  39.3 0.1 collective-permute-start.11
  39.4 1.2 %collective-permute-done.11 = f32[64,256]{1,0:T(8,128)S(1)} collective-permute-done((f32[64,256]{1,0:T(8,128)S(1)}, f32[64,256]{1,0:T(8,128)S(1)}, u32[]{:S(2)}, u32[]{:S(2)}) %collective-permute-start.11) | collective-permute-done | bytes 65568 | tf_op jit(solution)/shard_map/ppermute | solution.py:167
  40.7 0.5 collective-permute-start.12
  41.2 0.5 collective-permute-start.18
  41.7 3.4 %collective-permute-start.14 = (bf16[64,256]{1,0:T(8,128)(2,1)S(1)}, bf16[64,256]{1,0:T(8,128)(2,1)S(1)}, u32[]{:S(2)}, u32[]{:S(2)}) collective-permute-start(bf16[64,256]{1,0:T(8,128)(2,1)S(1)} %add_convert_fusion.2), channel_id=1, source_target_pairs={{24,0},{25,1},{26,2},{27,3},{28,4},{29,5},{30,6},{31,7},{16,8},{17... | collective-permute-start | bytes 98312 | tf_op jit(solution)/shard_map/ppermute | solution.py:167
  45.1 0.0 collective-permute-start.13
  45.2 2.5 %collective-permute-done.14 = bf16[64,256]{1,0:T(8,128)(2,1)S(1)} collective-permute-done((bf16[64,256]{1,0:T(8,128)(2,1)S(1)}, bf16[64,256]{1,0:T(8,128)(2,1)S(1)}, u32[]{:S(2)}, u32[]{:S(2)}) %collective-permute-start.14) | collective-permute-done | bytes 32800 | tf_op jit(solution)/shard_map/ppermute | solution.py:167
  47.6 2.3 %collective-permute-done.13 = bf16[64,256]{1,0:T(8,128)(2,1)S(1)} collective-permute-done((bf16[64,256]{1,0:T(8,128)(2,1)S(1)}, bf16[64,256]{1,0:T(8,128)(2,1)S(1)}, u32[]{:S(2)}, u32[]{:S(2)}) %collective-permute-start.13) | collective-permute-done | bytes 32800 | tf_op jit(solution)/shard_map/ppermute | solution.py:167
  50.0 1.6 %collective-permute-start.15 = (bf16[128,256]{1,0:T(8,128)(2,1)S(1)}, bf16[128,256]{1,0:T(8,128)(2,1)S(1)}, u32[]{:S(2)}, u32[]{:S(2)}) collective-permute-start(bf16[128,256]{1,0:T(8,128)(2,1)S(1)} %pad_maximum_fusion.2.refs_0_), channel_id=1, source_target_pairs={{4,0},{5,1},{6,2},{7,3},{0,4},{1,5},{2,6},{3,7},{12,8},{13,9},{14,... | collective-permute-start | bytes 196616 | tf_op jit(solution)/shard_map/ppermute | solution.py:167
  51.6 0.3 shard_map.69.base
  51.9 1.3 %shard_map.73.refs_2_ = bf16[4,2,256,256]{3,2,1,0:T(8,128)(2,1)S(1)} custom-call(s32[5]{0:T(128)S(1)} %copy-done.7, s32[3,8,8]{2,1,0:T(8,128)S(1)} %copy-done.5, bf16[3,1,256,256]{3,2,1,0:T(8,128)(2,1)S(1)} %copy-done, bf16[3,1,256,512]{3,2,1,0:T(8,128)(2,1)S(1)} %copy-done.1, bf16[1,1,256,512]{3,2,1,0:T(8,128)(2,1)S(1)} %collective-permute-done.9.refs_2_), custom_call_target="tpu_custom_call" | custom-call | tf_op jit(solution)/shard_map/pallas_call | solution.py:49
  53.1 1.2 %collective-permute-done.15.refs_1_ = bf16[128,256]{1,0:T(8,128)(2,1)S(1)} collective-permute-done((bf16[128,256]{1,0:T(8,128)(2,1)S(1)}, bf16[128,256]{1,0:T(8,128)(2,1)S(1)}, u32[]{:S(2)}, u32[]{:S(2)}) %collective-permute-start.15) | collective-permute-done | bytes 65568 | tf_op jit(solution)/shard_map/ppermute | solution.py:167
  54.3 0.3 shard_map.74
  54.6 0.1 collective-permute-start.16
  54.7 1.2 %collective-permute-done.16 = f32[64,256]{1,0:T(8,128)S(1)} collective-permute-done((f32[64,256]{1,0:T(8,128)S(1)}, f32[64,256]{1,0:T(8,128)S(1)}, u32[]{:S(2)}, u32[]{:S(2)}) %collective-permute-start.16) | collective-permute-done | bytes 65568 | tf_op jit(solution)/shard_map/ppermute | solution.py:167
  56.0 0.5 collective-permute-start.19
  56.5 1.4 %collective-permute-start.21 = (bf16[64,256]{1,0:T(8,128)(2,1)S(1)}, bf16[64,256]{1,0:T(8,128)(2,1)S(1)}, u32[]{:S(2)}, u32[]{:S(2)}) collective-permute-start(bf16[64,256]{1,0:T(8,128)(2,1)S(1)} %add_convert_fusion.1), channel_id=1, source_target_pairs={{24,0},{25,1},{26,2},{27,3},{28,4},{29,5},{30,6},{31,7},{16,8},{17... | collective-permute-start | bytes 98312 | tf_op jit(solution)/shard_map/ppermute | solution.py:167
  57.8 1.7 %collective-permute-start.20 = (bf16[64,256]{1,0:T(8,128)(2,1)S(1)}, bf16[64,256]{1,0:T(8,128)(2,1)S(1)}, u32[]{:S(2)}, u32[]{:S(2)}) collective-permute-start(bf16[64,256]{1,0:T(8,128)(2,1)S(1)} %add_convert_fusion.1), channel_id=1, source_target_pairs={{16,0},{17,1},{18,2},{19,3},{20,4},{21,5},{22,6},{23,7},{24,8},{25... | collective-permute-start | bytes 98312 | tf_op jit(solution)/shard_map/ppermute | solution.py:167
  59.5 0.5 collective-permute-start.17
  60.1 2.1 %collective-permute-done.21 = bf16[64,256]{1,0:T(8,128)(2,1)S(1)} collective-permute-done((bf16[64,256]{1,0:T(8,128)(2,1)S(1)}, bf16[64,256]{1,0:T(8,128)(2,1)S(1)}, u32[]{:S(2)}, u32[]{:S(2)}) %collective-permute-start.21) | collective-permute-done | bytes 32800 | tf_op jit(solution)/shard_map/ppermute | solution.py:167
  62.2 0.9 %collective-permute-done.20 = bf16[64,256]{1,0:T(8,128)(2,1)S(1)} collective-permute-done((bf16[64,256]{1,0:T(8,128)(2,1)S(1)}, bf16[64,256]{1,0:T(8,128)(2,1)S(1)}, u32[]{:S(2)}, u32[]{:S(2)}) %collective-permute-start.20) | collective-permute-done | bytes 32800 | tf_op jit(solution)/shard_map/ppermute | solution.py:167
  63.1 1.3 %shard_map.75.refs_2_ = bf16[4,2,256,256]{3,2,1,0:T(8,128)(2,1)S(1)} custom-call(s32[5]{0:T(128)S(1)} %copy-done.7, s32[3,8,8]{2,1,0:T(8,128)S(1)} %copy-done.5, bf16[3,1,256,256]{3,2,1,0:T(8,128)(2,1)S(1)} %copy-done, bf16[3,1,256,512]{3,2,1,0:T(8,128)(2,1)S(1)} %copy-done.1, bf16[2,1,256,512]{3,2,1,0:T(8,128)(2,1)S(1)} %collective-permute-done.18.refs_2_), custom_call_target="tpu_custom_call" | custom-call | tf_op jit(solution)/shard_map/pallas_call | solution.py:49
  64.4 1.6 %collective-permute-start.22 = (bf16[128,256]{1,0:T(8,128)(2,1)S(1)}, bf16[128,256]{1,0:T(8,128)(2,1)S(1)}, u32[]{:S(2)}, u32[]{:S(2)}) collective-permute-start(bf16[128,256]{1,0:T(8,128)(2,1)S(1)} %pad_maximum_fusion.4.refs_0_), channel_id=1, source_target_pairs={{4,0},{5,1},{6,2},{7,3},{0,4},{1,5},{2,6},{3,7},{12,8},{13,9},{14,... | collective-permute-start | bytes 196616 | tf_op jit(solution)/shard_map/ppermute | solution.py:167
  66.0 1.3 %shard_map.77.refs_2_ = bf16[4,2,256,256]{3,2,1,0:T(8,128)(2,1)S(1)} custom-call(s32[5]{0:T(128)S(1)} %copy-done.7, s32[3,8,8]{2,1,0:T(8,128)S(1)} %copy-done.5, bf16[3,1,256,256]{3,2,1,0:T(8,128)(2,1)S(1)} %copy-done, bf16[3,1,256,512]{3,2,1,0:T(8,128)(2,1)S(1)} %copy-done.1, bf16[2,1,256,512]{3,2,1,0:T(8,128)(2,1)S(1)} %collective-permute-done.18.refs_2_), custom_call_target="tpu_custom_call" | custom-call | tf_op jit(solution)/shard_map/pallas_call | solution.py:49
  67.3 0.3 shard_map.76.base
  67.6 1.1 %collective-permute-done.22.refs_1_ = bf16[128,256]{1,0:T(8,128)(2,1)S(1)} collective-permute-done((bf16[128,256]{1,0:T(8,128)(2,1)S(1)}, bf16[128,256]{1,0:T(8,128)(2,1)S(1)}, u32[]{:S(2)}, u32[]{:S(2)}) %collective-permute-start.22) | collective-permute-done | bytes 65568 | tf_op jit(solution)/shard_map/ppermute | solution.py:167
  68.7 0.3 shard_map.78
  69.1 0.1 collective-permute-start.23
  69.1 1.2 %collective-permute-done.23 = f32[64,256]{1,0:T(8,128)S(1)} collective-permute-done((f32[64,256]{1,0:T(8,128)S(1)}, f32[64,256]{1,0:T(8,128)S(1)}, u32[]{:S(2)}, u32[]{:S(2)}) %collective-permute-start.23) | collective-permute-done | bytes 65568 | tf_op jit(solution)/shard_map/ppermute | solution.py:167
  70.4 1.4 %collective-permute-start.24 = (bf16[64,256]{1,0:T(8,128)(2,1)S(1)}, bf16[64,256]{1,0:T(8,128)(2,1)S(1)}, u32[]{:S(2)}, u32[]{:S(2)}) collective-permute-start(bf16[64,256]{1,0:T(8,128)(2,1)S(1)} %add_convert_fusion.refs_2_), channel_id=1, source_target_pairs={{2,0},{3,1},{0,2},{1,3},{6,4},{7,5},{4,6},{5,7},{10,8},{11,9},{8,1... | collective-permute-start | bytes 98312 | tf_op jit(solution)/shard_map/ppermute | solution.py:167
  71.8 2.6 %collective-permute-done.24.refs_3_ = bf16[64,256]{1,0:T(8,128)(2,1)S(1)} collective-permute-done((bf16[64,256]{1,0:T(8,128)(2,1)S(1)}, bf16[64,256]{1,0:T(8,128)(2,1)S(1)}, u32[]{:S(2)}, u32[]{:S(2)}) %collective-permute-start.24) | collective-permute-done | bytes 32800 | tf_op jit(solution)/shard_map/ppermute | solution.py:167
  74.4 1.4 %shard_map.79 = bf16[3,1,256,128]{3,2,1,0:T(8,128)(2,1)} custom-call(s32[5]{0:T(128)S(1)} %copy-done.7, bf16[128,256]{1,0:T(8,128)(2,1)S(1)} %pad_maximum_fusion.3.refs_0_, bf16[128,256]{1,0:T(8,128)(2,1)S(1)} %collective-permute-done.17.refs_1_, bf16[64,256]{1,0:T(8,128)(2,1)S(1)} %add_convert_fusion.refs_2_, ...), custom_call_target="tpu_custom_call" | custom-call | tf_op jit(solution)/shard_map/pallas_call | solution.py:49
  (42 shorter events, 0.2 us)
Async XLA Ops:
  0.0 11.2 %copy-start.1 = (bf16[3,1,256,512]{3,2,1,0:T(8,128)(2,1)S(1)}, bf16[3,1,256,512]{3,2,1,0:T(8,128)(2,1)}, u32[]{:S(2)}) copy-start(bf16[3,1,256,512]{3,2,1,0:T(8,128)(2,1)} %refs_1_.11) | copy-start | bytes 2359300
  0.0 20.7 %collective-permute-start.4 = (bf16[3,1,256,512]{3,2,1,0:T(8,128)(2,1)}, bf16[3,1,256,512]{3,2,1,0:T(8,128)(2,1)S(1)}, u32[]{:S(2)}, u32[]{:S(2)}) collective-permute-start(bf16[3,1,256,512]{3,2,1,0:T(8,128)(2,1)} %refs_2_.3), channel_id=1, source_target_pairs={{2,0},{3,1},{0,2},{1,3},{6,4},{7,5},{4,6},{5,7},{10,8},{11,9},{8,1... | collective-permute-start | bytes 2359304 | tf_op jit(solution)/shard_map/ppermute | solution.py:167
  5.3 8.6 %collective-permute-start = (bf16[64,256]{1,0:T(8,128)(2,1)}, bf16[64,256]{1,0:T(8,128)(2,1)S(1)}, u32[]{:S(2)}, u32[]{:S(2)}) collective-permute-start(bf16[64,256]{1,0:T(8,128)(2,1)} %shard_map.64.first), channel_id=1, source_target_pairs={{8,0},{9,1},{10,2},{11,3},{12,4},{13,5},{14,6},{15,7},{0,8},{1,9},... | collective-permute-start | bytes 98312 | tf_op jit(solution)/shard_map/ppermute | solution.py:167
  6.9 7.0 %collective-permute-start.2 = (bf16[64,256]{1,0:T(8,128)(2,1)}, bf16[64,256]{1,0:T(8,128)(2,1)S(1)}, u32[]{:S(2)}, u32[]{:S(2)}) collective-permute-start(bf16[64,256]{1,0:T(8,128)(2,1)} %shard_map.64.first), channel_id=1, source_target_pairs={{24,0},{25,1},{26,2},{27,3},{28,4},{29,5},{30,6},{31,7},{16,8},{17... | collective-permute-start | bytes 98312 | tf_op jit(solution)/shard_map/ppermute | solution.py:167
  9.4 5.4 %collective-permute-start.1 = (bf16[64,256]{1,0:T(8,128)(2,1)}, bf16[64,256]{1,0:T(8,128)(2,1)S(1)}, u32[]{:S(2)}, u32[]{:S(2)}) collective-permute-start(bf16[64,256]{1,0:T(8,128)(2,1)} %shard_map.64.first), channel_id=1, source_target_pairs={{16,0},{17,1},{18,2},{19,3},{20,4},{21,5},{22,6},{23,7},{24,8},{25... | collective-permute-start | bytes 98312 | tf_op jit(solution)/shard_map/ppermute | solution.py:167
  11.2 1.1 %copy-start = (bf16[3,1,256,256]{3,2,1,0:T(8,128)(2,1)S(1)}, bf16[3,1,256,256]{3,2,1,0:T(8,128)(2,1)}, u32[]{:S(2)}) copy-start(bf16[3,1,256,256]{3,2,1,0:T(8,128)(2,1)} %refs_0_.11) | copy-start | bytes 1179652
  11.2 1.3 %copy-start.2 = (bf16[3,1,256,256]{3,2,1,0:T(8,128)(2,1)S(1)}, bf16[3,1,256,256]{3,2,1,0:T(8,128)(2,1)}, u32[]{:S(2)}) copy-start(bf16[3,1,256,256]{3,2,1,0:T(8,128)(2,1)} %refs_1_.8) | copy-start | bytes 1179652
  11.2 1.3 %copy-start.4 = (bf16[3,1,256,128]{3,2,1,0:T(8,128)(2,1)S(1)}, bf16[3,1,256,128]{3,2,1,0:T(8,128)(2,1)}, u32[]{:S(2)}) copy-start(bf16[3,1,256,128]{3,2,1,0:T(8,128)(2,1)} %rhs.3) | copy-start | bytes 589828
  11.2 1.3 %copy-start.6 = (bf16[64,256]{1,0:T(8,128)(2,1)S(1)}, bf16[64,256]{1,0:T(8,128)(2,1)}, u32[]{:S(2)}) copy-start(bf16[64,256]{1,0:T(8,128)(2,1)} %shard_map.64.first) | copy-start | bytes 98308
  11.2 1.3 %copy-start.7 = (s32[5]{0:T(128)S(1)}, s32[5]{0:T(128)}, u32[]{:S(2)}) copy-start(s32[5]{0:T(128)} %stack.23.spot) | copy-start | bytes 64
  12.0 8.7 %copy-start.3 = (bf16[3,1,256,512]{3,2,1,0:T(8,128)(2,1)S(1)}, bf16[3,1,256,512]{3,2,1,0:T(8,128)(2,1)}, u32[]{:S(2)}) copy-start(bf16[3,1,256,512]{3,2,1,0:T(8,128)(2,1)} %refs_2_.3) | copy-start | bytes 2359300
  14.8 5.9 %copy-start.5 = (s32[3,8,8]{2,1,0:T(8,128)S(1)}, s32[3,8,8]{2,1,0:T(8,128)}, u32[]{:S(2)}) copy-start(s32[3,8,8]{2,1,0:T(8,128)} %pattern.11) | copy-start | bytes 2308
  14.8 7.2 %collective-permute-start.3 = (bf16[128,256]{1,0:T(8,128)(2,1)S(1)}, bf16[128,256]{1,0:T(8,128)(2,1)S(1)}, u32[]{:S(2)}, u32[]{:S(2)}) collective-permute-start(bf16[128,256]{1,0:T(8,128)(2,1)S(1)} %pad_maximum_fusion.refs_0_), channel_id=1, source_target_pairs={{4,0},{5,1},{6,2},{7,3},{0,4},{1,5},{2,6},{3,7},{12,8},{13,9},{14,... | collective-permute-start | bytes 196616 | tf_op jit(solution)/shard_map/ppermute | solution.py:167
  22.0 3.6 %copy-start.9 = (bf16[1,1,256,512]{3,2,1,0:T(8,128)(2,1)S(1)}, bf16[1,1,256,512]{3,2,1,0:T(8,128)(2,1)}, u32[]{:S(2)}) copy-start(bf16[1,1,256,512]{3,2,1,0:T(8,128)(2,1)} %slice.6) | copy-start | bytes 786436
  22.3 1.3 %collective-permute-start.5 = (f32[64,256]{1,0:T(8,128)S(1)}, f32[64,256]{1,0:T(8,128)S(1)}, u32[]{:S(2)}, u32[]{:S(2)}) collective-permute-start(f32[64,256]{1,0:T(8,128)S(1)} %shard_map.67), channel_id=1, source_target_pairs={{1,0},{0,1},{3,2},{2,3},{5,4},{4,5},{7,6},{6,7},{9,8},{8,9},{11,10... | collective-permute-start | bytes 196616 | tf_op jit(solution)/shard_map/ppermute | solution.py:167
  23.6 6.0 %collective-permute-start.6 = (bf16[64,256]{1,0:T(8,128)(2,1)S(1)}, bf16[64,256]{1,0:T(8,128)(2,1)S(1)}, u32[]{:S(2)}, u32[]{:S(2)}) collective-permute-start(bf16[64,256]{1,0:T(8,128)(2,1)S(1)} %add_convert_fusion.3), channel_id=1, source_target_pairs={{8,0},{9,1},{10,2},{11,3},{12,4},{13,5},{14,6},{15,7},{0,8},{1,9},... | collective-permute-start | bytes 98312 | tf_op jit(solution)/shard_map/ppermute | solution.py:167
  25.5 9.2 %collective-permute-start.9 = (bf16[1,1,256,512]{3,2,1,0:T(8,128)(2,1)S(1)}, bf16[1,1,256,512]{3,2,1,0:T(8,128)(2,1)S(1)}, u32[]{:S(2)}, u32[]{:S(2)}) collective-permute-start(bf16[1,1,256,512]{3,2,1,0:T(8,128)(2,1)S(1)} %copy-done.9), channel_id=1, source_target_pairs={{2,0},{3,1},{0,2},{1,3},{6,4},{7,5},{4,6},{5,7},{10,8},{11,9},{8,1... | collective-permute-start | bytes 786440 | tf_op jit(solution)/shard_map/ppermute | solution.py:167
  27.0 6.1 %collective-permute-start.8 = (bf16[64,256]{1,0:T(8,128)(2,1)S(1)}, bf16[64,256]{1,0:T(8,128)(2,1)S(1)}, u32[]{:S(2)}, u32[]{:S(2)}) collective-permute-start(bf16[64,256]{1,0:T(8,128)(2,1)S(1)} %add_convert_fusion.3), channel_id=1, source_target_pairs={{24,0},{25,1},{26,2},{27,3},{28,4},{29,5},{30,6},{31,7},{16,8},{17... | collective-permute-start | bytes 98312 | tf_op jit(solution)/shard_map/ppermute | solution.py:167
  29.5 5.2 %collective-permute-start.7 = (bf16[64,256]{1,0:T(8,128)(2,1)S(1)}, bf16[64,256]{1,0:T(8,128)(2,1)S(1)}, u32[]{:S(2)}, u32[]{:S(2)}) collective-permute-start(bf16[64,256]{1,0:T(8,128)(2,1)S(1)} %add_convert_fusion.3), channel_id=1, source_target_pairs={{16,0},{17,1},{18,2},{19,3},{20,4},{21,5},{22,6},{23,7},{24,8},{25... | collective-permute-start | bytes 98312 | tf_op jit(solution)/shard_map/ppermute | solution.py:167
  34.7 4.3 %collective-permute-start.10 = (bf16[128,256]{1,0:T(8,128)(2,1)S(1)}, bf16[128,256]{1,0:T(8,128)(2,1)S(1)}, u32[]{:S(2)}, u32[]{:S(2)}) collective-permute-start(bf16[128,256]{1,0:T(8,128)(2,1)S(1)} %pad_maximum_fusion.1.refs_0_), channel_id=1, source_target_pairs={{4,0},{5,1},{6,2},{7,3},{0,4},{1,5},{2,6},{3,7},{12,8},{13,9},{14,... | collective-permute-start | bytes 196616 | tf_op jit(solution)/shard_map/ppermute | solution.py:167
  39.0 2.1 %copy-start.8 = (bf16[2,1,256,512]{3,2,1,0:T(8,128)(2,1)S(1)}, bf16[2,1,256,512]{3,2,1,0:T(8,128)(2,1)}, u32[]{:S(2)}) copy-start(bf16[2,1,256,512]{3,2,1,0:T(8,128)(2,1)} %slice.7) | copy-start | bytes 1572868
  39.3 1.3 %collective-permute-start.11 = (f32[64,256]{1,0:T(8,128)S(1)}, f32[64,256]{1,0:T(8,128)S(1)}, u32[]{:S(2)}, u32[]{:S(2)}) collective-permute-start(f32[64,256]{1,0:T(8,128)S(1)} %shard_map.72), channel_id=1, source_target_pairs={{1,0},{0,1},{3,2},{2,3},{5,4},{4,5},{7,6},{6,7},{9,8},{8,9},{11,10... | collective-permute-start | bytes 196616 | tf_op jit(solution)/shard_map/ppermute | solution.py:167
  40.7 4.5 %collective-permute-start.12 = (bf16[64,256]{1,0:T(8,128)(2,1)S(1)}, bf16[64,256]{1,0:T(8,128)(2,1)S(1)}, u32[]{:S(2)}, u32[]{:S(2)}) collective-permute-start(bf16[64,256]{1,0:T(8,128)(2,1)S(1)} %add_convert_fusion.2), channel_id=1, source_target_pairs={{8,0},{9,1},{10,2},{11,3},{12,4},{13,5},{14,6},{15,7},{0,8},{1,9},... | collective-permute-start | bytes 98312 | tf_op jit(solution)/shard_map/ppermute | solution.py:167
  41.2 14.8 %collective-permute-start.18 = (bf16[2,1,256,512]{3,2,1,0:T(8,128)(2,1)S(1)}, bf16[2,1,256,512]{3,2,1,0:T(8,128)(2,1)S(1)}, u32[]{:S(2)}, u32[]{:S(2)}) collective-permute-start(bf16[2,1,256,512]{3,2,1,0:T(8,128)(2,1)S(1)} %copy-done.8), channel_id=1, source_target_pairs={{2,0},{3,1},{0,2},{1,3},{6,4},{7,5},{4,6},{5,7},{10,8},{11,9},{8,1... | collective-permute-start | bytes 1572872 | tf_op jit(solution)/shard_map/ppermute | solution.py:167
  41.7 5.9 %collective-permute-start.14 = (bf16[64,256]{1,0:T(8,128)(2,1)S(1)}, bf16[64,256]{1,0:T(8,128)(2,1)S(1)}, u32[]{:S(2)}, u32[]{:S(2)}) collective-permute-start(bf16[64,256]{1,0:T(8,128)(2,1)S(1)} %add_convert_fusion.2), channel_id=1, source_target_pairs={{24,0},{25,1},{26,2},{27,3},{28,4},{29,5},{30,6},{31,7},{16,8},{17... | collective-permute-start | bytes 98312 | tf_op jit(solution)/shard_map/ppermute | solution.py:167
  45.1 4.8 %collective-permute-start.13 = (bf16[64,256]{1,0:T(8,128)(2,1)S(1)}, bf16[64,256]{1,0:T(8,128)(2,1)S(1)}, u32[]{:S(2)}, u32[]{:S(2)}) collective-permute-start(bf16[64,256]{1,0:T(8,128)(2,1)S(1)} %add_convert_fusion.2), channel_id=1, source_target_pairs={{16,0},{17,1},{18,2},{19,3},{20,4},{21,5},{22,6},{23,7},{24,8},{25... | collective-permute-start | bytes 98312 | tf_op jit(solution)/shard_map/ppermute | solution.py:167
  50.0 4.3 %collective-permute-start.15 = (bf16[128,256]{1,0:T(8,128)(2,1)S(1)}, bf16[128,256]{1,0:T(8,128)(2,1)S(1)}, u32[]{:S(2)}, u32[]{:S(2)}) collective-permute-start(bf16[128,256]{1,0:T(8,128)(2,1)S(1)} %pad_maximum_fusion.2.refs_0_), channel_id=1, source_target_pairs={{4,0},{5,1},{6,2},{7,3},{0,4},{1,5},{2,6},{3,7},{12,8},{13,9},{14,... | collective-permute-start | bytes 196616 | tf_op jit(solution)/shard_map/ppermute | solution.py:167
  54.6 1.3 %collective-permute-start.16 = (f32[64,256]{1,0:T(8,128)S(1)}, f32[64,256]{1,0:T(8,128)S(1)}, u32[]{:S(2)}, u32[]{:S(2)}) collective-permute-start(f32[64,256]{1,0:T(8,128)S(1)} %shard_map.74), channel_id=1, source_target_pairs={{1,0},{0,1},{3,2},{2,3},{5,4},{4,5},{7,6},{6,7},{9,8},{8,9},{11,10... | collective-permute-start | bytes 196616 | tf_op jit(solution)/shard_map/ppermute | solution.py:167
  56.0 4.1 %collective-permute-start.19 = (bf16[64,256]{1,0:T(8,128)(2,1)S(1)}, bf16[64,256]{1,0:T(8,128)(2,1)S(1)}, u32[]{:S(2)}, u32[]{:S(2)}) collective-permute-start(bf16[64,256]{1,0:T(8,128)(2,1)S(1)} %add_convert_fusion.1), channel_id=1, source_target_pairs={{8,0},{9,1},{10,2},{11,3},{12,4},{13,5},{14,6},{15,7},{0,8},{1,9},... | collective-permute-start | bytes 98312 | tf_op jit(solution)/shard_map/ppermute | solution.py:167
  56.5 5.7 %collective-permute-start.21 = (bf16[64,256]{1,0:T(8,128)(2,1)S(1)}, bf16[64,256]{1,0:T(8,128)(2,1)S(1)}, u32[]{:S(2)}, u32[]{:S(2)}) collective-permute-start(bf16[64,256]{1,0:T(8,128)(2,1)S(1)} %add_convert_fusion.1), channel_id=1, source_target_pairs={{24,0},{25,1},{26,2},{27,3},{28,4},{29,5},{30,6},{31,7},{16,8},{17... | collective-permute-start | bytes 98312 | tf_op jit(solution)/shard_map/ppermute | solution.py:167
  57.8 5.3 %collective-permute-start.20 = (bf16[64,256]{1,0:T(8,128)(2,1)S(1)}, bf16[64,256]{1,0:T(8,128)(2,1)S(1)}, u32[]{:S(2)}, u32[]{:S(2)}) collective-permute-start(bf16[64,256]{1,0:T(8,128)(2,1)S(1)} %add_convert_fusion.1), channel_id=1, source_target_pairs={{16,0},{17,1},{18,2},{19,3},{20,4},{21,5},{22,6},{23,7},{24,8},{25... | collective-permute-start | bytes 98312 | tf_op jit(solution)/shard_map/ppermute | solution.py:167
  59.5 7.8 %collective-permute-start.17 = (bf16[128,256]{1,0:T(8,128)(2,1)S(1)}, bf16[128,256]{1,0:T(8,128)(2,1)S(1)}, u32[]{:S(2)}, u32[]{:S(2)}) collective-permute-start(bf16[128,256]{1,0:T(8,128)(2,1)S(1)} %pad_maximum_fusion.3.refs_0_), channel_id=1, source_target_pairs={{2,0},{3,1},{0,2},{1,3},{6,4},{7,5},{4,6},{5,7},{10,8},{11,9},{8,1... | collective-permute-start | bytes 196616 | tf_op jit(solution)/shard_map/ppermute | solution.py:167
  64.4 4.3 %collective-permute-start.22 = (bf16[128,256]{1,0:T(8,128)(2,1)S(1)}, bf16[128,256]{1,0:T(8,128)(2,1)S(1)}, u32[]{:S(2)}, u32[]{:S(2)}) collective-permute-start(bf16[128,256]{1,0:T(8,128)(2,1)S(1)} %pad_maximum_fusion.4.refs_0_), channel_id=1, source_target_pairs={{4,0},{5,1},{6,2},{7,3},{0,4},{1,5},{2,6},{3,7},{12,8},{13,9},{14,... | collective-permute-start | bytes 196616 | tf_op jit(solution)/shard_map/ppermute | solution.py:167
  69.1 1.3 %collective-permute-start.23 = (f32[64,256]{1,0:T(8,128)S(1)}, f32[64,256]{1,0:T(8,128)S(1)}, u32[]{:S(2)}, u32[]{:S(2)}) collective-permute-start(f32[64,256]{1,0:T(8,128)S(1)} %shard_map.78), channel_id=1, source_target_pairs={{1,0},{0,1},{3,2},{2,3},{5,4},{4,5},{7,6},{6,7},{9,8},{8,9},{11,10... | collective-permute-start | bytes 196616 | tf_op jit(solution)/shard_map/ppermute | solution.py:167
  70.4 4.0 %collective-permute-start.24 = (bf16[64,256]{1,0:T(8,128)(2,1)S(1)}, bf16[64,256]{1,0:T(8,128)(2,1)S(1)}, u32[]{:S(2)}, u32[]{:S(2)}) collective-permute-start(bf16[64,256]{1,0:T(8,128)(2,1)S(1)} %add_convert_fusion.refs_2_), channel_id=1, source_target_pairs={{2,0},{3,1},{0,2},{1,3},{6,4},{7,5},{4,6},{5,7},{10,8},{11,9},{8,1... | collective-permute-start | bytes 98312 | tf_op jit(solution)/shard_map/ppermute | solution.py:167
where the time goes:
time: 75.9 us; the launch traced here: 75.7 us
  starting transfers between devices  29.7 us (39%)
  waiting for transfers between devices  26.7 us (35%)
  Pallas kernels  15.4 us (20%)
  local copies, waits for them, and re-layouts  3.58 us (5%)
    ppermute x25, starting transfers between devices, send(): return lax.ppermute(value, ('prow', 'pcol'), pairs)  29.7 us
    ppermute x25, waiting for transfers between devices, send(): return lax.ppermute(value, ('prow', 'pcol'), pairs)  26.7 us
    pallas_call x16, Pallas kernels, call(): pl.pallas_call(kernel, grid=(1,), out_shape=shapes, in_specs=specs, out_s...  15.4 us
    slice x2, local copies, waits for them, and re-layouts, body(): parts = (upper_blocks[last_pair:], upper_blocks[:last_pair])  2.49 us
  transfers between devices with their start and end apart: 25, of which 16 were waited for; matrix products, arithmetic and copies ran while one was open for 4% of the time, Pallas kernels for 17%

commit v1 on v0

--- a/solution.py
+++ b/solution.py
@@ -62,7 +62,8 @@
     return turned[pl.ds(pl.multiple_of(chip * share, share), share), :]
 
 
-def first_kernel(share, spot, rhs, inverse, out, turned):
+def first_kernel(share, spot, rhs, inverse, blocks, out, copied, turned):
+    copied[...] = blocks[...]
     value = exact(inverse[0, 0], rhs[0, 0])
     out[...] = share_of(value, turned, share, spot[CHIP]).astype(out.dtype)
 
@@ -112,6 +113,11 @@
                     out[slot, low] = part
 
 
+def pick_kernel(parts, sign, *refs):
+    for (is_upper, start), out in zip(parts, refs[2:]):
+        out[...] = refs[1 if is_upper else 0][start : start + out.shape[0]]
+
+
 def step_kernel(lines, base, *refs):
     out = refs[-1]
     refs = refs[:-1]
@@ -227,10 +233,11 @@
                 operands += stacks + [matrix]
             return call(functools.partial(step_kernel, lines), piece, operands)
 
-        first = call(
+        single = jax.ShapeDtypeStruct((1,) + lower_blocks.shape[1:], jnp.bfloat16)
+        first, first_blocks = call(
             functools.partial(first_kernel, share),
-            chunk,
-            [spot, level_of(right_side, 0), level_of(lower_inverse, 0)],
+            [chunk, single],
+            [spot, level_of(right_side, 0), level_of(lower_inverse, 0), level_of(lower_blocks, 0)],
             scalars=1,
             scratch=[turned],
             room=FULL_BYTES,
@@ -244,44 +251,49 @@
         )
         ends, starts = panels[:levels], [None] + list(panels[levels:])
 
-        low_all = relay(lower_blocks)
         last_pair = pair_index(top, top - 1)
-        parts = (upper_blocks[last_pair:], upper_blocks[:last_pair])
-        stack = deep(first, lambda sign: panels)
-        stack, upper_one, upper_rest = lax.optimization_barrier((stack,) + parts)
-        high_one = relay(upper_one)
-        high_rest = relay(upper_rest)
+        parts = ((False, 1), (True, last_pair), (True, 0))
+        counts = (lower_blocks.shape[0] - 1, 1, last_pair)
+        picked = call(
+            functools.partial(pick_kernel, parts),
+            [jax.ShapeDtypeStruct((n,) + single.shape[1:], single.dtype) for n in counts],
+            [after(spot, first), lower_blocks, upper_blocks],
+            scalars=1,
+        )
+        low_one = relay(first_blocks)
+        low_rest = relay(after(picked[0], *low_one))
+        high_one = relay(after(picked[1], *low_rest))
+        high_rest = relay(after(picked[2], *high_one))
 
         def fold_lower(later, both, sign):
+            moved = low_one if later == 1 else low_rest
             pairs = [pair_index(later, e) for e in range(later)]
-            picks = tuple((pair, 0, False) for pair in pairs)
+            picks = tuple((pair, min(later - 1, 1), False) for pair in pairs)
             inverses = [level_of(lower_inverse, later)]
             if both:
                 inverses = [level_of(upper_inverse, later)] + inverses
-            found = dict(zip(pairs, fold(picks, inverses, [lower_blocks] + low_all, sign)))
-            (backward if both else forward).update(found)
-            return list(found.values())
+            found = fold(picks, inverses, [lower_blocks] + moved, sign)
+            kept = backward if both else forward
+            kept.update({(later, e): value for e, value in enumerate(found)})
+            return found
 
         def fold_upper(later, earlier, sign):
             pair = pair_index(later, earlier)
+            moved = high_one if pair == last_pair else high_rest
             picks = ((pair, pair if pair == last_pair else 0, True),)
-            moved = high_one if pair == last_pair else high_rest
             inverses = [level_of(upper_inverse, earlier)]
-            found = fold(picks, inverses, [upper_blocks] + moved, sign)[0]
-            upward[later, earlier] = found
-            return [found]
+            upward[later, earlier] = fold(picks, inverses, [upper_blocks] + moved, sign)[0]
 
         fetched, back, solved = {}, {}, {}
         forward, backward, upward = {}, {}, {}
+        stack = deep(first, lambda sign: list(panels) + list(picked))
         fetched[0] = wide(stack)
         for level in range(1, top):
             fold_lower(level, False, stack)
             value = starts[level]
             for earlier in range(level):
-                value = step(value, [(fetched[earlier], forward[pair_index(level, earlier)])])
+                value = step(value, [(fetched[earlier], forward[level, earlier])])
             stack = deep(settle(value), lambda sign: fold_lower(level, True, sign))
-            if level == top - 1:
-                stack = after(stack, *high_one)
             fetched[level] = wide(stack)
         fold_lower(top, True, stack)
 
@@ -291,22 +303,15 @@
                 results = collect(jnp.concatenate([solved[k] for k in range(1, levels)], axis=0))
                 value = after(value, *results)
             for earlier in range(level):
-                value = step(value, [(fetched[earlier], backward[pair_index(level, earlier)])])
+                value = step(value, [(fetched[earlier], backward[level, earlier])])
             for later in reversed(range(level + 1, levels)):
                 value = step(value, [(back[later], upward[later, level])])
             solved[level] = settle(value)
             if level > 0:
-                work = None
-                if level < top:
-                    work = lambda sign: fold_upper(top, level - 1, sign)
-                found = solved[level]
-                if level == 1:
-                    found = after(found, *high_rest)
-                stack = deep(found, work)
+                stack = deep(solved[level])
                 back[level] = wide(stack)
                 for later in range(level, levels):
-                    if (later, level - 1) not in upward:
-                        fold_upper(later, level - 1, stack)
+                    fold_upper(later, level - 1, stack)
         results += collect(solved[0])
         return call(
             functools.partial(last_kernel, levels, chips),

time: 75.9 us -> 79.1 us (1.042)
  waiting for transfers between devices: 26.7 us -> 28.8 us
  starting transfers between devices: 29.7 us -> 30.5 us
  Pallas kernels: 15.4 us -> 16.2 us
    slice x2 -> x0, local copies, waits for them, and re-layouts: 2.49 us -> none  [body(): parts = (upper_blocks[last_pair:], upper_blocks[:last_pair])]
    ppermute x25 -> x26, waiting for transfers between devices: 26.7 us -> 28.8 us  [send(): return lax.ppermute(value, ('prow', 'pcol'), pairs)]
    unnamed x20 -> x18, local copies, waits for them, and re-layouts: 0.52 us -> 2.34 us
    ppermute x25 -> x26, starting transfers between devices: 29.7 us -> 30.5 us  [send(): return lax.ppermute(value, ('prow', 'pcol'), pairs)]
    pallas_call x16 -> x17, Pallas kernels: 15.4 us -> 16.2 us  [call(): pl.pallas_call(kernel, grid=(1,), out_shape=shapes, in_specs=specs, out_s...]
  transfers between devices with their start and end apart: 25 -> 26, of which waited for: 16 -> 15; matrix products, arithmetic and copies ran while one was open for 4% -> 0% of each run, Pallas kernels for 17% -> 15%
where the time goes in v1:
time: 79.1 us; the launch traced here: 78.9 us
  starting transfers between devices  30.5 us (39%)
  waiting for transfers between devices  28.8 us (36%)
  Pallas kernels  16.2 us (20%)
  local copies, waits for them, and re-layouts  2.97 us (4%)
    ppermute x26, starting transfers between devices, send(): return lax.ppermute(value, ('prow', 'pcol'), pairs)  30.5 us
    ppermute x26, waiting for transfers between devices, send(): return lax.ppermute(value, ('prow', 'pcol'), pairs)  28.8 us
    pallas_call x17, Pallas kernels, call(): pl.pallas_call(kernel, grid=(1,), out_shape=shapes, in_specs=specs, out_s...  16.2 us
    unnamed x18, local copies, waits for them, and re-layouts  2.34 us
  transfers between devices with their start and end apart: 26, of which 15 were waited for; matrix products, arithmetic and copies ran while one was open for 0% of the time, Pallas kernels for 15%

profile of v1, /device:TPU:0, one launch (start us, length us, event | category | flops | bytes accessed | tf_op | source)
XLA Modules:
  0.0 78.9 jit_solution(10621265530639065030)
XLA Ops:
  0.0 0.6 stack.23.spot.sign
  0.6 2.0 %shard_map.64 = (bf16[64,256]{1,0:T(8,128)(2,1)}, bf16[1,1,256,512]{3,2,1,0:T(8,128)(2,1)}) custom-call(s32[5]{0:T(128)} %stack.23.spot.sign, bf16[3,1,256,128]{3,2,1,0:T(8,128)(2,1)} %rhs.3, bf16[3,1,256,256]{3,2,1,0:T(8,128)(2,1)} %refs_1_.10, bf16[3,1,256,512]{3,2,1,0:T(8,128)(2,1)} %refs_2_.3), custom_call_target="tpu_custom_call" | custom-call | tf_op jit(solution)/shard_map/pallas_call | solution.py:49
  2.7 3.0 %collective-permute-start = (bf16[64,256]{1,0:T(8,128)(2,1)}, bf16[64,256]{1,0:T(8,128)(2,1)S(1)}, u32[]{:S(2)}, u32[]{:S(2)}) collective-permute-start(bf16[64,256]{1,0:T(8,128)(2,1)} %get-tuple-element.28.first), channel_id=1, source_target_pairs={{8,0},{9,1},{10,2},{11,3},{12,4},{13,5},{14,6},{15,7},{0,8},{1,9},... | collective-permute-start | bytes 98312 | tf_op jit(solution)/shard_map/ppermute | solution.py:173
  5.7 2.5 %collective-permute-start.2 = (bf16[64,256]{1,0:T(8,128)(2,1)}, bf16[64,256]{1,0:T(8,128)(2,1)S(1)}, u32[]{:S(2)}, u32[]{:S(2)}) collective-permute-start(bf16[64,256]{1,0:T(8,128)(2,1)} %get-tuple-element.28.first), channel_id=1, source_target_pairs={{24,0},{25,1},{26,2},{27,3},{28,4},{29,5},{30,6},{31,7},{16,8},{17... | collective-permute-start | bytes 98312 | tf_op jit(solution)/shard_map/ppermute | solution.py:173
  8.2 0.1 collective-permute-start.1
  8.3 1.5 %collective-permute-start.4 = (bf16[1,1,256,512]{3,2,1,0:T(8,128)(2,1)}, bf16[1,1,256,512]{3,2,1,0:T(8,128)(2,1)S(1)}, u32[]{:S(2)}, u32[]{:S(2)}) collective-permute-start(bf16[1,1,256,512]{3,2,1,0:T(8,128)(2,1)} %get-tuple-element.39), channel_id=1, source_target_pairs={{2,0},{3,1},{0,2},{1,3},{6,4},{7,5},{4,6},{5,7},{10,8},{11,9},{8,1... | collective-permute-start | bytes 786440 | tf_op jit(solution)/shard_map/ppermute | solution.py:173
  9.8 0.9 %copy-done.4 = bf16[3,1,256,128]{3,2,1,0:T(8,128)(2,1)S(1)} copy-done((bf16[3,1,256,128]{3,2,1,0:T(8,128)(2,1)S(1)}, bf16[3,1,256,128]{3,2,1,0:T(8,128)(2,1)}, u32[]{:S(2)}) %copy-start.4) | copy-done | bytes 196632
  10.7 0.8 copy-done.6
  11.5 0.6 copy-done.7
  12.1 1.4 %shard_map.65 = (f32[64,256]{1,0:T(8,128)S(1)}, f32[64,256]{1,0:T(8,128)S(1)}, f32[64,256]{1,0:T(8,128)S(1)}, f32[64,256]{1,0:T(8,128)S(1)}) custom-call(s32[5]{0:T(128)S(1)} %copy-done.7, bf16[64,256]{1,0:T(8,128)(2,1)S(1)} %copy-done.6, bf16[3,1,256,128]{3,2,1,0:T(8,128)(2,1)S(1)} %copy-done.4, bf16[3,1,256,256]{3,2,1,0:T(8,128)(2,1)S(1)} %copy-done.3, ...), custom_call_target="tpu_custom_call" | custom-call | tf_op jit(solution)/shard_map/pallas_call | solution.py:49
  13.5 0.6 shard_map.66
  14.2 0.0 collective-permute-done.1
  14.2 0.0 copy-start.5
  14.2 1.6 %collective-permute-start.3 = (bf16[128,256]{1,0:T(8,128)(2,1)S(1)}, bf16[128,256]{1,0:T(8,128)(2,1)S(1)}, u32[]{:S(2)}, u32[]{:S(2)}) collective-permute-start(bf16[128,256]{1,0:T(8,128)(2,1)S(1)} %pad_maximum_fusion.refs_0_), channel_id=1, source_target_pairs={{4,0},{5,1},{6,2},{7,3},{0,4},{1,5},{2,6},{3,7},{12,8},{13,9},{14,... | collective-permute-start | bytes 196616 | tf_op jit(solution)/shard_map/ppermute | solution.py:173
  15.8 0.1 collective-permute-done.4.refs_2_.refs_3_
  16.0 1.3 %shard_map.67.refs_2_ = bf16[4,2,256,256]{3,2,1,0:T(8,128)(2,1)S(1)} custom-call(s32[5]{0:T(128)S(1)} %copy-done.7, s32[3,8,8]{2,1,0:T(8,128)S(1)} %copy-done.5, bf16[3,1,256,256]{3,2,1,0:T(8,128)(2,1)S(1)} %copy-done.3, bf16[3,1,256,512]{3,2,1,0:T(8,128)(2,1)S(1)} %copy-done, bf16[1,1,256,512]{3,2,1,0:T(8,128)(2,1)S(1)} %collective-permute-done.4.refs_2_.refs_3_), custom_call_target="tpu_custom_call" | custom-call | tf_op jit(solution)/shard_map/pallas_call | solution.py:49
  17.3 1.3 %collective-permute-done.3.refs_1_ = bf16[128,256]{1,0:T(8,128)(2,1)S(1)} collective-permute-done((bf16[128,256]{1,0:T(8,128)(2,1)S(1)}, bf16[128,256]{1,0:T(8,128)(2,1)S(1)}, u32[]{:S(2)}, u32[]{:S(2)}) %collective-permute-start.3) | collective-permute-done | bytes 65568 | tf_op jit(solution)/shard_map/ppermute | solution.py:173
  18.6 0.3 shard_map.68
  18.9 0.1 collective-permute-start.5
  19.0 1.2 %collective-permute-done.5 = f32[64,256]{1,0:T(8,128)S(1)} collective-permute-done((f32[64,256]{1,0:T(8,128)S(1)}, f32[64,256]{1,0:T(8,128)S(1)}, u32[]{:S(2)}, u32[]{:S(2)}) %collective-permute-start.5) | collective-permute-done | bytes 65568 | tf_op jit(solution)/shard_map/ppermute | solution.py:173
  20.2 1.9 %collective-permute-start.6 = (bf16[64,256]{1,0:T(8,128)(2,1)S(1)}, bf16[64,256]{1,0:T(8,128)(2,1)S(1)}, u32[]{:S(2)}, u32[]{:S(2)}) collective-permute-start(bf16[64,256]{1,0:T(8,128)(2,1)S(1)} %add_convert_fusion.3), channel_id=1, source_target_pairs={{8,0},{9,1},{10,2},{11,3},{12,4},{13,5},{14,6},{15,7},{0,8},{1,9},... | collective-permute-start | bytes 98312 | tf_op jit(solution)/shard_map/ppermute | solution.py:173
  22.1 0.5 collective-permute-start.9
  22.6 2.5 %collective-permute-start.8 = (bf16[64,256]{1,0:T(8,128)(2,1)S(1)}, bf16[64,256]{1,0:T(8,128)(2,1)S(1)}, u32[]{:S(2)}, u32[]{:S(2)}) collective-permute-start(bf16[64,256]{1,0:T(8,128)(2,1)S(1)} %add_convert_fusion.3), channel_id=1, source_target_pairs={{24,0},{25,1},{26,2},{27,3},{28,4},{29,5},{30,6},{31,7},{16,8},{17... | collective-permute-start | bytes 98312 | tf_op jit(solution)/shard_map/ppermute | solution.py:173
  25.1 1.6 %shard_map.69.refs_2_ = bf16[4,2,256,256]{3,2,1,0:T(8,128)(2,1)S(1)} custom-call(s32[5]{0:T(128)S(1)} %copy-done.7, s32[3,8,8]{2,1,0:T(8,128)S(1)} %copy-done.5, bf16[3,1,256,256]{3,2,1,0:T(8,128)(2,1)S(1)} %copy-done.1, bf16[3,1,256,256]{3,2,1,0:T(8,128)(2,1)S(1)} %copy-done.3, bf16[3,1,256,512]{3,2,1,0:T(8,128)(2,1)S(1)} %copy-done, ...), custom_call_target="tpu_custom_call" | custom-call | tf_op jit(solution)/shard_map/pallas_call | solution.py:49
  26.7 1.7 %collective-permute-done.8 = bf16[64,256]{1,0:T(8,128)(2,1)S(1)} collective-permute-done((bf16[64,256]{1,0:T(8,128)(2,1)S(1)}, bf16[64,256]{1,0:T(8,128)(2,1)S(1)}, u32[]{:S(2)}, u32[]{:S(2)}) %collective-permute-start.8) | collective-permute-done | bytes 32800 | tf_op jit(solution)/shard_map/ppermute | solution.py:173
  28.4 1.5 %collective-permute-done.7 = bf16[64,256]{1,0:T(8,128)(2,1)S(1)} collective-permute-done((bf16[64,256]{1,0:T(8,128)(2,1)S(1)}, bf16[64,256]{1,0:T(8,128)(2,1)S(1)}, u32[]{:S(2)}, u32[]{:S(2)}) %collective-permute-start.7) | collective-permute-done | bytes 32800 | tf_op jit(solution)/shard_map/ppermute | solution.py:173
  29.9 1.6 %collective-permute-start.10 = (bf16[128,256]{1,0:T(8,128)(2,1)S(1)}, bf16[128,256]{1,0:T(8,128)(2,1)S(1)}, u32[]{:S(2)}, u32[]{:S(2)}) collective-permute-start(bf16[128,256]{1,0:T(8,128)(2,1)S(1)} %pad_maximum_fusion.1.refs_0_), channel_id=1, source_target_pairs={{4,0},{5,1},{6,2},{7,3},{0,4},{1,5},{2,6},{3,7},{12,8},{13,9},{14,... | collective-permute-start | bytes 196616 | tf_op jit(solution)/shard_map/ppermute | solution.py:173
  31.5 4.3 %collective-permute-done.9.refs_3_ = bf16[2,1,256,512]{3,2,1,0:T(8,128)(2,1)S(1)} collective-permute-done((bf16[2,1,256,512]{3,2,1,0:T(8,128)(2,1)S(1)}, bf16[2,1,256,512]{3,2,1,0:T(8,128)(2,1)S(1)}, u32[]{:S(2)}, u32[]{:S(2)}) %collective-permute-start.9) | collective-permute-done | bytes 524320 | tf_op jit(solution)/shard_map/ppermute | solution.py:173
  35.8 2.0 %shard_map.71 = (bf16[4,2,256,256]{3,2,1,0:T(8,128)(2,1)S(1)}, bf16[4,2,256,256]{3,2,1,0:T(8,128)(2,1)S(1)}) custom-call(s32[5]{0:T(128)S(1)} %copy-done.7, s32[3,8,8]{2,1,0:T(8,128)S(1)} %copy-done.5, bf16[3,1,256,256]{3,2,1,0:T(8,128)(2,1)S(1)} %copy-done.1, bf16[3,1,256,256]{3,2,1,0:T(8,128)(2,1)S(1)} %copy-done.3, bf16[3,1,256,512]{3,2,1,0:T(8,128)(2,1)S(1)} %copy-done, ...), custom_call_target="tpu_custom_call" | custom-call | tf_op jit(solution)/shard_map/pallas_call | solution.py:49
  37.8 0.3 shard_map.72.base
  38.1 0.0 collective-permute-done.10.refs_1_
  38.1 0.3 shard_map.73
  38.4 0.1 collective-permute-start.11
  38.5 1.2 %collective-permute-done.11 = f32[64,256]{1,0:T(8,128)S(1)} collective-permute-done((f32[64,256]{1,0:T(8,128)S(1)}, f32[64,256]{1,0:T(8,128)S(1)}, u32[]{:S(2)}, u32[]{:S(2)}) %collective-permute-start.11) | collective-permute-done | bytes 65568 | tf_op jit(solution)/shard_map/ppermute | solution.py:173
  39.8 0.4 collective-permute-start.12
  40.2 0.7 collective-permute-start.16
  40.9 2.6 %collective-permute-start.14 = (bf16[64,256]{1,0:T(8,128)(2,1)S(1)}, bf16[64,256]{1,0:T(8,128)(2,1)S(1)}, u32[]{:S(2)}, u32[]{:S(2)}) collective-permute-start(bf16[64,256]{1,0:T(8,128)(2,1)S(1)} %add_convert_fusion.2), channel_id=1, source_target_pairs={{24,0},{25,1},{26,2},{27,3},{28,4},{29,5},{30,6},{31,7},{16,8},{17... | collective-permute-start | bytes 98312 | tf_op jit(solution)/shard_map/ppermute | solution.py:173
  43.5 0.3 collective-permute-start.13
  43.9 3.1 %collective-permute-done.14 = bf16[64,256]{1,0:T(8,128)(2,1)S(1)} collective-permute-done((bf16[64,256]{1,0:T(8,128)(2,1)S(1)}, bf16[64,256]{1,0:T(8,128)(2,1)S(1)}, u32[]{:S(2)}, u32[]{:S(2)}) %collective-permute-start.14) | collective-permute-done | bytes 32800 | tf_op jit(solution)/shard_map/ppermute | solution.py:173
  47.0 1.6 %collective-permute-done.13 = bf16[64,256]{1,0:T(8,128)(2,1)S(1)} collective-permute-done((bf16[64,256]{1,0:T(8,128)(2,1)S(1)}, bf16[64,256]{1,0:T(8,128)(2,1)S(1)}, u32[]{:S(2)}, u32[]{:S(2)}) %collective-permute-start.13) | collective-permute-done | bytes 32800 | tf_op jit(solution)/shard_map/ppermute | solution.py:173
  48.6 1.6 %collective-permute-start.15 = (bf16[128,256]{1,0:T(8,128)(2,1)S(1)}, bf16[128,256]{1,0:T(8,128)(2,1)S(1)}, u32[]{:S(2)}, u32[]{:S(2)}) collective-permute-start(bf16[128,256]{1,0:T(8,128)(2,1)S(1)} %pad_maximum_fusion.2.refs_0_), channel_id=1, source_target_pairs={{4,0},{5,1},{6,2},{7,3},{0,4},{1,5},{2,6},{3,7},{12,8},{13,9},{14,... | collective-permute-start | bytes 196616 | tf_op jit(solution)/shard_map/ppermute | solution.py:173
  50.2 0.3 shard_map.70.base
  50.5 1.3 %shard_map.74.refs_2_ = bf16[4,2,256,256]{3,2,1,0:T(8,128)(2,1)S(1)} custom-call(s32[5]{0:T(128)S(1)} %copy-done.8, s32[3,8,8]{2,1,0:T(8,128)S(1)} %copy-done.5, bf16[3,1,256,256]{3,2,1,0:T(8,128)(2,1)S(1)} %copy-done.1, bf16[3,1,256,512]{3,2,1,0:T(8,128)(2,1)S(1)} %copy-done.2, bf16[1,1,256,512]{3,2,1,0:T(8,128)(2,1)S(1)} %collective-permute-done.16.refs_2_), custom_call_target="tpu_custom_call" | custom-call | tf_op jit(solution)/shard_map/pallas_call | solution.py:49
  51.8 1.1 %collective-permute-done.15.refs_1_ = bf16[128,256]{1,0:T(8,128)(2,1)S(1)} collective-permute-done((bf16[128,256]{1,0:T(8,128)(2,1)S(1)}, bf16[128,256]{1,0:T(8,128)(2,1)S(1)}, u32[]{:S(2)}, u32[]{:S(2)}) %collective-permute-start.15) | collective-permute-done | bytes 65568 | tf_op jit(solution)/shard_map/ppermute | solution.py:173
  52.9 0.3 shard_map.75
  53.2 0.1 collective-permute-start.17
  53.3 1.6 %collective-permute-start.22 = (bf16[2,1,256,512]{3,2,1,0:T(8,128)(2,1)S(1)}, bf16[2,1,256,512]{3,2,1,0:T(8,128)(2,1)S(1)}, u32[]{:S(2)}, u32[]{:S(2)}) collective-permute-start(bf16[2,1,256,512]{3,2,1,0:T(8,128)(2,1)S(1)} %get-tuple-element.50), channel_id=1, source_target_pairs={{2,0},{3,1},{0,2},{1,3},{6,4},{7,5},{4,6},{5,7},{10,8},{11,9},{8,1... | collective-permute-start | bytes 1572872 | tf_op jit(solution)/shard_map/ppermute | solution.py:173
  54.9 0.3 collective-permute-start.19
  55.2 1.4 %collective-permute-start.21 = (bf16[64,256]{1,0:T(8,128)(2,1)S(1)}, bf16[64,256]{1,0:T(8,128)(2,1)S(1)}, u32[]{:S(2)}, u32[]{:S(2)}) collective-permute-start(bf16[64,256]{1,0:T(8,128)(2,1)S(1)} %add_convert_fusion.1), channel_id=1, source_target_pairs={{24,0},{25,1},{26,2},{27,3},{28,4},{29,5},{30,6},{31,7},{16,8},{17... | collective-permute-start | bytes 98312 | tf_op jit(solution)/shard_map/ppermute | solution.py:173
  56.6 1.9 %collective-permute-start.20 = (bf16[64,256]{1,0:T(8,128)(2,1)S(1)}, bf16[64,256]{1,0:T(8,128)(2,1)S(1)}, u32[]{:S(2)}, u32[]{:S(2)}) collective-permute-start(bf16[64,256]{1,0:T(8,128)(2,1)S(1)} %add_convert_fusion.1), channel_id=1, source_target_pairs={{16,0},{17,1},{18,2},{19,3},{20,4},{21,5},{22,6},{23,7},{24,8},{25... | collective-permute-start | bytes 98312 | tf_op jit(solution)/shard_map/ppermute | solution.py:173
  58.4 1.2 %collective-permute-start.18 = (bf16[128,256]{1,0:T(8,128)(2,1)S(1)}, bf16[128,256]{1,0:T(8,128)(2,1)S(1)}, u32[]{:S(2)}, u32[]{:S(2)}) collective-permute-start(bf16[128,256]{1,0:T(8,128)(2,1)S(1)} %pad_maximum_fusion.3.refs_0_), channel_id=1, source_target_pairs={{2,0},{3,1},{0,2},{1,3},{6,4},{7,5},{4,6},{5,7},{10,8},{11,9},{8,1... | collective-permute-start | bytes 196616 | tf_op jit(solution)/shard_map/ppermute | solution.py:173
  59.6 1.3 %collective-permute-done.21 = bf16[64,256]{1,0:T(8,128)(2,1)S(1)} collective-permute-done((bf16[64,256]{1,0:T(8,128)(2,1)S(1)}, bf16[64,256]{1,0:T(8,128)(2,1)S(1)}, u32[]{:S(2)}, u32[]{:S(2)}) %collective-permute-start.21) | collective-permute-done | bytes 32800 | tf_op jit(solution)/shard_map/ppermute | solution.py:173
  60.9 1.2 %collective-permute-done.20 = bf16[64,256]{1,0:T(8,128)(2,1)S(1)} collective-permute-done((bf16[64,256]{1,0:T(8,128)(2,1)S(1)}, bf16[64,256]{1,0:T(8,128)(2,1)S(1)}, u32[]{:S(2)}, u32[]{:S(2)}) %collective-permute-start.20) | collective-permute-done | bytes 32800 | tf_op jit(solution)/shard_map/ppermute | solution.py:173
  62.1 1.6 %collective-permute-start.23 = (bf16[128,256]{1,0:T(8,128)(2,1)S(1)}, bf16[128,256]{1,0:T(8,128)(2,1)S(1)}, u32[]{:S(2)}, u32[]{:S(2)}) collective-permute-start(bf16[128,256]{1,0:T(8,128)(2,1)S(1)} %pad_maximum_fusion.4.refs_0_), channel_id=1, source_target_pairs={{4,0},{5,1},{6,2},{7,3},{0,4},{1,5},{2,6},{3,7},{12,8},{13,9},{14,... | collective-permute-start | bytes 196616 | tf_op jit(solution)/shard_map/ppermute | solution.py:173
  63.7 5.4 %collective-permute-done.18.refs_1_ = bf16[128,256]{1,0:T(8,128)(2,1)S(1)} collective-permute-done((bf16[128,256]{1,0:T(8,128)(2,1)S(1)}, bf16[128,256]{1,0:T(8,128)(2,1)S(1)}, u32[]{:S(2)}, u32[]{:S(2)}) %collective-permute-start.18) | collective-permute-done | bytes 65568 | tf_op jit(solution)/shard_map/ppermute | solution.py:173
  69.0 1.3 %shard_map.78.refs_2_ = bf16[4,2,256,256]{3,2,1,0:T(8,128)(2,1)S(1)} custom-call(s32[5]{0:T(128)S(1)} %copy-done.8, s32[3,8,8]{2,1,0:T(8,128)S(1)} %copy-done.5, bf16[3,1,256,256]{3,2,1,0:T(8,128)(2,1)S(1)} %copy-done.1, bf16[3,1,256,512]{3,2,1,0:T(8,128)(2,1)S(1)} %copy-done.2, bf16[2,1,256,512]{3,2,1,0:T(8,128)(2,1)S(1)} %collective-permute-done.22.refs_2_), custom_call_target="tpu_custom_call" | custom-call | tf_op jit(solution)/shard_map/pallas_call | solution.py:49
  70.3 1.3 %shard_map.76.refs_2_ = bf16[4,2,256,256]{3,2,1,0:T(8,128)(2,1)S(1)} custom-call(s32[5]{0:T(128)S(1)} %copy-done.8, s32[3,8,8]{2,1,0:T(8,128)S(1)} %copy-done.5, bf16[3,1,256,256]{3,2,1,0:T(8,128)(2,1)S(1)} %copy-done.1, bf16[3,1,256,512]{3,2,1,0:T(8,128)(2,1)S(1)} %copy-done.2, bf16[2,1,256,512]{3,2,1,0:T(8,128)(2,1)S(1)} %collective-permute-done.22.refs_2_), custom_call_target="tpu_custom_call" | custom-call | tf_op jit(solution)/shard_map/pallas_call | solution.py:49
  71.6 0.3 shard_map.77.base
  71.9 0.3 shard_map.79
  72.2 0.1 collective-permute-start.24
  72.3 1.2 %collective-permute-done.24 = f32[64,256]{1,0:T(8,128)S(1)} collective-permute-done((f32[64,256]{1,0:T(8,128)S(1)}, f32[64,256]{1,0:T(8,128)S(1)}, u32[]{:S(2)}, u32[]{:S(2)}) %collective-permute-start.24) | collective-permute-done | bytes 65568 | tf_op jit(solution)/shard_map/ppermute | solution.py:173
  73.6 1.6 %collective-permute-start.25 = (bf16[64,256]{1,0:T(8,128)(2,1)S(1)}, bf16[64,256]{1,0:T(8,128)(2,1)S(1)}, u32[]{:S(2)}, u32[]{:S(2)}) collective-permute-start(bf16[64,256]{1,0:T(8,128)(2,1)S(1)} %add_convert_fusion.refs_2_), channel_id=1, source_target_pairs={{2,0},{3,1},{0,2},{1,3},{6,4},{7,5},{4,6},{5,7},{10,8},{11,9},{8,1... | collective-permute-start | bytes 98312 | tf_op jit(solution)/shard_map/ppermute | solution.py:173
  75.1 2.4 %collective-permute-done.25.refs_3_ = bf16[64,256]{1,0:T(8,128)(2,1)S(1)} collective-permute-done((bf16[64,256]{1,0:T(8,128)(2,1)S(1)}, bf16[64,256]{1,0:T(8,128)(2,1)S(1)}, u32[]{:S(2)}, u32[]{:S(2)}) %collective-permute-start.25) | collective-permute-done | bytes 32800 | tf_op jit(solution)/shard_map/ppermute | solution.py:173
  77.5 1.4 %shard_map.80 = bf16[3,1,256,128]{3,2,1,0:T(8,128)(2,1)} custom-call(s32[5]{0:T(128)S(1)} %copy-done.8, bf16[128,256]{1,0:T(8,128)(2,1)S(1)} %pad_maximum_fusion.3.refs_0_, bf16[128,256]{1,0:T(8,128)(2,1)S(1)} %collective-permute-done.18.refs_1_, bf16[64,256]{1,0:T(8,128)(2,1)S(1)} %add_convert_fusion.refs_2_, ...), custom_call_target="tpu_custom_call" | custom-call | tf_op jit(solution)/shard_map/pallas_call | solution.py:49
  (41 shorter events, 0.2 us)
Async XLA Ops:
  0.0 9.8 %copy-start.3 = (bf16[3,1,256,256]{3,2,1,0:T(8,128)(2,1)S(1)}, bf16[3,1,256,256]{3,2,1,0:T(8,128)(2,1)}, u32[]{:S(2)}) copy-start(bf16[3,1,256,256]{3,2,1,0:T(8,128)(2,1)} %refs_1_.10) | copy-start | bytes 1179652
  0.6 9.1 %copy-start.1 = (bf16[3,1,256,256]{3,2,1,0:T(8,128)(2,1)S(1)}, bf16[3,1,256,256]{3,2,1,0:T(8,128)(2,1)}, u32[]{:S(2)}) copy-start(bf16[3,1,256,256]{3,2,1,0:T(8,128)(2,1)} %refs_0_.13) | copy-start | bytes 1179652
  0.6 12.9 %copy-start.2 = (bf16[3,1,256,512]{3,2,1,0:T(8,128)(2,1)S(1)}, bf16[3,1,256,512]{3,2,1,0:T(8,128)(2,1)}, u32[]{:S(2)}) copy-start(bf16[3,1,256,512]{3,2,1,0:T(8,128)(2,1)} %refs_1_.13) | copy-start | bytes 2359300
  2.7 10.9 %copy-start = (bf16[3,1,256,512]{3,2,1,0:T(8,128)(2,1)S(1)}, bf16[3,1,256,512]{3,2,1,0:T(8,128)(2,1)}, u32[]{:S(2)}) copy-start(bf16[3,1,256,512]{3,2,1,0:T(8,128)(2,1)} %refs_2_.3) | copy-start | bytes 2359300
  2.7 11.5 %collective-permute-start = (bf16[64,256]{1,0:T(8,128)(2,1)}, bf16[64,256]{1,0:T(8,128)(2,1)S(1)}, u32[]{:S(2)}, u32[]{:S(2)}) collective-permute-start(bf16[64,256]{1,0:T(8,128)(2,1)} %get-tuple-element.28.first), channel_id=1, source_target_pairs={{8,0},{9,1},{10,2},{11,3},{12,4},{13,5},{14,6},{15,7},{0,8},{1,9},... | collective-permute-start | bytes 98312 | tf_op jit(solution)/shard_map/ppermute | solution.py:173
  5.7 8.5 %collective-permute-start.2 = (bf16[64,256]{1,0:T(8,128)(2,1)}, bf16[64,256]{1,0:T(8,128)(2,1)S(1)}, u32[]{:S(2)}, u32[]{:S(2)}) collective-permute-start(bf16[64,256]{1,0:T(8,128)(2,1)} %get-tuple-element.28.first), channel_id=1, source_target_pairs={{24,0},{25,1},{26,2},{27,3},{28,4},{29,5},{30,6},{31,7},{16,8},{17... | collective-permute-start | bytes 98312 | tf_op jit(solution)/shard_map/ppermute | solution.py:173
  8.2 6.0 %collective-permute-start.1 = (bf16[64,256]{1,0:T(8,128)(2,1)}, bf16[64,256]{1,0:T(8,128)(2,1)S(1)}, u32[]{:S(2)}, u32[]{:S(2)}) collective-permute-start(bf16[64,256]{1,0:T(8,128)(2,1)} %get-tuple-element.28.first), channel_id=1, source_target_pairs={{16,0},{17,1},{18,2},{19,3},{20,4},{21,5},{22,6},{23,7},{24,8},{25... | collective-permute-start | bytes 98312 | tf_op jit(solution)/shard_map/ppermute | solution.py:173
  8.3 7.7 %collective-permute-start.4 = (bf16[1,1,256,512]{3,2,1,0:T(8,128)(2,1)}, bf16[1,1,256,512]{3,2,1,0:T(8,128)(2,1)S(1)}, u32[]{:S(2)}, u32[]{:S(2)}) collective-permute-start(bf16[1,1,256,512]{3,2,1,0:T(8,128)(2,1)} %get-tuple-element.39), channel_id=1, source_target_pairs={{2,0},{3,1},{0,2},{1,3},{6,4},{7,5},{4,6},{5,7},{10,8},{11,9},{8,1... | collective-permute-start | bytes 786440 | tf_op jit(solution)/shard_map/ppermute | solution.py:173
  9.8 0.9 %copy-start.4 = (bf16[3,1,256,128]{3,2,1,0:T(8,128)(2,1)S(1)}, bf16[3,1,256,128]{3,2,1,0:T(8,128)(2,1)}, u32[]{:S(2)}) copy-start(bf16[3,1,256,128]{3,2,1,0:T(8,128)(2,1)} %rhs.3) | copy-start | bytes 589828
  10.7 0.8 copy-start.6
  11.5 0.6 copy-start.7
  14.2 1.7 %copy-start.5 = (s32[3,8,8]{2,1,0:T(8,128)S(1)}, s32[3,8,8]{2,1,0:T(8,128)}, u32[]{:S(2)}) copy-start(s32[3,8,8]{2,1,0:T(8,128)} %pattern.11) | copy-start | bytes 2308
  14.2 4.3 %collective-permute-start.3 = (bf16[128,256]{1,0:T(8,128)(2,1)S(1)}, bf16[128,256]{1,0:T(8,128)(2,1)S(1)}, u32[]{:S(2)}, u32[]{:S(2)}) collective-permute-start(bf16[128,256]{1,0:T(8,128)(2,1)S(1)} %pad_maximum_fusion.refs_0_), channel_id=1, source_target_pairs={{4,0},{5,1},{6,2},{7,3},{0,4},{1,5},{2,6},{3,7},{12,8},{13,9},{14,... | collective-permute-start | bytes 196616 | tf_op jit(solution)/shard_map/ppermute | solution.py:173
  18.9 1.3 %collective-permute-start.5 = (f32[64,256]{1,0:T(8,128)S(1)}, f32[64,256]{1,0:T(8,128)S(1)}, u32[]{:S(2)}, u32[]{:S(2)}) collective-permute-start(f32[64,256]{1,0:T(8,128)S(1)} %shard_map.68), channel_id=1, source_target_pairs={{1,0},{0,1},{3,2},{2,3},{5,4},{4,5},{7,6},{6,7},{9,8},{8,9},{11,10... | collective-permute-start | bytes 196616 | tf_op jit(solution)/shard_map/ppermute | solution.py:173
  20.2 4.9 %collective-permute-start.6 = (bf16[64,256]{1,0:T(8,128)(2,1)S(1)}, bf16[64,256]{1,0:T(8,128)(2,1)S(1)}, u32[]{:S(2)}, u32[]{:S(2)}) collective-permute-start(bf16[64,256]{1,0:T(8,128)(2,1)S(1)} %add_convert_fusion.3), channel_id=1, source_target_pairs={{8,0},{9,1},{10,2},{11,3},{12,4},{13,5},{14,6},{15,7},{0,8},{1,9},... | collective-permute-start | bytes 98312 | tf_op jit(solution)/shard_map/ppermute | solution.py:173
  22.1 13.7 %collective-permute-start.9 = (bf16[2,1,256,512]{3,2,1,0:T(8,128)(2,1)S(1)}, bf16[2,1,256,512]{3,2,1,0:T(8,128)(2,1)S(1)}, u32[]{:S(2)}, u32[]{:S(2)}) collective-permute-start(bf16[2,1,256,512]{3,2,1,0:T(8,128)(2,1)S(1)} %get-tuple-element.43), channel_id=1, source_target_pairs={{2,0},{3,1},{0,2},{1,3},{6,4},{7,5},{4,6},{5,7},{10,8},{11,9},{8,1... | collective-permute-start | bytes 1572872 | tf_op jit(solution)/shard_map/ppermute | solution.py:173
  22.6 5.8 %collective-permute-start.8 = (bf16[64,256]{1,0:T(8,128)(2,1)S(1)}, bf16[64,256]{1,0:T(8,128)(2,1)S(1)}, u32[]{:S(2)}, u32[]{:S(2)}) collective-permute-start(bf16[64,256]{1,0:T(8,128)(2,1)S(1)} %add_convert_fusion.3), channel_id=1, source_target_pairs={{24,0},{25,1},{26,2},{27,3},{28,4},{29,5},{30,6},{31,7},{16,8},{17... | collective-permute-start | bytes 98312 | tf_op jit(solution)/shard_map/ppermute | solution.py:173
  25.1 4.8 %collective-permute-start.7 = (bf16[64,256]{1,0:T(8,128)(2,1)S(1)}, bf16[64,256]{1,0:T(8,128)(2,1)S(1)}, u32[]{:S(2)}, u32[]{:S(2)}) collective-permute-start(bf16[64,256]{1,0:T(8,128)(2,1)S(1)} %add_convert_fusion.3), channel_id=1, source_target_pairs={{16,0},{17,1},{18,2},{19,3},{20,4},{21,5},{22,6},{23,7},{24,8},{25... | collective-permute-start | bytes 98312 | tf_op jit(solution)/shard_map/ppermute | solution.py:173
  29.9 8.2 %collective-permute-start.10 = (bf16[128,256]{1,0:T(8,128)(2,1)S(1)}, bf16[128,256]{1,0:T(8,128)(2,1)S(1)}, u32[]{:S(2)}, u32[]{:S(2)}) collective-permute-start(bf16[128,256]{1,0:T(8,128)(2,1)S(1)} %pad_maximum_fusion.1.refs_0_), channel_id=1, source_target_pairs={{4,0},{5,1},{6,2},{7,3},{0,4},{1,5},{2,6},{3,7},{12,8},{13,9},{14,... | collective-permute-start | bytes 196616 | tf_op jit(solution)/shard_map/ppermute | solution.py:173
  38.4 1.3 %collective-permute-start.11 = (f32[64,256]{1,0:T(8,128)S(1)}, f32[64,256]{1,0:T(8,128)S(1)}, u32[]{:S(2)}, u32[]{:S(2)}) collective-permute-start(f32[64,256]{1,0:T(8,128)S(1)} %shard_map.73), channel_id=1, source_target_pairs={{1,0},{0,1},{3,2},{2,3},{5,4},{4,5},{7,6},{6,7},{9,8},{8,9},{11,10... | collective-permute-start | bytes 196616 | tf_op jit(solution)/shard_map/ppermute | solution.py:173
  39.8 4.1 %collective-permute-start.12 = (bf16[64,256]{1,0:T(8,128)(2,1)S(1)}, bf16[64,256]{1,0:T(8,128)(2,1)S(1)}, u32[]{:S(2)}, u32[]{:S(2)}) collective-permute-start(bf16[64,256]{1,0:T(8,128)(2,1)S(1)} %add_convert_fusion.2), channel_id=1, source_target_pairs={{8,0},{9,1},{10,2},{11,3},{12,4},{13,5},{14,6},{15,7},{0,8},{1,9},... | collective-permute-start | bytes 98312 | tf_op jit(solution)/shard_map/ppermute | solution.py:173
  40.2 10.3 %collective-permute-start.16 = (bf16[1,1,256,512]{3,2,1,0:T(8,128)(2,1)S(1)}, bf16[1,1,256,512]{3,2,1,0:T(8,128)(2,1)S(1)}, u32[]{:S(2)}, u32[]{:S(2)}) collective-permute-start(bf16[1,1,256,512]{3,2,1,0:T(8,128)(2,1)S(1)} %get-tuple-element.47), channel_id=1, source_target_pairs={{2,0},{3,1},{0,2},{1,3},{6,4},{7,5},{4,6},{5,7},{10,8},{11,9},{8,1... | collective-permute-start | bytes 786440 | tf_op jit(solution)/shard_map/ppermute | solution.py:173
  40.9 6.1 %collective-permute-start.14 = (bf16[64,256]{1,0:T(8,128)(2,1)S(1)}, bf16[64,256]{1,0:T(8,128)(2,1)S(1)}, u32[]{:S(2)}, u32[]{:S(2)}) collective-permute-start(bf16[64,256]{1,0:T(8,128)(2,1)S(1)} %add_convert_fusion.2), channel_id=1, source_target_pairs={{24,0},{25,1},{26,2},{27,3},{28,4},{29,5},{30,6},{31,7},{16,8},{17... | collective-permute-start | bytes 98312 | tf_op jit(solution)/shard_map/ppermute | solution.py:173
  43.5 5.0 %collective-permute-start.13 = (bf16[64,256]{1,0:T(8,128)(2,1)S(1)}, bf16[64,256]{1,0:T(8,128)(2,1)S(1)}, u32[]{:S(2)}, u32[]{:S(2)}) collective-permute-start(bf16[64,256]{1,0:T(8,128)(2,1)S(1)} %add_convert_fusion.2), channel_id=1, source_target_pairs={{16,0},{17,1},{18,2},{19,3},{20,4},{21,5},{22,6},{23,7},{24,8},{25... | collective-permute-start | bytes 98312 | tf_op jit(solution)/shard_map/ppermute | solution.py:173
  48.6 1.9 %copy-start.8 = (s32[5]{0:T(128)S(1)}, s32[5]{0:T(128)}, u32[]{:S(2)}) copy-start(s32[5]{0:T(128)} %stack.23.spot.sign) | copy-start | bytes 64
  48.6 4.3 %collective-permute-start.15 = (bf16[128,256]{1,0:T(8,128)(2,1)S(1)}, bf16[128,256]{1,0:T(8,128)(2,1)S(1)}, u32[]{:S(2)}, u32[]{:S(2)}) collective-permute-start(bf16[128,256]{1,0:T(8,128)(2,1)S(1)} %pad_maximum_fusion.2.refs_0_), channel_id=1, source_target_pairs={{4,0},{5,1},{6,2},{7,3},{0,4},{1,5},{2,6},{3,7},{12,8},{13,9},{14,... | collective-permute-start | bytes 196616 | tf_op jit(solution)/shard_map/ppermute | solution.py:173
  53.2 1.6 %collective-permute-start.17 = (f32[64,256]{1,0:T(8,128)S(1)}, f32[64,256]{1,0:T(8,128)S(1)}, u32[]{:S(2)}, u32[]{:S(2)}) collective-permute-start(f32[64,256]{1,0:T(8,128)S(1)} %shard_map.75), channel_id=1, source_target_pairs={{1,0},{0,1},{3,2},{2,3},{5,4},{4,5},{7,6},{6,7},{9,8},{8,9},{11,10... | collective-permute-start | bytes 196616 | tf_op jit(solution)/shard_map/ppermute | solution.py:173
  53.3 15.7 %collective-permute-start.22 = (bf16[2,1,256,512]{3,2,1,0:T(8,128)(2,1)S(1)}, bf16[2,1,256,512]{3,2,1,0:T(8,128)(2,1)S(1)}, u32[]{:S(2)}, u32[]{:S(2)}) collective-permute-start(bf16[2,1,256,512]{3,2,1,0:T(8,128)(2,1)S(1)} %get-tuple-element.50), channel_id=1, source_target_pairs={{2,0},{3,1},{0,2},{1,3},{6,4},{7,5},{4,6},{5,7},{10,8},{11,9},{8,1... | collective-permute-start | bytes 1572872 | tf_op jit(solution)/shard_map/ppermute | solution.py:173
  54.9 4.7 %collective-permute-start.19 = (bf16[64,256]{1,0:T(8,128)(2,1)S(1)}, bf16[64,256]{1,0:T(8,128)(2,1)S(1)}, u32[]{:S(2)}, u32[]{:S(2)}) collective-permute-start(bf16[64,256]{1,0:T(8,128)(2,1)S(1)} %add_convert_fusion.1), channel_id=1, source_target_pairs={{8,0},{9,1},{10,2},{11,3},{12,4},{13,5},{14,6},{15,7},{0,8},{1,9},... | collective-permute-start | bytes 98312 | tf_op jit(solution)/shard_map/ppermute | solution.py:173
  55.2 5.7 %collective-permute-start.21 = (bf16[64,256]{1,0:T(8,128)(2,1)S(1)}, bf16[64,256]{1,0:T(8,128)(2,1)S(1)}, u32[]{:S(2)}, u32[]{:S(2)}) collective-permute-start(bf16[64,256]{1,0:T(8,128)(2,1)S(1)} %add_convert_fusion.1), channel_id=1, source_target_pairs={{24,0},{25,1},{26,2},{27,3},{28,4},{29,5},{30,6},{31,7},{16,8},{17... | collective-permute-start | bytes 98312 | tf_op jit(solution)/shard_map/ppermute | solution.py:173
  56.6 5.5 %collective-permute-start.20 = (bf16[64,256]{1,0:T(8,128)(2,1)S(1)}, bf16[64,256]{1,0:T(8,128)(2,1)S(1)}, u32[]{:S(2)}, u32[]{:S(2)}) collective-permute-start(bf16[64,256]{1,0:T(8,128)(2,1)S(1)} %add_convert_fusion.1), channel_id=1, source_target_pairs={{16,0},{17,1},{18,2},{19,3},{20,4},{21,5},{22,6},{23,7},{24,8},{25... | collective-permute-start | bytes 98312 | tf_op jit(solution)/shard_map/ppermute | solution.py:173
  58.4 10.6 %collective-permute-start.18 = (bf16[128,256]{1,0:T(8,128)(2,1)S(1)}, bf16[128,256]{1,0:T(8,128)(2,1)S(1)}, u32[]{:S(2)}, u32[]{:S(2)}) collective-permute-start(bf16[128,256]{1,0:T(8,128)(2,1)S(1)} %pad_maximum_fusion.3.refs_0_), channel_id=1, source_target_pairs={{2,0},{3,1},{0,2},{1,3},{6,4},{7,5},{4,6},{5,7},{10,8},{11,9},{8,1... | collective-permute-start | bytes 196616 | tf_op jit(solution)/shard_map/ppermute | solution.py:173
  62.1 9.8 %collective-permute-start.23 = (bf16[128,256]{1,0:T(8,128)(2,1)S(1)}, bf16[128,256]{1,0:T(8,128)(2,1)S(1)}, u32[]{:S(2)}, u32[]{:S(2)}) collective-permute-start(bf16[128,256]{1,0:T(8,128)(2,1)S(1)} %pad_maximum_fusion.4.refs_0_), channel_id=1, source_target_pairs={{4,0},{5,1},{6,2},{7,3},{0,4},{1,5},{2,6},{3,7},{12,8},{13,9},{14,... | collective-permute-start | bytes 196616 | tf_op jit(solution)/shard_map/ppermute | solution.py:173
  72.2 1.3 %collective-permute-start.24 = (f32[64,256]{1,0:T(8,128)S(1)}, f32[64,256]{1,0:T(8,128)S(1)}, u32[]{:S(2)}, u32[]{:S(2)}) collective-permute-start(f32[64,256]{1,0:T(8,128)S(1)} %shard_map.79), channel_id=1, source_target_pairs={{1,0},{0,1},{3,2},{2,3},{5,4},{4,5},{7,6},{6,7},{9,8},{8,9},{11,10... | collective-permute-start | bytes 196616 | tf_op jit(solution)/shard_map/ppermute | solution.py:173
  73.6 4.0 %collective-permute-start.25 = (bf16[64,256]{1,0:T(8,128)(2,1)S(1)}, bf16[64,256]{1,0:T(8,128)(2,1)S(1)}, u32[]{:S(2)}, u32[]{:S(2)}) collective-permute-start(bf16[64,256]{1,0:T(8,128)(2,1)S(1)} %add_convert_fusion.refs_2_), channel_id=1, source_target_pairs={{2,0},{3,1},{0,2},{1,3},{6,4},{7,5},{4,6},{5,7},{10,8},{11,9},{8,1... | collective-permute-start | bytes 98312 | tf_op jit(solution)/shard_map/ppermute | solution.py:173

commit v2 on v0

--- a/solution.py
+++ b/solution.py
@@ -35,7 +35,7 @@
     return array, pl.BlockSpec(shape, lambda step: (level,) + (0,) * (len(shape) - 1))
 
 
-def call(kernel, shapes, operands, scalars=0, scratch=(), room=VMEM_BYTES):
+def call(kernel, shapes, operands, scalars=0, scratch=(), room=VMEM_BYTES, out_spec=None, aliases=None):
     arrays, specs = [], []
     for place, operand in enumerate(operands):
         if isinstance(operand, tuple):
@@ -51,7 +51,9 @@
         grid=(1,),
         out_shape=shapes,
         in_specs=specs,
-        out_specs=jax.tree.map(lambda _: pl.BlockSpec(memory_space=pltpu.VMEM), shapes),
+        out_specs=out_spec
+        or jax.tree.map(lambda _: pl.BlockSpec(memory_space=pltpu.VMEM), shapes),
+        input_output_aliases=aliases or {},
         scratch_shapes=list(scratch),
         compiler_params=pltpu.CompilerParams(vmem_limit_bytes=room),
     )(*arrays)
@@ -112,6 +114,35 @@
                     out[slot, low] = part
 
 
+def direct_kernel(pair, lines, chips, spot, pattern, base, inverse, *refs):
+    pieces, stacks, out, blocks = refs[:chips], refs[chips:-2], refs[-2], refs[-1]
+    row, chip, core = spot[ROW], spot[CHIP], spot[CORE]
+    depth, line = spot[DEPTH], spot[LINE]
+    share, size = base.shape
+    for index, stack in enumerate(stacks):
+        for turn in range(chips):
+            blocks[index * chips + turn] = stack[turn * share : (turn + 1) * share, :]
+
+    def times(left, right):
+        return lax.dot_general(
+            left, right, (((1,), (1,)), ((), ())), preferred_element_type=jnp.float32
+        )
+
+    total = jnp.zeros((share, size), jnp.float32)
+    for index, piece in enumerate(pieces):
+        deep = (chip ^ index) * CORES + core
+        turn = (deep // CORES) ^ (depth // CORES)
+        for across in range(lines):
+            keep = pattern[pair, row, deep * lines + across]
+            matrix = piece[0, 0, :, across * size : (across + 1) * size]
+            matrix = jnp.where(keep > 0, matrix, jnp.zeros_like(matrix))
+            total = total + times(blocks[(across ^ line) * chips + turn], matrix)
+    value = base[...]
+    for part in split(total, 3):
+        value = value - times(part, inverse[0, 0])
+    out[...] = value
+
+
 def step_kernel(lines, base, *refs):
     out = refs[-1]
     refs = refs[:-1]
@@ -129,19 +160,25 @@
     out[...] = total
 
 
-def last_kernel(levels, chips, spot, *refs):
+def late_kernel(levels, chips, spot, *refs):
     out, turned = refs[-2], refs[-1]
     share = turned.shape[0] // chips
-    chip = spot[CHIP]
-    at = [pl.ds(pl.multiple_of((chip ^ b) * share, share), share) for b in range(chips)]
-    for level in range(levels):
+    out[0] = jnp.zeros_like(out[0])
+    for level in range(1, levels):
         for b in range(chips):
-            if level > 0:
-                part = refs[b][(level - 1) * share : level * share, :]
-            else:
-                part = refs[chips + b][...]
-            turned[at[b], :] = part.astype(jnp.float32)
+            at = pl.ds(pl.multiple_of((spot[CHIP] ^ b) * share, share), share)
+            part = refs[b][(level - 1) * share : level * share, :]
+            turned[at, :] = part.astype(jnp.float32)
         out[level, 0] = turned[...].T.astype(out.dtype)
+
+
+def last_kernel(chips, spot, whole, *refs):
+    out, turned = refs[-2], refs[-1]
+    share = turned.shape[0] // chips
+    for b in range(chips):
+        at = pl.ds(pl.multiple_of((spot[CHIP] ^ b) * share, share), share)
+        turned[at, :] = refs[b][...].astype(jnp.float32)
+    out[0, 0] = turned[...].T.astype(out.dtype)
 
 
 def make_body(rows, cols):
@@ -275,10 +312,20 @@
         forward, backward, upward = {}, {}, {}
         fetched[0] = wide(stack)
         for level in range(1, top):
-            fold_lower(level, False, stack)
             value = starts[level]
-            for earlier in range(level):
-                value = step(value, [(fetched[earlier], forward[pair_index(level, earlier)])])
+            if level == 1:
+                pieces = [level_of(blocks, 0) for blocks in [lower_blocks] + low_all]
+                value = call(
+                    functools.partial(direct_kernel, 0, lines, chips),
+                    piece,
+                    [spot, pattern, value, level_of(lower_inverse, 1)] + pieces + fetched[0],
+                    scalars=2,
+                    scratch=[pltpu.VMEM((near * lines, share, size), jnp.bfloat16)],
+                )
+            else:
+                fold_lower(level, False, stack)
+                for earlier in range(level):
+                    value = step(value, [(fetched[earlier], forward[pair_index(level, earlier)])])
             stack = deep(settle(value), lambda sign: fold_lower(level, True, sign))
             if level == top - 1:
                 stack = after(stack, *high_one)
@@ -296,24 +343,30 @@
                 value = step(value, [(back[later], upward[later, level])])
             solved[level] = settle(value)
             if level > 0:
-                work = None
-                if level < top:
-                    work = lambda sign: fold_upper(top, level - 1, sign)
                 found = solved[level]
                 if level == 1:
                     found = after(found, *high_rest)
-                stack = deep(found, work)
+                stack = deep(found)
                 back[level] = wide(stack)
                 for later in range(level, levels):
-                    if (later, level - 1) not in upward:
-                        fold_upper(later, level - 1, stack)
-        results += collect(solved[0])
-        return call(
-            functools.partial(last_kernel, levels, chips),
-            jax.ShapeDtypeStruct((levels, 1, size, width), jnp.bfloat16),
+                    fold_upper(later, level - 1, stack)
+        shape = jax.ShapeDtypeStruct((levels, 1, size, width), jnp.bfloat16)
+        whole = call(
+            functools.partial(late_kernel, levels, chips),
+            shape,
             [spot] + results,
             scalars=1,
             scratch=[turned],
+        )
+        operands = [spot, (whole, pl.BlockSpec(memory_space=pl.ANY))] + collect(solved[0])
+        return call(
+            functools.partial(last_kernel, chips),
+            shape,
+            operands,
+            scalars=1,
+            scratch=[turned],
+            out_spec=pl.BlockSpec((1, 1, size, width), lambda step: (0, 0, 0, 0)),
+            aliases={1: 0},
         )
 
     return body

time: 75.9 us -> 74.5 us (0.982)
  waiting for transfers between devices: 26.7 us -> 24.2 us
  Pallas kernels: 15.4 us -> 16.5 us
    ppermute x25, waiting for transfers between devices: 26.7 us -> 24.2 us  [send(): return lax.ppermute(value, ('prow', 'pcol'), pairs)]
    pallas_call x16, Pallas kernels: 15.4 us -> 16.5 us  [call(): pl.pallas_call(kernel, grid=(1,), out_shape=shapes, in_specs=specs, out_s...]
  transfers between devices with their start and end apart: 25 -> 25, of which waited for: 16 -> 16; matrix products, arithmetic and copies ran while one was open for 4% -> 4% of each run, Pallas kernels for 17% -> 18%
where the time goes in v2:
time: 74.5 us; the launch traced here: 74.3 us
  starting transfers between devices  29.7 us (40%)
  waiting for transfers between devices  24.2 us (32%)
  Pallas kernels  16.5 us (22%)
  local copies, waits for them, and re-layouts  3.58 us (5%)
    ppermute x25, starting transfers between devices, send(): return lax.ppermute(value, ('prow', 'pcol'), pairs)  29.7 us
    ppermute x25, waiting for transfers between devices, send(): return lax.ppermute(value, ('prow', 'pcol'), pairs)  24.2 us
    pallas_call x16, Pallas kernels, call(): pl.pallas_call(kernel, grid=(1,), out_shape=shapes, in_specs=specs, out_s...  16.5 us
    slice x2, local copies, waits for them, and re-layouts, body(): parts = (upper_blocks[last_pair:], upper_blocks[:last_pair])  2.49 us
  transfers between devices with their start and end apart: 25, of which 16 were waited for; matrix products, arithmetic and copies ran while one was open for 4% of the time, Pallas kernels for 18%

profile of v2, /device:TPU:0, one launch (start us, length us, event | category | flops | bytes accessed | tf_op | source)
XLA Modules:
  0.0 74.3 jit_solution(6367682159618532095)
XLA Ops:
  0.0 2.9 %collective-permute-start.4 = (bf16[3,1,256,512]{3,2,1,0:T(8,128)(2,1)}, bf16[3,1,256,512]{3,2,1,0:T(8,128)(2,1)S(1)}, u32[]{:S(2)}, u32[]{:S(2)}) collective-permute-start(bf16[3,1,256,512]{3,2,1,0:T(8,128)(2,1)} %refs_2_.3), channel_id=1, source_target_pairs={{2,0},{3,1},{0,2},{1,3},{6,4},{7,5},{4,6},{5,7},{10,8},{11,9},{8,1... | collective-permute-start | bytes 2359304 | tf_op jit(solution)/shard_map/ppermute | solution.py:204
  2.9 0.6 stack.23.spot
  3.5 1.8 %shard_map.64.first = bf16[64,256]{1,0:T(8,128)(2,1)} custom-call(s32[5]{0:T(128)} %stack.23.spot, bf16[3,1,256,128]{3,2,1,0:T(8,128)(2,1)} %rhs.3, bf16[3,1,256,256]{3,2,1,0:T(8,128)(2,1)} %refs_1_.6), custom_call_target="tpu_custom_call" | custom-call | tf_op jit(solution)/shard_map/pallas_call | solution.py:49
  5.3 1.6 %collective-permute-start = (bf16[64,256]{1,0:T(8,128)(2,1)}, bf16[64,256]{1,0:T(8,128)(2,1)S(1)}, u32[]{:S(2)}, u32[]{:S(2)}) collective-permute-start(bf16[64,256]{1,0:T(8,128)(2,1)} %shard_map.64.first), channel_id=1, source_target_pairs={{8,0},{9,1},{10,2},{11,3},{12,4},{13,5},{14,6},{15,7},{0,8},{1,9},... | collective-permute-start | bytes 98312 | tf_op jit(solution)/shard_map/ppermute | solution.py:204
  6.9 2.5 %collective-permute-start.2 = (bf16[64,256]{1,0:T(8,128)(2,1)}, bf16[64,256]{1,0:T(8,128)(2,1)S(1)}, u32[]{:S(2)}, u32[]{:S(2)}) collective-permute-start(bf16[64,256]{1,0:T(8,128)(2,1)} %shard_map.64.first), channel_id=1, source_target_pairs={{24,0},{25,1},{26,2},{27,3},{28,4},{29,5},{30,6},{31,7},{16,8},{17... | collective-permute-start | bytes 98312 | tf_op jit(solution)/shard_map/ppermute | solution.py:204
  9.4 0.1 collective-permute-start.1
  9.5 1.7 %slice.6 = bf16[1,1,256,512]{3,2,1,0:T(8,128)(2,1)} slice(bf16[3,1,256,512]{3,2,1,0:T(8,128)(2,1)} %refs_1_.9), slice={[2:3], [0:1], [0:256], [0:512]} | slice | bytes 524288 | tf_op jit(solution)/shard_map/slice | solution.py:286
  11.2 0.0 copy-start.6
  11.2 0.8 %slice.7 = bf16[2,1,256,512]{3,2,1,0:T(8,128)(2,1)} slice(bf16[3,1,256,512]{3,2,1,0:T(8,128)(2,1)S(1)} %copy-done.1), slice={[0:2], [0:1], [0:256], [0:512]} | slice | bytes 1048576 | tf_op jit(solution)/shard_map/slice | solution.py:286
  12.0 0.2 copy-done
  12.2 0.2 copy-done.2
  12.5 0.0 copy-done.4
  12.5 1.4 %shard_map.65 = (f32[64,256]{1,0:T(8,128)S(1)}, f32[64,256]{1,0:T(8,128)S(1)}, f32[64,256]{1,0:T(8,128)S(1)}, f32[64,256]{1,0:T(8,128)S(1)}) custom-call(s32[5]{0:T(128)S(1)} %copy-done.7, bf16[64,256]{1,0:T(8,128)(2,1)S(1)} %copy-done.6, bf16[3,1,256,128]{3,2,1,0:T(8,128)(2,1)S(1)} %copy-done.4, bf16[3,1,256,256]{3,2,1,0:T(8,128)(2,1)S(1)} %copy-done.2, ...), custom_call_target="tpu_custom_call" | custom-call | tf_op jit(solution)/shard_map/pallas_call | solution.py:49
  13.9 0.0 collective-permute-done
  14.0 0.8 %collective-permute-done.1 = bf16[64,256]{1,0:T(8,128)(2,1)S(1)} collective-permute-done((bf16[64,256]{1,0:T(8,128)(2,1)}, bf16[64,256]{1,0:T(8,128)(2,1)S(1)}, u32[]{:S(2)}, u32[]{:S(2)}) %collective-permute-start.1) | collective-permute-done | bytes 32800 | tf_op jit(solution)/shard_map/ppermute | solution.py:204
  14.8 1.6 %collective-permute-start.3 = (bf16[128,256]{1,0:T(8,128)(2,1)S(1)}, bf16[128,256]{1,0:T(8,128)(2,1)S(1)}, u32[]{:S(2)}, u32[]{:S(2)}) collective-permute-start(bf16[128,256]{1,0:T(8,128)(2,1)S(1)} %pad_maximum_fusion.refs_2_.refs_0_), channel_id=1, source_target_pairs={{4,0},{5,1},{6,2},{7,3},{0,4},{1,5},{2,6},{3,7},{12,8},{13,9},{14,... | collective-permute-start | bytes 196616 | tf_op jit(solution)/shard_map/ppermute | solution.py:204
  16.4 2.7 %collective-permute-done.3.refs_3_.refs_1_ = bf16[128,256]{1,0:T(8,128)(2,1)S(1)} collective-permute-done((bf16[128,256]{1,0:T(8,128)(2,1)S(1)}, bf16[128,256]{1,0:T(8,128)(2,1)S(1)}, u32[]{:S(2)}, u32[]{:S(2)}) %collective-permute-start.3) | collective-permute-done | bytes 65568 | tf_op jit(solution)/shard_map/ppermute | solution.py:204
  19.1 1.6 %collective-permute-done.4.refs_1_.refs_3_ = bf16[3,1,256,512]{3,2,1,0:T(8,128)(2,1)S(1)} collective-permute-done((bf16[3,1,256,512]{3,2,1,0:T(8,128)(2,1)}, bf16[3,1,256,512]{3,2,1,0:T(8,128)(2,1)S(1)}, u32[]{:S(2)}, u32[]{:S(2)}) %collective-permute-start.4) | collective-permute-done | bytes 786464 | tf_op jit(solution)/shard_map/ppermute | solution.py:204
  20.7 1.4 %shard_map.66 = f32[64,256]{1,0:T(8,128)S(1)} custom-call(s32[5]{0:T(128)S(1)} %copy-done.7, s32[3,8,8]{2,1,0:T(8,128)S(1)} %copy-done.5, f32[64,256]{1,0:T(8,128)S(1)} %get-tuple-element.26.base, bf16[3,1,256,256]{3,2,1,0:T(8,128)(2,1)S(1)} %copy-done.2, bf16[3,1,256,512]{3,2,1,0:T(8,128)(2,1)S(1)} %copy-done.3, ...), custom_call_target="tpu_custom_call" | custom-call | tf_op jit(solution)/shard_map/pallas_call | solution.py:49
  22.1 0.1 collective-permute-start.5
  22.2 1.2 %collective-permute-done.5 = f32[64,256]{1,0:T(8,128)S(1)} collective-permute-done((f32[64,256]{1,0:T(8,128)S(1)}, f32[64,256]{1,0:T(8,128)S(1)}, u32[]{:S(2)}, u32[]{:S(2)}) %collective-permute-start.5) | collective-permute-done | bytes 65568 | tf_op jit(solution)/shard_map/ppermute | solution.py:204
  23.4 1.9 %collective-permute-start.6 = (bf16[64,256]{1,0:T(8,128)(2,1)S(1)}, bf16[64,256]{1,0:T(8,128)(2,1)S(1)}, u32[]{:S(2)}, u32[]{:S(2)}) collective-permute-start(bf16[64,256]{1,0:T(8,128)(2,1)S(1)} %add_convert_fusion.3), channel_id=1, source_target_pairs={{8,0},{9,1},{10,2},{11,3},{12,4},{13,5},{14,6},{15,7},{0,8},{1,9},... | collective-permute-start | bytes 98312 | tf_op jit(solution)/shard_map/ppermute | solution.py:204
  25.3 1.5 %collective-permute-start.9 = (bf16[1,1,256,512]{3,2,1,0:T(8,128)(2,1)S(1)}, bf16[1,1,256,512]{3,2,1,0:T(8,128)(2,1)S(1)}, u32[]{:S(2)}, u32[]{:S(2)}) collective-permute-start(bf16[1,1,256,512]{3,2,1,0:T(8,128)(2,1)S(1)} %copy-done.9), channel_id=1, source_target_pairs={{2,0},{3,1},{0,2},{1,3},{6,4},{7,5},{4,6},{5,7},{10,8},{11,9},{8,1... | collective-permute-start | bytes 786440 | tf_op jit(solution)/shard_map/ppermute | solution.py:204
  26.8 2.5 %collective-permute-start.8 = (bf16[64,256]{1,0:T(8,128)(2,1)S(1)}, bf16[64,256]{1,0:T(8,128)(2,1)S(1)}, u32[]{:S(2)}, u32[]{:S(2)}) collective-permute-start(bf16[64,256]{1,0:T(8,128)(2,1)S(1)} %add_convert_fusion.3), channel_id=1, source_target_pairs={{24,0},{25,1},{26,2},{27,3},{28,4},{29,5},{30,6},{31,7},{16,8},{17... | collective-permute-start | bytes 98312 | tf_op jit(solution)/shard_map/ppermute | solution.py:204
  29.3 0.1 collective-permute-start.7
  29.4 1.6 %shard_map.67.refs_2_ = bf16[4,2,256,256]{3,2,1,0:T(8,128)(2,1)S(1)} custom-call(s32[5]{0:T(128)S(1)} %copy-done.7, s32[3,8,8]{2,1,0:T(8,128)S(1)} %copy-done.5, bf16[3,1,256,256]{3,2,1,0:T(8,128)(2,1)S(1)} %copy-done, bf16[3,1,256,256]{3,2,1,0:T(8,128)(2,1)S(1)} %copy-done.2, bf16[3,1,256,512]{3,2,1,0:T(8,128)(2,1)S(1)} %copy-done.3, ...), custom_call_target="tpu_custom_call" | custom-call | tf_op jit(solution)/shard_map/pallas_call | solution.py:49
  31.0 1.9 %collective-permute-done.8 = bf16[64,256]{1,0:T(8,128)(2,1)S(1)} collective-permute-done((bf16[64,256]{1,0:T(8,128)(2,1)S(1)}, bf16[64,256]{1,0:T(8,128)(2,1)S(1)}, u32[]{:S(2)}, u32[]{:S(2)}) %collective-permute-start.8) | collective-permute-done | bytes 32800 | tf_op jit(solution)/shard_map/ppermute | solution.py:204
  33.0 1.5 %collective-permute-done.7 = bf16[64,256]{1,0:T(8,128)(2,1)S(1)} collective-permute-done((bf16[64,256]{1,0:T(8,128)(2,1)S(1)}, bf16[64,256]{1,0:T(8,128)(2,1)S(1)}, u32[]{:S(2)}, u32[]{:S(2)}) %collective-permute-start.7) | collective-permute-done | bytes 32800 | tf_op jit(solution)/shard_map/ppermute | solution.py:204
  34.5 1.6 %collective-permute-start.10 = (bf16[128,256]{1,0:T(8,128)(2,1)S(1)}, bf16[128,256]{1,0:T(8,128)(2,1)S(1)}, u32[]{:S(2)}, u32[]{:S(2)}) collective-permute-start(bf16[128,256]{1,0:T(8,128)(2,1)S(1)} %pad_maximum_fusion.1.refs_0_), channel_id=1, source_target_pairs={{4,0},{5,1},{6,2},{7,3},{0,4},{1,5},{2,6},{3,7},{12,8},{13,9},{14,... | collective-permute-start | bytes 196616 | tf_op jit(solution)/shard_map/ppermute | solution.py:204
  36.1 2.0 %shard_map.69 = (bf16[4,2,256,256]{3,2,1,0:T(8,128)(2,1)S(1)}, bf16[4,2,256,256]{3,2,1,0:T(8,128)(2,1)S(1)}) custom-call(s32[5]{0:T(128)S(1)} %copy-done.7, s32[3,8,8]{2,1,0:T(8,128)S(1)} %copy-done.5, bf16[3,1,256,256]{3,2,1,0:T(8,128)(2,1)S(1)} %copy-done, bf16[3,1,256,256]{3,2,1,0:T(8,128)(2,1)S(1)} %copy-done.2, bf16[3,1,256,512]{3,2,1,0:T(8,128)(2,1)S(1)} %copy-done.3, ...), custom_call_target="tpu_custom_call" | custom-call | tf_op jit(solution)/shard_map/pallas_call | solution.py:49
  38.1 0.3 shard_map.70.base
  38.4 0.4 collective-permute-done.10.refs_1_
  38.8 0.3 shard_map.71
  39.1 0.1 collective-permute-start.11
  39.2 1.2 %collective-permute-done.11 = f32[64,256]{1,0:T(8,128)S(1)} collective-permute-done((f32[64,256]{1,0:T(8,128)S(1)}, f32[64,256]{1,0:T(8,128)S(1)}, u32[]{:S(2)}, u32[]{:S(2)}) %collective-permute-start.11) | collective-permute-done | bytes 65568 | tf_op jit(solution)/shard_map/ppermute | solution.py:204
  40.5 0.5 collective-permute-start.12
  41.0 0.5 collective-permute-start.18
  41.5 3.4 %collective-permute-start.14 = (bf16[64,256]{1,0:T(8,128)(2,1)S(1)}, bf16[64,256]{1,0:T(8,128)(2,1)S(1)}, u32[]{:S(2)}, u32[]{:S(2)}) collective-permute-start(bf16[64,256]{1,0:T(8,128)(2,1)S(1)} %add_convert_fusion.2), channel_id=1, source_target_pairs={{24,0},{25,1},{26,2},{27,3},{28,4},{29,5},{30,6},{31,7},{16,8},{17... | collective-permute-start | bytes 98312 | tf_op jit(solution)/shard_map/ppermute | solution.py:204
  45.0 2.5 %collective-permute-done.14 = bf16[64,256]{1,0:T(8,128)(2,1)S(1)} collective-permute-done((bf16[64,256]{1,0:T(8,128)(2,1)S(1)}, bf16[64,256]{1,0:T(8,128)(2,1)S(1)}, u32[]{:S(2)}, u32[]{:S(2)}) %collective-permute-start.14) | collective-permute-done | bytes 32800 | tf_op jit(solution)/shard_map/ppermute | solution.py:204
  47.4 2.3 %collective-permute-done.13 = bf16[64,256]{1,0:T(8,128)(2,1)S(1)} collective-permute-done((bf16[64,256]{1,0:T(8,128)(2,1)S(1)}, bf16[64,256]{1,0:T(8,128)(2,1)S(1)}, u32[]{:S(2)}, u32[]{:S(2)}) %collective-permute-start.13) | collective-permute-done | bytes 32800 | tf_op jit(solution)/shard_map/ppermute | solution.py:204
  49.8 1.6 %collective-permute-start.15 = (bf16[128,256]{1,0:T(8,128)(2,1)S(1)}, bf16[128,256]{1,0:T(8,128)(2,1)S(1)}, u32[]{:S(2)}, u32[]{:S(2)}) collective-permute-start(bf16[128,256]{1,0:T(8,128)(2,1)S(1)} %pad_maximum_fusion.2.refs_0_), channel_id=1, source_target_pairs={{4,0},{5,1},{6,2},{7,3},{0,4},{1,5},{2,6},{3,7},{12,8},{13,9},{14,... | collective-permute-start | bytes 196616 | tf_op jit(solution)/shard_map/ppermute | solution.py:204
  51.4 0.3 shard_map.68.base
  51.7 1.3 %shard_map.72.refs_2_ = bf16[4,2,256,256]{3,2,1,0:T(8,128)(2,1)S(1)} custom-call(s32[5]{0:T(128)S(1)} %copy-done.7, s32[3,8,8]{2,1,0:T(8,128)S(1)} %copy-done.5, bf16[3,1,256,256]{3,2,1,0:T(8,128)(2,1)S(1)} %copy-done, bf16[3,1,256,512]{3,2,1,0:T(8,128)(2,1)S(1)} %copy-done.1, bf16[1,1,256,512]{3,2,1,0:T(8,128)(2,1)S(1)} %collective-permute-done.9.refs_2_), custom_call_target="tpu_custom_call" | custom-call | tf_op jit(solution)/shard_map/pallas_call | solution.py:49
  52.9 1.2 %collective-permute-done.15.refs_1_ = bf16[128,256]{1,0:T(8,128)(2,1)S(1)} collective-permute-done((bf16[128,256]{1,0:T(8,128)(2,1)S(1)}, bf16[128,256]{1,0:T(8,128)(2,1)S(1)}, u32[]{:S(2)}, u32[]{:S(2)}) %collective-permute-start.15) | collective-permute-done | bytes 65568 | tf_op jit(solution)/shard_map/ppermute | solution.py:204
  54.1 0.3 shard_map.73
  54.4 0.1 collective-permute-start.16
  54.5 1.2 %collective-permute-done.16 = f32[64,256]{1,0:T(8,128)S(1)} collective-permute-done((f32[64,256]{1,0:T(8,128)S(1)}, f32[64,256]{1,0:T(8,128)S(1)}, u32[]{:S(2)}, u32[]{:S(2)}) %collective-permute-start.16) | collective-permute-done | bytes 65568 | tf_op jit(solution)/shard_map/ppermute | solution.py:204
  55.8 0.5 collective-permute-start.19
  56.3 1.4 %collective-permute-start.21 = (bf16[64,256]{1,0:T(8,128)(2,1)S(1)}, bf16[64,256]{1,0:T(8,128)(2,1)S(1)}, u32[]{:S(2)}, u32[]{:S(2)}) collective-permute-start(bf16[64,256]{1,0:T(8,128)(2,1)S(1)} %add_convert_fusion.1), channel_id=1, source_target_pairs={{24,0},{25,1},{26,2},{27,3},{28,4},{29,5},{30,6},{31,7},{16,8},{17... | collective-permute-start | bytes 98312 | tf_op jit(solution)/shard_map/ppermute | solution.py:204
  57.6 1.7 %collective-permute-start.20 = (bf16[64,256]{1,0:T(8,128)(2,1)S(1)}, bf16[64,256]{1,0:T(8,128)(2,1)S(1)}, u32[]{:S(2)}, u32[]{:S(2)}) collective-permute-start(bf16[64,256]{1,0:T(8,128)(2,1)S(1)} %add_convert_fusion.1), channel_id=1, source_target_pairs={{16,0},{17,1},{18,2},{19,3},{20,4},{21,5},{22,6},{23,7},{24,8},{25... | collective-permute-start | bytes 98312 | tf_op jit(solution)/shard_map/ppermute | solution.py:204
  59.3 0.5 collective-permute-start.17
  59.9 2.1 %collective-permute-done.21 = bf16[64,256]{1,0:T(8,128)(2,1)S(1)} collective-permute-done((bf16[64,256]{1,0:T(8,128)(2,1)S(1)}, bf16[64,256]{1,0:T(8,128)(2,1)S(1)}, u32[]{:S(2)}, u32[]{:S(2)}) %collective-permute-start.21) | collective-permute-done | bytes 32800 | tf_op jit(solution)/shard_map/ppermute | solution.py:204
  62.0 0.9 %collective-permute-done.20 = bf16[64,256]{1,0:T(8,128)(2,1)S(1)} collective-permute-done((bf16[64,256]{1,0:T(8,128)(2,1)S(1)}, bf16[64,256]{1,0:T(8,128)(2,1)S(1)}, u32[]{:S(2)}, u32[]{:S(2)}) %collective-permute-start.20) | collective-permute-done | bytes 32800 | tf_op jit(solution)/shard_map/ppermute | solution.py:204
  62.9 1.6 %collective-permute-start.22 = (bf16[128,256]{1,0:T(8,128)(2,1)S(1)}, bf16[128,256]{1,0:T(8,128)(2,1)S(1)}, u32[]{:S(2)}, u32[]{:S(2)}) collective-permute-start(bf16[128,256]{1,0:T(8,128)(2,1)S(1)} %pad_maximum_fusion.4.refs_0_), channel_id=1, source_target_pairs={{4,0},{5,1},{6,2},{7,3},{0,4},{1,5},{2,6},{3,7},{12,8},{13,9},{14,... | collective-permute-start | bytes 196616 | tf_op jit(solution)/shard_map/ppermute | solution.py:204
  64.5 1.3 %shard_map.77.refs_2_ = bf16[4,2,256,256]{3,2,1,0:T(8,128)(2,1)S(1)} custom-call(s32[5]{0:T(128)S(1)} %copy-done.7, s32[3,8,8]{2,1,0:T(8,128)S(1)} %copy-done.5, bf16[3,1,256,256]{3,2,1,0:T(8,128)(2,1)S(1)} %copy-done, bf16[3,1,256,512]{3,2,1,0:T(8,128)(2,1)S(1)} %copy-done.1, bf16[2,1,256,512]{3,2,1,0:T(8,128)(2,1)S(1)} %collective-permute-done.18.refs_2_), custom_call_target="tpu_custom_call" | custom-call | tf_op jit(solution)/shard_map/pallas_call | solution.py:49
  65.8 1.3 %shard_map.75.refs_2_ = bf16[4,2,256,256]{3,2,1,0:T(8,128)(2,1)S(1)} custom-call(s32[5]{0:T(128)S(1)} %copy-done.7, s32[3,8,8]{2,1,0:T(8,128)S(1)} %copy-done.5, bf16[3,1,256,256]{3,2,1,0:T(8,128)(2,1)S(1)} %copy-done, bf16[3,1,256,512]{3,2,1,0:T(8,128)(2,1)S(1)} %copy-done.1, bf16[2,1,256,512]{3,2,1,0:T(8,128)(2,1)S(1)} %collective-permute-done.18.refs_2_), custom_call_target="tpu_custom_call" | custom-call | tf_op jit(solution)/shard_map/pallas_call | solution.py:49
  67.1 0.3 shard_map.76.base
  67.4 0.3 shard_map.78
  67.7 0.1 collective-permute-start.23
  67.8 1.2 %collective-permute-done.23 = f32[64,256]{1,0:T(8,128)S(1)} collective-permute-done((f32[64,256]{1,0:T(8,128)S(1)}, f32[64,256]{1,0:T(8,128)S(1)}, u32[]{:S(2)}, u32[]{:S(2)}) %collective-permute-start.23) | collective-permute-done | bytes 65568 | tf_op jit(solution)/shard_map/ppermute | solution.py:204
  69.1 1.4 %collective-permute-start.24 = (bf16[64,256]{1,0:T(8,128)(2,1)S(1)}, bf16[64,256]{1,0:T(8,128)(2,1)S(1)}, u32[]{:S(2)}, u32[]{:S(2)}) collective-permute-start(bf16[64,256]{1,0:T(8,128)(2,1)S(1)} %add_convert_fusion.refs_0_), channel_id=1, source_target_pairs={{2,0},{3,1},{0,2},{1,3},{6,4},{7,5},{4,6},{5,7},{10,8},{11,9},{8,1... | collective-permute-start | bytes 98312 | tf_op jit(solution)/shard_map/ppermute | solution.py:204
  70.5 1.4 %shard_map.74.whole = bf16[3,1,256,128]{3,2,1,0:T(8,128)(2,1)} custom-call(s32[5]{0:T(128)S(1)} %copy-done.7, bf16[128,256]{1,0:T(8,128)(2,1)S(1)} %pad_maximum_fusion.3.refs_0_, bf16[128,256]{1,0:T(8,128)(2,1)S(1)} %collective-permute-done.17.refs_1_), custom_call_target="tpu_custom_call" | custom-call | tf_op jit(solution)/shard_map/pallas_call | solution.py:49
  71.8 1.2 %collective-permute-done.24.refs_1_ = bf16[64,256]{1,0:T(8,128)(2,1)S(1)} collective-permute-done((bf16[64,256]{1,0:T(8,128)(2,1)S(1)}, bf16[64,256]{1,0:T(8,128)(2,1)S(1)}, u32[]{:S(2)}, u32[]{:S(2)}) %collective-permute-start.24) | collective-permute-done | bytes 32800 | tf_op jit(solution)/shard_map/ppermute | solution.py:204
  73.0 1.3 %shard_map.79 = bf16[3,1,256,128]{3,2,1,0:T(8,128)(2,1)} custom-call(s32[5]{0:T(128)S(1)} %copy-done.7, bf16[3,1,256,128]{3,2,1,0:T(8,128)(2,1)} %shard_map.74.whole, bf16[64,256]{1,0:T(8,128)(2,1)S(1)} %add_convert_fusion.refs_0_, bf16[64,256]{1,0:T(8,128)(2,1)S(1)} %collective-permute-done.24.refs_1_), custom_call_target="tpu_custom_call", output_to_operand_aliasing={{}: (1, {})} | custom-call | tf_op jit(solution)/shard_map/pallas_call | solution.py:49
  (42 shorter events, 0.2 us)
Async XLA Ops:
  0.0 11.2 %copy-start.1 = (bf16[3,1,256,512]{3,2,1,0:T(8,128)(2,1)S(1)}, bf16[3,1,256,512]{3,2,1,0:T(8,128)(2,1)}, u32[]{:S(2)}) copy-start(bf16[3,1,256,512]{3,2,1,0:T(8,128)(2,1)} %refs_1_.9) | copy-start | bytes 2359300
  0.0 20.7 %collective-permute-start.4 = (bf16[3,1,256,512]{3,2,1,0:T(8,128)(2,1)}, bf16[3,1,256,512]{3,2,1,0:T(8,128)(2,1)S(1)}, u32[]{:S(2)}, u32[]{:S(2)}) collective-permute-start(bf16[3,1,256,512]{3,2,1,0:T(8,128)(2,1)} %refs_2_.3), channel_id=1, source_target_pairs={{2,0},{3,1},{0,2},{1,3},{6,4},{7,5},{4,6},{5,7},{10,8},{11,9},{8,1... | collective-permute-start | bytes 2359304 | tf_op jit(solution)/shard_map/ppermute | solution.py:204
  5.3 8.6 %collective-permute-start = (bf16[64,256]{1,0:T(8,128)(2,1)}, bf16[64,256]{1,0:T(8,128)(2,1)S(1)}, u32[]{:S(2)}, u32[]{:S(2)}) collective-permute-start(bf16[64,256]{1,0:T(8,128)(2,1)} %shard_map.64.first), channel_id=1, source_target_pairs={{8,0},{9,1},{10,2},{11,3},{12,4},{13,5},{14,6},{15,7},{0,8},{1,9},... | collective-permute-start | bytes 98312 | tf_op jit(solution)/shard_map/ppermute | solution.py:204
  6.9 7.0 %collective-permute-start.2 = (bf16[64,256]{1,0:T(8,128)(2,1)}, bf16[64,256]{1,0:T(8,128)(2,1)S(1)}, u32[]{:S(2)}, u32[]{:S(2)}) collective-permute-start(bf16[64,256]{1,0:T(8,128)(2,1)} %shard_map.64.first), channel_id=1, source_target_pairs={{24,0},{25,1},{26,2},{27,3},{28,4},{29,5},{30,6},{31,7},{16,8},{17... | collective-permute-start | bytes 98312 | tf_op jit(solution)/shard_map/ppermute | solution.py:204
  9.4 5.4 %collective-permute-start.1 = (bf16[64,256]{1,0:T(8,128)(2,1)}, bf16[64,256]{1,0:T(8,128)(2,1)S(1)}, u32[]{:S(2)}, u32[]{:S(2)}) collective-permute-start(bf16[64,256]{1,0:T(8,128)(2,1)} %shard_map.64.first), channel_id=1, source_target_pairs={{16,0},{17,1},{18,2},{19,3},{20,4},{21,5},{22,6},{23,7},{24,8},{25... | collective-permute-start | bytes 98312 | tf_op jit(solution)/shard_map/ppermute | solution.py:204
  11.2 1.1 %copy-start = (bf16[3,1,256,256]{3,2,1,0:T(8,128)(2,1)S(1)}, bf16[3,1,256,256]{3,2,1,0:T(8,128)(2,1)}, u32[]{:S(2)}) copy-start(bf16[3,1,256,256]{3,2,1,0:T(8,128)(2,1)} %refs_0_.11) | copy-start | bytes 1179652
  11.2 1.3 %copy-start.2 = (bf16[3,1,256,256]{3,2,1,0:T(8,128)(2,1)S(1)}, bf16[3,1,256,256]{3,2,1,0:T(8,128)(2,1)}, u32[]{:S(2)}) copy-start(bf16[3,1,256,256]{3,2,1,0:T(8,128)(2,1)} %refs_1_.6) | copy-start | bytes 1179652
  11.2 1.3 %copy-start.4 = (bf16[3,1,256,128]{3,2,1,0:T(8,128)(2,1)S(1)}, bf16[3,1,256,128]{3,2,1,0:T(8,128)(2,1)}, u32[]{:S(2)}) copy-start(bf16[3,1,256,128]{3,2,1,0:T(8,128)(2,1)} %rhs.3) | copy-start | bytes 589828
  11.2 1.3 %copy-start.6 = (bf16[64,256]{1,0:T(8,128)(2,1)S(1)}, bf16[64,256]{1,0:T(8,128)(2,1)}, u32[]{:S(2)}) copy-start(bf16[64,256]{1,0:T(8,128)(2,1)} %shard_map.64.first) | copy-start | bytes 98308
  11.2 1.3 %copy-start.7 = (s32[5]{0:T(128)S(1)}, s32[5]{0:T(128)}, u32[]{:S(2)}) copy-start(s32[5]{0:T(128)} %stack.23.spot) | copy-start | bytes 64
  12.0 8.7 %copy-start.3 = (bf16[3,1,256,512]{3,2,1,0:T(8,128)(2,1)S(1)}, bf16[3,1,256,512]{3,2,1,0:T(8,128)(2,1)}, u32[]{:S(2)}) copy-start(bf16[3,1,256,512]{3,2,1,0:T(8,128)(2,1)} %refs_2_.3) | copy-start | bytes 2359300
  14.8 5.9 %copy-start.5 = (s32[3,8,8]{2,1,0:T(8,128)S(1)}, s32[3,8,8]{2,1,0:T(8,128)}, u32[]{:S(2)}) copy-start(s32[3,8,8]{2,1,0:T(8,128)} %pattern.11) | copy-start | bytes 2308
  14.8 10.5 %copy-start.9 = (bf16[1,1,256,512]{3,2,1,0:T(8,128)(2,1)S(1)}, bf16[1,1,256,512]{3,2,1,0:T(8,128)(2,1)}, u32[]{:S(2)}) copy-start(bf16[1,1,256,512]{3,2,1,0:T(8,128)(2,1)} %slice.6) | copy-start | bytes 786436
  14.8 4.3 %collective-permute-start.3 = (bf16[128,256]{1,0:T(8,128)(2,1)S(1)}, bf16[128,256]{1,0:T(8,128)(2,1)S(1)}, u32[]{:S(2)}, u32[]{:S(2)}) collective-permute-start(bf16[128,256]{1,0:T(8,128)(2,1)S(1)} %pad_maximum_fusion.refs_2_.refs_0_), channel_id=1, source_target_pairs={{4,0},{5,1},{6,2},{7,3},{0,4},{1,5},{2,6},{3,7},{12,8},{13,9},{14,... | collective-permute-start | bytes 196616 | tf_op jit(solution)/shard_map/ppermute | solution.py:204
  22.1 1.3 %collective-permute-start.5 = (f32[64,256]{1,0:T(8,128)S(1)}, f32[64,256]{1,0:T(8,128)S(1)}, u32[]{:S(2)}, u32[]{:S(2)}) collective-permute-start(f32[64,256]{1,0:T(8,128)S(1)} %shard_map.66), channel_id=1, source_target_pairs={{1,0},{0,1},{3,2},{2,3},{5,4},{4,5},{7,6},{6,7},{9,8},{8,9},{11,10... | collective-permute-start | bytes 196616 | tf_op jit(solution)/shard_map/ppermute | solution.py:204
  23.4 6.0 %collective-permute-start.6 = (bf16[64,256]{1,0:T(8,128)(2,1)S(1)}, bf16[64,256]{1,0:T(8,128)(2,1)S(1)}, u32[]{:S(2)}, u32[]{:S(2)}) collective-permute-start(bf16[64,256]{1,0:T(8,128)(2,1)S(1)} %add_convert_fusion.3), channel_id=1, source_target_pairs={{8,0},{9,1},{10,2},{11,3},{12,4},{13,5},{14,6},{15,7},{0,8},{1,9},... | collective-permute-start | bytes 98312 | tf_op jit(solution)/shard_map/ppermute | solution.py:204
  25.3 9.2 %collective-permute-start.9 = (bf16[1,1,256,512]{3,2,1,0:T(8,128)(2,1)S(1)}, bf16[1,1,256,512]{3,2,1,0:T(8,128)(2,1)S(1)}, u32[]{:S(2)}, u32[]{:S(2)}) collective-permute-start(bf16[1,1,256,512]{3,2,1,0:T(8,128)(2,1)S(1)} %copy-done.9), channel_id=1, source_target_pairs={{2,0},{3,1},{0,2},{1,3},{6,4},{7,5},{4,6},{5,7},{10,8},{11,9},{8,1... | collective-permute-start | bytes 786440 | tf_op jit(solution)/shard_map/ppermute | solution.py:204
  26.8 6.1 %collective-permute-start.8 = (bf16[64,256]{1,0:T(8,128)(2,1)S(1)}, bf16[64,256]{1,0:T(8,128)(2,1)S(1)}, u32[]{:S(2)}, u32[]{:S(2)}) collective-permute-start(bf16[64,256]{1,0:T(8,128)(2,1)S(1)} %add_convert_fusion.3), channel_id=1, source_target_pairs={{24,0},{25,1},{26,2},{27,3},{28,4},{29,5},{30,6},{31,7},{16,8},{17... | collective-permute-start | bytes 98312 | tf_op jit(solution)/shard_map/ppermute | solution.py:204
  29.3 5.2 %collective-permute-start.7 = (bf16[64,256]{1,0:T(8,128)(2,1)S(1)}, bf16[64,256]{1,0:T(8,128)(2,1)S(1)}, u32[]{:S(2)}, u32[]{:S(2)}) collective-permute-start(bf16[64,256]{1,0:T(8,128)(2,1)S(1)} %add_convert_fusion.3), channel_id=1, source_target_pairs={{16,0},{17,1},{18,2},{19,3},{20,4},{21,5},{22,6},{23,7},{24,8},{25... | collective-permute-start | bytes 98312 | tf_op jit(solution)/shard_map/ppermute | solution.py:204
  34.5 4.3 %collective-permute-start.10 = (bf16[128,256]{1,0:T(8,128)(2,1)S(1)}, bf16[128,256]{1,0:T(8,128)(2,1)S(1)}, u32[]{:S(2)}, u32[]{:S(2)}) collective-permute-start(bf16[128,256]{1,0:T(8,128)(2,1)S(1)} %pad_maximum_fusion.1.refs_0_), channel_id=1, source_target_pairs={{4,0},{5,1},{6,2},{7,3},{0,4},{1,5},{2,6},{3,7},{12,8},{13,9},{14,... | collective-permute-start | bytes 196616 | tf_op jit(solution)/shard_map/ppermute | solution.py:204
  38.8 2.1 %copy-start.8 = (bf16[2,1,256,512]{3,2,1,0:T(8,128)(2,1)S(1)}, bf16[2,1,256,512]{3,2,1,0:T(8,128)(2,1)}, u32[]{:S(2)}) copy-start(bf16[2,1,256,512]{3,2,1,0:T(8,128)(2,1)} %slice.7) | copy-start | bytes 1572868
  39.1 1.3 %collective-permute-start.11 = (f32[64,256]{1,0:T(8,128)S(1)}, f32[64,256]{1,0:T(8,128)S(1)}, u32[]{:S(2)}, u32[]{:S(2)}) collective-permute-start(f32[64,256]{1,0:T(8,128)S(1)} %shard_map.71), channel_id=1, source_target_pairs={{1,0},{0,1},{3,2},{2,3},{5,4},{4,5},{7,6},{6,7},{9,8},{8,9},{11,10... | collective-permute-start | bytes 196616 | tf_op jit(solution)/shard_map/ppermute | solution.py:204
  40.5 4.5 %collective-permute-start.12 = (bf16[64,256]{1,0:T(8,128)(2,1)S(1)}, bf16[64,256]{1,0:T(8,128)(2,1)S(1)}, u32[]{:S(2)}, u32[]{:S(2)}) collective-permute-start(bf16[64,256]{1,0:T(8,128)(2,1)S(1)} %add_convert_fusion.2), channel_id=1, source_target_pairs={{8,0},{9,1},{10,2},{11,3},{12,4},{13,5},{14,6},{15,7},{0,8},{1,9},... | collective-permute-start | bytes 98312 | tf_op jit(solution)/shard_map/ppermute | solution.py:204
  41.0 14.8 %collective-permute-start.18 = (bf16[2,1,256,512]{3,2,1,0:T(8,128)(2,1)S(1)}, bf16[2,1,256,512]{3,2,1,0:T(8,128)(2,1)S(1)}, u32[]{:S(2)}, u32[]{:S(2)}) collective-permute-start(bf16[2,1,256,512]{3,2,1,0:T(8,128)(2,1)S(1)} %copy-done.8), channel_id=1, source_target_pairs={{2,0},{3,1},{0,2},{1,3},{6,4},{7,5},{4,6},{5,7},{10,8},{11,9},{8,1... | collective-permute-start | bytes 1572872 | tf_op jit(solution)/shard_map/ppermute | solution.py:204
  41.5 5.9 %collective-permute-start.14 = (bf16[64,256]{1,0:T(8,128)(2,1)S(1)}, bf16[64,256]{1,0:T(8,128)(2,1)S(1)}, u32[]{:S(2)}, u32[]{:S(2)}) collective-permute-start(bf16[64,256]{1,0:T(8,128)(2,1)S(1)} %add_convert_fusion.2), channel_id=1, source_target_pairs={{24,0},{25,1},{26,2},{27,3},{28,4},{29,5},{30,6},{31,7},{16,8},{17... | collective-permute-start | bytes 98312 | tf_op jit(solution)/shard_map/ppermute | solution.py:204
  44.9 4.8 %collective-permute-start.13 = (bf16[64,256]{1,0:T(8,128)(2,1)S(1)}, bf16[64,256]{1,0:T(8,128)(2,1)S(1)}, u32[]{:S(2)}, u32[]{:S(2)}) collective-permute-start(bf16[64,256]{1,0:T(8,128)(2,1)S(1)} %add_convert_fusion.2), channel_id=1, source_target_pairs={{16,0},{17,1},{18,2},{19,3},{20,4},{21,5},{22,6},{23,7},{24,8},{25... | collective-permute-start | bytes 98312 | tf_op jit(solution)/shard_map/ppermute | solution.py:204
  49.8 4.3 %collective-permute-start.15 = (bf16[128,256]{1,0:T(8,128)(2,1)S(1)}, bf16[128,256]{1,0:T(8,128)(2,1)S(1)}, u32[]{:S(2)}, u32[]{:S(2)}) collective-permute-start(bf16[128,256]{1,0:T(8,128)(2,1)S(1)} %pad_maximum_fusion.2.refs_0_), channel_id=1, source_target_pairs={{4,0},{5,1},{6,2},{7,3},{0,4},{1,5},{2,6},{3,7},{12,8},{13,9},{14,... | collective-permute-start | bytes 196616 | tf_op jit(solution)/shard_map/ppermute | solution.py:204
  54.4 1.3 %collective-permute-start.16 = (f32[64,256]{1,0:T(8,128)S(1)}, f32[64,256]{1,0:T(8,128)S(1)}, u32[]{:S(2)}, u32[]{:S(2)}) collective-permute-start(f32[64,256]{1,0:T(8,128)S(1)} %shard_map.73), channel_id=1, source_target_pairs={{1,0},{0,1},{3,2},{2,3},{5,4},{4,5},{7,6},{6,7},{9,8},{8,9},{11,10... | collective-permute-start | bytes 196616 | tf_op jit(solution)/shard_map/ppermute | solution.py:204
  55.8 4.1 %collective-permute-start.19 = (bf16[64,256]{1,0:T(8,128)(2,1)S(1)}, bf16[64,256]{1,0:T(8,128)(2,1)S(1)}, u32[]{:S(2)}, u32[]{:S(2)}) collective-permute-start(bf16[64,256]{1,0:T(8,128)(2,1)S(1)} %add_convert_fusion.1), channel_id=1, source_target_pairs={{8,0},{9,1},{10,2},{11,3},{12,4},{13,5},{14,6},{15,7},{0,8},{1,9},... | collective-permute-start | bytes 98312 | tf_op jit(solution)/shard_map/ppermute | solution.py:204
  56.3 5.7 %collective-permute-start.21 = (bf16[64,256]{1,0:T(8,128)(2,1)S(1)}, bf16[64,256]{1,0:T(8,128)(2,1)S(1)}, u32[]{:S(2)}, u32[]{:S(2)}) collective-permute-start(bf16[64,256]{1,0:T(8,128)(2,1)S(1)} %add_convert_fusion.1), channel_id=1, source_target_pairs={{24,0},{25,1},{26,2},{27,3},{28,4},{29,5},{30,6},{31,7},{16,8},{17... | collective-permute-start | bytes 98312 | tf_op jit(solution)/shard_map/ppermute | solution.py:204
  57.6 5.3 %collective-permute-start.20 = (bf16[64,256]{1,0:T(8,128)(2,1)S(1)}, bf16[64,256]{1,0:T(8,128)(2,1)S(1)}, u32[]{:S(2)}, u32[]{:S(2)}) collective-permute-start(bf16[64,256]{1,0:T(8,128)(2,1)S(1)} %add_convert_fusion.1), channel_id=1, source_target_pairs={{16,0},{17,1},{18,2},{19,3},{20,4},{21,5},{22,6},{23,7},{24,8},{25... | collective-permute-start | bytes 98312 | tf_op jit(solution)/shard_map/ppermute | solution.py:204
  59.3 7.8 %collective-permute-start.17 = (bf16[128,256]{1,0:T(8,128)(2,1)S(1)}, bf16[128,256]{1,0:T(8,128)(2,1)S(1)}, u32[]{:S(2)}, u32[]{:S(2)}) collective-permute-start(bf16[128,256]{1,0:T(8,128)(2,1)S(1)} %pad_maximum_fusion.3.refs_0_), channel_id=1, source_target_pairs={{2,0},{3,1},{0,2},{1,3},{6,4},{7,5},{4,6},{5,7},{10,8},{11,9},{8,1... | collective-permute-start | bytes 196616 | tf_op jit(solution)/shard_map/ppermute | solution.py:204
  62.9 4.5 %collective-permute-start.22 = (bf16[128,256]{1,0:T(8,128)(2,1)S(1)}, bf16[128,256]{1,0:T(8,128)(2,1)S(1)}, u32[]{:S(2)}, u32[]{:S(2)}) collective-permute-start(bf16[128,256]{1,0:T(8,128)(2,1)S(1)} %pad_maximum_fusion.4.refs_0_), channel_id=1, source_target_pairs={{4,0},{5,1},{6,2},{7,3},{0,4},{1,5},{2,6},{3,7},{12,8},{13,9},{14,... | collective-permute-start | bytes 196616 | tf_op jit(solution)/shard_map/ppermute | solution.py:204
  67.7 1.3 %collective-permute-start.23 = (f32[64,256]{1,0:T(8,128)S(1)}, f32[64,256]{1,0:T(8,128)S(1)}, u32[]{:S(2)}, u32[]{:S(2)}) collective-permute-start(f32[64,256]{1,0:T(8,128)S(1)} %shard_map.78), channel_id=1, source_target_pairs={{1,0},{0,1},{3,2},{2,3},{5,4},{4,5},{7,6},{6,7},{9,8},{8,9},{11,10... | collective-permute-start | bytes 196616 | tf_op jit(solution)/shard_map/ppermute | solution.py:204
  69.1 4.0 %collective-permute-start.24 = (bf16[64,256]{1,0:T(8,128)(2,1)S(1)}, bf16[64,256]{1,0:T(8,128)(2,1)S(1)}, u32[]{:S(2)}, u32[]{:S(2)}) collective-permute-start(bf16[64,256]{1,0:T(8,128)(2,1)S(1)} %add_convert_fusion.refs_0_), channel_id=1, source_target_pairs={{2,0},{3,1},{0,2},{1,3},{6,4},{7,5},{4,6},{5,7},{10,8},{11,9},{8,1... | collective-permute-start | bytes 98312 | tf_op jit(solution)/shard_map/ppermute | solution.py:204

commit v3 on v2

--- a/solution.py
+++ b/solution.py
@@ -86,17 +86,17 @@
             outs[levels + level - 1][...] = jnp.where(mine, value, 0.0)
 
 
-def fold_kernel(picks, left_count, spot, pattern, *refs):
+def fold_kernel(picks, lefts, spot, pattern, *refs):
     outs = refs[-len(picks) :]
-    pieces = refs[left_count : -len(picks)]
+    pieces = refs[len(lefts) : -len(picks)]
     row, chip, core = spot[ROW], spot[CHIP], spot[CORE]
     depth, line = spot[DEPTH], spot[LINE]
     size = outs[0].shape[-1]
     group = pieces[0].shape[-1] // size
-    if left_count == 1:
-        sides = [refs[0][0, 0]]
+    if len(lefts) == 1:
+        sides = [refs[0][lefts[0], 0]]
     else:
-        sides = split(exact(refs[0][0, 0], refs[1][0, 0]), 3)
+        sides = split(exact(refs[0][lefts[0], 0], refs[1][lefts[1], 0]), 3)
     for index, piece in enumerate(pieces):
         deep = (chip ^ index) * CORES + core
         turn = (deep // CORES) ^ (depth // CORES)
@@ -134,12 +134,12 @@
         turn = (deep // CORES) ^ (depth // CORES)
         for across in range(lines):
             keep = pattern[pair, row, deep * lines + across]
-            matrix = piece[0, 0, :, across * size : (across + 1) * size]
+            matrix = piece[pair, 0, :, across * size : (across + 1) * size]
             matrix = jnp.where(keep > 0, matrix, jnp.zeros_like(matrix))
             total = total + times(blocks[(across ^ line) * chips + turn], matrix)
     value = base[...]
     for part in split(total, 3):
-        value = value - times(part, inverse[0, 0])
+        value = value - times(part, inverse[1, 0])
     out[...] = value
 
 
@@ -224,10 +224,10 @@
                 for b in range(1, chips)
             ]
 
-        def fold(picks, inverses, pieces, sign):
+        def fold(picks, lefts, inverses, pieces, sign):
             shape = jax.ShapeDtypeStruct((near * lines, 2, size, size), jnp.bfloat16)
             return call(
-                functools.partial(fold_kernel, picks, len(inverses)),
+                functools.partial(fold_kernel, picks, lefts),
                 [shape] * len(picks),
                 [after(spot, sign), pattern] + inverses + pieces,
                 scalars=2,
@@ -292,10 +292,10 @@
         def fold_lower(later, both, sign):
             pairs = [pair_index(later, e) for e in range(later)]
             picks = tuple((pair, 0, False) for pair in pairs)
-            inverses = [level_of(lower_inverse, later)]
-            if both:
-                inverses = [level_of(upper_inverse, later)] + inverses
-            found = dict(zip(pairs, fold(picks, inverses, [lower_blocks] + low_all, sign)))
+            inverses = [upper_inverse, lower_inverse] if both else [lower_inverse]
+            lefts = (later,) * len(inverses)
+            found = fold(picks, lefts, inverses, [lower_blocks] + low_all, sign)
+            found = dict(zip(pairs, found))
             (backward if both else forward).update(found)
             return list(found.values())
 
@@ -303,8 +303,7 @@
             pair = pair_index(later, earlier)
             picks = ((pair, pair if pair == last_pair else 0, True),)
             moved = high_one if pair == last_pair else high_rest
-            inverses = [level_of(upper_inverse, earlier)]
-            found = fold(picks, inverses, [upper_blocks] + moved, sign)[0]
+            found = fold(picks, (earlier,), [upper_inverse], [upper_blocks] + moved, sign)[0]
             upward[later, earlier] = found
             return [found]
 
@@ -314,11 +313,11 @@
         for level in range(1, top):
             value = starts[level]
             if level == 1:
-                pieces = [level_of(blocks, 0) for blocks in [lower_blocks] + low_all]
+                pieces = [lower_blocks] + low_all
                 value = call(
                     functools.partial(direct_kernel, 0, lines, chips),
                     piece,
-                    [spot, pattern, value, level_of(lower_inverse, 1)] + pieces + fetched[0],
+                    [spot, pattern, value, lower_inverse] + pieces + fetched[0],
                     scalars=2,
                     scratch=[pltpu.VMEM((near * lines, share, size), jnp.bfloat16)],
                 )

time: 74.5 us -> 74.5 us (level)
  no operation moved by 1% of the time
where the time goes in v3:
time: 74.5 us; the launch traced here: 74.3 us
  starting transfers between devices  29.7 us (40%)
  waiting for transfers between devices  24.2 us (32%)
  Pallas kernels  16.5 us (22%)
  local copies, waits for them, and re-layouts  3.58 us (5%)
    ppermute x25, starting transfers between devices, send(): return lax.ppermute(value, ('prow', 'pcol'), pairs)  29.7 us
    ppermute x25, waiting for transfers between devices, send(): return lax.ppermute(value, ('prow', 'pcol'), pairs)  24.2 us
    pallas_call x16, Pallas kernels, call(): pl.pallas_call(kernel, grid=(1,), out_shape=shapes, in_specs=specs, out_s...  16.5 us
    slice x2, local copies, waits for them, and re-layouts, body(): parts = (upper_blocks[last_pair:], upper_blocks[:last_pair])  2.49 us
  transfers between devices with their start and end apart: 25, of which 16 were waited for; matrix products, arithmetic and copies ran while one was open for 4% of the time, Pallas kernels for 18%

profile of v3, /device:TPU:0, one launch (start us, length us, event | category | flops | bytes accessed | tf_op | source)
XLA Modules:
  0.0 74.3 jit_solution(6367682159618532095)
XLA Ops:
  0.0 2.9 %collective-permute-start.4 = (bf16[3,1,256,512]{3,2,1,0:T(8,128)(2,1)}, bf16[3,1,256,512]{3,2,1,0:T(8,128)(2,1)S(1)}, u32[]{:S(2)}, u32[]{:S(2)}) collective-permute-start(bf16[3,1,256,512]{3,2,1,0:T(8,128)(2,1)} %refs_2_.3), channel_id=1, source_target_pairs={{2,0},{3,1},{0,2},{1,3},{6,4},{7,5},{4,6},{5,7},{10,8},{11,9},{8,1... | collective-permute-start | bytes 2359304 | tf_op jit(solution)/shard_map/ppermute | solution.py:204
  2.9 0.6 stack.23.spot
  3.5 1.8 %shard_map.64.first = bf16[64,256]{1,0:T(8,128)(2,1)} custom-call(s32[5]{0:T(128)} %stack.23.spot, bf16[3,1,256,128]{3,2,1,0:T(8,128)(2,1)} %rhs.3, bf16[3,1,256,256]{3,2,1,0:T(8,128)(2,1)} %refs_1_.6), custom_call_target="tpu_custom_call" | custom-call | tf_op jit(solution)/shard_map/pallas_call | solution.py:49
  5.3 1.6 %collective-permute-start = (bf16[64,256]{1,0:T(8,128)(2,1)}, bf16[64,256]{1,0:T(8,128)(2,1)S(1)}, u32[]{:S(2)}, u32[]{:S(2)}) collective-permute-start(bf16[64,256]{1,0:T(8,128)(2,1)} %shard_map.64.first), channel_id=1, source_target_pairs={{8,0},{9,1},{10,2},{11,3},{12,4},{13,5},{14,6},{15,7},{0,8},{1,9},... | collective-permute-start | bytes 98312 | tf_op jit(solution)/shard_map/ppermute | solution.py:204
  6.9 2.5 %collective-permute-start.2 = (bf16[64,256]{1,0:T(8,128)(2,1)}, bf16[64,256]{1,0:T(8,128)(2,1)S(1)}, u32[]{:S(2)}, u32[]{:S(2)}) collective-permute-start(bf16[64,256]{1,0:T(8,128)(2,1)} %shard_map.64.first), channel_id=1, source_target_pairs={{24,0},{25,1},{26,2},{27,3},{28,4},{29,5},{30,6},{31,7},{16,8},{17... | collective-permute-start | bytes 98312 | tf_op jit(solution)/shard_map/ppermute | solution.py:204
  9.4 0.1 collective-permute-start.1
  9.5 1.7 %slice.6 = bf16[1,1,256,512]{3,2,1,0:T(8,128)(2,1)} slice(bf16[3,1,256,512]{3,2,1,0:T(8,128)(2,1)} %refs_1_.9), slice={[2:3], [0:1], [0:256], [0:512]} | slice | bytes 524288 | tf_op jit(solution)/shard_map/slice | solution.py:286
  11.2 0.0 copy-start.6
  11.2 0.8 %slice.7 = bf16[2,1,256,512]{3,2,1,0:T(8,128)(2,1)} slice(bf16[3,1,256,512]{3,2,1,0:T(8,128)(2,1)S(1)} %copy-done.1), slice={[0:2], [0:1], [0:256], [0:512]} | slice | bytes 1048576 | tf_op jit(solution)/shard_map/slice | solution.py:286
  12.0 0.2 copy-done
  12.2 0.2 copy-done.2
  12.5 0.0 copy-done.4
  12.5 1.4 %shard_map.65 = (f32[64,256]{1,0:T(8,128)S(1)}, f32[64,256]{1,0:T(8,128)S(1)}, f32[64,256]{1,0:T(8,128)S(1)}, f32[64,256]{1,0:T(8,128)S(1)}) custom-call(s32[5]{0:T(128)S(1)} %copy-done.7, bf16[64,256]{1,0:T(8,128)(2,1)S(1)} %copy-done.6, bf16[3,1,256,128]{3,2,1,0:T(8,128)(2,1)S(1)} %copy-done.4, bf16[3,1,256,256]{3,2,1,0:T(8,128)(2,1)S(1)} %copy-done.2, ...), custom_call_target="tpu_custom_call" | custom-call | tf_op jit(solution)/shard_map/pallas_call | solution.py:49
  13.9 0.0 collective-permute-done
  14.0 0.8 %collective-permute-done.1 = bf16[64,256]{1,0:T(8,128)(2,1)S(1)} collective-permute-done((bf16[64,256]{1,0:T(8,128)(2,1)}, bf16[64,256]{1,0:T(8,128)(2,1)S(1)}, u32[]{:S(2)}, u32[]{:S(2)}) %collective-permute-start.1) | collective-permute-done | bytes 32800 | tf_op jit(solution)/shard_map/ppermute | solution.py:204
  14.8 1.6 %collective-permute-start.3 = (bf16[128,256]{1,0:T(8,128)(2,1)S(1)}, bf16[128,256]{1,0:T(8,128)(2,1)S(1)}, u32[]{:S(2)}, u32[]{:S(2)}) collective-permute-start(bf16[128,256]{1,0:T(8,128)(2,1)S(1)} %pad_maximum_fusion.refs_2_.refs_0_), channel_id=1, source_target_pairs={{4,0},{5,1},{6,2},{7,3},{0,4},{1,5},{2,6},{3,7},{12,8},{13,9},{14,... | collective-permute-start | bytes 196616 | tf_op jit(solution)/shard_map/ppermute | solution.py:204
  16.4 2.7 %collective-permute-done.3.refs_3_.refs_1_ = bf16[128,256]{1,0:T(8,128)(2,1)S(1)} collective-permute-done((bf16[128,256]{1,0:T(8,128)(2,1)S(1)}, bf16[128,256]{1,0:T(8,128)(2,1)S(1)}, u32[]{:S(2)}, u32[]{:S(2)}) %collective-permute-start.3) | collective-permute-done | bytes 65568 | tf_op jit(solution)/shard_map/ppermute | solution.py:204
  19.1 1.6 %collective-permute-done.4.refs_1_.refs_3_ = bf16[3,1,256,512]{3,2,1,0:T(8,128)(2,1)S(1)} collective-permute-done((bf16[3,1,256,512]{3,2,1,0:T(8,128)(2,1)}, bf16[3,1,256,512]{3,2,1,0:T(8,128)(2,1)S(1)}, u32[]{:S(2)}, u32[]{:S(2)}) %collective-permute-start.4) | collective-permute-done | bytes 786464 | tf_op jit(solution)/shard_map/ppermute | solution.py:204
  20.7 1.4 %shard_map.66 = f32[64,256]{1,0:T(8,128)S(1)} custom-call(s32[5]{0:T(128)S(1)} %copy-done.7, s32[3,8,8]{2,1,0:T(8,128)S(1)} %copy-done.5, f32[64,256]{1,0:T(8,128)S(1)} %get-tuple-element.26.base, bf16[3,1,256,256]{3,2,1,0:T(8,128)(2,1)S(1)} %copy-done.2, bf16[3,1,256,512]{3,2,1,0:T(8,128)(2,1)S(1)} %copy-done.3, ...), custom_call_target="tpu_custom_call" | custom-call | tf_op jit(solution)/shard_map/pallas_call | solution.py:49
  22.1 0.1 collective-permute-start.5
  22.2 1.2 %collective-permute-done.5 = f32[64,256]{1,0:T(8,128)S(1)} collective-permute-done((f32[64,256]{1,0:T(8,128)S(1)}, f32[64,256]{1,0:T(8,128)S(1)}, u32[]{:S(2)}, u32[]{:S(2)}) %collective-permute-start.5) | collective-permute-done | bytes 65568 | tf_op jit(solution)/shard_map/ppermute | solution.py:204
  23.4 1.9 %collective-permute-start.6 = (bf16[64,256]{1,0:T(8,128)(2,1)S(1)}, bf16[64,256]{1,0:T(8,128)(2,1)S(1)}, u32[]{:S(2)}, u32[]{:S(2)}) collective-permute-start(bf16[64,256]{1,0:T(8,128)(2,1)S(1)} %add_convert_fusion.3), channel_id=1, source_target_pairs={{8,0},{9,1},{10,2},{11,3},{12,4},{13,5},{14,6},{15,7},{0,8},{1,9},... | collective-permute-start | bytes 98312 | tf_op jit(solution)/shard_map/ppermute | solution.py:204
  25.3 1.5 %collective-permute-start.9 = (bf16[1,1,256,512]{3,2,1,0:T(8,128)(2,1)S(1)}, bf16[1,1,256,512]{3,2,1,0:T(8,128)(2,1)S(1)}, u32[]{:S(2)}, u32[]{:S(2)}) collective-permute-start(bf16[1,1,256,512]{3,2,1,0:T(8,128)(2,1)S(1)} %copy-done.9), channel_id=1, source_target_pairs={{2,0},{3,1},{0,2},{1,3},{6,4},{7,5},{4,6},{5,7},{10,8},{11,9},{8,1... | collective-permute-start | bytes 786440 | tf_op jit(solution)/shard_map/ppermute | solution.py:204
  26.8 2.5 %collective-permute-start.8 = (bf16[64,256]{1,0:T(8,128)(2,1)S(1)}, bf16[64,256]{1,0:T(8,128)(2,1)S(1)}, u32[]{:S(2)}, u32[]{:S(2)}) collective-permute-start(bf16[64,256]{1,0:T(8,128)(2,1)S(1)} %add_convert_fusion.3), channel_id=1, source_target_pairs={{24,0},{25,1},{26,2},{27,3},{28,4},{29,5},{30,6},{31,7},{16,8},{17... | collective-permute-start | bytes 98312 | tf_op jit(solution)/shard_map/ppermute | solution.py:204
  29.3 0.1 collective-permute-start.7
  29.4 1.6 %shard_map.67.refs_2_ = bf16[4,2,256,256]{3,2,1,0:T(8,128)(2,1)S(1)} custom-call(s32[5]{0:T(128)S(1)} %copy-done.7, s32[3,8,8]{2,1,0:T(8,128)S(1)} %copy-done.5, bf16[3,1,256,256]{3,2,1,0:T(8,128)(2,1)S(1)} %copy-done, bf16[3,1,256,256]{3,2,1,0:T(8,128)(2,1)S(1)} %copy-done.2, bf16[3,1,256,512]{3,2,1,0:T(8,128)(2,1)S(1)} %copy-done.3, ...), custom_call_target="tpu_custom_call" | custom-call | tf_op jit(solution)/shard_map/pallas_call | solution.py:49
  31.0 1.9 %collective-permute-done.8 = bf16[64,256]{1,0:T(8,128)(2,1)S(1)} collective-permute-done((bf16[64,256]{1,0:T(8,128)(2,1)S(1)}, bf16[64,256]{1,0:T(8,128)(2,1)S(1)}, u32[]{:S(2)}, u32[]{:S(2)}) %collective-permute-start.8) | collective-permute-done | bytes 32800 | tf_op jit(solution)/shard_map/ppermute | solution.py:204
  33.0 1.5 %collective-permute-done.7 = bf16[64,256]{1,0:T(8,128)(2,1)S(1)} collective-permute-done((bf16[64,256]{1,0:T(8,128)(2,1)S(1)}, bf16[64,256]{1,0:T(8,128)(2,1)S(1)}, u32[]{:S(2)}, u32[]{:S(2)}) %collective-permute-start.7) | collective-permute-done | bytes 32800 | tf_op jit(solution)/shard_map/ppermute | solution.py:204
  34.5 1.6 %collective-permute-start.10 = (bf16[128,256]{1,0:T(8,128)(2,1)S(1)}, bf16[128,256]{1,0:T(8,128)(2,1)S(1)}, u32[]{:S(2)}, u32[]{:S(2)}) collective-permute-start(bf16[128,256]{1,0:T(8,128)(2,1)S(1)} %pad_maximum_fusion.1.refs_0_), channel_id=1, source_target_pairs={{4,0},{5,1},{6,2},{7,3},{0,4},{1,5},{2,6},{3,7},{12,8},{13,9},{14,... | collective-permute-start | bytes 196616 | tf_op jit(solution)/shard_map/ppermute | solution.py:204
  36.1 2.0 %shard_map.69 = (bf16[4,2,256,256]{3,2,1,0:T(8,128)(2,1)S(1)}, bf16[4,2,256,256]{3,2,1,0:T(8,128)(2,1)S(1)}) custom-call(s32[5]{0:T(128)S(1)} %copy-done.7, s32[3,8,8]{2,1,0:T(8,128)S(1)} %copy-done.5, bf16[3,1,256,256]{3,2,1,0:T(8,128)(2,1)S(1)} %copy-done, bf16[3,1,256,256]{3,2,1,0:T(8,128)(2,1)S(1)} %copy-done.2, bf16[3,1,256,512]{3,2,1,0:T(8,128)(2,1)S(1)} %copy-done.3, ...), custom_call_target="tpu_custom_call" | custom-call | tf_op jit(solution)/shard_map/pallas_call | solution.py:49
  38.1 0.3 shard_map.70.base
  38.4 0.4 collective-permute-done.10.refs_1_
  38.8 0.3 shard_map.71
  39.1 0.1 collective-permute-start.11
  39.2 1.2 %collective-permute-done.11 = f32[64,256]{1,0:T(8,128)S(1)} collective-permute-done((f32[64,256]{1,0:T(8,128)S(1)}, f32[64,256]{1,0:T(8,128)S(1)}, u32[]{:S(2)}, u32[]{:S(2)}) %collective-permute-start.11) | collective-permute-done | bytes 65568 | tf_op jit(solution)/shard_map/ppermute | solution.py:204
  40.5 0.5 collective-permute-start.12
  41.0 0.5 collective-permute-start.18
  41.5 3.4 %collective-permute-start.14 = (bf16[64,256]{1,0:T(8,128)(2,1)S(1)}, bf16[64,256]{1,0:T(8,128)(2,1)S(1)}, u32[]{:S(2)}, u32[]{:S(2)}) collective-permute-start(bf16[64,256]{1,0:T(8,128)(2,1)S(1)} %add_convert_fusion.2), channel_id=1, source_target_pairs={{24,0},{25,1},{26,2},{27,3},{28,4},{29,5},{30,6},{31,7},{16,8},{17... | collective-permute-start | bytes 98312 | tf_op jit(solution)/shard_map/ppermute | solution.py:204
  45.0 2.5 %collective-permute-done.14 = bf16[64,256]{1,0:T(8,128)(2,1)S(1)} collective-permute-done((bf16[64,256]{1,0:T(8,128)(2,1)S(1)}, bf16[64,256]{1,0:T(8,128)(2,1)S(1)}, u32[]{:S(2)}, u32[]{:S(2)}) %collective-permute-start.14) | collective-permute-done | bytes 32800 | tf_op jit(solution)/shard_map/ppermute | solution.py:204
  47.4 2.3 %collective-permute-done.13 = bf16[64,256]{1,0:T(8,128)(2,1)S(1)} collective-permute-done((bf16[64,256]{1,0:T(8,128)(2,1)S(1)}, bf16[64,256]{1,0:T(8,128)(2,1)S(1)}, u32[]{:S(2)}, u32[]{:S(2)}) %collective-permute-start.13) | collective-permute-done | bytes 32800 | tf_op jit(solution)/shard_map/ppermute | solution.py:204
  49.8 1.6 %collective-permute-start.15 = (bf16[128,256]{1,0:T(8,128)(2,1)S(1)}, bf16[128,256]{1,0:T(8,128)(2,1)S(1)}, u32[]{:S(2)}, u32[]{:S(2)}) collective-permute-start(bf16[128,256]{1,0:T(8,128)(2,1)S(1)} %pad_maximum_fusion.2.refs_0_), channel_id=1, source_target_pairs={{4,0},{5,1},{6,2},{7,3},{0,4},{1,5},{2,6},{3,7},{12,8},{13,9},{14,... | collective-permute-start | bytes 196616 | tf_op jit(solution)/shard_map/ppermute | solution.py:204
  51.4 0.3 shard_map.68.base
  51.7 1.3 %shard_map.72.refs_2_ = bf16[4,2,256,256]{3,2,1,0:T(8,128)(2,1)S(1)} custom-call(s32[5]{0:T(128)S(1)} %copy-done.7, s32[3,8,8]{2,1,0:T(8,128)S(1)} %copy-done.5, bf16[3,1,256,256]{3,2,1,0:T(8,128)(2,1)S(1)} %copy-done, bf16[3,1,256,512]{3,2,1,0:T(8,128)(2,1)S(1)} %copy-done.1, bf16[1,1,256,512]{3,2,1,0:T(8,128)(2,1)S(1)} %collective-permute-done.9.refs_2_), custom_call_target="tpu_custom_call" | custom-call | tf_op jit(solution)/shard_map/pallas_call | solution.py:49
  52.9 1.2 %collective-permute-done.15.refs_1_ = bf16[128,256]{1,0:T(8,128)(2,1)S(1)} collective-permute-done((bf16[128,256]{1,0:T(8,128)(2,1)S(1)}, bf16[128,256]{1,0:T(8,128)(2,1)S(1)}, u32[]{:S(2)}, u32[]{:S(2)}) %collective-permute-start.15) | collective-permute-done | bytes 65568 | tf_op jit(solution)/shard_map/ppermute | solution.py:204
  54.1 0.3 shard_map.73
  54.4 0.1 collective-permute-start.16
  54.5 1.2 %collective-permute-done.16 = f32[64,256]{1,0:T(8,128)S(1)} collective-permute-done((f32[64,256]{1,0:T(8,128)S(1)}, f32[64,256]{1,0:T(8,128)S(1)}, u32[]{:S(2)}, u32[]{:S(2)}) %collective-permute-start.16) | collective-permute-done | bytes 65568 | tf_op jit(solution)/shard_map/ppermute | solution.py:204
  55.8 0.5 collective-permute-start.19
  56.3 1.4 %collective-permute-start.21 = (bf16[64,256]{1,0:T(8,128)(2,1)S(1)}, bf16[64,256]{1,0:T(8,128)(2,1)S(1)}, u32[]{:S(2)}, u32[]{:S(2)}) collective-permute-start(bf16[64,256]{1,0:T(8,128)(2,1)S(1)} %add_convert_fusion.1), channel_id=1, source_target_pairs={{24,0},{25,1},{26,2},{27,3},{28,4},{29,5},{30,6},{31,7},{16,8},{17... | collective-permute-start | bytes 98312 | tf_op jit(solution)/shard_map/ppermute | solution.py:204
  57.6 1.7 %collective-permute-start.20 = (bf16[64,256]{1,0:T(8,128)(2,1)S(1)}, bf16[64,256]{1,0:T(8,128)(2,1)S(1)}, u32[]{:S(2)}, u32[]{:S(2)}) collective-permute-start(bf16[64,256]{1,0:T(8,128)(2,1)S(1)} %add_convert_fusion.1), channel_id=1, source_target_pairs={{16,0},{17,1},{18,2},{19,3},{20,4},{21,5},{22,6},{23,7},{24,8},{25... | collective-permute-start | bytes 98312 | tf_op jit(solution)/shard_map/ppermute | solution.py:204
  59.3 0.5 collective-permute-start.17
  59.9 2.1 %collective-permute-done.21 = bf16[64,256]{1,0:T(8,128)(2,1)S(1)} collective-permute-done((bf16[64,256]{1,0:T(8,128)(2,1)S(1)}, bf16[64,256]{1,0:T(8,128)(2,1)S(1)}, u32[]{:S(2)}, u32[]{:S(2)}) %collective-permute-start.21) | collective-permute-done | bytes 32800 | tf_op jit(solution)/shard_map/ppermute | solution.py:204
  62.0 0.9 %collective-permute-done.20 = bf16[64,256]{1,0:T(8,128)(2,1)S(1)} collective-permute-done((bf16[64,256]{1,0:T(8,128)(2,1)S(1)}, bf16[64,256]{1,0:T(8,128)(2,1)S(1)}, u32[]{:S(2)}, u32[]{:S(2)}) %collective-permute-start.20) | collective-permute-done | bytes 32800 | tf_op jit(solution)/shard_map/ppermute | solution.py:204
  62.9 1.6 %collective-permute-start.22 = (bf16[128,256]{1,0:T(8,128)(2,1)S(1)}, bf16[128,256]{1,0:T(8,128)(2,1)S(1)}, u32[]{:S(2)}, u32[]{:S(2)}) collective-permute-start(bf16[128,256]{1,0:T(8,128)(2,1)S(1)} %pad_maximum_fusion.4.refs_0_), channel_id=1, source_target_pairs={{4,0},{5,1},{6,2},{7,3},{0,4},{1,5},{2,6},{3,7},{12,8},{13,9},{14,... | collective-permute-start | bytes 196616 | tf_op jit(solution)/shard_map/ppermute | solution.py:204
  64.5 1.3 %shard_map.77.refs_2_ = bf16[4,2,256,256]{3,2,1,0:T(8,128)(2,1)S(1)} custom-call(s32[5]{0:T(128)S(1)} %copy-done.7, s32[3,8,8]{2,1,0:T(8,128)S(1)} %copy-done.5, bf16[3,1,256,256]{3,2,1,0:T(8,128)(2,1)S(1)} %copy-done, bf16[3,1,256,512]{3,2,1,0:T(8,128)(2,1)S(1)} %copy-done.1, bf16[2,1,256,512]{3,2,1,0:T(8,128)(2,1)S(1)} %collective-permute-done.18.refs_2_), custom_call_target="tpu_custom_call" | custom-call | tf_op jit(solution)/shard_map/pallas_call | solution.py:49
  65.8 1.3 %shard_map.75.refs_2_ = bf16[4,2,256,256]{3,2,1,0:T(8,128)(2,1)S(1)} custom-call(s32[5]{0:T(128)S(1)} %copy-done.7, s32[3,8,8]{2,1,0:T(8,128)S(1)} %copy-done.5, bf16[3,1,256,256]{3,2,1,0:T(8,128)(2,1)S(1)} %copy-done, bf16[3,1,256,512]{3,2,1,0:T(8,128)(2,1)S(1)} %copy-done.1, bf16[2,1,256,512]{3,2,1,0:T(8,128)(2,1)S(1)} %collective-permute-done.18.refs_2_), custom_call_target="tpu_custom_call" | custom-call | tf_op jit(solution)/shard_map/pallas_call | solution.py:49
  67.1 0.3 shard_map.76.base
  67.4 0.3 shard_map.78
  67.7 0.1 collective-permute-start.23
  67.8 1.2 %collective-permute-done.23 = f32[64,256]{1,0:T(8,128)S(1)} collective-permute-done((f32[64,256]{1,0:T(8,128)S(1)}, f32[64,256]{1,0:T(8,128)S(1)}, u32[]{:S(2)}, u32[]{:S(2)}) %collective-permute-start.23) | collective-permute-done | bytes 65568 | tf_op jit(solution)/shard_map/ppermute | solution.py:204
  69.1 1.4 %collective-permute-start.24 = (bf16[64,256]{1,0:T(8,128)(2,1)S(1)}, bf16[64,256]{1,0:T(8,128)(2,1)S(1)}, u32[]{:S(2)}, u32[]{:S(2)}) collective-permute-start(bf16[64,256]{1,0:T(8,128)(2,1)S(1)} %add_convert_fusion.refs_0_), channel_id=1, source_target_pairs={{2,0},{3,1},{0,2},{1,3},{6,4},{7,5},{4,6},{5,7},{10,8},{11,9},{8,1... | collective-permute-start | bytes 98312 | tf_op jit(solution)/shard_map/ppermute | solution.py:204
  70.5 1.4 %shard_map.74.whole = bf16[3,1,256,128]{3,2,1,0:T(8,128)(2,1)} custom-call(s32[5]{0:T(128)S(1)} %copy-done.7, bf16[128,256]{1,0:T(8,128)(2,1)S(1)} %pad_maximum_fusion.3.refs_0_, bf16[128,256]{1,0:T(8,128)(2,1)S(1)} %collective-permute-done.17.refs_1_), custom_call_target="tpu_custom_call" | custom-call | tf_op jit(solution)/shard_map/pallas_call | solution.py:49
  71.8 1.2 %collective-permute-done.24.refs_1_ = bf16[64,256]{1,0:T(8,128)(2,1)S(1)} collective-permute-done((bf16[64,256]{1,0:T(8,128)(2,1)S(1)}, bf16[64,256]{1,0:T(8,128)(2,1)S(1)}, u32[]{:S(2)}, u32[]{:S(2)}) %collective-permute-start.24) | collective-permute-done | bytes 32800 | tf_op jit(solution)/shard_map/ppermute | solution.py:204
  73.0 1.3 %shard_map.79 = bf16[3,1,256,128]{3,2,1,0:T(8,128)(2,1)} custom-call(s32[5]{0:T(128)S(1)} %copy-done.7, bf16[3,1,256,128]{3,2,1,0:T(8,128)(2,1)} %shard_map.74.whole, bf16[64,256]{1,0:T(8,128)(2,1)S(1)} %add_convert_fusion.refs_0_, bf16[64,256]{1,0:T(8,128)(2,1)S(1)} %collective-permute-done.24.refs_1_), custom_call_target="tpu_custom_call", output_to_operand_aliasing={{}: (1, {})} | custom-call | tf_op jit(solution)/shard_map/pallas_call | solution.py:49
  (42 shorter events, 0.2 us)
Async XLA Ops:
  0.0 11.2 %copy-start.1 = (bf16[3,1,256,512]{3,2,1,0:T(8,128)(2,1)S(1)}, bf16[3,1,256,512]{3,2,1,0:T(8,128)(2,1)}, u32[]{:S(2)}) copy-start(bf16[3,1,256,512]{3,2,1,0:T(8,128)(2,1)} %refs_1_.9) | copy-start | bytes 2359300
  0.0 20.7 %collective-permute-start.4 = (bf16[3,1,256,512]{3,2,1,0:T(8,128)(2,1)}, bf16[3,1,256,512]{3,2,1,0:T(8,128)(2,1)S(1)}, u32[]{:S(2)}, u32[]{:S(2)}) collective-permute-start(bf16[3,1,256,512]{3,2,1,0:T(8,128)(2,1)} %refs_2_.3), channel_id=1, source_target_pairs={{2,0},{3,1},{0,2},{1,3},{6,4},{7,5},{4,6},{5,7},{10,8},{11,9},{8,1... | collective-permute-start | bytes 2359304 | tf_op jit(solution)/shard_map/ppermute | solution.py:204
  5.3 8.6 %collective-permute-start = (bf16[64,256]{1,0:T(8,128)(2,1)}, bf16[64,256]{1,0:T(8,128)(2,1)S(1)}, u32[]{:S(2)}, u32[]{:S(2)}) collective-permute-start(bf16[64,256]{1,0:T(8,128)(2,1)} %shard_map.64.first), channel_id=1, source_target_pairs={{8,0},{9,1},{10,2},{11,3},{12,4},{13,5},{14,6},{15,7},{0,8},{1,9},... | collective-permute-start | bytes 98312 | tf_op jit(solution)/shard_map/ppermute | solution.py:204
  6.9 7.0 %collective-permute-start.2 = (bf16[64,256]{1,0:T(8,128)(2,1)}, bf16[64,256]{1,0:T(8,128)(2,1)S(1)}, u32[]{:S(2)}, u32[]{:S(2)}) collective-permute-start(bf16[64,256]{1,0:T(8,128)(2,1)} %shard_map.64.first), channel_id=1, source_target_pairs={{24,0},{25,1},{26,2},{27,3},{28,4},{29,5},{30,6},{31,7},{16,8},{17... | collective-permute-start | bytes 98312 | tf_op jit(solution)/shard_map/ppermute | solution.py:204
  9.4 5.4 %collective-permute-start.1 = (bf16[64,256]{1,0:T(8,128)(2,1)}, bf16[64,256]{1,0:T(8,128)(2,1)S(1)}, u32[]{:S(2)}, u32[]{:S(2)}) collective-permute-start(bf16[64,256]{1,0:T(8,128)(2,1)} %shard_map.64.first), channel_id=1, source_target_pairs={{16,0},{17,1},{18,2},{19,3},{20,4},{21,5},{22,6},{23,7},{24,8},{25... | collective-permute-start | bytes 98312 | tf_op jit(solution)/shard_map/ppermute | solution.py:204
  11.2 1.1 %copy-start = (bf16[3,1,256,256]{3,2,1,0:T(8,128)(2,1)S(1)}, bf16[3,1,256,256]{3,2,1,0:T(8,128)(2,1)}, u32[]{:S(2)}) copy-start(bf16[3,1,256,256]{3,2,1,0:T(8,128)(2,1)} %refs_0_.11) | copy-start | bytes 1179652
  11.2 1.3 %copy-start.2 = (bf16[3,1,256,256]{3,2,1,0:T(8,128)(2,1)S(1)}, bf16[3,1,256,256]{3,2,1,0:T(8,128)(2,1)}, u32[]{:S(2)}) copy-start(bf16[3,1,256,256]{3,2,1,0:T(8,128)(2,1)} %refs_1_.6) | copy-start | bytes 1179652
  11.2 1.3 %copy-start.4 = (bf16[3,1,256,128]{3,2,1,0:T(8,128)(2,1)S(1)}, bf16[3,1,256,128]{3,2,1,0:T(8,128)(2,1)}, u32[]{:S(2)}) copy-start(bf16[3,1,256,128]{3,2,1,0:T(8,128)(2,1)} %rhs.3) | copy-start | bytes 589828
  11.2 1.3 %copy-start.6 = (bf16[64,256]{1,0:T(8,128)(2,1)S(1)}, bf16[64,256]{1,0:T(8,128)(2,1)}, u32[]{:S(2)}) copy-start(bf16[64,256]{1,0:T(8,128)(2,1)} %shard_map.64.first) | copy-start | bytes 98308
  11.2 1.3 %copy-start.7 = (s32[5]{0:T(128)S(1)}, s32[5]{0:T(128)}, u32[]{:S(2)}) copy-start(s32[5]{0:T(128)} %stack.23.spot) | copy-start | bytes 64
  12.0 8.7 %copy-start.3 = (bf16[3,1,256,512]{3,2,1,0:T(8,128)(2,1)S(1)}, bf16[3,1,256,512]{3,2,1,0:T(8,128)(2,1)}, u32[]{:S(2)}) copy-start(bf16[3,1,256,512]{3,2,1,0:T(8,128)(2,1)} %refs_2_.3) | copy-start | bytes 2359300
  14.8 5.9 %copy-start.5 = (s32[3,8,8]{2,1,0:T(8,128)S(1)}, s32[3,8,8]{2,1,0:T(8,128)}, u32[]{:S(2)}) copy-start(s32[3,8,8]{2,1,0:T(8,128)} %pattern.11) | copy-start | bytes 2308
  14.8 10.5 %copy-start.9 = (bf16[1,1,256,512]{3,2,1,0:T(8,128)(2,1)S(1)}, bf16[1,1,256,512]{3,2,1,0:T(8,128)(2,1)}, u32[]{:S(2)}) copy-start(bf16[1,1,256,512]{3,2,1,0:T(8,128)(2,1)} %slice.6) | copy-start | bytes 786436
  14.8 4.3 %collective-permute-start.3 = (bf16[128,256]{1,0:T(8,128)(2,1)S(1)}, bf16[128,256]{1,0:T(8,128)(2,1)S(1)}, u32[]{:S(2)}, u32[]{:S(2)}) collective-permute-start(bf16[128,256]{1,0:T(8,128)(2,1)S(1)} %pad_maximum_fusion.refs_2_.refs_0_), channel_id=1, source_target_pairs={{4,0},{5,1},{6,2},{7,3},{0,4},{1,5},{2,6},{3,7},{12,8},{13,9},{14,... | collective-permute-start | bytes 196616 | tf_op jit(solution)/shard_map/ppermute | solution.py:204
  22.1 1.3 %collective-permute-start.5 = (f32[64,256]{1,0:T(8,128)S(1)}, f32[64,256]{1,0:T(8,128)S(1)}, u32[]{:S(2)}, u32[]{:S(2)}) collective-permute-start(f32[64,256]{1,0:T(8,128)S(1)} %shard_map.66), channel_id=1, source_target_pairs={{1,0},{0,1},{3,2},{2,3},{5,4},{4,5},{7,6},{6,7},{9,8},{8,9},{11,10... | collective-permute-start | bytes 196616 | tf_op jit(solution)/shard_map/ppermute | solution.py:204
  23.4 6.0 %collective-permute-start.6 = (bf16[64,256]{1,0:T(8,128)(2,1)S(1)}, bf16[64,256]{1,0:T(8,128)(2,1)S(1)}, u32[]{:S(2)}, u32[]{:S(2)}) collective-permute-start(bf16[64,256]{1,0:T(8,128)(2,1)S(1)} %add_convert_fusion.3), channel_id=1, source_target_pairs={{8,0},{9,1},{10,2},{11,3},{12,4},{13,5},{14,6},{15,7},{0,8},{1,9},... | collective-permute-start | bytes 98312 | tf_op jit(solution)/shard_map/ppermute | solution.py:204
  25.3 9.2 %collective-permute-start.9 = (bf16[1,1,256,512]{3,2,1,0:T(8,128)(2,1)S(1)}, bf16[1,1,256,512]{3,2,1,0:T(8,128)(2,1)S(1)}, u32[]{:S(2)}, u32[]{:S(2)}) collective-permute-start(bf16[1,1,256,512]{3,2,1,0:T(8,128)(2,1)S(1)} %copy-done.9), channel_id=1, source_target_pairs={{2,0},{3,1},{0,2},{1,3},{6,4},{7,5},{4,6},{5,7},{10,8},{11,9},{8,1... | collective-permute-start | bytes 786440 | tf_op jit(solution)/shard_map/ppermute | solution.py:204
  26.8 6.1 %collective-permute-start.8 = (bf16[64,256]{1,0:T(8,128)(2,1)S(1)}, bf16[64,256]{1,0:T(8,128)(2,1)S(1)}, u32[]{:S(2)}, u32[]{:S(2)}) collective-permute-start(bf16[64,256]{1,0:T(8,128)(2,1)S(1)} %add_convert_fusion.3), channel_id=1, source_target_pairs={{24,0},{25,1},{26,2},{27,3},{28,4},{29,5},{30,6},{31,7},{16,8},{17... | collective-permute-start | bytes 98312 | tf_op jit(solution)/shard_map/ppermute | solution.py:204
  29.3 5.2 %collective-permute-start.7 = (bf16[64,256]{1,0:T(8,128)(2,1)S(1)}, bf16[64,256]{1,0:T(8,128)(2,1)S(1)}, u32[]{:S(2)}, u32[]{:S(2)}) collective-permute-start(bf16[64,256]{1,0:T(8,128)(2,1)S(1)} %add_convert_fusion.3), channel_id=1, source_target_pairs={{16,0},{17,1},{18,2},{19,3},{20,4},{21,5},{22,6},{23,7},{24,8},{25... | collective-permute-start | bytes 98312 | tf_op jit(solution)/shard_map/ppermute | solution.py:204
  34.5 4.3 %collective-permute-start.10 = (bf16[128,256]{1,0:T(8,128)(2,1)S(1)}, bf16[128,256]{1,0:T(8,128)(2,1)S(1)}, u32[]{:S(2)}, u32[]{:S(2)}) collective-permute-start(bf16[128,256]{1,0:T(8,128)(2,1)S(1)} %pad_maximum_fusion.1.refs_0_), channel_id=1, source_target_pairs={{4,0},{5,1},{6,2},{7,3},{0,4},{1,5},{2,6},{3,7},{12,8},{13,9},{14,... | collective-permute-start | bytes 196616 | tf_op jit(solution)/shard_map/ppermute | solution.py:204
  38.8 2.1 %copy-start.8 = (bf16[2,1,256,512]{3,2,1,0:T(8,128)(2,1)S(1)}, bf16[2,1,256,512]{3,2,1,0:T(8,128)(2,1)}, u32[]{:S(2)}) copy-start(bf16[2,1,256,512]{3,2,1,0:T(8,128)(2,1)} %slice.7) | copy-start | bytes 1572868
  39.1 1.3 %collective-permute-start.11 = (f32[64,256]{1,0:T(8,128)S(1)}, f32[64,256]{1,0:T(8,128)S(1)}, u32[]{:S(2)}, u32[]{:S(2)}) collective-permute-start(f32[64,256]{1,0:T(8,128)S(1)} %shard_map.71), channel_id=1, source_target_pairs={{1,0},{0,1},{3,2},{2,3},{5,4},{4,5},{7,6},{6,7},{9,8},{8,9},{11,10... | collective-permute-start | bytes 196616 | tf_op jit(solution)/shard_map/ppermute | solution.py:204
  40.5 4.5 %collective-permute-start.12 = (bf16[64,256]{1,0:T(8,128)(2,1)S(1)}, bf16[64,256]{1,0:T(8,128)(2,1)S(1)}, u32[]{:S(2)}, u32[]{:S(2)}) collective-permute-start(bf16[64,256]{1,0:T(8,128)(2,1)S(1)} %add_convert_fusion.2), channel_id=1, source_target_pairs={{8,0},{9,1},{10,2},{11,3},{12,4},{13,5},{14,6},{15,7},{0,8},{1,9},... | collective-permute-start | bytes 98312 | tf_op jit(solution)/shard_map/ppermute | solution.py:204
  41.0 14.8 %collective-permute-start.18 = (bf16[2,1,256,512]{3,2,1,0:T(8,128)(2,1)S(1)}, bf16[2,1,256,512]{3,2,1,0:T(8,128)(2,1)S(1)}, u32[]{:S(2)}, u32[]{:S(2)}) collective-permute-start(bf16[2,1,256,512]{3,2,1,0:T(8,128)(2,1)S(1)} %copy-done.8), channel_id=1, source_target_pairs={{2,0},{3,1},{0,2},{1,3},{6,4},{7,5},{4,6},{5,7},{10,8},{11,9},{8,1... | collective-permute-start | bytes 1572872 | tf_op jit(solution)/shard_map/ppermute | solution.py:204
  41.5 5.9 %collective-permute-start.14 = (bf16[64,256]{1,0:T(8,128)(2,1)S(1)}, bf16[64,256]{1,0:T(8,128)(2,1)S(1)}, u32[]{:S(2)}, u32[]{:S(2)}) collective-permute-start(bf16[64,256]{1,0:T(8,128)(2,1)S(1)} %add_convert_fusion.2), channel_id=1, source_target_pairs={{24,0},{25,1},{26,2},{27,3},{28,4},{29,5},{30,6},{31,7},{16,8},{17... | collective-permute-start | bytes 98312 | tf_op jit(solution)/shard_map/ppermute | solution.py:204
  44.9 4.8 %collective-permute-start.13 = (bf16[64,256]{1,0:T(8,128)(2,1)S(1)}, bf16[64,256]{1,0:T(8,128)(2,1)S(1)}, u32[]{:S(2)}, u32[]{:S(2)}) collective-permute-start(bf16[64,256]{1,0:T(8,128)(2,1)S(1)} %add_convert_fusion.2), channel_id=1, source_target_pairs={{16,0},{17,1},{18,2},{19,3},{20,4},{21,5},{22,6},{23,7},{24,8},{25... | collective-permute-start | bytes 98312 | tf_op jit(solution)/shard_map/ppermute | solution.py:204
  49.8 4.3 %collective-permute-start.15 = (bf16[128,256]{1,0:T(8,128)(2,1)S(1)}, bf16[128,256]{1,0:T(8,128)(2,1)S(1)}, u32[]{:S(2)}, u32[]{:S(2)}) collective-permute-start(bf16[128,256]{1,0:T(8,128)(2,1)S(1)} %pad_maximum_fusion.2.refs_0_), channel_id=1, source_target_pairs={{4,0},{5,1},{6,2},{7,3},{0,4},{1,5},{2,6},{3,7},{12,8},{13,9},{14,... | collective-permute-start | bytes 196616 | tf_op jit(solution)/shard_map/ppermute | solution.py:204
  54.4 1.3 %collective-permute-start.16 = (f32[64,256]{1,0:T(8,128)S(1)}, f32[64,256]{1,0:T(8,128)S(1)}, u32[]{:S(2)}, u32[]{:S(2)}) collective-permute-start(f32[64,256]{1,0:T(8,128)S(1)} %shard_map.73), channel_id=1, source_target_pairs={{1,0},{0,1},{3,2},{2,3},{5,4},{4,5},{7,6},{6,7},{9,8},{8,9},{11,10... | collective-permute-start | bytes 196616 | tf_op jit(solution)/shard_map/ppermute | solution.py:204
  55.8 4.1 %collective-permute-start.19 = (bf16[64,256]{1,0:T(8,128)(2,1)S(1)}, bf16[64,256]{1,0:T(8,128)(2,1)S(1)}, u32[]{:S(2)}, u32[]{:S(2)}) collective-permute-start(bf16[64,256]{1,0:T(8,128)(2,1)S(1)} %add_convert_fusion.1), channel_id=1, source_target_pairs={{8,0},{9,1},{10,2},{11,3},{12,4},{13,5},{14,6},{15,7},{0,8},{1,9},... | collective-permute-start | bytes 98312 | tf_op jit(solution)/shard_map/ppermute | solution.py:204
  56.3 5.7 %collective-permute-start.21 = (bf16[64,256]{1,0:T(8,128)(2,1)S(1)}, bf16[64,256]{1,0:T(8,128)(2,1)S(1)}, u32[]{:S(2)}, u32[]{:S(2)}) collective-permute-start(bf16[64,256]{1,0:T(8,128)(2,1)S(1)} %add_convert_fusion.1), channel_id=1, source_target_pairs={{24,0},{25,1},{26,2},{27,3},{28,4},{29,5},{30,6},{31,7},{16,8},{17... | collective-permute-start | bytes 98312 | tf_op jit(solution)/shard_map/ppermute | solution.py:204
  57.6 5.3 %collective-permute-start.20 = (bf16[64,256]{1,0:T(8,128)(2,1)S(1)}, bf16[64,256]{1,0:T(8,128)(2,1)S(1)}, u32[]{:S(2)}, u32[]{:S(2)}) collective-permute-start(bf16[64,256]{1,0:T(8,128)(2,1)S(1)} %add_convert_fusion.1), channel_id=1, source_target_pairs={{16,0},{17,1},{18,2},{19,3},{20,4},{21,5},{22,6},{23,7},{24,8},{25... | collective-permute-start | bytes 98312 | tf_op jit(solution)/shard_map/ppermute | solution.py:204
  59.3 7.8 %collective-permute-start.17 = (bf16[128,256]{1,0:T(8,128)(2,1)S(1)}, bf16[128,256]{1,0:T(8,128)(2,1)S(1)}, u32[]{:S(2)}, u32[]{:S(2)}) collective-permute-start(bf16[128,256]{1,0:T(8,128)(2,1)S(1)} %pad_maximum_fusion.3.refs_0_), channel_id=1, source_target_pairs={{2,0},{3,1},{0,2},{1,3},{6,4},{7,5},{4,6},{5,7},{10,8},{11,9},{8,1... | collective-permute-start | bytes 196616 | tf_op jit(solution)/shard_map/ppermute | solution.py:204
  62.9 4.5 %collective-permute-start.22 = (bf16[128,256]{1,0:T(8,128)(2,1)S(1)}, bf16[128,256]{1,0:T(8,128)(2,1)S(1)}, u32[]{:S(2)}, u32[]{:S(2)}) collective-permute-start(bf16[128,256]{1,0:T(8,128)(2,1)S(1)} %pad_maximum_fusion.4.refs_0_), channel_id=1, source_target_pairs={{4,0},{5,1},{6,2},{7,3},{0,4},{1,5},{2,6},{3,7},{12,8},{13,9},{14,... | collective-permute-start | bytes 196616 | tf_op jit(solution)/shard_map/ppermute | solution.py:204
  67.7 1.3 %collective-permute-start.23 = (f32[64,256]{1,0:T(8,128)S(1)}, f32[64,256]{1,0:T(8,128)S(1)}, u32[]{:S(2)}, u32[]{:S(2)}) collective-permute-start(f32[64,256]{1,0:T(8,128)S(1)} %shard_map.78), channel_id=1, source_target_pairs={{1,0},{0,1},{3,2},{2,3},{5,4},{4,5},{7,6},{6,7},{9,8},{8,9},{11,10... | collective-permute-start | bytes 196616 | tf_op jit(solution)/shard_map/ppermute | solution.py:204
  69.1 4.0 %collective-permute-start.24 = (bf16[64,256]{1,0:T(8,128)(2,1)S(1)}, bf16[64,256]{1,0:T(8,128)(2,1)S(1)}, u32[]{:S(2)}, u32[]{:S(2)}) collective-permute-start(bf16[64,256]{1,0:T(8,128)(2,1)S(1)} %add_convert_fusion.refs_0_), channel_id=1, source_target_pairs={{2,0},{3,1},{0,2},{1,3},{6,4},{7,5},{4,6},{5,7},{10,8},{11,9},{8,1... | collective-permute-start | bytes 98312 | tf_op jit(solution)/shard_map/ppermute | solution.py:204

commit v4 on v2

--- a/solution.py
+++ b/solution.py
@@ -118,29 +118,24 @@
     pieces, stacks, out, blocks = refs[:chips], refs[chips:-2], refs[-2], refs[-1]
     row, chip, core = spot[ROW], spot[CHIP], spot[CORE]
     depth, line = spot[DEPTH], spot[LINE]
-    share, size = base.shape
+    share = base.shape[0]
+    size = base.shape[1]
     for index, stack in enumerate(stacks):
         for turn in range(chips):
-            blocks[index * chips + turn] = stack[turn * share : (turn + 1) * share, :]
-
-    def times(left, right):
-        return lax.dot_general(
-            left, right, (((1,), (1,)), ((), ())), preferred_element_type=jnp.float32
-        )
-
-    total = jnp.zeros((share, size), jnp.float32)
+            block = stack[turn * share : (turn + 1) * share, :].astype(jnp.float32)
+            blocks[index * chips + turn] = block.T.astype(jnp.bfloat16)
+    total = jnp.zeros((size, share), jnp.float32)
     for index, piece in enumerate(pieces):
         deep = (chip ^ index) * CORES + core
         turn = (deep // CORES) ^ (depth // CORES)
         for across in range(lines):
             keep = pattern[pair, row, deep * lines + across]
-            matrix = piece[0, 0, :, across * size : (across + 1) * size]
-            matrix = jnp.where(keep > 0, matrix, jnp.zeros_like(matrix))
-            total = total + times(blocks[(across ^ line) * chips + turn], matrix)
-    value = base[...]
-    for part in split(total, 3):
-        value = value - times(part, inverse[0, 0])
-    out[...] = value
+            block = blocks[(across ^ line) * chips + turn]
+            block = jnp.where(keep > 0, block, jnp.zeros_like(block))
+            columns = slice(across * size, (across + 1) * size)
+            total = total + exact(piece[0, 0, :, columns], block)
+    value = sum(exact(inverse[0, 0], part) for part in split(total, 3))
+    out[...] = base[...] - value.T
 
 
 def step_kernel(lines, base, *refs):
@@ -320,7 +315,7 @@
                     piece,
                     [spot, pattern, value, level_of(lower_inverse, 1)] + pieces + fetched[0],
                     scalars=2,
-                    scratch=[pltpu.VMEM((near * lines, share, size), jnp.bfloat16)],
+                    scratch=[pltpu.VMEM((near * lines, size, share), jnp.bfloat16)],
                 )
             else:
                 fold_lower(level, False, stack)

time: 74.5 us -> 74.6 us (level)
  no operation moved by 1% of the time
where the time goes in v4:
time: 74.6 us; the launch traced here: 74.4 us
  starting transfers between devices  29.7 us (40%)
  waiting for transfers between devices  24.2 us (32%)
  Pallas kernels  16.6 us (22%)
  local copies, waits for them, and re-layouts  3.58 us (5%)
    ppermute x25, starting transfers between devices, send(): return lax.ppermute(value, ('prow', 'pcol'), pairs)  29.7 us
    ppermute x25, waiting for transfers between devices, send(): return lax.ppermute(value, ('prow', 'pcol'), pairs)  24.2 us
    pallas_call x16, Pallas kernels, call(): pl.pallas_call(kernel, grid=(1,), out_shape=shapes, in_specs=specs, out_s...  16.6 us
    slice x2, local copies, waits for them, and re-layouts, body(): parts = (upper_blocks[last_pair:], upper_blocks[:last_pair])  2.49 us
  transfers between devices with their start and end apart: 25, of which 16 were waited for; matrix products, arithmetic and copies ran while one was open for 4% of the time, Pallas kernels for 18%

profile of v4, /device:TPU:0, one launch (start us, length us, event | category | flops | bytes accessed | tf_op | source)
XLA Modules:
  0.0 74.4 jit_solution(7689408657995636797)
XLA Ops:
  0.0 2.9 %collective-permute-start.4 = (bf16[3,1,256,512]{3,2,1,0:T(8,128)(2,1)}, bf16[3,1,256,512]{3,2,1,0:T(8,128)(2,1)S(1)}, u32[]{:S(2)}, u32[]{:S(2)}) collective-permute-start(bf16[3,1,256,512]{3,2,1,0:T(8,128)(2,1)} %refs_2_.3), channel_id=1, source_target_pairs={{2,0},{3,1},{0,2},{1,3},{6,4},{7,5},{4,6},{5,7},{10,8},{11,9},{8,1... | collective-permute-start | bytes 2359304 | tf_op jit(solution)/shard_map/ppermute | solution.py:199
  2.9 0.6 stack.23.spot
  3.5 1.8 %shard_map.64.first = bf16[64,256]{1,0:T(8,128)(2,1)} custom-call(s32[5]{0:T(128)} %stack.23.spot, bf16[3,1,256,128]{3,2,1,0:T(8,128)(2,1)} %rhs.3, bf16[3,1,256,256]{3,2,1,0:T(8,128)(2,1)} %refs_1_.6), custom_call_target="tpu_custom_call" | custom-call | tf_op jit(solution)/shard_map/pallas_call | solution.py:49
  5.3 1.6 %collective-permute-start = (bf16[64,256]{1,0:T(8,128)(2,1)}, bf16[64,256]{1,0:T(8,128)(2,1)S(1)}, u32[]{:S(2)}, u32[]{:S(2)}) collective-permute-start(bf16[64,256]{1,0:T(8,128)(2,1)} %shard_map.64.first), channel_id=1, source_target_pairs={{8,0},{9,1},{10,2},{11,3},{12,4},{13,5},{14,6},{15,7},{0,8},{1,9},... | collective-permute-start | bytes 98312 | tf_op jit(solution)/shard_map/ppermute | solution.py:199
  6.9 2.5 %collective-permute-start.2 = (bf16[64,256]{1,0:T(8,128)(2,1)}, bf16[64,256]{1,0:T(8,128)(2,1)S(1)}, u32[]{:S(2)}, u32[]{:S(2)}) collective-permute-start(bf16[64,256]{1,0:T(8,128)(2,1)} %shard_map.64.first), channel_id=1, source_target_pairs={{24,0},{25,1},{26,2},{27,3},{28,4},{29,5},{30,6},{31,7},{16,8},{17... | collective-permute-start | bytes 98312 | tf_op jit(solution)/shard_map/ppermute | solution.py:199
  9.4 0.1 collective-permute-start.1
  9.5 1.7 %slice.6 = bf16[1,1,256,512]{3,2,1,0:T(8,128)(2,1)} slice(bf16[3,1,256,512]{3,2,1,0:T(8,128)(2,1)} %refs_1_.9), slice={[2:3], [0:1], [0:256], [0:512]} | slice | bytes 524288 | tf_op jit(solution)/shard_map/slice | solution.py:281
  11.2 0.0 copy-start.6
  11.2 0.8 %slice.7 = bf16[2,1,256,512]{3,2,1,0:T(8,128)(2,1)} slice(bf16[3,1,256,512]{3,2,1,0:T(8,128)(2,1)S(1)} %copy-done.1), slice={[0:2], [0:1], [0:256], [0:512]} | slice | bytes 1048576 | tf_op jit(solution)/shard_map/slice | solution.py:281
  12.0 0.2 copy-done
  12.2 0.2 copy-done.2
  12.5 0.0 copy-done.4
  12.5 1.4 %shard_map.65 = (f32[64,256]{1,0:T(8,128)S(1)}, f32[64,256]{1,0:T(8,128)S(1)}, f32[64,256]{1,0:T(8,128)S(1)}, f32[64,256]{1,0:T(8,128)S(1)}) custom-call(s32[5]{0:T(128)S(1)} %copy-done.7, bf16[64,256]{1,0:T(8,128)(2,1)S(1)} %copy-done.6, bf16[3,1,256,128]{3,2,1,0:T(8,128)(2,1)S(1)} %copy-done.4, bf16[3,1,256,256]{3,2,1,0:T(8,128)(2,1)S(1)} %copy-done.2, ...), custom_call_target="tpu_custom_call" | custom-call | tf_op jit(solution)/shard_map/pallas_call | solution.py:49
  13.9 0.0 collective-permute-done
  14.0 0.8 %collective-permute-done.1 = bf16[64,256]{1,0:T(8,128)(2,1)S(1)} collective-permute-done((bf16[64,256]{1,0:T(8,128)(2,1)}, bf16[64,256]{1,0:T(8,128)(2,1)S(1)}, u32[]{:S(2)}, u32[]{:S(2)}) %collective-permute-start.1) | collective-permute-done | bytes 32800 | tf_op jit(solution)/shard_map/ppermute | solution.py:199
  14.8 1.6 %collective-permute-start.3 = (bf16[128,256]{1,0:T(8,128)(2,1)S(1)}, bf16[128,256]{1,0:T(8,128)(2,1)S(1)}, u32[]{:S(2)}, u32[]{:S(2)}) collective-permute-start(bf16[128,256]{1,0:T(8,128)(2,1)S(1)} %pad_maximum_fusion.refs_2_.refs_0_), channel_id=1, source_target_pairs={{4,0},{5,1},{6,2},{7,3},{0,4},{1,5},{2,6},{3,7},{12,8},{13,9},{14,... | collective-permute-start | bytes 196616 | tf_op jit(solution)/shard_map/ppermute | solution.py:199
  16.4 2.7 %collective-permute-done.3.refs_3_.refs_1_ = bf16[128,256]{1,0:T(8,128)(2,1)S(1)} collective-permute-done((bf16[128,256]{1,0:T(8,128)(2,1)S(1)}, bf16[128,256]{1,0:T(8,128)(2,1)S(1)}, u32[]{:S(2)}, u32[]{:S(2)}) %collective-permute-start.3) | collective-permute-done | bytes 65568 | tf_op jit(solution)/shard_map/ppermute | solution.py:199
  19.1 1.6 %collective-permute-done.4.refs_1_.refs_3_ = bf16[3,1,256,512]{3,2,1,0:T(8,128)(2,1)S(1)} collective-permute-done((bf16[3,1,256,512]{3,2,1,0:T(8,128)(2,1)}, bf16[3,1,256,512]{3,2,1,0:T(8,128)(2,1)S(1)}, u32[]{:S(2)}, u32[]{:S(2)}) %collective-permute-start.4) | collective-permute-done | bytes 786464 | tf_op jit(solution)/shard_map/ppermute | solution.py:199
  20.7 1.5 %shard_map.66 = f32[64,256]{1,0:T(8,128)S(1)} custom-call(s32[5]{0:T(128)S(1)} %copy-done.7, s32[3,8,8]{2,1,0:T(8,128)S(1)} %copy-done.5, f32[64,256]{1,0:T(8,128)S(1)} %get-tuple-element.26.base, bf16[3,1,256,256]{3,2,1,0:T(8,128)(2,1)S(1)} %copy-done.2, bf16[3,1,256,512]{3,2,1,0:T(8,128)(2,1)S(1)} %copy-done.3, ...), custom_call_target="tpu_custom_call" | custom-call | tf_op jit(solution)/shard_map/pallas_call | solution.py:49
  22.2 0.1 collective-permute-start.5
  22.3 1.2 %collective-permute-done.5 = f32[64,256]{1,0:T(8,128)S(1)} collective-permute-done((f32[64,256]{1,0:T(8,128)S(1)}, f32[64,256]{1,0:T(8,128)S(1)}, u32[]{:S(2)}, u32[]{:S(2)}) %collective-permute-start.5) | collective-permute-done | bytes 65568 | tf_op jit(solution)/shard_map/ppermute | solution.py:199
  23.6 1.9 %collective-permute-start.6 = (bf16[64,256]{1,0:T(8,128)(2,1)S(1)}, bf16[64,256]{1,0:T(8,128)(2,1)S(1)}, u32[]{:S(2)}, u32[]{:S(2)}) collective-permute-start(bf16[64,256]{1,0:T(8,128)(2,1)S(1)} %add_convert_fusion.3), channel_id=1, source_target_pairs={{8,0},{9,1},{10,2},{11,3},{12,4},{13,5},{14,6},{15,7},{0,8},{1,9},... | collective-permute-start | bytes 98312 | tf_op jit(solution)/shard_map/ppermute | solution.py:199
  25.4 1.5 %collective-permute-start.9 = (bf16[1,1,256,512]{3,2,1,0:T(8,128)(2,1)S(1)}, bf16[1,1,256,512]{3,2,1,0:T(8,128)(2,1)S(1)}, u32[]{:S(2)}, u32[]{:S(2)}) collective-permute-start(bf16[1,1,256,512]{3,2,1,0:T(8,128)(2,1)S(1)} %copy-done.9), channel_id=1, source_target_pairs={{2,0},{3,1},{0,2},{1,3},{6,4},{7,5},{4,6},{5,7},{10,8},{11,9},{8,1... | collective-permute-start | bytes 786440 | tf_op jit(solution)/shard_map/ppermute | solution.py:199
  26.9 2.5 %collective-permute-start.8 = (bf16[64,256]{1,0:T(8,128)(2,1)S(1)}, bf16[64,256]{1,0:T(8,128)(2,1)S(1)}, u32[]{:S(2)}, u32[]{:S(2)}) collective-permute-start(bf16[64,256]{1,0:T(8,128)(2,1)S(1)} %add_convert_fusion.3), channel_id=1, source_target_pairs={{24,0},{25,1},{26,2},{27,3},{28,4},{29,5},{30,6},{31,7},{16,8},{17... | collective-permute-start | bytes 98312 | tf_op jit(solution)/shard_map/ppermute | solution.py:199
  29.4 0.1 collective-permute-start.7
  29.5 1.6 %shard_map.67.refs_2_ = bf16[4,2,256,256]{3,2,1,0:T(8,128)(2,1)S(1)} custom-call(s32[5]{0:T(128)S(1)} %copy-done.7, s32[3,8,8]{2,1,0:T(8,128)S(1)} %copy-done.5, bf16[3,1,256,256]{3,2,1,0:T(8,128)(2,1)S(1)} %copy-done, bf16[3,1,256,256]{3,2,1,0:T(8,128)(2,1)S(1)} %copy-done.2, bf16[3,1,256,512]{3,2,1,0:T(8,128)(2,1)S(1)} %copy-done.3, ...), custom_call_target="tpu_custom_call" | custom-call | tf_op jit(solution)/shard_map/pallas_call | solution.py:49
  31.1 1.9 %collective-permute-done.8 = bf16[64,256]{1,0:T(8,128)(2,1)S(1)} collective-permute-done((bf16[64,256]{1,0:T(8,128)(2,1)S(1)}, bf16[64,256]{1,0:T(8,128)(2,1)S(1)}, u32[]{:S(2)}, u32[]{:S(2)}) %collective-permute-start.8) | collective-permute-done | bytes 32800 | tf_op jit(solution)/shard_map/ppermute | solution.py:199
  33.1 1.5 %collective-permute-done.7 = bf16[64,256]{1,0:T(8,128)(2,1)S(1)} collective-permute-done((bf16[64,256]{1,0:T(8,128)(2,1)S(1)}, bf16[64,256]{1,0:T(8,128)(2,1)S(1)}, u32[]{:S(2)}, u32[]{:S(2)}) %collective-permute-start.7) | collective-permute-done | bytes 32800 | tf_op jit(solution)/shard_map/ppermute | solution.py:199
  34.6 1.6 %collective-permute-start.10 = (bf16[128,256]{1,0:T(8,128)(2,1)S(1)}, bf16[128,256]{1,0:T(8,128)(2,1)S(1)}, u32[]{:S(2)}, u32[]{:S(2)}) collective-permute-start(bf16[128,256]{1,0:T(8,128)(2,1)S(1)} %pad_maximum_fusion.1.refs_0_), channel_id=1, source_target_pairs={{4,0},{5,1},{6,2},{7,3},{0,4},{1,5},{2,6},{3,7},{12,8},{13,9},{14,... | collective-permute-start | bytes 196616 | tf_op jit(solution)/shard_map/ppermute | solution.py:199
  36.2 2.0 %shard_map.69 = (bf16[4,2,256,256]{3,2,1,0:T(8,128)(2,1)S(1)}, bf16[4,2,256,256]{3,2,1,0:T(8,128)(2,1)S(1)}) custom-call(s32[5]{0:T(128)S(1)} %copy-done.7, s32[3,8,8]{2,1,0:T(8,128)S(1)} %copy-done.5, bf16[3,1,256,256]{3,2,1,0:T(8,128)(2,1)S(1)} %copy-done, bf16[3,1,256,256]{3,2,1,0:T(8,128)(2,1)S(1)} %copy-done.2, bf16[3,1,256,512]{3,2,1,0:T(8,128)(2,1)S(1)} %copy-done.3, ...), custom_call_target="tpu_custom_call" | custom-call | tf_op jit(solution)/shard_map/pallas_call | solution.py:49
  38.2 0.3 shard_map.70.base
  38.5 0.4 collective-permute-done.10.refs_1_
  38.9 0.3 shard_map.71
  39.2 0.1 collective-permute-start.11
  39.3 1.2 %collective-permute-done.11 = f32[64,256]{1,0:T(8,128)S(1)} collective-permute-done((f32[64,256]{1,0:T(8,128)S(1)}, f32[64,256]{1,0:T(8,128)S(1)}, u32[]{:S(2)}, u32[]{:S(2)}) %collective-permute-start.11) | collective-permute-done | bytes 65568 | tf_op jit(solution)/shard_map/ppermute | solution.py:199
  40.6 0.5 collective-permute-start.12
  41.1 0.5 collective-permute-start.18
  41.6 3.4 %collective-permute-start.14 = (bf16[64,256]{1,0:T(8,128)(2,1)S(1)}, bf16[64,256]{1,0:T(8,128)(2,1)S(1)}, u32[]{:S(2)}, u32[]{:S(2)}) collective-permute-start(bf16[64,256]{1,0:T(8,128)(2,1)S(1)} %add_convert_fusion.2), channel_id=1, source_target_pairs={{24,0},{25,1},{26,2},{27,3},{28,4},{29,5},{30,6},{31,7},{16,8},{17... | collective-permute-start | bytes 98312 | tf_op jit(solution)/shard_map/ppermute | solution.py:199
  45.1 2.5 %collective-permute-done.14 = bf16[64,256]{1,0:T(8,128)(2,1)S(1)} collective-permute-done((bf16[64,256]{1,0:T(8,128)(2,1)S(1)}, bf16[64,256]{1,0:T(8,128)(2,1)S(1)}, u32[]{:S(2)}, u32[]{:S(2)}) %collective-permute-start.14) | collective-permute-done | bytes 32800 | tf_op jit(solution)/shard_map/ppermute | solution.py:199
  47.6 2.3 %collective-permute-done.13 = bf16[64,256]{1,0:T(8,128)(2,1)S(1)} collective-permute-done((bf16[64,256]{1,0:T(8,128)(2,1)S(1)}, bf16[64,256]{1,0:T(8,128)(2,1)S(1)}, u32[]{:S(2)}, u32[]{:S(2)}) %collective-permute-start.13) | collective-permute-done | bytes 32800 | tf_op jit(solution)/shard_map/ppermute | solution.py:199
  49.9 1.6 %collective-permute-start.15 = (bf16[128,256]{1,0:T(8,128)(2,1)S(1)}, bf16[128,256]{1,0:T(8,128)(2,1)S(1)}, u32[]{:S(2)}, u32[]{:S(2)}) collective-permute-start(bf16[128,256]{1,0:T(8,128)(2,1)S(1)} %pad_maximum_fusion.2.refs_0_), channel_id=1, source_target_pairs={{4,0},{5,1},{6,2},{7,3},{0,4},{1,5},{2,6},{3,7},{12,8},{13,9},{14,... | collective-permute-start | bytes 196616 | tf_op jit(solution)/shard_map/ppermute | solution.py:199
  51.5 0.3 shard_map.68.base
  51.8 1.3 %shard_map.72.refs_2_ = bf16[4,2,256,256]{3,2,1,0:T(8,128)(2,1)S(1)} custom-call(s32[5]{0:T(128)S(1)} %copy-done.7, s32[3,8,8]{2,1,0:T(8,128)S(1)} %copy-done.5, bf16[3,1,256,256]{3,2,1,0:T(8,128)(2,1)S(1)} %copy-done, bf16[3,1,256,512]{3,2,1,0:T(8,128)(2,1)S(1)} %copy-done.1, bf16[1,1,256,512]{3,2,1,0:T(8,128)(2,1)S(1)} %collective-permute-done.9.refs_2_), custom_call_target="tpu_custom_call" | custom-call | tf_op jit(solution)/shard_map/pallas_call | solution.py:49
  53.1 1.2 %collective-permute-done.15.refs_1_ = bf16[128,256]{1,0:T(8,128)(2,1)S(1)} collective-permute-done((bf16[128,256]{1,0:T(8,128)(2,1)S(1)}, bf16[128,256]{1,0:T(8,128)(2,1)S(1)}, u32[]{:S(2)}, u32[]{:S(2)}) %collective-permute-start.15) | collective-permute-done | bytes 65568 | tf_op jit(solution)/shard_map/ppermute | solution.py:199
  54.2 0.3 shard_map.73
  54.5 0.1 collective-permute-start.16
  54.6 1.2 %collective-permute-done.16 = f32[64,256]{1,0:T(8,128)S(1)} collective-permute-done((f32[64,256]{1,0:T(8,128)S(1)}, f32[64,256]{1,0:T(8,128)S(1)}, u32[]{:S(2)}, u32[]{:S(2)}) %collective-permute-start.16) | collective-permute-done | bytes 65568 | tf_op jit(solution)/shard_map/ppermute | solution.py:199
  55.9 0.5 collective-permute-start.19
  56.4 1.4 %collective-permute-start.21 = (bf16[64,256]{1,0:T(8,128)(2,1)S(1)}, bf16[64,256]{1,0:T(8,128)(2,1)S(1)}, u32[]{:S(2)}, u32[]{:S(2)}) collective-permute-start(bf16[64,256]{1,0:T(8,128)(2,1)S(1)} %add_convert_fusion.1), channel_id=1, source_target_pairs={{24,0},{25,1},{26,2},{27,3},{28,4},{29,5},{30,6},{31,7},{16,8},{17... | collective-permute-start | bytes 98312 | tf_op jit(solution)/shard_map/ppermute | solution.py:199
  57.8 1.7 %collective-permute-start.20 = (bf16[64,256]{1,0:T(8,128)(2,1)S(1)}, bf16[64,256]{1,0:T(8,128)(2,1)S(1)}, u32[]{:S(2)}, u32[]{:S(2)}) collective-permute-start(bf16[64,256]{1,0:T(8,128)(2,1)S(1)} %add_convert_fusion.1), channel_id=1, source_target_pairs={{16,0},{17,1},{18,2},{19,3},{20,4},{21,5},{22,6},{23,7},{24,8},{25... | collective-permute-start | bytes 98312 | tf_op jit(solution)/shard_map/ppermute | solution.py:199
  59.4 0.5 collective-permute-start.17
  60.0 2.1 %collective-permute-done.21 = bf16[64,256]{1,0:T(8,128)(2,1)S(1)} collective-permute-done((bf16[64,256]{1,0:T(8,128)(2,1)S(1)}, bf16[64,256]{1,0:T(8,128)(2,1)S(1)}, u32[]{:S(2)}, u32[]{:S(2)}) %collective-permute-start.21) | collective-permute-done | bytes 32800 | tf_op jit(solution)/shard_map/ppermute | solution.py:199
  62.1 0.9 %collective-permute-done.20 = bf16[64,256]{1,0:T(8,128)(2,1)S(1)} collective-permute-done((bf16[64,256]{1,0:T(8,128)(2,1)S(1)}, bf16[64,256]{1,0:T(8,128)(2,1)S(1)}, u32[]{:S(2)}, u32[]{:S(2)}) %collective-permute-start.20) | collective-permute-done | bytes 32800 | tf_op jit(solution)/shard_map/ppermute | solution.py:199
  63.1 1.6 %collective-permute-start.22 = (bf16[128,256]{1,0:T(8,128)(2,1)S(1)}, bf16[128,256]{1,0:T(8,128)(2,1)S(1)}, u32[]{:S(2)}, u32[]{:S(2)}) collective-permute-start(bf16[128,256]{1,0:T(8,128)(2,1)S(1)} %pad_maximum_fusion.4.refs_0_), channel_id=1, source_target_pairs={{4,0},{5,1},{6,2},{7,3},{0,4},{1,5},{2,6},{3,7},{12,8},{13,9},{14,... | collective-permute-start | bytes 196616 | tf_op jit(solution)/shard_map/ppermute | solution.py:199
  64.6 1.3 %shard_map.77.refs_2_ = bf16[4,2,256,256]{3,2,1,0:T(8,128)(2,1)S(1)} custom-call(s32[5]{0:T(128)S(1)} %copy-done.7, s32[3,8,8]{2,1,0:T(8,128)S(1)} %copy-done.5, bf16[3,1,256,256]{3,2,1,0:T(8,128)(2,1)S(1)} %copy-done, bf16[3,1,256,512]{3,2,1,0:T(8,128)(2,1)S(1)} %copy-done.1, bf16[2,1,256,512]{3,2,1,0:T(8,128)(2,1)S(1)} %collective-permute-done.18.refs_2_), custom_call_target="tpu_custom_call" | custom-call | tf_op jit(solution)/shard_map/pallas_call | solution.py:49
  65.9 1.3 %shard_map.75.refs_2_ = bf16[4,2,256,256]{3,2,1,0:T(8,128)(2,1)S(1)} custom-call(s32[5]{0:T(128)S(1)} %copy-done.7, s32[3,8,8]{2,1,0:T(8,128)S(1)} %copy-done.5, bf16[3,1,256,256]{3,2,1,0:T(8,128)(2,1)S(1)} %copy-done, bf16[3,1,256,512]{3,2,1,0:T(8,128)(2,1)S(1)} %copy-done.1, bf16[2,1,256,512]{3,2,1,0:T(8,128)(2,1)S(1)} %collective-permute-done.18.refs_2_), custom_call_target="tpu_custom_call" | custom-call | tf_op jit(solution)/shard_map/pallas_call | solution.py:49
  67.2 0.3 shard_map.76.base
  67.5 0.3 shard_map.78
  67.8 0.1 collective-permute-start.23
  67.9 1.2 %collective-permute-done.23 = f32[64,256]{1,0:T(8,128)S(1)} collective-permute-done((f32[64,256]{1,0:T(8,128)S(1)}, f32[64,256]{1,0:T(8,128)S(1)}, u32[]{:S(2)}, u32[]{:S(2)}) %collective-permute-start.23) | collective-permute-done | bytes 65568 | tf_op jit(solution)/shard_map/ppermute | solution.py:199
  69.2 1.4 %collective-permute-start.24 = (bf16[64,256]{1,0:T(8,128)(2,1)S(1)}, bf16[64,256]{1,0:T(8,128)(2,1)S(1)}, u32[]{:S(2)}, u32[]{:S(2)}) collective-permute-start(bf16[64,256]{1,0:T(8,128)(2,1)S(1)} %add_convert_fusion.refs_0_), channel_id=1, source_target_pairs={{2,0},{3,1},{0,2},{1,3},{6,4},{7,5},{4,6},{5,7},{10,8},{11,9},{8,1... | collective-permute-start | bytes 98312 | tf_op jit(solution)/shard_map/ppermute | solution.py:199
  70.6 1.4 %shard_map.74.whole = bf16[3,1,256,128]{3,2,1,0:T(8,128)(2,1)} custom-call(s32[5]{0:T(128)S(1)} %copy-done.7, bf16[128,256]{1,0:T(8,128)(2,1)S(1)} %pad_maximum_fusion.3.refs_0_, bf16[128,256]{1,0:T(8,128)(2,1)S(1)} %collective-permute-done.17.refs_1_), custom_call_target="tpu_custom_call" | custom-call | tf_op jit(solution)/shard_map/pallas_call | solution.py:49
  71.9 1.2 %collective-permute-done.24.refs_1_ = bf16[64,256]{1,0:T(8,128)(2,1)S(1)} collective-permute-done((bf16[64,256]{1,0:T(8,128)(2,1)S(1)}, bf16[64,256]{1,0:T(8,128)(2,1)S(1)}, u32[]{:S(2)}, u32[]{:S(2)}) %collective-permute-start.24) | collective-permute-done | bytes 32800 | tf_op jit(solution)/shard_map/ppermute | solution.py:199
  73.1 1.3 %shard_map.79 = bf16[3,1,256,128]{3,2,1,0:T(8,128)(2,1)} custom-call(s32[5]{0:T(128)S(1)} %copy-done.7, bf16[3,1,256,128]{3,2,1,0:T(8,128)(2,1)} %shard_map.74.whole, bf16[64,256]{1,0:T(8,128)(2,1)S(1)} %add_convert_fusion.refs_0_, bf16[64,256]{1,0:T(8,128)(2,1)S(1)} %collective-permute-done.24.refs_1_), custom_call_target="tpu_custom_call", output_to_operand_aliasing={{}: (1, {})} | custom-call | tf_op jit(solution)/shard_map/pallas_call | solution.py:49
  (42 shorter events, 0.2 us)
Async XLA Ops:
  0.0 11.2 %copy-start.1 = (bf16[3,1,256,512]{3,2,1,0:T(8,128)(2,1)S(1)}, bf16[3,1,256,512]{3,2,1,0:T(8,128)(2,1)}, u32[]{:S(2)}) copy-start(bf16[3,1,256,512]{3,2,1,0:T(8,128)(2,1)} %refs_1_.9) | copy-start | bytes 2359300
  0.0 20.7 %collective-permute-start.4 = (bf16[3,1,256,512]{3,2,1,0:T(8,128)(2,1)}, bf16[3,1,256,512]{3,2,1,0:T(8,128)(2,1)S(1)}, u32[]{:S(2)}, u32[]{:S(2)}) collective-permute-start(bf16[3,1,256,512]{3,2,1,0:T(8,128)(2,1)} %refs_2_.3), channel_id=1, source_target_pairs={{2,0},{3,1},{0,2},{1,3},{6,4},{7,5},{4,6},{5,7},{10,8},{11,9},{8,1... | collective-permute-start | bytes 2359304 | tf_op jit(solution)/shard_map/ppermute | solution.py:199
  5.3 8.6 %collective-permute-start = (bf16[64,256]{1,0:T(8,128)(2,1)}, bf16[64,256]{1,0:T(8,128)(2,1)S(1)}, u32[]{:S(2)}, u32[]{:S(2)}) collective-permute-start(bf16[64,256]{1,0:T(8,128)(2,1)} %shard_map.64.first), channel_id=1, source_target_pairs={{8,0},{9,1},{10,2},{11,3},{12,4},{13,5},{14,6},{15,7},{0,8},{1,9},... | collective-permute-start | bytes 98312 | tf_op jit(solution)/shard_map/ppermute | solution.py:199
  6.9 7.0 %collective-permute-start.2 = (bf16[64,256]{1,0:T(8,128)(2,1)}, bf16[64,256]{1,0:T(8,128)(2,1)S(1)}, u32[]{:S(2)}, u32[]{:S(2)}) collective-permute-start(bf16[64,256]{1,0:T(8,128)(2,1)} %shard_map.64.first), channel_id=1, source_target_pairs={{24,0},{25,1},{26,2},{27,3},{28,4},{29,5},{30,6},{31,7},{16,8},{17... | collective-permute-start | bytes 98312 | tf_op jit(solution)/shard_map/ppermute | solution.py:199
  9.4 5.4 %collective-permute-start.1 = (bf16[64,256]{1,0:T(8,128)(2,1)}, bf16[64,256]{1,0:T(8,128)(2,1)S(1)}, u32[]{:S(2)}, u32[]{:S(2)}) collective-permute-start(bf16[64,256]{1,0:T(8,128)(2,1)} %shard_map.64.first), channel_id=1, source_target_pairs={{16,0},{17,1},{18,2},{19,3},{20,4},{21,5},{22,6},{23,7},{24,8},{25... | collective-permute-start | bytes 98312 | tf_op jit(solution)/shard_map/ppermute | solution.py:199
  11.2 1.1 %copy-start = (bf16[3,1,256,256]{3,2,1,0:T(8,128)(2,1)S(1)}, bf16[3,1,256,256]{3,2,1,0:T(8,128)(2,1)}, u32[]{:S(2)}) copy-start(bf16[3,1,256,256]{3,2,1,0:T(8,128)(2,1)} %refs_0_.11) | copy-start | bytes 1179652
  11.2 1.3 %copy-start.2 = (bf16[3,1,256,256]{3,2,1,0:T(8,128)(2,1)S(1)}, bf16[3,1,256,256]{3,2,1,0:T(8,128)(2,1)}, u32[]{:S(2)}) copy-start(bf16[3,1,256,256]{3,2,1,0:T(8,128)(2,1)} %refs_1_.6) | copy-start | bytes 1179652
  11.2 1.3 %copy-start.4 = (bf16[3,1,256,128]{3,2,1,0:T(8,128)(2,1)S(1)}, bf16[3,1,256,128]{3,2,1,0:T(8,128)(2,1)}, u32[]{:S(2)}) copy-start(bf16[3,1,256,128]{3,2,1,0:T(8,128)(2,1)} %rhs.3) | copy-start | bytes 589828
  11.2 1.3 %copy-start.6 = (bf16[64,256]{1,0:T(8,128)(2,1)S(1)}, bf16[64,256]{1,0:T(8,128)(2,1)}, u32[]{:S(2)}) copy-start(bf16[64,256]{1,0:T(8,128)(2,1)} %shard_map.64.first) | copy-start | bytes 98308
  11.2 1.3 %copy-start.7 = (s32[5]{0:T(128)S(1)}, s32[5]{0:T(128)}, u32[]{:S(2)}) copy-start(s32[5]{0:T(128)} %stack.23.spot) | copy-start | bytes 64
  12.0 8.7 %copy-start.3 = (bf16[3,1,256,512]{3,2,1,0:T(8,128)(2,1)S(1)}, bf16[3,1,256,512]{3,2,1,0:T(8,128)(2,1)}, u32[]{:S(2)}) copy-start(bf16[3,1,256,512]{3,2,1,0:T(8,128)(2,1)} %refs_2_.3) | copy-start | bytes 2359300
  14.8 5.9 %copy-start.5 = (s32[3,8,8]{2,1,0:T(8,128)S(1)}, s32[3,8,8]{2,1,0:T(8,128)}, u32[]{:S(2)}) copy-start(s32[3,8,8]{2,1,0:T(8,128)} %pattern.11) | copy-start | bytes 2308
  14.8 10.7 %copy-start.9 = (bf16[1,1,256,512]{3,2,1,0:T(8,128)(2,1)S(1)}, bf16[1,1,256,512]{3,2,1,0:T(8,128)(2,1)}, u32[]{:S(2)}) copy-start(bf16[1,1,256,512]{3,2,1,0:T(8,128)(2,1)} %slice.6) | copy-start | bytes 786436
  14.8 4.3 %collective-permute-start.3 = (bf16[128,256]{1,0:T(8,128)(2,1)S(1)}, bf16[128,256]{1,0:T(8,128)(2,1)S(1)}, u32[]{:S(2)}, u32[]{:S(2)}) collective-permute-start(bf16[128,256]{1,0:T(8,128)(2,1)S(1)} %pad_maximum_fusion.refs_2_.refs_0_), channel_id=1, source_target_pairs={{4,0},{5,1},{6,2},{7,3},{0,4},{1,5},{2,6},{3,7},{12,8},{13,9},{14,... | collective-permute-start | bytes 196616 | tf_op jit(solution)/shard_map/ppermute | solution.py:199
  22.2 1.3 %collective-permute-start.5 = (f32[64,256]{1,0:T(8,128)S(1)}, f32[64,256]{1,0:T(8,128)S(1)}, u32[]{:S(2)}, u32[]{:S(2)}) collective-permute-start(f32[64,256]{1,0:T(8,128)S(1)} %shard_map.66), channel_id=1, source_target_pairs={{1,0},{0,1},{3,2},{2,3},{5,4},{4,5},{7,6},{6,7},{9,8},{8,9},{11,10... | collective-permute-start | bytes 196616 | tf_op jit(solution)/shard_map/ppermute | solution.py:199
  23.6 6.0 %collective-permute-start.6 = (bf16[64,256]{1,0:T(8,128)(2,1)S(1)}, bf16[64,256]{1,0:T(8,128)(2,1)S(1)}, u32[]{:S(2)}, u32[]{:S(2)}) collective-permute-start(bf16[64,256]{1,0:T(8,128)(2,1)S(1)} %add_convert_fusion.3), channel_id=1, source_target_pairs={{8,0},{9,1},{10,2},{11,3},{12,4},{13,5},{14,6},{15,7},{0,8},{1,9},... | collective-permute-start | bytes 98312 | tf_op jit(solution)/shard_map/ppermute | solution.py:199
  25.4 9.2 %collective-permute-start.9 = (bf16[1,1,256,512]{3,2,1,0:T(8,128)(2,1)S(1)}, bf16[1,1,256,512]{3,2,1,0:T(8,128)(2,1)S(1)}, u32[]{:S(2)}, u32[]{:S(2)}) collective-permute-start(bf16[1,1,256,512]{3,2,1,0:T(8,128)(2,1)S(1)} %copy-done.9), channel_id=1, source_target_pairs={{2,0},{3,1},{0,2},{1,3},{6,4},{7,5},{4,6},{5,7},{10,8},{11,9},{8,1... | collective-permute-start | bytes 786440 | tf_op jit(solution)/shard_map/ppermute | solution.py:199
  26.9 6.1 %collective-permute-start.8 = (bf16[64,256]{1,0:T(8,128)(2,1)S(1)}, bf16[64,256]{1,0:T(8,128)(2,1)S(1)}, u32[]{:S(2)}, u32[]{:S(2)}) collective-permute-start(bf16[64,256]{1,0:T(8,128)(2,1)S(1)} %add_convert_fusion.3), channel_id=1, source_target_pairs={{24,0},{25,1},{26,2},{27,3},{28,4},{29,5},{30,6},{31,7},{16,8},{17... | collective-permute-start | bytes 98312 | tf_op jit(solution)/shard_map/ppermute | solution.py:199
  29.4 5.2 %collective-permute-start.7 = (bf16[64,256]{1,0:T(8,128)(2,1)S(1)}, bf16[64,256]{1,0:T(8,128)(2,1)S(1)}, u32[]{:S(2)}, u32[]{:S(2)}) collective-permute-start(bf16[64,256]{1,0:T(8,128)(2,1)S(1)} %add_convert_fusion.3), channel_id=1, source_target_pairs={{16,0},{17,1},{18,2},{19,3},{20,4},{21,5},{22,6},{23,7},{24,8},{25... | collective-permute-start | bytes 98312 | tf_op jit(solution)/shard_map/ppermute | solution.py:199
  34.6 4.3 %collective-permute-start.10 = (bf16[128,256]{1,0:T(8,128)(2,1)S(1)}, bf16[128,256]{1,0:T(8,128)(2,1)S(1)}, u32[]{:S(2)}, u32[]{:S(2)}) collective-permute-start(bf16[128,256]{1,0:T(8,128)(2,1)S(1)} %pad_maximum_fusion.1.refs_0_), channel_id=1, source_target_pairs={{4,0},{5,1},{6,2},{7,3},{0,4},{1,5},{2,6},{3,7},{12,8},{13,9},{14,... | collective-permute-start | bytes 196616 | tf_op jit(solution)/shard_map/ppermute | solution.py:199
  38.9 2.1 %copy-start.8 = (bf16[2,1,256,512]{3,2,1,0:T(8,128)(2,1)S(1)}, bf16[2,1,256,512]{3,2,1,0:T(8,128)(2,1)}, u32[]{:S(2)}) copy-start(bf16[2,1,256,512]{3,2,1,0:T(8,128)(2,1)} %slice.7) | copy-start | bytes 1572868
  39.2 1.3 %collective-permute-start.11 = (f32[64,256]{1,0:T(8,128)S(1)}, f32[64,256]{1,0:T(8,128)S(1)}, u32[]{:S(2)}, u32[]{:S(2)}) collective-permute-start(f32[64,256]{1,0:T(8,128)S(1)} %shard_map.71), channel_id=1, source_target_pairs={{1,0},{0,1},{3,2},{2,3},{5,4},{4,5},{7,6},{6,7},{9,8},{8,9},{11,10... | collective-permute-start | bytes 196616 | tf_op jit(solution)/shard_map/ppermute | solution.py:199
  40.6 4.5 %collective-permute-start.12 = (bf16[64,256]{1,0:T(8,128)(2,1)S(1)}, bf16[64,256]{1,0:T(8,128)(2,1)S(1)}, u32[]{:S(2)}, u32[]{:S(2)}) collective-permute-start(bf16[64,256]{1,0:T(8,128)(2,1)S(1)} %add_convert_fusion.2), channel_id=1, source_target_pairs={{8,0},{9,1},{10,2},{11,3},{12,4},{13,5},{14,6},{15,7},{0,8},{1,9},... | collective-permute-start | bytes 98312 | tf_op jit(solution)/shard_map/ppermute | solution.py:199
  41.1 14.8 %collective-permute-start.18 = (bf16[2,1,256,512]{3,2,1,0:T(8,128)(2,1)S(1)}, bf16[2,1,256,512]{3,2,1,0:T(8,128)(2,1)S(1)}, u32[]{:S(2)}, u32[]{:S(2)}) collective-permute-start(bf16[2,1,256,512]{3,2,1,0:T(8,128)(2,1)S(1)} %copy-done.8), channel_id=1, source_target_pairs={{2,0},{3,1},{0,2},{1,3},{6,4},{7,5},{4,6},{5,7},{10,8},{11,9},{8,1... | collective-permute-start | bytes 1572872 | tf_op jit(solution)/shard_map/ppermute | solution.py:199
  41.6 5.9 %collective-permute-start.14 = (bf16[64,256]{1,0:T(8,128)(2,1)S(1)}, bf16[64,256]{1,0:T(8,128)(2,1)S(1)}, u32[]{:S(2)}, u32[]{:S(2)}) collective-permute-start(bf16[64,256]{1,0:T(8,128)(2,1)S(1)} %add_convert_fusion.2), channel_id=1, source_target_pairs={{24,0},{25,1},{26,2},{27,3},{28,4},{29,5},{30,6},{31,7},{16,8},{17... | collective-permute-start | bytes 98312 | tf_op jit(solution)/shard_map/ppermute | solution.py:199
  45.1 4.8 %collective-permute-start.13 = (bf16[64,256]{1,0:T(8,128)(2,1)S(1)}, bf16[64,256]{1,0:T(8,128)(2,1)S(1)}, u32[]{:S(2)}, u32[]{:S(2)}) collective-permute-start(bf16[64,256]{1,0:T(8,128)(2,1)S(1)} %add_convert_fusion.2), channel_id=1, source_target_pairs={{16,0},{17,1},{18,2},{19,3},{20,4},{21,5},{22,6},{23,7},{24,8},{25... | collective-permute-start | bytes 98312 | tf_op jit(solution)/shard_map/ppermute | solution.py:199
  49.9 4.3 %collective-permute-start.15 = (bf16[128,256]{1,0:T(8,128)(2,1)S(1)}, bf16[128,256]{1,0:T(8,128)(2,1)S(1)}, u32[]{:S(2)}, u32[]{:S(2)}) collective-permute-start(bf16[128,256]{1,0:T(8,128)(2,1)S(1)} %pad_maximum_fusion.2.refs_0_), channel_id=1, source_target_pairs={{4,0},{5,1},{6,2},{7,3},{0,4},{1,5},{2,6},{3,7},{12,8},{13,9},{14,... | collective-permute-start | bytes 196616 | tf_op jit(solution)/shard_map/ppermute | solution.py:199
  54.5 1.3 %collective-permute-start.16 = (f32[64,256]{1,0:T(8,128)S(1)}, f32[64,256]{1,0:T(8,128)S(1)}, u32[]{:S(2)}, u32[]{:S(2)}) collective-permute-start(f32[64,256]{1,0:T(8,128)S(1)} %shard_map.73), channel_id=1, source_target_pairs={{1,0},{0,1},{3,2},{2,3},{5,4},{4,5},{7,6},{6,7},{9,8},{8,9},{11,10... | collective-permute-start | bytes 196616 | tf_op jit(solution)/shard_map/ppermute | solution.py:199
  55.9 4.1 %collective-permute-start.19 = (bf16[64,256]{1,0:T(8,128)(2,1)S(1)}, bf16[64,256]{1,0:T(8,128)(2,1)S(1)}, u32[]{:S(2)}, u32[]{:S(2)}) collective-permute-start(bf16[64,256]{1,0:T(8,128)(2,1)S(1)} %add_convert_fusion.1), channel_id=1, source_target_pairs={{8,0},{9,1},{10,2},{11,3},{12,4},{13,5},{14,6},{15,7},{0,8},{1,9},... | collective-permute-start | bytes 98312 | tf_op jit(solution)/shard_map/ppermute | solution.py:199
  56.4 5.7 %collective-permute-start.21 = (bf16[64,256]{1,0:T(8,128)(2,1)S(1)}, bf16[64,256]{1,0:T(8,128)(2,1)S(1)}, u32[]{:S(2)}, u32[]{:S(2)}) collective-permute-start(bf16[64,256]{1,0:T(8,128)(2,1)S(1)} %add_convert_fusion.1), channel_id=1, source_target_pairs={{24,0},{25,1},{26,2},{27,3},{28,4},{29,5},{30,6},{31,7},{16,8},{17... | collective-permute-start | bytes 98312 | tf_op jit(solution)/shard_map/ppermute | solution.py:199
  57.8 5.3 %collective-permute-start.20 = (bf16[64,256]{1,0:T(8,128)(2,1)S(1)}, bf16[64,256]{1,0:T(8,128)(2,1)S(1)}, u32[]{:S(2)}, u32[]{:S(2)}) collective-permute-start(bf16[64,256]{1,0:T(8,128)(2,1)S(1)} %add_convert_fusion.1), channel_id=1, source_target_pairs={{16,0},{17,1},{18,2},{19,3},{20,4},{21,5},{22,6},{23,7},{24,8},{25... | collective-permute-start | bytes 98312 | tf_op jit(solution)/shard_map/ppermute | solution.py:199
  59.4 7.8 %collective-permute-start.17 = (bf16[128,256]{1,0:T(8,128)(2,1)S(1)}, bf16[128,256]{1,0:T(8,128)(2,1)S(1)}, u32[]{:S(2)}, u32[]{:S(2)}) collective-permute-start(bf16[128,256]{1,0:T(8,128)(2,1)S(1)} %pad_maximum_fusion.3.refs_0_), channel_id=1, source_target_pairs={{2,0},{3,1},{0,2},{1,3},{6,4},{7,5},{4,6},{5,7},{10,8},{11,9},{8,1... | collective-permute-start | bytes 196616 | tf_op jit(solution)/shard_map/ppermute | solution.py:199
  63.1 4.5 %collective-permute-start.22 = (bf16[128,256]{1,0:T(8,128)(2,1)S(1)}, bf16[128,256]{1,0:T(8,128)(2,1)S(1)}, u32[]{:S(2)}, u32[]{:S(2)}) collective-permute-start(bf16[128,256]{1,0:T(8,128)(2,1)S(1)} %pad_maximum_fusion.4.refs_0_), channel_id=1, source_target_pairs={{4,0},{5,1},{6,2},{7,3},{0,4},{1,5},{2,6},{3,7},{12,8},{13,9},{14,... | collective-permute-start | bytes 196616 | tf_op jit(solution)/shard_map/ppermute | solution.py:199
  67.8 1.3 %collective-permute-start.23 = (f32[64,256]{1,0:T(8,128)S(1)}, f32[64,256]{1,0:T(8,128)S(1)}, u32[]{:S(2)}, u32[]{:S(2)}) collective-permute-start(f32[64,256]{1,0:T(8,128)S(1)} %shard_map.78), channel_id=1, source_target_pairs={{1,0},{0,1},{3,2},{2,3},{5,4},{4,5},{7,6},{6,7},{9,8},{8,9},{11,10... | collective-permute-start | bytes 196616 | tf_op jit(solution)/shard_map/ppermute | solution.py:199
  69.2 4.0 %collective-permute-start.24 = (bf16[64,256]{1,0:T(8,128)(2,1)S(1)}, bf16[64,256]{1,0:T(8,128)(2,1)S(1)}, u32[]{:S(2)}, u32[]{:S(2)}) collective-permute-start(bf16[64,256]{1,0:T(8,128)(2,1)S(1)} %add_convert_fusion.refs_0_), channel_id=1, source_target_pairs={{2,0},{3,1},{0,2},{1,3},{6,4},{7,5},{4,6},{5,7},{10,8},{11,9},{8,1... | collective-permute-start | bytes 98312 | tf_op jit(solution)/shard_map/ppermute | solution.py:199

commit v5 on v2

--- a/solution.py
+++ b/solution.py
@@ -234,15 +234,20 @@
             )
 
         def deep(value, work=None):
-            found = [value]
-            for m in range(1, depths):
-                found.append(send(value, lambda z, y, x, core, m=m: (z ^ m, y, x, core)))
-            parts = [
-                jnp.where((row // lines) % CORES == core, found[m], found[m + 1])
-                for m in range(0, depths, CORES)
-            ]
+            even = (row // lines) % CORES == core
+            found = []
+            for t in range(near):
+
+                def source(z, y, x, core, t=t):
+                    m = CORES * t + 1
+                    if z % CORES == core and t < near - 1:
+                        return z ^ (m + 1), y, x, core
+                    return z ^ m, y, x, 1 - core
+
+                found.append(send(value, source))
+            parts = [jnp.where(even, ([value] + found)[t], found[t]) for t in range(near)]
             stack = jnp.concatenate(parts, axis=0)
-            return after(stack, *work(found[1])) if work else stack
+            return after(stack, *work(found[0])) if work else stack
 
         def wide(stack):
             return [stack] + [

time: 74.5 us -> 75.8 us (1.017)
  waiting for transfers between devices: 24.2 us -> 28.3 us
  starting transfers between devices: 29.7 us -> 26.9 us
    ppermute x25 -> x21, waiting for transfers between devices: 24.2 us -> 28.3 us  [send(): return lax.ppermute(value, ('prow', 'pcol'), pairs)]
    ppermute x25 -> x21, starting transfers between devices: 29.7 us -> 26.9 us  [send(): return lax.ppermute(value, ('prow', 'pcol'), pairs)]
  transfers between devices with their start and end apart: 25 -> 21, of which waited for: 16 -> 17; matrix products, arithmetic and copies ran while one was open for 4% -> 4% of each run, Pallas kernels for 18% -> 17%
where the time goes in v5:
time: 75.8 us; the launch traced here: 75.6 us
  waiting for transfers between devices  28.3 us (37%)
  starting transfers between devices  26.9 us (35%)
  Pallas kernels  16.5 us (22%)
  local copies, waits for them, and re-layouts  3.58 us (5%)
    ppermute x21, waiting for transfers between devices, send(): return lax.ppermute(value, ('prow', 'pcol'), pairs)  28.3 us
    ppermute x21, starting transfers between devices, send(): return lax.ppermute(value, ('prow', 'pcol'), pairs)  26.9 us
    pallas_call x16, Pallas kernels, call(): pl.pallas_call(kernel, grid=(1,), out_shape=shapes, in_specs=specs, out_s...  16.5 us
    slice x2, local copies, waits for them, and re-layouts, body(): parts = (upper_blocks[last_pair:], upper_blocks[:last_pair])  2.49 us
  transfers between devices with their start and end apart: 21, of which 17 were waited for; matrix products, arithmetic and copies ran while one was open for 4% of the time, Pallas kernels for 17%

profile of v5, /device:TPU:0, one launch (start us, length us, event | category | flops | bytes accessed | tf_op | source)
XLA Modules:
  0.0 75.6 jit_solution(14368564732002637617)
XLA Ops:
  0.0 2.9 %collective-permute-start.3 = (bf16[3,1,256,512]{3,2,1,0:T(8,128)(2,1)}, bf16[3,1,256,512]{3,2,1,0:T(8,128)(2,1)S(1)}, u32[]{:S(2)}, u32[]{:S(2)}) collective-permute-start(bf16[3,1,256,512]{3,2,1,0:T(8,128)(2,1)} %refs_2_.3), channel_id=1, source_target_pairs={{2,0},{3,1},{0,2},{1,3},{6,4},{7,5},{4,6},{5,7},{10,8},{11,9},{8,1... | collective-permute-start | bytes 2359304 | tf_op jit(solution)/shard_map/ppermute | solution.py:204
  2.9 0.6 stack.23.spot
  3.5 1.8 %shard_map.64.first = bf16[64,256]{1,0:T(8,128)(2,1)} custom-call(s32[5]{0:T(128)} %stack.23.spot, bf16[3,1,256,128]{3,2,1,0:T(8,128)(2,1)} %rhs.3, bf16[3,1,256,256]{3,2,1,0:T(8,128)(2,1)} %refs_1_.6), custom_call_target="tpu_custom_call" | custom-call | tf_op jit(solution)/shard_map/pallas_call | solution.py:49
  5.3 2.8 %collective-permute-start.1 = (bf16[64,256]{1,0:T(8,128)(2,1)}, bf16[64,256]{1,0:T(8,128)(2,1)S(1)}, u32[]{:S(2)}, u32[]{:S(2)}) collective-permute-start(bf16[64,256]{1,0:T(8,128)(2,1)} %shard_map.64.first), channel_id=1, source_target_pairs={{25,0},{24,1},{27,2},{26,3},{29,4},{28,5},{31,6},{30,7},{17,8},{16... | collective-permute-start | bytes 98312 | tf_op jit(solution)/shard_map/ppermute | solution.py:204
  8.1 0.0 collective-permute-start
  8.1 1.7 %slice.6 = bf16[1,1,256,512]{3,2,1,0:T(8,128)(2,1)} slice(bf16[3,1,256,512]{3,2,1,0:T(8,128)(2,1)} %refs_1_.9), slice={[2:3], [0:1], [0:256], [0:512]} | slice | bytes 524288 | tf_op jit(solution)/shard_map/slice | solution.py:291
  9.8 0.0 copy-start.6
  9.8 0.8 %slice.7 = bf16[2,1,256,512]{3,2,1,0:T(8,128)(2,1)} slice(bf16[3,1,256,512]{3,2,1,0:T(8,128)(2,1)S(1)} %copy-done.1), slice={[0:2], [0:1], [0:256], [0:512]} | slice | bytes 1048576 | tf_op jit(solution)/shard_map/slice | solution.py:291
  10.6 0.2 copy-done
  10.8 0.2 copy-done.2
  11.1 0.0 copy-done.4
  11.1 1.4 %shard_map.65 = (f32[64,256]{1,0:T(8,128)S(1)}, f32[64,256]{1,0:T(8,128)S(1)}, f32[64,256]{1,0:T(8,128)S(1)}, f32[64,256]{1,0:T(8,128)S(1)}) custom-call(s32[5]{0:T(128)S(1)} %copy-done.7, bf16[64,256]{1,0:T(8,128)(2,1)S(1)} %copy-done.6, bf16[3,1,256,128]{3,2,1,0:T(8,128)(2,1)S(1)} %copy-done.4, bf16[3,1,256,256]{3,2,1,0:T(8,128)(2,1)S(1)} %copy-done.2, ...), custom_call_target="tpu_custom_call" | custom-call | tf_op jit(solution)/shard_map/pallas_call | solution.py:49
  12.5 0.0 collective-permute-done.1
  12.5 0.6 collective-permute-done
  13.1 0.0 copy-start.5
  13.2 1.6 %collective-permute-start.2 = (bf16[128,256]{1,0:T(8,128)(2,1)S(1)}, bf16[128,256]{1,0:T(8,128)(2,1)S(1)}, u32[]{:S(2)}, u32[]{:S(2)}) collective-permute-start(bf16[128,256]{1,0:T(8,128)(2,1)S(1)} %pad_maximum_fusion.refs_2_.refs_0_), channel_id=1, source_target_pairs={{4,0},{5,1},{6,2},{7,3},{0,4},{1,5},{2,6},{3,7},{12,8},{13,9},{14,... | collective-permute-start | bytes 196616 | tf_op jit(solution)/shard_map/ppermute | solution.py:204
  14.8 2.8 %collective-permute-done.2.refs_3_.refs_1_ = bf16[128,256]{1,0:T(8,128)(2,1)S(1)} collective-permute-done((bf16[128,256]{1,0:T(8,128)(2,1)S(1)}, bf16[128,256]{1,0:T(8,128)(2,1)S(1)}, u32[]{:S(2)}, u32[]{:S(2)}) %collective-permute-start.2) | collective-permute-done | bytes 65568 | tf_op jit(solution)/shard_map/ppermute | solution.py:204
  17.6 3.1 %collective-permute-done.3.refs_1_.refs_3_ = bf16[3,1,256,512]{3,2,1,0:T(8,128)(2,1)S(1)} collective-permute-done((bf16[3,1,256,512]{3,2,1,0:T(8,128)(2,1)}, bf16[3,1,256,512]{3,2,1,0:T(8,128)(2,1)S(1)}, u32[]{:S(2)}, u32[]{:S(2)}) %collective-permute-start.3) | collective-permute-done | bytes 786464 | tf_op jit(solution)/shard_map/ppermute | solution.py:204
  20.7 1.4 %shard_map.66 = f32[64,256]{1,0:T(8,128)S(1)} custom-call(s32[5]{0:T(128)S(1)} %copy-done.7, s32[3,8,8]{2,1,0:T(8,128)S(1)} %copy-done.5, f32[64,256]{1,0:T(8,128)S(1)} %get-tuple-element.26.base, bf16[3,1,256,256]{3,2,1,0:T(8,128)(2,1)S(1)} %copy-done.2, bf16[3,1,256,512]{3,2,1,0:T(8,128)(2,1)S(1)} %copy-done.3, ...), custom_call_target="tpu_custom_call" | custom-call | tf_op jit(solution)/shard_map/pallas_call | solution.py:49
  22.1 0.1 collective-permute-start.4
  22.2 1.2 %collective-permute-done.4 = f32[64,256]{1,0:T(8,128)S(1)} collective-permute-done((f32[64,256]{1,0:T(8,128)S(1)}, f32[64,256]{1,0:T(8,128)S(1)}, u32[]{:S(2)}, u32[]{:S(2)}) %collective-permute-start.4) | collective-permute-done | bytes 65568 | tf_op jit(solution)/shard_map/ppermute | solution.py:204
  23.4 2.9 %collective-permute-start.5 = (bf16[64,256]{1,0:T(8,128)(2,1)S(1)}, bf16[64,256]{1,0:T(8,128)(2,1)S(1)}, u32[]{:S(2)}, u32[]{:S(2)}) collective-permute-start(bf16[64,256]{1,0:T(8,128)(2,1)S(1)} %add_convert_fusion.3), channel_id=1, source_target_pairs={{16,0},{8,1},{18,2},{10,3},{20,4},{12,5},{22,6},{14,7},{1,8},{25,9... | collective-permute-start | bytes 98312 | tf_op jit(solution)/shard_map/ppermute | solution.py:204
  26.3 0.9 %collective-permute-start.6 = (bf16[64,256]{1,0:T(8,128)(2,1)S(1)}, bf16[64,256]{1,0:T(8,128)(2,1)S(1)}, u32[]{:S(2)}, u32[]{:S(2)}) collective-permute-start(bf16[64,256]{1,0:T(8,128)(2,1)S(1)} %add_convert_fusion.3), channel_id=1, source_target_pairs={{25,0},{24,1},{27,2},{26,3},{29,4},{28,5},{31,6},{30,7},{17,8},{16... | collective-permute-start | bytes 98312 | tf_op jit(solution)/shard_map/ppermute | solution.py:204
  27.2 1.5 %collective-permute-start.7 = (bf16[1,1,256,512]{3,2,1,0:T(8,128)(2,1)S(1)}, bf16[1,1,256,512]{3,2,1,0:T(8,128)(2,1)S(1)}, u32[]{:S(2)}, u32[]{:S(2)}) collective-permute-start(bf16[1,1,256,512]{3,2,1,0:T(8,128)(2,1)S(1)} %copy-done.9), channel_id=1, source_target_pairs={{2,0},{3,1},{0,2},{1,3},{6,4},{7,5},{4,6},{5,7},{10,8},{11,9},{8,1... | collective-permute-start | bytes 786440 | tf_op jit(solution)/shard_map/ppermute | solution.py:204
  28.7 0.0 collective-permute-done.5
  28.7 1.6 %shard_map.67.refs_2_ = bf16[4,2,256,256]{3,2,1,0:T(8,128)(2,1)S(1)} custom-call(s32[5]{0:T(128)S(1)} %copy-done.7, s32[3,8,8]{2,1,0:T(8,128)S(1)} %copy-done.5, bf16[3,1,256,256]{3,2,1,0:T(8,128)(2,1)S(1)} %copy-done, bf16[3,1,256,256]{3,2,1,0:T(8,128)(2,1)S(1)} %copy-done.2, bf16[3,1,256,512]{3,2,1,0:T(8,128)(2,1)S(1)} %copy-done.3, ...), custom_call_target="tpu_custom_call" | custom-call | tf_op jit(solution)/shard_map/pallas_call | solution.py:49
  30.3 1.2 %collective-permute-done.6 = bf16[64,256]{1,0:T(8,128)(2,1)S(1)} collective-permute-done((bf16[64,256]{1,0:T(8,128)(2,1)S(1)}, bf16[64,256]{1,0:T(8,128)(2,1)S(1)}, u32[]{:S(2)}, u32[]{:S(2)}) %collective-permute-start.6) | collective-permute-done | bytes 32800 | tf_op jit(solution)/shard_map/ppermute | solution.py:204
  31.5 4.4 %collective-permute-done.7.refs_2_ = bf16[1,1,256,512]{3,2,1,0:T(8,128)(2,1)S(1)} collective-permute-done((bf16[1,1,256,512]{3,2,1,0:T(8,128)(2,1)S(1)}, bf16[1,1,256,512]{3,2,1,0:T(8,128)(2,1)S(1)}, u32[]{:S(2)}, u32[]{:S(2)}) %collective-permute-start.7) | collective-permute-done | bytes 262176 | tf_op jit(solution)/shard_map/ppermute | solution.py:204
  35.9 1.5 %collective-permute-start.8 = (bf16[128,256]{1,0:T(8,128)(2,1)S(1)}, bf16[128,256]{1,0:T(8,128)(2,1)S(1)}, u32[]{:S(2)}, u32[]{:S(2)}) collective-permute-start(bf16[128,256]{1,0:T(8,128)(2,1)S(1)} %pad_maximum_fusion.1.refs_0_), channel_id=1, source_target_pairs={{4,0},{5,1},{6,2},{7,3},{0,4},{1,5},{2,6},{3,7},{12,8},{13,9},{14,... | collective-permute-start | bytes 196616 | tf_op jit(solution)/shard_map/ppermute | solution.py:204
  37.4 2.0 %shard_map.69 = (bf16[4,2,256,256]{3,2,1,0:T(8,128)(2,1)S(1)}, bf16[4,2,256,256]{3,2,1,0:T(8,128)(2,1)S(1)}) custom-call(s32[5]{0:T(128)S(1)} %copy-done.7, s32[3,8,8]{2,1,0:T(8,128)S(1)} %copy-done.5, bf16[3,1,256,256]{3,2,1,0:T(8,128)(2,1)S(1)} %copy-done, bf16[3,1,256,256]{3,2,1,0:T(8,128)(2,1)S(1)} %copy-done.2, bf16[3,1,256,512]{3,2,1,0:T(8,128)(2,1)S(1)} %copy-done.3, ...), custom_call_target="tpu_custom_call" | custom-call | tf_op jit(solution)/shard_map/pallas_call | solution.py:49
  39.4 0.3 shard_map.70.base
  39.7 0.4 collective-permute-done.8.refs_1_
  40.2 0.3 shard_map.71
  40.5 0.1 collective-permute-start.9
  40.6 1.2 %collective-permute-done.9 = f32[64,256]{1,0:T(8,128)S(1)} collective-permute-done((f32[64,256]{1,0:T(8,128)S(1)}, f32[64,256]{1,0:T(8,128)S(1)}, u32[]{:S(2)}, u32[]{:S(2)}) %collective-permute-start.9) | collective-permute-done | bytes 65568 | tf_op jit(solution)/shard_map/ppermute | solution.py:204
  41.8 1.6 %collective-permute-start.11 = (bf16[64,256]{1,0:T(8,128)(2,1)S(1)}, bf16[64,256]{1,0:T(8,128)(2,1)S(1)}, u32[]{:S(2)}, u32[]{:S(2)}) collective-permute-start(bf16[64,256]{1,0:T(8,128)(2,1)S(1)} %add_convert_fusion.2), channel_id=1, source_target_pairs={{25,0},{24,1},{27,2},{26,3},{29,4},{28,5},{31,6},{30,7},{17,8},{16... | collective-permute-start | bytes 98312 | tf_op jit(solution)/shard_map/ppermute | solution.py:204
  43.4 1.5 %collective-permute-start.15 = (bf16[2,1,256,512]{3,2,1,0:T(8,128)(2,1)S(1)}, bf16[2,1,256,512]{3,2,1,0:T(8,128)(2,1)S(1)}, u32[]{:S(2)}, u32[]{:S(2)}) collective-permute-start(bf16[2,1,256,512]{3,2,1,0:T(8,128)(2,1)S(1)} %copy-done.8), channel_id=1, source_target_pairs={{2,0},{3,1},{0,2},{1,3},{6,4},{7,5},{4,6},{5,7},{10,8},{11,9},{8,1... | collective-permute-start | bytes 1572872 | tf_op jit(solution)/shard_map/ppermute | solution.py:204
  44.9 2.1 %collective-permute-done.11 = bf16[64,256]{1,0:T(8,128)(2,1)S(1)} collective-permute-done((bf16[64,256]{1,0:T(8,128)(2,1)S(1)}, bf16[64,256]{1,0:T(8,128)(2,1)S(1)}, u32[]{:S(2)}, u32[]{:S(2)}) %collective-permute-start.11) | collective-permute-done | bytes 32800 | tf_op jit(solution)/shard_map/ppermute | solution.py:204
  47.0 1.2 %collective-permute-done.10 = bf16[64,256]{1,0:T(8,128)(2,1)S(1)} collective-permute-done((bf16[64,256]{1,0:T(8,128)(2,1)S(1)}, bf16[64,256]{1,0:T(8,128)(2,1)S(1)}, u32[]{:S(2)}, u32[]{:S(2)}) %collective-permute-start.10) | collective-permute-done | bytes 32800 | tf_op jit(solution)/shard_map/ppermute | solution.py:204
  48.3 1.6 %collective-permute-start.12 = (bf16[128,256]{1,0:T(8,128)(2,1)S(1)}, bf16[128,256]{1,0:T(8,128)(2,1)S(1)}, u32[]{:S(2)}, u32[]{:S(2)}) collective-permute-start(bf16[128,256]{1,0:T(8,128)(2,1)S(1)} %pad_maximum_fusion.2.refs_0_), channel_id=1, source_target_pairs={{4,0},{5,1},{6,2},{7,3},{0,4},{1,5},{2,6},{3,7},{12,8},{13,9},{14,... | collective-permute-start | bytes 196616 | tf_op jit(solution)/shard_map/ppermute | solution.py:204
  49.9 0.3 shard_map.68.base
  50.2 1.3 %shard_map.72.refs_2_ = bf16[4,2,256,256]{3,2,1,0:T(8,128)(2,1)S(1)} custom-call(s32[5]{0:T(128)S(1)} %copy-done.7, s32[3,8,8]{2,1,0:T(8,128)S(1)} %copy-done.5, bf16[3,1,256,256]{3,2,1,0:T(8,128)(2,1)S(1)} %copy-done, bf16[3,1,256,512]{3,2,1,0:T(8,128)(2,1)S(1)} %copy-done.1, bf16[1,1,256,512]{3,2,1,0:T(8,128)(2,1)S(1)} %collective-permute-done.7.refs_2_), custom_call_target="tpu_custom_call" | custom-call | tf_op jit(solution)/shard_map/pallas_call | solution.py:49
  51.4 1.2 %collective-permute-done.12.refs_1_ = bf16[128,256]{1,0:T(8,128)(2,1)S(1)} collective-permute-done((bf16[128,256]{1,0:T(8,128)(2,1)S(1)}, bf16[128,256]{1,0:T(8,128)(2,1)S(1)}, u32[]{:S(2)}, u32[]{:S(2)}) %collective-permute-start.12) | collective-permute-done | bytes 65568 | tf_op jit(solution)/shard_map/ppermute | solution.py:204
  52.6 0.3 shard_map.73
  52.9 0.1 collective-permute-start.13
  53.0 1.2 %collective-permute-done.13 = f32[64,256]{1,0:T(8,128)S(1)} collective-permute-done((f32[64,256]{1,0:T(8,128)S(1)}, f32[64,256]{1,0:T(8,128)S(1)}, u32[]{:S(2)}, u32[]{:S(2)}) %collective-permute-start.13) | collective-permute-done | bytes 65568 | tf_op jit(solution)/shard_map/ppermute | solution.py:204
  54.2 3.4 %collective-permute-done.15.refs_2_ = bf16[2,1,256,512]{3,2,1,0:T(8,128)(2,1)S(1)} collective-permute-done((bf16[2,1,256,512]{3,2,1,0:T(8,128)(2,1)S(1)}, bf16[2,1,256,512]{3,2,1,0:T(8,128)(2,1)S(1)}, u32[]{:S(2)}, u32[]{:S(2)}) %collective-permute-start.15) | collective-permute-done | bytes 524320 | tf_op jit(solution)/shard_map/ppermute | solution.py:204
  57.6 1.2 %collective-permute-start.17 = (bf16[64,256]{1,0:T(8,128)(2,1)S(1)}, bf16[64,256]{1,0:T(8,128)(2,1)S(1)}, u32[]{:S(2)}, u32[]{:S(2)}) collective-permute-start(bf16[64,256]{1,0:T(8,128)(2,1)S(1)} %add_convert_fusion.1), channel_id=1, source_target_pairs={{25,0},{24,1},{27,2},{26,3},{29,4},{28,5},{31,6},{30,7},{17,8},{16... | collective-permute-start | bytes 98312 | tf_op jit(solution)/shard_map/ppermute | solution.py:204
  58.8 2.0 %collective-permute-start.16 = (bf16[64,256]{1,0:T(8,128)(2,1)S(1)}, bf16[64,256]{1,0:T(8,128)(2,1)S(1)}, u32[]{:S(2)}, u32[]{:S(2)}) collective-permute-start(bf16[64,256]{1,0:T(8,128)(2,1)S(1)} %add_convert_fusion.1), channel_id=1, source_target_pairs={{16,0},{8,1},{18,2},{10,3},{20,4},{12,5},{22,6},{14,7},{1,8},{25,9... | collective-permute-start | bytes 98312 | tf_op jit(solution)/shard_map/ppermute | solution.py:204
  60.8 1.5 %collective-permute-start.14 = (bf16[128,256]{1,0:T(8,128)(2,1)S(1)}, bf16[128,256]{1,0:T(8,128)(2,1)S(1)}, u32[]{:S(2)}, u32[]{:S(2)}) collective-permute-start(bf16[128,256]{1,0:T(8,128)(2,1)S(1)} %pad_maximum_fusion.3.refs_0_), channel_id=1, source_target_pairs={{2,0},{3,1},{0,2},{1,3},{6,4},{7,5},{4,6},{5,7},{10,8},{11,9},{8,1... | collective-permute-start | bytes 196616 | tf_op jit(solution)/shard_map/ppermute | solution.py:204
  62.3 0.6 collective-permute-done.17
  62.9 1.4 %collective-permute-done.16 = bf16[64,256]{1,0:T(8,128)(2,1)S(1)} collective-permute-done((bf16[64,256]{1,0:T(8,128)(2,1)S(1)}, bf16[64,256]{1,0:T(8,128)(2,1)S(1)}, u32[]{:S(2)}, u32[]{:S(2)}) %collective-permute-start.16) | collective-permute-done | bytes 32800 | tf_op jit(solution)/shard_map/ppermute | solution.py:204
  64.3 1.6 %collective-permute-start.18 = (bf16[128,256]{1,0:T(8,128)(2,1)S(1)}, bf16[128,256]{1,0:T(8,128)(2,1)S(1)}, u32[]{:S(2)}, u32[]{:S(2)}) collective-permute-start(bf16[128,256]{1,0:T(8,128)(2,1)S(1)} %pad_maximum_fusion.4.refs_0_), channel_id=1, source_target_pairs={{4,0},{5,1},{6,2},{7,3},{0,4},{1,5},{2,6},{3,7},{12,8},{13,9},{14,... | collective-permute-start | bytes 196616 | tf_op jit(solution)/shard_map/ppermute | solution.py:204
  65.9 1.3 %shard_map.77.refs_2_ = bf16[4,2,256,256]{3,2,1,0:T(8,128)(2,1)S(1)} custom-call(s32[5]{0:T(128)S(1)} %copy-done.7, s32[3,8,8]{2,1,0:T(8,128)S(1)} %copy-done.5, bf16[3,1,256,256]{3,2,1,0:T(8,128)(2,1)S(1)} %copy-done, bf16[3,1,256,512]{3,2,1,0:T(8,128)(2,1)S(1)} %copy-done.1, bf16[2,1,256,512]{3,2,1,0:T(8,128)(2,1)S(1)} %collective-permute-done.15.refs_2_), custom_call_target="tpu_custom_call" | custom-call | tf_op jit(solution)/shard_map/pallas_call | solution.py:49
  67.1 1.3 %shard_map.75.refs_2_ = bf16[4,2,256,256]{3,2,1,0:T(8,128)(2,1)S(1)} custom-call(s32[5]{0:T(128)S(1)} %copy-done.7, s32[3,8,8]{2,1,0:T(8,128)S(1)} %copy-done.5, bf16[3,1,256,256]{3,2,1,0:T(8,128)(2,1)S(1)} %copy-done, bf16[3,1,256,512]{3,2,1,0:T(8,128)(2,1)S(1)} %copy-done.1, bf16[2,1,256,512]{3,2,1,0:T(8,128)(2,1)S(1)} %collective-permute-done.15.refs_2_), custom_call_target="tpu_custom_call" | custom-call | tf_op jit(solution)/shard_map/pallas_call | solution.py:49
  68.4 0.3 shard_map.76.base
  68.7 0.0 collective-permute-done.18.refs_1_
  68.7 0.3 shard_map.78
  69.0 0.1 collective-permute-start.19
  69.1 1.2 %collective-permute-done.19 = f32[64,256]{1,0:T(8,128)S(1)} collective-permute-done((f32[64,256]{1,0:T(8,128)S(1)}, f32[64,256]{1,0:T(8,128)S(1)}, u32[]{:S(2)}, u32[]{:S(2)}) %collective-permute-start.19) | collective-permute-done | bytes 65568 | tf_op jit(solution)/shard_map/ppermute | solution.py:204
  70.4 1.6 %collective-permute-start.20 = (bf16[64,256]{1,0:T(8,128)(2,1)S(1)}, bf16[64,256]{1,0:T(8,128)(2,1)S(1)}, u32[]{:S(2)}, u32[]{:S(2)}) collective-permute-start(bf16[64,256]{1,0:T(8,128)(2,1)S(1)} %add_convert_fusion.refs_0_), channel_id=1, source_target_pairs={{2,0},{3,1},{0,2},{1,3},{6,4},{7,5},{4,6},{5,7},{10,8},{11,9},{8,1... | collective-permute-start | bytes 98312 | tf_op jit(solution)/shard_map/ppermute | solution.py:204
  71.9 1.4 %shard_map.74.whole = bf16[3,1,256,128]{3,2,1,0:T(8,128)(2,1)} custom-call(s32[5]{0:T(128)S(1)} %copy-done.7, bf16[128,256]{1,0:T(8,128)(2,1)S(1)} %pad_maximum_fusion.3.refs_0_, bf16[128,256]{1,0:T(8,128)(2,1)S(1)} %collective-permute-done.14.refs_1_), custom_call_target="tpu_custom_call" | custom-call | tf_op jit(solution)/shard_map/pallas_call | solution.py:49
  73.3 1.1 %collective-permute-done.20.refs_1_ = bf16[64,256]{1,0:T(8,128)(2,1)S(1)} collective-permute-done((bf16[64,256]{1,0:T(8,128)(2,1)S(1)}, bf16[64,256]{1,0:T(8,128)(2,1)S(1)}, u32[]{:S(2)}, u32[]{:S(2)}) %collective-permute-start.20) | collective-permute-done | bytes 32800 | tf_op jit(solution)/shard_map/ppermute | solution.py:204
  74.4 1.3 %shard_map.79 = bf16[3,1,256,128]{3,2,1,0:T(8,128)(2,1)} custom-call(s32[5]{0:T(128)S(1)} %copy-done.7, bf16[3,1,256,128]{3,2,1,0:T(8,128)(2,1)} %shard_map.74.whole, bf16[64,256]{1,0:T(8,128)(2,1)S(1)} %add_convert_fusion.refs_0_, bf16[64,256]{1,0:T(8,128)(2,1)S(1)} %collective-permute-done.20.refs_1_), custom_call_target="tpu_custom_call", output_to_operand_aliasing={{}: (1, {})} | custom-call | tf_op jit(solution)/shard_map/pallas_call | solution.py:49
  (30 shorter events, 0.1 us)
Async XLA Ops:
  0.0 9.8 %copy-start.1 = (bf16[3,1,256,512]{3,2,1,0:T(8,128)(2,1)S(1)}, bf16[3,1,256,512]{3,2,1,0:T(8,128)(2,1)}, u32[]{:S(2)}) copy-start(bf16[3,1,256,512]{3,2,1,0:T(8,128)(2,1)} %refs_1_.9) | copy-start | bytes 2359300
  0.0 20.7 %collective-permute-start.3 = (bf16[3,1,256,512]{3,2,1,0:T(8,128)(2,1)}, bf16[3,1,256,512]{3,2,1,0:T(8,128)(2,1)S(1)}, u32[]{:S(2)}, u32[]{:S(2)}) collective-permute-start(bf16[3,1,256,512]{3,2,1,0:T(8,128)(2,1)} %refs_2_.3), channel_id=1, source_target_pairs={{2,0},{3,1},{0,2},{1,3},{6,4},{7,5},{4,6},{5,7},{10,8},{11,9},{8,1... | collective-permute-start | bytes 2359304 | tf_op jit(solution)/shard_map/ppermute | solution.py:204
  5.3 7.2 %collective-permute-start.1 = (bf16[64,256]{1,0:T(8,128)(2,1)}, bf16[64,256]{1,0:T(8,128)(2,1)S(1)}, u32[]{:S(2)}, u32[]{:S(2)}) collective-permute-start(bf16[64,256]{1,0:T(8,128)(2,1)} %shard_map.64.first), channel_id=1, source_target_pairs={{25,0},{24,1},{27,2},{26,3},{29,4},{28,5},{31,6},{30,7},{17,8},{16... | collective-permute-start | bytes 98312 | tf_op jit(solution)/shard_map/ppermute | solution.py:204
  8.1 5.0 %collective-permute-start = (bf16[64,256]{1,0:T(8,128)(2,1)}, bf16[64,256]{1,0:T(8,128)(2,1)S(1)}, u32[]{:S(2)}, u32[]{:S(2)}) collective-permute-start(bf16[64,256]{1,0:T(8,128)(2,1)} %shard_map.64.first), channel_id=1, source_target_pairs={{16,0},{8,1},{18,2},{10,3},{20,4},{12,5},{22,6},{14,7},{1,8},{25,9... | collective-permute-start | bytes 98312 | tf_op jit(solution)/shard_map/ppermute | solution.py:204
  9.8 1.1 %copy-start = (bf16[3,1,256,256]{3,2,1,0:T(8,128)(2,1)S(1)}, bf16[3,1,256,256]{3,2,1,0:T(8,128)(2,1)}, u32[]{:S(2)}) copy-start(bf16[3,1,256,256]{3,2,1,0:T(8,128)(2,1)} %refs_0_.11) | copy-start | bytes 1179652
  9.8 1.3 %copy-start.2 = (bf16[3,1,256,256]{3,2,1,0:T(8,128)(2,1)S(1)}, bf16[3,1,256,256]{3,2,1,0:T(8,128)(2,1)}, u32[]{:S(2)}) copy-start(bf16[3,1,256,256]{3,2,1,0:T(8,128)(2,1)} %refs_1_.6) | copy-start | bytes 1179652
  9.8 1.3 %copy-start.4 = (bf16[3,1,256,128]{3,2,1,0:T(8,128)(2,1)S(1)}, bf16[3,1,256,128]{3,2,1,0:T(8,128)(2,1)}, u32[]{:S(2)}) copy-start(bf16[3,1,256,128]{3,2,1,0:T(8,128)(2,1)} %rhs.3) | copy-start | bytes 589828
  9.8 1.3 %copy-start.6 = (bf16[64,256]{1,0:T(8,128)(2,1)S(1)}, bf16[64,256]{1,0:T(8,128)(2,1)}, u32[]{:S(2)}) copy-start(bf16[64,256]{1,0:T(8,128)(2,1)} %shard_map.64.first) | copy-start | bytes 98308
  9.8 1.3 %copy-start.7 = (s32[5]{0:T(128)S(1)}, s32[5]{0:T(128)}, u32[]{:S(2)}) copy-start(s32[5]{0:T(128)} %stack.23.spot) | copy-start | bytes 64
  10.6 10.1 %copy-start.3 = (bf16[3,1,256,512]{3,2,1,0:T(8,128)(2,1)S(1)}, bf16[3,1,256,512]{3,2,1,0:T(8,128)(2,1)}, u32[]{:S(2)}) copy-start(bf16[3,1,256,512]{3,2,1,0:T(8,128)(2,1)} %refs_2_.3) | copy-start | bytes 2359300
  13.1 7.6 %copy-start.5 = (s32[3,8,8]{2,1,0:T(8,128)S(1)}, s32[3,8,8]{2,1,0:T(8,128)}, u32[]{:S(2)}) copy-start(s32[3,8,8]{2,1,0:T(8,128)} %pattern.11) | copy-start | bytes 2308
  13.2 14.0 %copy-start.9 = (bf16[1,1,256,512]{3,2,1,0:T(8,128)(2,1)S(1)}, bf16[1,1,256,512]{3,2,1,0:T(8,128)(2,1)}, u32[]{:S(2)}) copy-start(bf16[1,1,256,512]{3,2,1,0:T(8,128)(2,1)} %slice.6) | copy-start | bytes 786436
  13.2 4.4 %collective-permute-start.2 = (bf16[128,256]{1,0:T(8,128)(2,1)S(1)}, bf16[128,256]{1,0:T(8,128)(2,1)S(1)}, u32[]{:S(2)}, u32[]{:S(2)}) collective-permute-start(bf16[128,256]{1,0:T(8,128)(2,1)S(1)} %pad_maximum_fusion.refs_2_.refs_0_), channel_id=1, source_target_pairs={{4,0},{5,1},{6,2},{7,3},{0,4},{1,5},{2,6},{3,7},{12,8},{13,9},{14,... | collective-permute-start | bytes 196616 | tf_op jit(solution)/shard_map/ppermute | solution.py:204
  22.1 1.3 %collective-permute-start.4 = (f32[64,256]{1,0:T(8,128)S(1)}, f32[64,256]{1,0:T(8,128)S(1)}, u32[]{:S(2)}, u32[]{:S(2)}) collective-permute-start(f32[64,256]{1,0:T(8,128)S(1)} %shard_map.66), channel_id=1, source_target_pairs={{1,0},{0,1},{3,2},{2,3},{5,4},{4,5},{7,6},{6,7},{9,8},{8,9},{11,10... | collective-permute-start | bytes 196616 | tf_op jit(solution)/shard_map/ppermute | solution.py:204
  23.4 5.2 %collective-permute-start.5 = (bf16[64,256]{1,0:T(8,128)(2,1)S(1)}, bf16[64,256]{1,0:T(8,128)(2,1)S(1)}, u32[]{:S(2)}, u32[]{:S(2)}) collective-permute-start(bf16[64,256]{1,0:T(8,128)(2,1)S(1)} %add_convert_fusion.3), channel_id=1, source_target_pairs={{16,0},{8,1},{18,2},{10,3},{20,4},{12,5},{22,6},{14,7},{1,8},{25,9... | collective-permute-start | bytes 98312 | tf_op jit(solution)/shard_map/ppermute | solution.py:204
  26.3 5.1 %collective-permute-start.6 = (bf16[64,256]{1,0:T(8,128)(2,1)S(1)}, bf16[64,256]{1,0:T(8,128)(2,1)S(1)}, u32[]{:S(2)}, u32[]{:S(2)}) collective-permute-start(bf16[64,256]{1,0:T(8,128)(2,1)S(1)} %add_convert_fusion.3), channel_id=1, source_target_pairs={{25,0},{24,1},{27,2},{26,3},{29,4},{28,5},{31,6},{30,7},{17,8},{16... | collective-permute-start | bytes 98312 | tf_op jit(solution)/shard_map/ppermute | solution.py:204
  27.2 8.7 %collective-permute-start.7 = (bf16[1,1,256,512]{3,2,1,0:T(8,128)(2,1)S(1)}, bf16[1,1,256,512]{3,2,1,0:T(8,128)(2,1)S(1)}, u32[]{:S(2)}, u32[]{:S(2)}) collective-permute-start(bf16[1,1,256,512]{3,2,1,0:T(8,128)(2,1)S(1)} %copy-done.9), channel_id=1, source_target_pairs={{2,0},{3,1},{0,2},{1,3},{6,4},{7,5},{4,6},{5,7},{10,8},{11,9},{8,1... | collective-permute-start | bytes 786440 | tf_op jit(solution)/shard_map/ppermute | solution.py:204
  35.9 4.3 %collective-permute-start.8 = (bf16[128,256]{1,0:T(8,128)(2,1)S(1)}, bf16[128,256]{1,0:T(8,128)(2,1)S(1)}, u32[]{:S(2)}, u32[]{:S(2)}) collective-permute-start(bf16[128,256]{1,0:T(8,128)(2,1)S(1)} %pad_maximum_fusion.1.refs_0_), channel_id=1, source_target_pairs={{4,0},{5,1},{6,2},{7,3},{0,4},{1,5},{2,6},{3,7},{12,8},{13,9},{14,... | collective-permute-start | bytes 196616 | tf_op jit(solution)/shard_map/ppermute | solution.py:204
  40.2 3.3 %copy-start.8 = (bf16[2,1,256,512]{3,2,1,0:T(8,128)(2,1)S(1)}, bf16[2,1,256,512]{3,2,1,0:T(8,128)(2,1)}, u32[]{:S(2)}) copy-start(bf16[2,1,256,512]{3,2,1,0:T(8,128)(2,1)} %slice.7) | copy-start | bytes 1572868
  40.5 1.3 %collective-permute-start.9 = (f32[64,256]{1,0:T(8,128)S(1)}, f32[64,256]{1,0:T(8,128)S(1)}, u32[]{:S(2)}, u32[]{:S(2)}) collective-permute-start(f32[64,256]{1,0:T(8,128)S(1)} %shard_map.71), channel_id=1, source_target_pairs={{1,0},{0,1},{3,2},{2,3},{5,4},{4,5},{7,6},{6,7},{9,8},{8,9},{11,10... | collective-permute-start | bytes 196616 | tf_op jit(solution)/shard_map/ppermute | solution.py:204
  41.8 5.2 %collective-permute-start.11 = (bf16[64,256]{1,0:T(8,128)(2,1)S(1)}, bf16[64,256]{1,0:T(8,128)(2,1)S(1)}, u32[]{:S(2)}, u32[]{:S(2)}) collective-permute-start(bf16[64,256]{1,0:T(8,128)(2,1)S(1)} %add_convert_fusion.2), channel_id=1, source_target_pairs={{25,0},{24,1},{27,2},{26,3},{29,4},{28,5},{31,6},{30,7},{17,8},{16... | collective-permute-start | bytes 98312 | tf_op jit(solution)/shard_map/ppermute | solution.py:204
  43.4 4.8 %collective-permute-start.10 = (bf16[64,256]{1,0:T(8,128)(2,1)S(1)}, bf16[64,256]{1,0:T(8,128)(2,1)S(1)}, u32[]{:S(2)}, u32[]{:S(2)}) collective-permute-start(bf16[64,256]{1,0:T(8,128)(2,1)S(1)} %add_convert_fusion.2), channel_id=1, source_target_pairs={{16,0},{8,1},{18,2},{10,3},{20,4},{12,5},{22,6},{14,7},{1,8},{25,9... | collective-permute-start | bytes 98312 | tf_op jit(solution)/shard_map/ppermute | solution.py:204
  43.4 14.2 %collective-permute-start.15 = (bf16[2,1,256,512]{3,2,1,0:T(8,128)(2,1)S(1)}, bf16[2,1,256,512]{3,2,1,0:T(8,128)(2,1)S(1)}, u32[]{:S(2)}, u32[]{:S(2)}) collective-permute-start(bf16[2,1,256,512]{3,2,1,0:T(8,128)(2,1)S(1)} %copy-done.8), channel_id=1, source_target_pairs={{2,0},{3,1},{0,2},{1,3},{6,4},{7,5},{4,6},{5,7},{10,8},{11,9},{8,1... | collective-permute-start | bytes 1572872 | tf_op jit(solution)/shard_map/ppermute | solution.py:204
  48.3 4.3 %collective-permute-start.12 = (bf16[128,256]{1,0:T(8,128)(2,1)S(1)}, bf16[128,256]{1,0:T(8,128)(2,1)S(1)}, u32[]{:S(2)}, u32[]{:S(2)}) collective-permute-start(bf16[128,256]{1,0:T(8,128)(2,1)S(1)} %pad_maximum_fusion.2.refs_0_), channel_id=1, source_target_pairs={{4,0},{5,1},{6,2},{7,3},{0,4},{1,5},{2,6},{3,7},{12,8},{13,9},{14,... | collective-permute-start | bytes 196616 | tf_op jit(solution)/shard_map/ppermute | solution.py:204
  52.9 1.3 %collective-permute-start.13 = (f32[64,256]{1,0:T(8,128)S(1)}, f32[64,256]{1,0:T(8,128)S(1)}, u32[]{:S(2)}, u32[]{:S(2)}) collective-permute-start(f32[64,256]{1,0:T(8,128)S(1)} %shard_map.73), channel_id=1, source_target_pairs={{1,0},{0,1},{3,2},{2,3},{5,4},{4,5},{7,6},{6,7},{9,8},{8,9},{11,10... | collective-permute-start | bytes 196616 | tf_op jit(solution)/shard_map/ppermute | solution.py:204
  57.6 5.3 %collective-permute-start.17 = (bf16[64,256]{1,0:T(8,128)(2,1)S(1)}, bf16[64,256]{1,0:T(8,128)(2,1)S(1)}, u32[]{:S(2)}, u32[]{:S(2)}) collective-permute-start(bf16[64,256]{1,0:T(8,128)(2,1)S(1)} %add_convert_fusion.1), channel_id=1, source_target_pairs={{25,0},{24,1},{27,2},{26,3},{29,4},{28,5},{31,6},{30,7},{17,8},{16... | collective-permute-start | bytes 98312 | tf_op jit(solution)/shard_map/ppermute | solution.py:204
  58.8 5.4 %collective-permute-start.16 = (bf16[64,256]{1,0:T(8,128)(2,1)S(1)}, bf16[64,256]{1,0:T(8,128)(2,1)S(1)}, u32[]{:S(2)}, u32[]{:S(2)}) collective-permute-start(bf16[64,256]{1,0:T(8,128)(2,1)S(1)} %add_convert_fusion.1), channel_id=1, source_target_pairs={{16,0},{8,1},{18,2},{10,3},{20,4},{12,5},{22,6},{14,7},{1,8},{25,9... | collective-permute-start | bytes 98312 | tf_op jit(solution)/shard_map/ppermute | solution.py:204
  60.8 7.6 %collective-permute-start.14 = (bf16[128,256]{1,0:T(8,128)(2,1)S(1)}, bf16[128,256]{1,0:T(8,128)(2,1)S(1)}, u32[]{:S(2)}, u32[]{:S(2)}) collective-permute-start(bf16[128,256]{1,0:T(8,128)(2,1)S(1)} %pad_maximum_fusion.3.refs_0_), channel_id=1, source_target_pairs={{2,0},{3,1},{0,2},{1,3},{6,4},{7,5},{4,6},{5,7},{10,8},{11,9},{8,1... | collective-permute-start | bytes 196616 | tf_op jit(solution)/shard_map/ppermute | solution.py:204
  64.3 4.5 %collective-permute-start.18 = (bf16[128,256]{1,0:T(8,128)(2,1)S(1)}, bf16[128,256]{1,0:T(8,128)(2,1)S(1)}, u32[]{:S(2)}, u32[]{:S(2)}) collective-permute-start(bf16[128,256]{1,0:T(8,128)(2,1)S(1)} %pad_maximum_fusion.4.refs_0_), channel_id=1, source_target_pairs={{4,0},{5,1},{6,2},{7,3},{0,4},{1,5},{2,6},{3,7},{12,8},{13,9},{14,... | collective-permute-start | bytes 196616 | tf_op jit(solution)/shard_map/ppermute | solution.py:204
  69.0 1.3 %collective-permute-start.19 = (f32[64,256]{1,0:T(8,128)S(1)}, f32[64,256]{1,0:T(8,128)S(1)}, u32[]{:S(2)}, u32[]{:S(2)}) collective-permute-start(f32[64,256]{1,0:T(8,128)S(1)} %shard_map.78), channel_id=1, source_target_pairs={{1,0},{0,1},{3,2},{2,3},{5,4},{4,5},{7,6},{6,7},{9,8},{8,9},{11,10... | collective-permute-start | bytes 196616 | tf_op jit(solution)/shard_map/ppermute | solution.py:204
  70.4 4.0 %collective-permute-start.20 = (bf16[64,256]{1,0:T(8,128)(2,1)S(1)}, bf16[64,256]{1,0:T(8,128)(2,1)S(1)}, u32[]{:S(2)}, u32[]{:S(2)}) collective-permute-start(bf16[64,256]{1,0:T(8,128)(2,1)S(1)} %add_convert_fusion.refs_0_), channel_id=1, source_target_pairs={{2,0},{3,1},{0,2},{1,3},{6,4},{7,5},{4,6},{5,7},{10,8},{11,9},{8,1... | collective-permute-start | bytes 98312 | tf_op jit(solution)/shard_map/ppermute | solution.py:204

commit v6 on v5

--- a/solution.py
+++ b/solution.py
@@ -332,8 +332,6 @@
                 for earlier in range(level):
                     value = step(value, [(fetched[earlier], forward[pair_index(level, earlier)])])
             stack = deep(settle(value), lambda sign: fold_lower(level, True, sign))
-            if level == top - 1:
-                stack = after(stack, *high_one)
             fetched[level] = wide(stack)
         fold_lower(top, True, stack)
 
@@ -343,6 +341,8 @@
                 results = collect(jnp.concatenate([solved[k] for k in range(1, levels)], axis=0))
                 value = after(value, *results)
             for earlier in range(level):
+                if level == top and earlier == top - 1:
+                    value = after(value, *high_one)
                 value = step(value, [(fetched[earlier], backward[pair_index(level, earlier)])])
             for later in reversed(range(level + 1, levels)):
                 value = step(value, [(back[later], upward[later, level])])

time: 75.8 us -> 73 us (0.963)
  waiting for transfers between devices: 28.3 us -> 26.2 us
    ppermute x21, waiting for transfers between devices: 28.3 us -> 26.2 us  [send(): return lax.ppermute(value, ('prow', 'pcol'), pairs)]
  transfers between devices with their start and end apart: 21 -> 21, of which waited for: 17 -> 17; matrix products, arithmetic and copies ran while one was open for 4% -> 4% of each run, Pallas kernels for 17% -> 18%
where the time goes in v6:
time: 73 us; the launch traced here: 72.8 us
  starting transfers between devices  26.2 us (36%)
  waiting for transfers between devices  26.2 us (36%)
  Pallas kernels  16.5 us (23%)
  local copies, waits for them, and re-layouts  3.58 us (5%)
    ppermute x21, waiting for transfers between devices, send(): return lax.ppermute(value, ('prow', 'pcol'), pairs)  26.2 us
    ppermute x21, starting transfers between devices, send(): return lax.ppermute(value, ('prow', 'pcol'), pairs)  26.2 us
    pallas_call x16, Pallas kernels, call(): pl.pallas_call(kernel, grid=(1,), out_shape=shapes, in_specs=specs, out_s...  16.5 us
    slice x2, local copies, waits for them, and re-layouts, body(): parts = (upper_blocks[last_pair:], upper_blocks[:last_pair])  2.49 us
  transfers between devices with their start and end apart: 21, of which 17 were waited for; matrix products, arithmetic and copies ran while one was open for 4% of the time, Pallas kernels for 18%

profile of v6, /device:TPU:0, one launch (start us, length us, event | category | flops | bytes accessed | tf_op | source)
XLA Modules:
  0.0 72.8 jit_solution(2738189384741036662)
XLA Ops:
  0.0 2.9 %collective-permute-start.3 = (bf16[3,1,256,512]{3,2,1,0:T(8,128)(2,1)}, bf16[3,1,256,512]{3,2,1,0:T(8,128)(2,1)S(1)}, u32[]{:S(2)}, u32[]{:S(2)}) collective-permute-start(bf16[3,1,256,512]{3,2,1,0:T(8,128)(2,1)} %refs_2_.3), channel_id=1, source_target_pairs={{2,0},{3,1},{0,2},{1,3},{6,4},{7,5},{4,6},{5,7},{10,8},{11,9},{8,1... | collective-permute-start | bytes 2359304 | tf_op jit(solution)/shard_map/ppermute | solution.py:204
  2.9 0.6 stack.23.spot
  3.5 1.8 %shard_map.64.first = bf16[64,256]{1,0:T(8,128)(2,1)} custom-call(s32[5]{0:T(128)} %stack.23.spot, bf16[3,1,256,128]{3,2,1,0:T(8,128)(2,1)} %rhs.3, bf16[3,1,256,256]{3,2,1,0:T(8,128)(2,1)} %refs_1_.6), custom_call_target="tpu_custom_call" | custom-call | tf_op jit(solution)/shard_map/pallas_call | solution.py:49
  5.3 2.8 %collective-permute-start.1 = (bf16[64,256]{1,0:T(8,128)(2,1)}, bf16[64,256]{1,0:T(8,128)(2,1)S(1)}, u32[]{:S(2)}, u32[]{:S(2)}) collective-permute-start(bf16[64,256]{1,0:T(8,128)(2,1)} %shard_map.64.first), channel_id=1, source_target_pairs={{25,0},{24,1},{27,2},{26,3},{29,4},{28,5},{31,6},{30,7},{17,8},{16... | collective-permute-start | bytes 98312 | tf_op jit(solution)/shard_map/ppermute | solution.py:204
  8.1 0.0 collective-permute-start
  8.1 1.7 %slice.6 = bf16[1,1,256,512]{3,2,1,0:T(8,128)(2,1)} slice(bf16[3,1,256,512]{3,2,1,0:T(8,128)(2,1)} %refs_1_.9), slice={[2:3], [0:1], [0:256], [0:512]} | slice | bytes 524288 | tf_op jit(solution)/shard_map/slice | solution.py:291
  9.8 0.0 copy-start.6
  9.8 0.8 %slice.7 = bf16[2,1,256,512]{3,2,1,0:T(8,128)(2,1)} slice(bf16[3,1,256,512]{3,2,1,0:T(8,128)(2,1)S(1)} %copy-done.1), slice={[0:2], [0:1], [0:256], [0:512]} | slice | bytes 1048576 | tf_op jit(solution)/shard_map/slice | solution.py:291
  10.6 0.2 copy-done
  10.8 0.2 copy-done.2
  11.1 0.0 copy-done.4
  11.1 1.4 %shard_map.65 = (f32[64,256]{1,0:T(8,128)S(1)}, f32[64,256]{1,0:T(8,128)S(1)}, f32[64,256]{1,0:T(8,128)S(1)}, f32[64,256]{1,0:T(8,128)S(1)}) custom-call(s32[5]{0:T(128)S(1)} %copy-done.7, bf16[64,256]{1,0:T(8,128)(2,1)S(1)} %copy-done.6, bf16[3,1,256,128]{3,2,1,0:T(8,128)(2,1)S(1)} %copy-done.4, bf16[3,1,256,256]{3,2,1,0:T(8,128)(2,1)S(1)} %copy-done.2, ...), custom_call_target="tpu_custom_call" | custom-call | tf_op jit(solution)/shard_map/pallas_call | solution.py:49
  12.5 0.0 collective-permute-done.1
  12.5 0.6 collective-permute-done
  13.1 0.0 copy-start.5
  13.2 1.6 %collective-permute-start.2 = (bf16[128,256]{1,0:T(8,128)(2,1)S(1)}, bf16[128,256]{1,0:T(8,128)(2,1)S(1)}, u32[]{:S(2)}, u32[]{:S(2)}) collective-permute-start(bf16[128,256]{1,0:T(8,128)(2,1)S(1)} %pad_maximum_fusion.refs_2_.refs_0_), channel_id=1, source_target_pairs={{4,0},{5,1},{6,2},{7,3},{0,4},{1,5},{2,6},{3,7},{12,8},{13,9},{14,... | collective-permute-start | bytes 196616 | tf_op jit(solution)/shard_map/ppermute | solution.py:204
  14.8 2.8 %collective-permute-done.2.refs_3_.refs_1_ = bf16[128,256]{1,0:T(8,128)(2,1)S(1)} collective-permute-done((bf16[128,256]{1,0:T(8,128)(2,1)S(1)}, bf16[128,256]{1,0:T(8,128)(2,1)S(1)}, u32[]{:S(2)}, u32[]{:S(2)}) %collective-permute-start.2) | collective-permute-done | bytes 65568 | tf_op jit(solution)/shard_map/ppermute | solution.py:204
  17.6 3.1 %collective-permute-done.3.refs_1_.refs_3_ = bf16[3,1,256,512]{3,2,1,0:T(8,128)(2,1)S(1)} collective-permute-done((bf16[3,1,256,512]{3,2,1,0:T(8,128)(2,1)}, bf16[3,1,256,512]{3,2,1,0:T(8,128)(2,1)S(1)}, u32[]{:S(2)}, u32[]{:S(2)}) %collective-permute-start.3) | collective-permute-done | bytes 786464 | tf_op jit(solution)/shard_map/ppermute | solution.py:204
  20.7 1.4 %shard_map.66 = f32[64,256]{1,0:T(8,128)S(1)} custom-call(s32[5]{0:T(128)S(1)} %copy-done.7, s32[3,8,8]{2,1,0:T(8,128)S(1)} %copy-done.5, f32[64,256]{1,0:T(8,128)S(1)} %get-tuple-element.26.base, bf16[3,1,256,256]{3,2,1,0:T(8,128)(2,1)S(1)} %copy-done.2, bf16[3,1,256,512]{3,2,1,0:T(8,128)(2,1)S(1)} %copy-done.3, ...), custom_call_target="tpu_custom_call" | custom-call | tf_op jit(solution)/shard_map/pallas_call | solution.py:49
  22.1 0.1 collective-permute-start.4
  22.2 1.2 %collective-permute-done.4 = f32[64,256]{1,0:T(8,128)S(1)} collective-permute-done((f32[64,256]{1,0:T(8,128)S(1)}, f32[64,256]{1,0:T(8,128)S(1)}, u32[]{:S(2)}, u32[]{:S(2)}) %collective-permute-start.4) | collective-permute-done | bytes 65568 | tf_op jit(solution)/shard_map/ppermute | solution.py:204
  23.4 3.7 %collective-permute-start.6 = (bf16[64,256]{1,0:T(8,128)(2,1)S(1)}, bf16[64,256]{1,0:T(8,128)(2,1)S(1)}, u32[]{:S(2)}, u32[]{:S(2)}) collective-permute-start(bf16[64,256]{1,0:T(8,128)(2,1)S(1)} %add_convert_fusion.3), channel_id=1, source_target_pairs={{25,0},{24,1},{27,2},{26,3},{29,4},{28,5},{31,6},{30,7},{17,8},{16... | collective-permute-start | bytes 98312 | tf_op jit(solution)/shard_map/ppermute | solution.py:204
  27.1 0.0 collective-permute-start.5
  27.1 1.5 %collective-permute-start.7 = (bf16[1,1,256,512]{3,2,1,0:T(8,128)(2,1)S(1)}, bf16[1,1,256,512]{3,2,1,0:T(8,128)(2,1)S(1)}, u32[]{:S(2)}, u32[]{:S(2)}) collective-permute-start(bf16[1,1,256,512]{3,2,1,0:T(8,128)(2,1)S(1)} %copy-done.9), channel_id=1, source_target_pairs={{2,0},{3,1},{0,2},{1,3},{6,4},{7,5},{4,6},{5,7},{10,8},{11,9},{8,1... | collective-permute-start | bytes 786440 | tf_op jit(solution)/shard_map/ppermute | solution.py:204
  28.6 0.3 collective-permute-done.6
  28.9 3.0 %collective-permute-done.5 = bf16[64,256]{1,0:T(8,128)(2,1)S(1)} collective-permute-done((bf16[64,256]{1,0:T(8,128)(2,1)S(1)}, bf16[64,256]{1,0:T(8,128)(2,1)S(1)}, u32[]{:S(2)}, u32[]{:S(2)}) %collective-permute-start.5) | collective-permute-done | bytes 32800 | tf_op jit(solution)/shard_map/ppermute | solution.py:204
  31.9 1.6 %shard_map.67.refs_2_ = bf16[4,2,256,256]{3,2,1,0:T(8,128)(2,1)S(1)} custom-call(s32[5]{0:T(128)S(1)} %copy-done.7, s32[3,8,8]{2,1,0:T(8,128)S(1)} %copy-done.5, bf16[3,1,256,256]{3,2,1,0:T(8,128)(2,1)S(1)} %copy-done, bf16[3,1,256,256]{3,2,1,0:T(8,128)(2,1)S(1)} %copy-done.2, bf16[3,1,256,512]{3,2,1,0:T(8,128)(2,1)S(1)} %copy-done.3, ...), custom_call_target="tpu_custom_call" | custom-call | tf_op jit(solution)/shard_map/pallas_call | solution.py:49
  33.6 1.6 %collective-permute-start.8 = (bf16[128,256]{1,0:T(8,128)(2,1)S(1)}, bf16[128,256]{1,0:T(8,128)(2,1)S(1)}, u32[]{:S(2)}, u32[]{:S(2)}) collective-permute-start(bf16[128,256]{1,0:T(8,128)(2,1)S(1)} %pad_maximum_fusion.1.refs_0_), channel_id=1, source_target_pairs={{4,0},{5,1},{6,2},{7,3},{0,4},{1,5},{2,6},{3,7},{12,8},{13,9},{14,... | collective-permute-start | bytes 196616 | tf_op jit(solution)/shard_map/ppermute | solution.py:204
  35.1 2.0 %shard_map.69 = (bf16[4,2,256,256]{3,2,1,0:T(8,128)(2,1)S(1)}, bf16[4,2,256,256]{3,2,1,0:T(8,128)(2,1)S(1)}) custom-call(s32[5]{0:T(128)S(1)} %copy-done.7, s32[3,8,8]{2,1,0:T(8,128)S(1)} %copy-done.5, bf16[3,1,256,256]{3,2,1,0:T(8,128)(2,1)S(1)} %copy-done, bf16[3,1,256,256]{3,2,1,0:T(8,128)(2,1)S(1)} %copy-done.2, bf16[3,1,256,512]{3,2,1,0:T(8,128)(2,1)S(1)} %copy-done.3, ...), custom_call_target="tpu_custom_call" | custom-call | tf_op jit(solution)/shard_map/pallas_call | solution.py:49
  37.2 0.3 shard_map.70.base
  37.5 0.4 collective-permute-done.8.refs_1_
  37.9 0.3 shard_map.71
  38.2 0.1 collective-permute-start.9
  38.3 1.2 %collective-permute-done.9 = f32[64,256]{1,0:T(8,128)S(1)} collective-permute-done((f32[64,256]{1,0:T(8,128)S(1)}, f32[64,256]{1,0:T(8,128)S(1)}, u32[]{:S(2)}, u32[]{:S(2)}) %collective-permute-start.9) | collective-permute-done | bytes 65568 | tf_op jit(solution)/shard_map/ppermute | solution.py:204
  39.5 0.6 collective-permute-start.11
  40.2 0.2 collective-permute-start.10
  40.4 1.5 %collective-permute-start.15 = (bf16[2,1,256,512]{3,2,1,0:T(8,128)(2,1)S(1)}, bf16[2,1,256,512]{3,2,1,0:T(8,128)(2,1)S(1)}, u32[]{:S(2)}, u32[]{:S(2)}) collective-permute-start(bf16[2,1,256,512]{3,2,1,0:T(8,128)(2,1)S(1)} %copy-done.8), channel_id=1, source_target_pairs={{2,0},{3,1},{0,2},{1,3},{6,4},{7,5},{4,6},{5,7},{10,8},{11,9},{8,1... | collective-permute-start | bytes 1572872 | tf_op jit(solution)/shard_map/ppermute | solution.py:204
  41.9 2.9 %collective-permute-done.11 = bf16[64,256]{1,0:T(8,128)(2,1)S(1)} collective-permute-done((bf16[64,256]{1,0:T(8,128)(2,1)S(1)}, bf16[64,256]{1,0:T(8,128)(2,1)S(1)}, u32[]{:S(2)}, u32[]{:S(2)}) %collective-permute-start.11) | collective-permute-done | bytes 32800 | tf_op jit(solution)/shard_map/ppermute | solution.py:204
  44.8 1.0 %collective-permute-done.10 = bf16[64,256]{1,0:T(8,128)(2,1)S(1)} collective-permute-done((bf16[64,256]{1,0:T(8,128)(2,1)S(1)}, bf16[64,256]{1,0:T(8,128)(2,1)S(1)}, u32[]{:S(2)}, u32[]{:S(2)}) %collective-permute-start.10) | collective-permute-done | bytes 32800 | tf_op jit(solution)/shard_map/ppermute | solution.py:204
  45.8 1.6 %collective-permute-start.12 = (bf16[128,256]{1,0:T(8,128)(2,1)S(1)}, bf16[128,256]{1,0:T(8,128)(2,1)S(1)}, u32[]{:S(2)}, u32[]{:S(2)}) collective-permute-start(bf16[128,256]{1,0:T(8,128)(2,1)S(1)} %pad_maximum_fusion.2.refs_0_), channel_id=1, source_target_pairs={{4,0},{5,1},{6,2},{7,3},{0,4},{1,5},{2,6},{3,7},{12,8},{13,9},{14,... | collective-permute-start | bytes 196616 | tf_op jit(solution)/shard_map/ppermute | solution.py:204
  47.4 0.3 shard_map.68.base
  47.7 1.3 %shard_map.72.refs_2_ = bf16[4,2,256,256]{3,2,1,0:T(8,128)(2,1)S(1)} custom-call(s32[5]{0:T(128)S(1)} %copy-done.7, s32[3,8,8]{2,1,0:T(8,128)S(1)} %copy-done.5, bf16[3,1,256,256]{3,2,1,0:T(8,128)(2,1)S(1)} %copy-done, bf16[3,1,256,512]{3,2,1,0:T(8,128)(2,1)S(1)} %copy-done.1, bf16[1,1,256,512]{3,2,1,0:T(8,128)(2,1)S(1)} %collective-permute-done.7.refs_2_), custom_call_target="tpu_custom_call" | custom-call | tf_op jit(solution)/shard_map/pallas_call | solution.py:49
  49.0 1.2 %collective-permute-done.12.refs_1_ = bf16[128,256]{1,0:T(8,128)(2,1)S(1)} collective-permute-done((bf16[128,256]{1,0:T(8,128)(2,1)S(1)}, bf16[128,256]{1,0:T(8,128)(2,1)S(1)}, u32[]{:S(2)}, u32[]{:S(2)}) %collective-permute-start.12) | collective-permute-done | bytes 65568 | tf_op jit(solution)/shard_map/ppermute | solution.py:204
  50.2 0.3 shard_map.73
  50.5 0.1 collective-permute-start.13
  50.5 1.2 %collective-permute-done.13 = f32[64,256]{1,0:T(8,128)S(1)} collective-permute-done((f32[64,256]{1,0:T(8,128)S(1)}, f32[64,256]{1,0:T(8,128)S(1)}, u32[]{:S(2)}, u32[]{:S(2)}) %collective-permute-start.13) | collective-permute-done | bytes 65568 | tf_op jit(solution)/shard_map/ppermute | solution.py:204
  51.8 2.8 %collective-permute-done.15.refs_2_ = bf16[2,1,256,512]{3,2,1,0:T(8,128)(2,1)S(1)} collective-permute-done((bf16[2,1,256,512]{3,2,1,0:T(8,128)(2,1)S(1)}, bf16[2,1,256,512]{3,2,1,0:T(8,128)(2,1)S(1)}, u32[]{:S(2)}, u32[]{:S(2)}) %collective-permute-start.15) | collective-permute-done | bytes 524320 | tf_op jit(solution)/shard_map/ppermute | solution.py:204
  54.6 1.9 %collective-permute-start.17 = (bf16[64,256]{1,0:T(8,128)(2,1)S(1)}, bf16[64,256]{1,0:T(8,128)(2,1)S(1)}, u32[]{:S(2)}, u32[]{:S(2)}) collective-permute-start(bf16[64,256]{1,0:T(8,128)(2,1)S(1)} %add_convert_fusion.1), channel_id=1, source_target_pairs={{25,0},{24,1},{27,2},{26,3},{29,4},{28,5},{31,6},{30,7},{17,8},{16... | collective-permute-start | bytes 98312 | tf_op jit(solution)/shard_map/ppermute | solution.py:204
  56.5 1.3 %collective-permute-start.16 = (bf16[64,256]{1,0:T(8,128)(2,1)S(1)}, bf16[64,256]{1,0:T(8,128)(2,1)S(1)}, u32[]{:S(2)}, u32[]{:S(2)}) collective-permute-start(bf16[64,256]{1,0:T(8,128)(2,1)S(1)} %add_convert_fusion.1), channel_id=1, source_target_pairs={{16,0},{8,1},{18,2},{10,3},{20,4},{12,5},{22,6},{14,7},{1,8},{25,9... | collective-permute-start | bytes 98312 | tf_op jit(solution)/shard_map/ppermute | solution.py:204
  57.9 1.5 %collective-permute-start.14 = (bf16[128,256]{1,0:T(8,128)(2,1)S(1)}, bf16[128,256]{1,0:T(8,128)(2,1)S(1)}, u32[]{:S(2)}, u32[]{:S(2)}) collective-permute-start(bf16[128,256]{1,0:T(8,128)(2,1)S(1)} %pad_maximum_fusion.3.refs_0_), channel_id=1, source_target_pairs={{2,0},{3,1},{0,2},{1,3},{6,4},{7,5},{4,6},{5,7},{10,8},{11,9},{8,1... | collective-permute-start | bytes 196616 | tf_op jit(solution)/shard_map/ppermute | solution.py:204
  59.3 0.5 collective-permute-done.17
  59.9 1.5 %collective-permute-done.16 = bf16[64,256]{1,0:T(8,128)(2,1)S(1)} collective-permute-done((bf16[64,256]{1,0:T(8,128)(2,1)S(1)}, bf16[64,256]{1,0:T(8,128)(2,1)S(1)}, u32[]{:S(2)}, u32[]{:S(2)}) %collective-permute-start.16) | collective-permute-done | bytes 32800 | tf_op jit(solution)/shard_map/ppermute | solution.py:204
  61.4 1.6 %collective-permute-start.18 = (bf16[128,256]{1,0:T(8,128)(2,1)S(1)}, bf16[128,256]{1,0:T(8,128)(2,1)S(1)}, u32[]{:S(2)}, u32[]{:S(2)}) collective-permute-start(bf16[128,256]{1,0:T(8,128)(2,1)S(1)} %pad_maximum_fusion.4.refs_0_), channel_id=1, source_target_pairs={{4,0},{5,1},{6,2},{7,3},{0,4},{1,5},{2,6},{3,7},{12,8},{13,9},{14,... | collective-permute-start | bytes 196616 | tf_op jit(solution)/shard_map/ppermute | solution.py:204
  63.0 1.3 %shard_map.77.refs_2_ = bf16[4,2,256,256]{3,2,1,0:T(8,128)(2,1)S(1)} custom-call(s32[5]{0:T(128)S(1)} %copy-done.7, s32[3,8,8]{2,1,0:T(8,128)S(1)} %copy-done.5, bf16[3,1,256,256]{3,2,1,0:T(8,128)(2,1)S(1)} %copy-done, bf16[3,1,256,512]{3,2,1,0:T(8,128)(2,1)S(1)} %copy-done.1, bf16[2,1,256,512]{3,2,1,0:T(8,128)(2,1)S(1)} %collective-permute-done.15.refs_2_), custom_call_target="tpu_custom_call" | custom-call | tf_op jit(solution)/shard_map/pallas_call | solution.py:49
  64.3 1.3 %shard_map.75.refs_2_ = bf16[4,2,256,256]{3,2,1,0:T(8,128)(2,1)S(1)} custom-call(s32[5]{0:T(128)S(1)} %copy-done.7, s32[3,8,8]{2,1,0:T(8,128)S(1)} %copy-done.5, bf16[3,1,256,256]{3,2,1,0:T(8,128)(2,1)S(1)} %copy-done, bf16[3,1,256,512]{3,2,1,0:T(8,128)(2,1)S(1)} %copy-done.1, bf16[2,1,256,512]{3,2,1,0:T(8,128)(2,1)S(1)} %collective-permute-done.15.refs_2_), custom_call_target="tpu_custom_call" | custom-call | tf_op jit(solution)/shard_map/pallas_call | solution.py:49
  65.5 0.0 collective-permute-done.14.refs_1_
  65.6 0.3 shard_map.76.base
  65.9 0.3 shard_map.78
  66.2 0.1 collective-permute-start.19
  66.3 1.2 %collective-permute-done.19 = f32[64,256]{1,0:T(8,128)S(1)} collective-permute-done((f32[64,256]{1,0:T(8,128)S(1)}, f32[64,256]{1,0:T(8,128)S(1)}, u32[]{:S(2)}, u32[]{:S(2)}) %collective-permute-start.19) | collective-permute-done | bytes 65568 | tf_op jit(solution)/shard_map/ppermute | solution.py:204
  67.5 1.6 %collective-permute-start.20 = (bf16[64,256]{1,0:T(8,128)(2,1)S(1)}, bf16[64,256]{1,0:T(8,128)(2,1)S(1)}, u32[]{:S(2)}, u32[]{:S(2)}) collective-permute-start(bf16[64,256]{1,0:T(8,128)(2,1)S(1)} %add_convert_fusion.refs_0_), channel_id=1, source_target_pairs={{2,0},{3,1},{0,2},{1,3},{6,4},{7,5},{4,6},{5,7},{10,8},{11,9},{8,1... | collective-permute-start | bytes 98312 | tf_op jit(solution)/shard_map/ppermute | solution.py:204
  69.1 1.4 %shard_map.74.whole = bf16[3,1,256,128]{3,2,1,0:T(8,128)(2,1)} custom-call(s32[5]{0:T(128)S(1)} %copy-done.7, bf16[128,256]{1,0:T(8,128)(2,1)S(1)} %pad_maximum_fusion.3.refs_0_, bf16[128,256]{1,0:T(8,128)(2,1)S(1)} %collective-permute-done.14.refs_1_), custom_call_target="tpu_custom_call" | custom-call | tf_op jit(solution)/shard_map/pallas_call | solution.py:49
  70.4 1.1 %collective-permute-done.20.refs_1_ = bf16[64,256]{1,0:T(8,128)(2,1)S(1)} collective-permute-done((bf16[64,256]{1,0:T(8,128)(2,1)S(1)}, bf16[64,256]{1,0:T(8,128)(2,1)S(1)}, u32[]{:S(2)}, u32[]{:S(2)}) %collective-permute-start.20) | collective-permute-done | bytes 32800 | tf_op jit(solution)/shard_map/ppermute | solution.py:204
  71.5 1.3 %shard_map.79 = bf16[3,1,256,128]{3,2,1,0:T(8,128)(2,1)} custom-call(s32[5]{0:T(128)S(1)} %copy-done.7, bf16[3,1,256,128]{3,2,1,0:T(8,128)(2,1)} %shard_map.74.whole, bf16[64,256]{1,0:T(8,128)(2,1)S(1)} %add_convert_fusion.refs_0_, bf16[64,256]{1,0:T(8,128)(2,1)S(1)} %collective-permute-done.20.refs_1_), custom_call_target="tpu_custom_call", output_to_operand_aliasing={{}: (1, {})} | custom-call | tf_op jit(solution)/shard_map/pallas_call | solution.py:49
  (30 shorter events, 0.1 us)
Async XLA Ops:
  0.0 9.8 %copy-start.1 = (bf16[3,1,256,512]{3,2,1,0:T(8,128)(2,1)S(1)}, bf16[3,1,256,512]{3,2,1,0:T(8,128)(2,1)}, u32[]{:S(2)}) copy-start(bf16[3,1,256,512]{3,2,1,0:T(8,128)(2,1)} %refs_1_.9) | copy-start | bytes 2359300
  0.0 20.7 %collective-permute-start.3 = (bf16[3,1,256,512]{3,2,1,0:T(8,128)(2,1)}, bf16[3,1,256,512]{3,2,1,0:T(8,128)(2,1)S(1)}, u32[]{:S(2)}, u32[]{:S(2)}) collective-permute-start(bf16[3,1,256,512]{3,2,1,0:T(8,128)(2,1)} %refs_2_.3), channel_id=1, source_target_pairs={{2,0},{3,1},{0,2},{1,3},{6,4},{7,5},{4,6},{5,7},{10,8},{11,9},{8,1... | collective-permute-start | bytes 2359304 | tf_op jit(solution)/shard_map/ppermute | solution.py:204
  5.3 7.2 %collective-permute-start.1 = (bf16[64,256]{1,0:T(8,128)(2,1)}, bf16[64,256]{1,0:T(8,128)(2,1)S(1)}, u32[]{:S(2)}, u32[]{:S(2)}) collective-permute-start(bf16[64,256]{1,0:T(8,128)(2,1)} %shard_map.64.first), channel_id=1, source_target_pairs={{25,0},{24,1},{27,2},{26,3},{29,4},{28,5},{31,6},{30,7},{17,8},{16... | collective-permute-start | bytes 98312 | tf_op jit(solution)/shard_map/ppermute | solution.py:204
  8.1 5.0 %collective-permute-start = (bf16[64,256]{1,0:T(8,128)(2,1)}, bf16[64,256]{1,0:T(8,128)(2,1)S(1)}, u32[]{:S(2)}, u32[]{:S(2)}) collective-permute-start(bf16[64,256]{1,0:T(8,128)(2,1)} %shard_map.64.first), channel_id=1, source_target_pairs={{16,0},{8,1},{18,2},{10,3},{20,4},{12,5},{22,6},{14,7},{1,8},{25,9... | collective-permute-start | bytes 98312 | tf_op jit(solution)/shard_map/ppermute | solution.py:204
  9.8 1.1 %copy-start = (bf16[3,1,256,256]{3,2,1,0:T(8,128)(2,1)S(1)}, bf16[3,1,256,256]{3,2,1,0:T(8,128)(2,1)}, u32[]{:S(2)}) copy-start(bf16[3,1,256,256]{3,2,1,0:T(8,128)(2,1)} %refs_0_.11) | copy-start | bytes 1179652
  9.8 1.3 %copy-start.2 = (bf16[3,1,256,256]{3,2,1,0:T(8,128)(2,1)S(1)}, bf16[3,1,256,256]{3,2,1,0:T(8,128)(2,1)}, u32[]{:S(2)}) copy-start(bf16[3,1,256,256]{3,2,1,0:T(8,128)(2,1)} %refs_1_.6) | copy-start | bytes 1179652
  9.8 1.3 %copy-start.4 = (bf16[3,1,256,128]{3,2,1,0:T(8,128)(2,1)S(1)}, bf16[3,1,256,128]{3,2,1,0:T(8,128)(2,1)}, u32[]{:S(2)}) copy-start(bf16[3,1,256,128]{3,2,1,0:T(8,128)(2,1)} %rhs.3) | copy-start | bytes 589828
  9.8 1.3 %copy-start.6 = (bf16[64,256]{1,0:T(8,128)(2,1)S(1)}, bf16[64,256]{1,0:T(8,128)(2,1)}, u32[]{:S(2)}) copy-start(bf16[64,256]{1,0:T(8,128)(2,1)} %shard_map.64.first) | copy-start | bytes 98308
  9.8 1.3 %copy-start.7 = (s32[5]{0:T(128)S(1)}, s32[5]{0:T(128)}, u32[]{:S(2)}) copy-start(s32[5]{0:T(128)} %stack.23.spot) | copy-start | bytes 64
  10.6 10.1 %copy-start.3 = (bf16[3,1,256,512]{3,2,1,0:T(8,128)(2,1)S(1)}, bf16[3,1,256,512]{3,2,1,0:T(8,128)(2,1)}, u32[]{:S(2)}) copy-start(bf16[3,1,256,512]{3,2,1,0:T(8,128)(2,1)} %refs_2_.3) | copy-start | bytes 2359300
  13.1 7.6 %copy-start.5 = (s32[3,8,8]{2,1,0:T(8,128)S(1)}, s32[3,8,8]{2,1,0:T(8,128)}, u32[]{:S(2)}) copy-start(s32[3,8,8]{2,1,0:T(8,128)} %pattern.11) | copy-start | bytes 2308
  13.2 14.0 %copy-start.9 = (bf16[1,1,256,512]{3,2,1,0:T(8,128)(2,1)S(1)}, bf16[1,1,256,512]{3,2,1,0:T(8,128)(2,1)}, u32[]{:S(2)}) copy-start(bf16[1,1,256,512]{3,2,1,0:T(8,128)(2,1)} %slice.6) | copy-start | bytes 786436
  13.2 4.4 %collective-permute-start.2 = (bf16[128,256]{1,0:T(8,128)(2,1)S(1)}, bf16[128,256]{1,0:T(8,128)(2,1)S(1)}, u32[]{:S(2)}, u32[]{:S(2)}) collective-permute-start(bf16[128,256]{1,0:T(8,128)(2,1)S(1)} %pad_maximum_fusion.refs_2_.refs_0_), channel_id=1, source_target_pairs={{4,0},{5,1},{6,2},{7,3},{0,4},{1,5},{2,6},{3,7},{12,8},{13,9},{14,... | collective-permute-start | bytes 196616 | tf_op jit(solution)/shard_map/ppermute | solution.py:204
  22.1 1.3 %collective-permute-start.4 = (f32[64,256]{1,0:T(8,128)S(1)}, f32[64,256]{1,0:T(8,128)S(1)}, u32[]{:S(2)}, u32[]{:S(2)}) collective-permute-start(f32[64,256]{1,0:T(8,128)S(1)} %shard_map.66), channel_id=1, source_target_pairs={{1,0},{0,1},{3,2},{2,3},{5,4},{4,5},{7,6},{6,7},{9,8},{8,9},{11,10... | collective-permute-start | bytes 196616 | tf_op jit(solution)/shard_map/ppermute | solution.py:204
  23.4 5.5 %collective-permute-start.6 = (bf16[64,256]{1,0:T(8,128)(2,1)S(1)}, bf16[64,256]{1,0:T(8,128)(2,1)S(1)}, u32[]{:S(2)}, u32[]{:S(2)}) collective-permute-start(bf16[64,256]{1,0:T(8,128)(2,1)S(1)} %add_convert_fusion.3), channel_id=1, source_target_pairs={{25,0},{24,1},{27,2},{26,3},{29,4},{28,5},{31,6},{30,7},{17,8},{16... | collective-permute-start | bytes 98312 | tf_op jit(solution)/shard_map/ppermute | solution.py:204
  27.1 4.8 %collective-permute-start.5 = (bf16[64,256]{1,0:T(8,128)(2,1)S(1)}, bf16[64,256]{1,0:T(8,128)(2,1)S(1)}, u32[]{:S(2)}, u32[]{:S(2)}) collective-permute-start(bf16[64,256]{1,0:T(8,128)(2,1)S(1)} %add_convert_fusion.3), channel_id=1, source_target_pairs={{16,0},{8,1},{18,2},{10,3},{20,4},{12,5},{22,6},{14,7},{1,8},{25,9... | collective-permute-start | bytes 98312 | tf_op jit(solution)/shard_map/ppermute | solution.py:204
  27.1 10.4 %collective-permute-start.7 = (bf16[1,1,256,512]{3,2,1,0:T(8,128)(2,1)S(1)}, bf16[1,1,256,512]{3,2,1,0:T(8,128)(2,1)S(1)}, u32[]{:S(2)}, u32[]{:S(2)}) collective-permute-start(bf16[1,1,256,512]{3,2,1,0:T(8,128)(2,1)S(1)} %copy-done.9), channel_id=1, source_target_pairs={{2,0},{3,1},{0,2},{1,3},{6,4},{7,5},{4,6},{5,7},{10,8},{11,9},{8,1... | collective-permute-start | bytes 786440 | tf_op jit(solution)/shard_map/ppermute | solution.py:204
  33.6 4.3 %collective-permute-start.8 = (bf16[128,256]{1,0:T(8,128)(2,1)S(1)}, bf16[128,256]{1,0:T(8,128)(2,1)S(1)}, u32[]{:S(2)}, u32[]{:S(2)}) collective-permute-start(bf16[128,256]{1,0:T(8,128)(2,1)S(1)} %pad_maximum_fusion.1.refs_0_), channel_id=1, source_target_pairs={{4,0},{5,1},{6,2},{7,3},{0,4},{1,5},{2,6},{3,7},{12,8},{13,9},{14,... | collective-permute-start | bytes 196616 | tf_op jit(solution)/shard_map/ppermute | solution.py:204
  37.9 2.5 %copy-start.8 = (bf16[2,1,256,512]{3,2,1,0:T(8,128)(2,1)S(1)}, bf16[2,1,256,512]{3,2,1,0:T(8,128)(2,1)}, u32[]{:S(2)}) copy-start(bf16[2,1,256,512]{3,2,1,0:T(8,128)(2,1)} %slice.7) | copy-start | bytes 1572868
  38.2 1.3 %collective-permute-start.9 = (f32[64,256]{1,0:T(8,128)S(1)}, f32[64,256]{1,0:T(8,128)S(1)}, u32[]{:S(2)}, u32[]{:S(2)}) collective-permute-start(f32[64,256]{1,0:T(8,128)S(1)} %shard_map.71), channel_id=1, source_target_pairs={{1,0},{0,1},{3,2},{2,3},{5,4},{4,5},{7,6},{6,7},{9,8},{8,9},{11,10... | collective-permute-start | bytes 196616 | tf_op jit(solution)/shard_map/ppermute | solution.py:204
  39.5 5.2 %collective-permute-start.11 = (bf16[64,256]{1,0:T(8,128)(2,1)S(1)}, bf16[64,256]{1,0:T(8,128)(2,1)S(1)}, u32[]{:S(2)}, u32[]{:S(2)}) collective-permute-start(bf16[64,256]{1,0:T(8,128)(2,1)S(1)} %add_convert_fusion.2), channel_id=1, source_target_pairs={{25,0},{24,1},{27,2},{26,3},{29,4},{28,5},{31,6},{30,7},{17,8},{16... | collective-permute-start | bytes 98312 | tf_op jit(solution)/shard_map/ppermute | solution.py:204
  40.2 5.6 %collective-permute-start.10 = (bf16[64,256]{1,0:T(8,128)(2,1)S(1)}, bf16[64,256]{1,0:T(8,128)(2,1)S(1)}, u32[]{:S(2)}, u32[]{:S(2)}) collective-permute-start(bf16[64,256]{1,0:T(8,128)(2,1)S(1)} %add_convert_fusion.2), channel_id=1, source_target_pairs={{16,0},{8,1},{18,2},{10,3},{20,4},{12,5},{22,6},{14,7},{1,8},{25,9... | collective-permute-start | bytes 98312 | tf_op jit(solution)/shard_map/ppermute | solution.py:204
  40.4 14.2 %collective-permute-start.15 = (bf16[2,1,256,512]{3,2,1,0:T(8,128)(2,1)S(1)}, bf16[2,1,256,512]{3,2,1,0:T(8,128)(2,1)S(1)}, u32[]{:S(2)}, u32[]{:S(2)}) collective-permute-start(bf16[2,1,256,512]{3,2,1,0:T(8,128)(2,1)S(1)} %copy-done.8), channel_id=1, source_target_pairs={{2,0},{3,1},{0,2},{1,3},{6,4},{7,5},{4,6},{5,7},{10,8},{11,9},{8,1... | collective-permute-start | bytes 1572872 | tf_op jit(solution)/shard_map/ppermute | solution.py:204
  45.8 4.3 %collective-permute-start.12 = (bf16[128,256]{1,0:T(8,128)(2,1)S(1)}, bf16[128,256]{1,0:T(8,128)(2,1)S(1)}, u32[]{:S(2)}, u32[]{:S(2)}) collective-permute-start(bf16[128,256]{1,0:T(8,128)(2,1)S(1)} %pad_maximum_fusion.2.refs_0_), channel_id=1, source_target_pairs={{4,0},{5,1},{6,2},{7,3},{0,4},{1,5},{2,6},{3,7},{12,8},{13,9},{14,... | collective-permute-start | bytes 196616 | tf_op jit(solution)/shard_map/ppermute | solution.py:204
  50.5 1.3 %collective-permute-start.13 = (f32[64,256]{1,0:T(8,128)S(1)}, f32[64,256]{1,0:T(8,128)S(1)}, u32[]{:S(2)}, u32[]{:S(2)}) collective-permute-start(f32[64,256]{1,0:T(8,128)S(1)} %shard_map.73), channel_id=1, source_target_pairs={{1,0},{0,1},{3,2},{2,3},{5,4},{4,5},{7,6},{6,7},{9,8},{8,9},{11,10... | collective-permute-start | bytes 196616 | tf_op jit(solution)/shard_map/ppermute | solution.py:204
  54.6 5.3 %collective-permute-start.17 = (bf16[64,256]{1,0:T(8,128)(2,1)S(1)}, bf16[64,256]{1,0:T(8,128)(2,1)S(1)}, u32[]{:S(2)}, u32[]{:S(2)}) collective-permute-start(bf16[64,256]{1,0:T(8,128)(2,1)S(1)} %add_convert_fusion.1), channel_id=1, source_target_pairs={{25,0},{24,1},{27,2},{26,3},{29,4},{28,5},{31,6},{30,7},{17,8},{16... | collective-permute-start | bytes 98312 | tf_op jit(solution)/shard_map/ppermute | solution.py:204
  56.5 4.8 %collective-permute-start.16 = (bf16[64,256]{1,0:T(8,128)(2,1)S(1)}, bf16[64,256]{1,0:T(8,128)(2,1)S(1)}, u32[]{:S(2)}, u32[]{:S(2)}) collective-permute-start(bf16[64,256]{1,0:T(8,128)(2,1)S(1)} %add_convert_fusion.1), channel_id=1, source_target_pairs={{16,0},{8,1},{18,2},{10,3},{20,4},{12,5},{22,6},{14,7},{1,8},{25,9... | collective-permute-start | bytes 98312 | tf_op jit(solution)/shard_map/ppermute | solution.py:204
  57.9 7.7 %collective-permute-start.14 = (bf16[128,256]{1,0:T(8,128)(2,1)S(1)}, bf16[128,256]{1,0:T(8,128)(2,1)S(1)}, u32[]{:S(2)}, u32[]{:S(2)}) collective-permute-start(bf16[128,256]{1,0:T(8,128)(2,1)S(1)} %pad_maximum_fusion.3.refs_0_), channel_id=1, source_target_pairs={{2,0},{3,1},{0,2},{1,3},{6,4},{7,5},{4,6},{5,7},{10,8},{11,9},{8,1... | collective-permute-start | bytes 196616 | tf_op jit(solution)/shard_map/ppermute | solution.py:204
  61.4 4.5 %collective-permute-start.18 = (bf16[128,256]{1,0:T(8,128)(2,1)S(1)}, bf16[128,256]{1,0:T(8,128)(2,1)S(1)}, u32[]{:S(2)}, u32[]{:S(2)}) collective-permute-start(bf16[128,256]{1,0:T(8,128)(2,1)S(1)} %pad_maximum_fusion.4.refs_0_), channel_id=1, source_target_pairs={{4,0},{5,1},{6,2},{7,3},{0,4},{1,5},{2,6},{3,7},{12,8},{13,9},{14,... | collective-permute-start | bytes 196616 | tf_op jit(solution)/shard_map/ppermute | solution.py:204
  66.2 1.3 %collective-permute-start.19 = (f32[64,256]{1,0:T(8,128)S(1)}, f32[64,256]{1,0:T(8,128)S(1)}, u32[]{:S(2)}, u32[]{:S(2)}) collective-permute-start(f32[64,256]{1,0:T(8,128)S(1)} %shard_map.78), channel_id=1, source_target_pairs={{1,0},{0,1},{3,2},{2,3},{5,4},{4,5},{7,6},{6,7},{9,8},{8,9},{11,10... | collective-permute-start | bytes 196616 | tf_op jit(solution)/shard_map/ppermute | solution.py:204
  67.5 4.0 %collective-permute-start.20 = (bf16[64,256]{1,0:T(8,128)(2,1)S(1)}, bf16[64,256]{1,0:T(8,128)(2,1)S(1)}, u32[]{:S(2)}, u32[]{:S(2)}) collective-permute-start(bf16[64,256]{1,0:T(8,128)(2,1)S(1)} %add_convert_fusion.refs_0_), channel_id=1, source_target_pairs={{2,0},{3,1},{0,2},{1,3},{6,4},{7,5},{4,6},{5,7},{10,8},{11,9},{8,1... | collective-permute-start | bytes 98312 | tf_op jit(solution)/shard_map/ppermute | solution.py:204

commit v7 on v6

--- a/solution.py
+++ b/solution.py
@@ -331,7 +331,8 @@
                 fold_lower(level, False, stack)
                 for earlier in range(level):
                     value = step(value, [(fetched[earlier], forward[pair_index(level, earlier)])])
-            stack = deep(settle(value), lambda sign: fold_lower(level, True, sign))
+            stack = deep(settle(value))
+            fold_lower(level, True, stack)
             fetched[level] = wide(stack)
         fold_lower(top, True, stack)
 

time: 73 us -> 71.3 us (0.977)
  waiting for transfers between devices: 26.2 us -> 24.2 us
    ppermute x21, waiting for transfers between devices: 26.2 us -> 24.2 us  [send(): return lax.ppermute(value, ('prow', 'pcol'), pairs)]
  transfers between devices with their start and end apart: 21 -> 21, of which waited for: 17 -> 16; matrix products, arithmetic and copies ran while one was open for 4% -> 4% of each run, Pallas kernels for 18% -> 19%
where the time goes in v7:
time: 71.3 us; the launch traced here: 71.2 us
  starting transfers between devices  26.5 us (37%)
  waiting for transfers between devices  24.2 us (34%)
  Pallas kernels  16.5 us (23%)
  local copies, waits for them, and re-layouts  3.58 us (5%)
    ppermute x21, starting transfers between devices, send(): return lax.ppermute(value, ('prow', 'pcol'), pairs)  26.5 us
    ppermute x21, waiting for transfers between devices, send(): return lax.ppermute(value, ('prow', 'pcol'), pairs)  24.2 us
    pallas_call x16, Pallas kernels, call(): pl.pallas_call(kernel, grid=(1,), out_shape=shapes, in_specs=specs, out_s...  16.5 us
    slice x2, local copies, waits for them, and re-layouts, body(): parts = (upper_blocks[last_pair:], upper_blocks[:last_pair])  2.49 us
  transfers between devices with their start and end apart: 21, of which 16 were waited for; matrix products, arithmetic and copies ran while one was open for 4% of the time, Pallas kernels for 19%

profile of v7, /device:TPU:0, one launch (start us, length us, event | category | flops | bytes accessed | tf_op | source)
XLA Modules:
  0.0 71.2 jit_solution(12493231973652146850)
XLA Ops:
  0.0 2.9 %collective-permute-start.3 = (bf16[3,1,256,512]{3,2,1,0:T(8,128)(2,1)}, bf16[3,1,256,512]{3,2,1,0:T(8,128)(2,1)S(1)}, u32[]{:S(2)}, u32[]{:S(2)}) collective-permute-start(bf16[3,1,256,512]{3,2,1,0:T(8,128)(2,1)} %refs_2_.3), channel_id=1, source_target_pairs={{2,0},{3,1},{0,2},{1,3},{6,4},{7,5},{4,6},{5,7},{10,8},{11,9},{8,1... | collective-permute-start | bytes 2359304 | tf_op jit(solution)/shard_map/ppermute | solution.py:204
  2.9 0.6 stack.23.spot
  3.5 1.8 %shard_map.64.first = bf16[64,256]{1,0:T(8,128)(2,1)} custom-call(s32[5]{0:T(128)} %stack.23.spot, bf16[3,1,256,128]{3,2,1,0:T(8,128)(2,1)} %rhs.3, bf16[3,1,256,256]{3,2,1,0:T(8,128)(2,1)} %refs_1_.6), custom_call_target="tpu_custom_call" | custom-call | tf_op jit(solution)/shard_map/pallas_call | solution.py:49
  5.3 2.8 %collective-permute-start.1 = (bf16[64,256]{1,0:T(8,128)(2,1)}, bf16[64,256]{1,0:T(8,128)(2,1)S(1)}, u32[]{:S(2)}, u32[]{:S(2)}) collective-permute-start(bf16[64,256]{1,0:T(8,128)(2,1)} %shard_map.64.first), channel_id=1, source_target_pairs={{25,0},{24,1},{27,2},{26,3},{29,4},{28,5},{31,6},{30,7},{17,8},{16... | collective-permute-start | bytes 98312 | tf_op jit(solution)/shard_map/ppermute | solution.py:204
  8.1 0.0 collective-permute-start
  8.1 1.7 %slice.6 = bf16[1,1,256,512]{3,2,1,0:T(8,128)(2,1)} slice(bf16[3,1,256,512]{3,2,1,0:T(8,128)(2,1)} %refs_1_.9), slice={[2:3], [0:1], [0:256], [0:512]} | slice | bytes 524288 | tf_op jit(solution)/shard_map/slice | solution.py:291
  9.8 0.0 copy-start.6
  9.8 0.8 %slice.7 = bf16[2,1,256,512]{3,2,1,0:T(8,128)(2,1)} slice(bf16[3,1,256,512]{3,2,1,0:T(8,128)(2,1)S(1)} %copy-done.1), slice={[0:2], [0:1], [0:256], [0:512]} | slice | bytes 1048576 | tf_op jit(solution)/shard_map/slice | solution.py:291
  10.6 0.2 copy-done
  10.8 0.2 copy-done.2
  11.1 0.0 copy-done.4
  11.1 1.4 %shard_map.65 = (f32[64,256]{1,0:T(8,128)S(1)}, f32[64,256]{1,0:T(8,128)S(1)}, f32[64,256]{1,0:T(8,128)S(1)}, f32[64,256]{1,0:T(8,128)S(1)}) custom-call(s32[5]{0:T(128)S(1)} %copy-done.7, bf16[64,256]{1,0:T(8,128)(2,1)S(1)} %copy-done.6, bf16[3,1,256,128]{3,2,1,0:T(8,128)(2,1)S(1)} %copy-done.4, bf16[3,1,256,256]{3,2,1,0:T(8,128)(2,1)S(1)} %copy-done.2, ...), custom_call_target="tpu_custom_call" | custom-call | tf_op jit(solution)/shard_map/pallas_call | solution.py:49
  12.5 0.0 collective-permute-done.1
  12.5 0.6 collective-permute-done
  13.1 0.0 copy-start.5
  13.2 1.6 %collective-permute-start.2 = (bf16[128,256]{1,0:T(8,128)(2,1)S(1)}, bf16[128,256]{1,0:T(8,128)(2,1)S(1)}, u32[]{:S(2)}, u32[]{:S(2)}) collective-permute-start(bf16[128,256]{1,0:T(8,128)(2,1)S(1)} %pad_maximum_fusion.refs_2_.refs_0_), channel_id=1, source_target_pairs={{4,0},{5,1},{6,2},{7,3},{0,4},{1,5},{2,6},{3,7},{12,8},{13,9},{14,... | collective-permute-start | bytes 196616 | tf_op jit(solution)/shard_map/ppermute | solution.py:204
  14.8 2.8 %collective-permute-done.2.refs_3_.refs_1_ = bf16[128,256]{1,0:T(8,128)(2,1)S(1)} collective-permute-done((bf16[128,256]{1,0:T(8,128)(2,1)S(1)}, bf16[128,256]{1,0:T(8,128)(2,1)S(1)}, u32[]{:S(2)}, u32[]{:S(2)}) %collective-permute-start.2) | collective-permute-done | bytes 65568 | tf_op jit(solution)/shard_map/ppermute | solution.py:204
  17.6 3.1 %collective-permute-done.3.refs_1_.refs_3_ = bf16[3,1,256,512]{3,2,1,0:T(8,128)(2,1)S(1)} collective-permute-done((bf16[3,1,256,512]{3,2,1,0:T(8,128)(2,1)}, bf16[3,1,256,512]{3,2,1,0:T(8,128)(2,1)S(1)}, u32[]{:S(2)}, u32[]{:S(2)}) %collective-permute-start.3) | collective-permute-done | bytes 786464 | tf_op jit(solution)/shard_map/ppermute | solution.py:204
  20.7 1.4 %shard_map.66 = f32[64,256]{1,0:T(8,128)S(1)} custom-call(s32[5]{0:T(128)S(1)} %copy-done.7, s32[3,8,8]{2,1,0:T(8,128)S(1)} %copy-done.5, f32[64,256]{1,0:T(8,128)S(1)} %get-tuple-element.24.base, bf16[3,1,256,256]{3,2,1,0:T(8,128)(2,1)S(1)} %copy-done.2, bf16[3,1,256,512]{3,2,1,0:T(8,128)(2,1)S(1)} %copy-done.3, ...), custom_call_target="tpu_custom_call" | custom-call | tf_op jit(solution)/shard_map/pallas_call | solution.py:49
  22.1 0.1 collective-permute-start.4
  22.2 1.2 %collective-permute-done.4 = f32[64,256]{1,0:T(8,128)S(1)} collective-permute-done((f32[64,256]{1,0:T(8,128)S(1)}, f32[64,256]{1,0:T(8,128)S(1)}, u32[]{:S(2)}, u32[]{:S(2)}) %collective-permute-start.4) | collective-permute-done | bytes 65568 | tf_op jit(solution)/shard_map/ppermute | solution.py:204
  23.4 3.7 %collective-permute-start.6 = (bf16[64,256]{1,0:T(8,128)(2,1)S(1)}, bf16[64,256]{1,0:T(8,128)(2,1)S(1)}, u32[]{:S(2)}, u32[]{:S(2)}) collective-permute-start(bf16[64,256]{1,0:T(8,128)(2,1)S(1)} %add_convert_fusion.3), channel_id=1, source_target_pairs={{25,0},{24,1},{27,2},{26,3},{29,4},{28,5},{31,6},{30,7},{17,8},{16... | collective-permute-start | bytes 98312 | tf_op jit(solution)/shard_map/ppermute | solution.py:204
  27.1 0.0 collective-permute-start.5
  27.1 1.5 %collective-permute-start.7 = (bf16[1,1,256,512]{3,2,1,0:T(8,128)(2,1)S(1)}, bf16[1,1,256,512]{3,2,1,0:T(8,128)(2,1)S(1)}, u32[]{:S(2)}, u32[]{:S(2)}) collective-permute-start(bf16[1,1,256,512]{3,2,1,0:T(8,128)(2,1)S(1)} %copy-done.9), channel_id=1, source_target_pairs={{2,0},{3,1},{0,2},{1,3},{6,4},{7,5},{4,6},{5,7},{10,8},{11,9},{8,1... | collective-permute-start | bytes 786440 | tf_op jit(solution)/shard_map/ppermute | solution.py:204
  28.6 0.3 collective-permute-done.6
  28.9 3.0 %collective-permute-done.5 = bf16[64,256]{1,0:T(8,128)(2,1)S(1)} collective-permute-done((bf16[64,256]{1,0:T(8,128)(2,1)S(1)}, bf16[64,256]{1,0:T(8,128)(2,1)S(1)}, u32[]{:S(2)}, u32[]{:S(2)}) %collective-permute-start.5) | collective-permute-done | bytes 32800 | tf_op jit(solution)/shard_map/ppermute | solution.py:204
  32.0 1.6 %collective-permute-start.8 = (bf16[128,256]{1,0:T(8,128)(2,1)S(1)}, bf16[128,256]{1,0:T(8,128)(2,1)S(1)}, u32[]{:S(2)}, u32[]{:S(2)}) collective-permute-start(bf16[128,256]{1,0:T(8,128)(2,1)S(1)} %pad_maximum_fusion.1.refs_0_), channel_id=1, source_target_pairs={{4,0},{5,1},{6,2},{7,3},{0,4},{1,5},{2,6},{3,7},{12,8},{13,9},{14,... | collective-permute-start | bytes 196616 | tf_op jit(solution)/shard_map/ppermute | solution.py:204
  33.5 2.0 %shard_map.69 = (bf16[4,2,256,256]{3,2,1,0:T(8,128)(2,1)S(1)}, bf16[4,2,256,256]{3,2,1,0:T(8,128)(2,1)S(1)}) custom-call(s32[5]{0:T(128)S(1)} %copy-done.7, s32[3,8,8]{2,1,0:T(8,128)S(1)} %copy-done.5, bf16[3,1,256,256]{3,2,1,0:T(8,128)(2,1)S(1)} %copy-done, bf16[3,1,256,256]{3,2,1,0:T(8,128)(2,1)S(1)} %copy-done.2, bf16[3,1,256,512]{3,2,1,0:T(8,128)(2,1)S(1)} %copy-done.3, ...), custom_call_target="tpu_custom_call" | custom-call | tf_op jit(solution)/shard_map/pallas_call | solution.py:49
  35.6 0.3 shard_map.70.base
  35.9 0.0 collective-permute-done.7.refs_2_
  35.9 0.4 collective-permute-done.8.refs_1_
  36.3 0.3 shard_map.71
  36.6 0.1 collective-permute-start.9
  36.7 1.2 %collective-permute-done.9 = f32[64,256]{1,0:T(8,128)S(1)} collective-permute-done((f32[64,256]{1,0:T(8,128)S(1)}, f32[64,256]{1,0:T(8,128)S(1)}, u32[]{:S(2)}, u32[]{:S(2)}) %collective-permute-start.9) | collective-permute-done | bytes 65568 | tf_op jit(solution)/shard_map/ppermute | solution.py:204
  37.9 0.6 collective-permute-start.11
  38.6 0.5 collective-permute-start.10
  39.0 1.6 %collective-permute-start.15 = (bf16[2,1,256,512]{3,2,1,0:T(8,128)(2,1)S(1)}, bf16[2,1,256,512]{3,2,1,0:T(8,128)(2,1)S(1)}, u32[]{:S(2)}, u32[]{:S(2)}) collective-permute-start(bf16[2,1,256,512]{3,2,1,0:T(8,128)(2,1)S(1)} %copy-done.8), channel_id=1, source_target_pairs={{2,0},{3,1},{0,2},{1,3},{6,4},{7,5},{4,6},{5,7},{10,8},{11,9},{8,1... | collective-permute-start | bytes 1572872 | tf_op jit(solution)/shard_map/ppermute | solution.py:204
  40.6 2.5 %collective-permute-done.11 = bf16[64,256]{1,0:T(8,128)(2,1)S(1)} collective-permute-done((bf16[64,256]{1,0:T(8,128)(2,1)S(1)}, bf16[64,256]{1,0:T(8,128)(2,1)S(1)}, u32[]{:S(2)}, u32[]{:S(2)}) %collective-permute-start.11) | collective-permute-done | bytes 32800 | tf_op jit(solution)/shard_map/ppermute | solution.py:204
  43.2 1.0 %collective-permute-done.10 = bf16[64,256]{1,0:T(8,128)(2,1)S(1)} collective-permute-done((bf16[64,256]{1,0:T(8,128)(2,1)S(1)}, bf16[64,256]{1,0:T(8,128)(2,1)S(1)}, u32[]{:S(2)}, u32[]{:S(2)}) %collective-permute-start.10) | collective-permute-done | bytes 32800 | tf_op jit(solution)/shard_map/ppermute | solution.py:204
  44.2 1.6 %collective-permute-start.12 = (bf16[128,256]{1,0:T(8,128)(2,1)S(1)}, bf16[128,256]{1,0:T(8,128)(2,1)S(1)}, u32[]{:S(2)}, u32[]{:S(2)}) collective-permute-start(bf16[128,256]{1,0:T(8,128)(2,1)S(1)} %pad_maximum_fusion.2.refs_0_), channel_id=1, source_target_pairs={{4,0},{5,1},{6,2},{7,3},{0,4},{1,5},{2,6},{3,7},{12,8},{13,9},{14,... | collective-permute-start | bytes 196616 | tf_op jit(solution)/shard_map/ppermute | solution.py:204
  45.8 1.6 %shard_map.67.refs_2_ = bf16[4,2,256,256]{3,2,1,0:T(8,128)(2,1)S(1)} custom-call(s32[5]{0:T(128)S(1)} %copy-done.7, s32[3,8,8]{2,1,0:T(8,128)S(1)} %copy-done.5, bf16[3,1,256,256]{3,2,1,0:T(8,128)(2,1)S(1)} %copy-done, bf16[3,1,256,256]{3,2,1,0:T(8,128)(2,1)S(1)} %copy-done.2, bf16[3,1,256,512]{3,2,1,0:T(8,128)(2,1)S(1)} %copy-done.3, ...), custom_call_target="tpu_custom_call" | custom-call | tf_op jit(solution)/shard_map/pallas_call | solution.py:49
  47.4 0.3 shard_map.68.base
  47.7 1.3 %shard_map.72.refs_2_ = bf16[4,2,256,256]{3,2,1,0:T(8,128)(2,1)S(1)} custom-call(s32[5]{0:T(128)S(1)} %copy-done.7, s32[3,8,8]{2,1,0:T(8,128)S(1)} %copy-done.5, bf16[3,1,256,256]{3,2,1,0:T(8,128)(2,1)S(1)} %copy-done, bf16[3,1,256,512]{3,2,1,0:T(8,128)(2,1)S(1)} %copy-done.1, bf16[1,1,256,512]{3,2,1,0:T(8,128)(2,1)S(1)} %collective-permute-done.7.refs_2_), custom_call_target="tpu_custom_call" | custom-call | tf_op jit(solution)/shard_map/pallas_call | solution.py:49
  49.0 0.0 collective-permute-done.12.refs_1_
  49.0 0.3 shard_map.73
  49.3 0.1 collective-permute-start.13
  49.4 1.2 %collective-permute-done.13 = f32[64,256]{1,0:T(8,128)S(1)} collective-permute-done((f32[64,256]{1,0:T(8,128)S(1)}, f32[64,256]{1,0:T(8,128)S(1)}, u32[]{:S(2)}, u32[]{:S(2)}) %collective-permute-start.13) | collective-permute-done | bytes 65568 | tf_op jit(solution)/shard_map/ppermute | solution.py:204
  50.6 2.3 %collective-permute-done.15.refs_2_ = bf16[2,1,256,512]{3,2,1,0:T(8,128)(2,1)S(1)} collective-permute-done((bf16[2,1,256,512]{3,2,1,0:T(8,128)(2,1)S(1)}, bf16[2,1,256,512]{3,2,1,0:T(8,128)(2,1)S(1)}, u32[]{:S(2)}, u32[]{:S(2)}) %collective-permute-start.15) | collective-permute-done | bytes 524320 | tf_op jit(solution)/shard_map/ppermute | solution.py:204
  53.0 1.9 %collective-permute-start.17 = (bf16[64,256]{1,0:T(8,128)(2,1)S(1)}, bf16[64,256]{1,0:T(8,128)(2,1)S(1)}, u32[]{:S(2)}, u32[]{:S(2)}) collective-permute-start(bf16[64,256]{1,0:T(8,128)(2,1)S(1)} %add_convert_fusion.1), channel_id=1, source_target_pairs={{25,0},{24,1},{27,2},{26,3},{29,4},{28,5},{31,6},{30,7},{17,8},{16... | collective-permute-start | bytes 98312 | tf_op jit(solution)/shard_map/ppermute | solution.py:204
  54.9 1.3 %collective-permute-start.16 = (bf16[64,256]{1,0:T(8,128)(2,1)S(1)}, bf16[64,256]{1,0:T(8,128)(2,1)S(1)}, u32[]{:S(2)}, u32[]{:S(2)}) collective-permute-start(bf16[64,256]{1,0:T(8,128)(2,1)S(1)} %add_convert_fusion.1), channel_id=1, source_target_pairs={{16,0},{8,1},{18,2},{10,3},{20,4},{12,5},{22,6},{14,7},{1,8},{25,9... | collective-permute-start | bytes 98312 | tf_op jit(solution)/shard_map/ppermute | solution.py:204
  56.2 1.5 %collective-permute-start.14 = (bf16[128,256]{1,0:T(8,128)(2,1)S(1)}, bf16[128,256]{1,0:T(8,128)(2,1)S(1)}, u32[]{:S(2)}, u32[]{:S(2)}) collective-permute-start(bf16[128,256]{1,0:T(8,128)(2,1)S(1)} %pad_maximum_fusion.3.refs_0_), channel_id=1, source_target_pairs={{2,0},{3,1},{0,2},{1,3},{6,4},{7,5},{4,6},{5,7},{10,8},{11,9},{8,1... | collective-permute-start | bytes 196616 | tf_op jit(solution)/shard_map/ppermute | solution.py:204
  57.7 0.4 collective-permute-done.17
  58.2 1.6 %collective-permute-done.16 = bf16[64,256]{1,0:T(8,128)(2,1)S(1)} collective-permute-done((bf16[64,256]{1,0:T(8,128)(2,1)S(1)}, bf16[64,256]{1,0:T(8,128)(2,1)S(1)}, u32[]{:S(2)}, u32[]{:S(2)}) %collective-permute-start.16) | collective-permute-done | bytes 32800 | tf_op jit(solution)/shard_map/ppermute | solution.py:204
  59.8 1.6 %collective-permute-start.18 = (bf16[128,256]{1,0:T(8,128)(2,1)S(1)}, bf16[128,256]{1,0:T(8,128)(2,1)S(1)}, u32[]{:S(2)}, u32[]{:S(2)}) collective-permute-start(bf16[128,256]{1,0:T(8,128)(2,1)S(1)} %pad_maximum_fusion.4.refs_0_), channel_id=1, source_target_pairs={{4,0},{5,1},{6,2},{7,3},{0,4},{1,5},{2,6},{3,7},{12,8},{13,9},{14,... | collective-permute-start | bytes 196616 | tf_op jit(solution)/shard_map/ppermute | solution.py:204
  61.4 1.3 %shard_map.77.refs_2_ = bf16[4,2,256,256]{3,2,1,0:T(8,128)(2,1)S(1)} custom-call(s32[5]{0:T(128)S(1)} %copy-done.7, s32[3,8,8]{2,1,0:T(8,128)S(1)} %copy-done.5, bf16[3,1,256,256]{3,2,1,0:T(8,128)(2,1)S(1)} %copy-done, bf16[3,1,256,512]{3,2,1,0:T(8,128)(2,1)S(1)} %copy-done.1, bf16[2,1,256,512]{3,2,1,0:T(8,128)(2,1)S(1)} %collective-permute-done.15.refs_2_), custom_call_target="tpu_custom_call" | custom-call | tf_op jit(solution)/shard_map/pallas_call | solution.py:49
  62.6 1.3 %shard_map.75.refs_2_ = bf16[4,2,256,256]{3,2,1,0:T(8,128)(2,1)S(1)} custom-call(s32[5]{0:T(128)S(1)} %copy-done.7, s32[3,8,8]{2,1,0:T(8,128)S(1)} %copy-done.5, bf16[3,1,256,256]{3,2,1,0:T(8,128)(2,1)S(1)} %copy-done, bf16[3,1,256,512]{3,2,1,0:T(8,128)(2,1)S(1)} %copy-done.1, bf16[2,1,256,512]{3,2,1,0:T(8,128)(2,1)S(1)} %collective-permute-done.15.refs_2_), custom_call_target="tpu_custom_call" | custom-call | tf_op jit(solution)/shard_map/pallas_call | solution.py:49
  63.9 0.3 shard_map.76.base
  64.3 0.3 shard_map.78
  64.6 0.1 collective-permute-start.19
  64.6 1.2 %collective-permute-done.19 = f32[64,256]{1,0:T(8,128)S(1)} collective-permute-done((f32[64,256]{1,0:T(8,128)S(1)}, f32[64,256]{1,0:T(8,128)S(1)}, u32[]{:S(2)}, u32[]{:S(2)}) %collective-permute-start.19) | collective-permute-done | bytes 65568 | tf_op jit(solution)/shard_map/ppermute | solution.py:204
  65.9 1.6 %collective-permute-start.20 = (bf16[64,256]{1,0:T(8,128)(2,1)S(1)}, bf16[64,256]{1,0:T(8,128)(2,1)S(1)}, u32[]{:S(2)}, u32[]{:S(2)}) collective-permute-start(bf16[64,256]{1,0:T(8,128)(2,1)S(1)} %add_convert_fusion.refs_0_), channel_id=1, source_target_pairs={{2,0},{3,1},{0,2},{1,3},{6,4},{7,5},{4,6},{5,7},{10,8},{11,9},{8,1... | collective-permute-start | bytes 98312 | tf_op jit(solution)/shard_map/ppermute | solution.py:204
  67.5 1.4 %shard_map.74.whole = bf16[3,1,256,128]{3,2,1,0:T(8,128)(2,1)} custom-call(s32[5]{0:T(128)S(1)} %copy-done.7, bf16[128,256]{1,0:T(8,128)(2,1)S(1)} %pad_maximum_fusion.3.refs_0_, bf16[128,256]{1,0:T(8,128)(2,1)S(1)} %collective-permute-done.14.refs_1_), custom_call_target="tpu_custom_call" | custom-call | tf_op jit(solution)/shard_map/pallas_call | solution.py:49
  68.8 1.1 %collective-permute-done.20.refs_1_ = bf16[64,256]{1,0:T(8,128)(2,1)S(1)} collective-permute-done((bf16[64,256]{1,0:T(8,128)(2,1)S(1)}, bf16[64,256]{1,0:T(8,128)(2,1)S(1)}, u32[]{:S(2)}, u32[]{:S(2)}) %collective-permute-start.20) | collective-permute-done | bytes 32800 | tf_op jit(solution)/shard_map/ppermute | solution.py:204
  69.9 1.3 %shard_map.79 = bf16[3,1,256,128]{3,2,1,0:T(8,128)(2,1)} custom-call(s32[5]{0:T(128)S(1)} %copy-done.7, bf16[3,1,256,128]{3,2,1,0:T(8,128)(2,1)} %shard_map.74.whole, bf16[64,256]{1,0:T(8,128)(2,1)S(1)} %add_convert_fusion.refs_0_, bf16[64,256]{1,0:T(8,128)(2,1)S(1)} %collective-permute-done.20.refs_1_), custom_call_target="tpu_custom_call", output_to_operand_aliasing={{}: (1, {})} | custom-call | tf_op jit(solution)/shard_map/pallas_call | solution.py:49
  (30 shorter events, 0.1 us)
Async XLA Ops:
  0.0 9.8 %copy-start.1 = (bf16[3,1,256,512]{3,2,1,0:T(8,128)(2,1)S(1)}, bf16[3,1,256,512]{3,2,1,0:T(8,128)(2,1)}, u32[]{:S(2)}) copy-start(bf16[3,1,256,512]{3,2,1,0:T(8,128)(2,1)} %refs_1_.9) | copy-start | bytes 2359300
  0.0 20.7 %collective-permute-start.3 = (bf16[3,1,256,512]{3,2,1,0:T(8,128)(2,1)}, bf16[3,1,256,512]{3,2,1,0:T(8,128)(2,1)S(1)}, u32[]{:S(2)}, u32[]{:S(2)}) collective-permute-start(bf16[3,1,256,512]{3,2,1,0:T(8,128)(2,1)} %refs_2_.3), channel_id=1, source_target_pairs={{2,0},{3,1},{0,2},{1,3},{6,4},{7,5},{4,6},{5,7},{10,8},{11,9},{8,1... | collective-permute-start | bytes 2359304 | tf_op jit(solution)/shard_map/ppermute | solution.py:204
  5.3 7.2 %collective-permute-start.1 = (bf16[64,256]{1,0:T(8,128)(2,1)}, bf16[64,256]{1,0:T(8,128)(2,1)S(1)}, u32[]{:S(2)}, u32[]{:S(2)}) collective-permute-start(bf16[64,256]{1,0:T(8,128)(2,1)} %shard_map.64.first), channel_id=1, source_target_pairs={{25,0},{24,1},{27,2},{26,3},{29,4},{28,5},{31,6},{30,7},{17,8},{16... | collective-permute-start | bytes 98312 | tf_op jit(solution)/shard_map/ppermute | solution.py:204
  8.1 5.0 %collective-permute-start = (bf16[64,256]{1,0:T(8,128)(2,1)}, bf16[64,256]{1,0:T(8,128)(2,1)S(1)}, u32[]{:S(2)}, u32[]{:S(2)}) collective-permute-start(bf16[64,256]{1,0:T(8,128)(2,1)} %shard_map.64.first), channel_id=1, source_target_pairs={{16,0},{8,1},{18,2},{10,3},{20,4},{12,5},{22,6},{14,7},{1,8},{25,9... | collective-permute-start | bytes 98312 | tf_op jit(solution)/shard_map/ppermute | solution.py:204
  9.8 1.1 %copy-start = (bf16[3,1,256,256]{3,2,1,0:T(8,128)(2,1)S(1)}, bf16[3,1,256,256]{3,2,1,0:T(8,128)(2,1)}, u32[]{:S(2)}) copy-start(bf16[3,1,256,256]{3,2,1,0:T(8,128)(2,1)} %refs_0_.11) | copy-start | bytes 1179652
  9.8 1.3 %copy-start.2 = (bf16[3,1,256,256]{3,2,1,0:T(8,128)(2,1)S(1)}, bf16[3,1,256,256]{3,2,1,0:T(8,128)(2,1)}, u32[]{:S(2)}) copy-start(bf16[3,1,256,256]{3,2,1,0:T(8,128)(2,1)} %refs_1_.6) | copy-start | bytes 1179652
  9.8 1.3 %copy-start.4 = (bf16[3,1,256,128]{3,2,1,0:T(8,128)(2,1)S(1)}, bf16[3,1,256,128]{3,2,1,0:T(8,128)(2,1)}, u32[]{:S(2)}) copy-start(bf16[3,1,256,128]{3,2,1,0:T(8,128)(2,1)} %rhs.3) | copy-start | bytes 589828
  9.8 1.3 %copy-start.6 = (bf16[64,256]{1,0:T(8,128)(2,1)S(1)}, bf16[64,256]{1,0:T(8,128)(2,1)}, u32[]{:S(2)}) copy-start(bf16[64,256]{1,0:T(8,128)(2,1)} %shard_map.64.first) | copy-start | bytes 98308
  9.8 1.3 %copy-start.7 = (s32[5]{0:T(128)S(1)}, s32[5]{0:T(128)}, u32[]{:S(2)}) copy-start(s32[5]{0:T(128)} %stack.23.spot) | copy-start | bytes 64
  10.6 10.1 %copy-start.3 = (bf16[3,1,256,512]{3,2,1,0:T(8,128)(2,1)S(1)}, bf16[3,1,256,512]{3,2,1,0:T(8,128)(2,1)}, u32[]{:S(2)}) copy-start(bf16[3,1,256,512]{3,2,1,0:T(8,128)(2,1)} %refs_2_.3) | copy-start | bytes 2359300
  13.1 7.6 %copy-start.5 = (s32[3,8,8]{2,1,0:T(8,128)S(1)}, s32[3,8,8]{2,1,0:T(8,128)}, u32[]{:S(2)}) copy-start(s32[3,8,8]{2,1,0:T(8,128)} %pattern.11) | copy-start | bytes 2308
  13.2 14.0 %copy-start.9 = (bf16[1,1,256,512]{3,2,1,0:T(8,128)(2,1)S(1)}, bf16[1,1,256,512]{3,2,1,0:T(8,128)(2,1)}, u32[]{:S(2)}) copy-start(bf16[1,1,256,512]{3,2,1,0:T(8,128)(2,1)} %slice.6) | copy-start | bytes 786436
  13.2 4.4 %collective-permute-start.2 = (bf16[128,256]{1,0:T(8,128)(2,1)S(1)}, bf16[128,256]{1,0:T(8,128)(2,1)S(1)}, u32[]{:S(2)}, u32[]{:S(2)}) collective-permute-start(bf16[128,256]{1,0:T(8,128)(2,1)S(1)} %pad_maximum_fusion.refs_2_.refs_0_), channel_id=1, source_target_pairs={{4,0},{5,1},{6,2},{7,3},{0,4},{1,5},{2,6},{3,7},{12,8},{13,9},{14,... | collective-permute-start | bytes 196616 | tf_op jit(solution)/shard_map/ppermute | solution.py:204
  22.1 1.3 %collective-permute-start.4 = (f32[64,256]{1,0:T(8,128)S(1)}, f32[64,256]{1,0:T(8,128)S(1)}, u32[]{:S(2)}, u32[]{:S(2)}) collective-permute-start(f32[64,256]{1,0:T(8,128)S(1)} %shard_map.66), channel_id=1, source_target_pairs={{1,0},{0,1},{3,2},{2,3},{5,4},{4,5},{7,6},{6,7},{9,8},{8,9},{11,10... | collective-permute-start | bytes 196616 | tf_op jit(solution)/shard_map/ppermute | solution.py:204
  23.4 5.5 %collective-permute-start.6 = (bf16[64,256]{1,0:T(8,128)(2,1)S(1)}, bf16[64,256]{1,0:T(8,128)(2,1)S(1)}, u32[]{:S(2)}, u32[]{:S(2)}) collective-permute-start(bf16[64,256]{1,0:T(8,128)(2,1)S(1)} %add_convert_fusion.3), channel_id=1, source_target_pairs={{25,0},{24,1},{27,2},{26,3},{29,4},{28,5},{31,6},{30,7},{17,8},{16... | collective-permute-start | bytes 98312 | tf_op jit(solution)/shard_map/ppermute | solution.py:204
  27.1 4.8 %collective-permute-start.5 = (bf16[64,256]{1,0:T(8,128)(2,1)S(1)}, bf16[64,256]{1,0:T(8,128)(2,1)S(1)}, u32[]{:S(2)}, u32[]{:S(2)}) collective-permute-start(bf16[64,256]{1,0:T(8,128)(2,1)S(1)} %add_convert_fusion.3), channel_id=1, source_target_pairs={{16,0},{8,1},{18,2},{10,3},{20,4},{12,5},{22,6},{14,7},{1,8},{25,9... | collective-permute-start | bytes 98312 | tf_op jit(solution)/shard_map/ppermute | solution.py:204
  27.1 8.7 %collective-permute-start.7 = (bf16[1,1,256,512]{3,2,1,0:T(8,128)(2,1)S(1)}, bf16[1,1,256,512]{3,2,1,0:T(8,128)(2,1)S(1)}, u32[]{:S(2)}, u32[]{:S(2)}) collective-permute-start(bf16[1,1,256,512]{3,2,1,0:T(8,128)(2,1)S(1)} %copy-done.9), channel_id=1, source_target_pairs={{2,0},{3,1},{0,2},{1,3},{6,4},{7,5},{4,6},{5,7},{10,8},{11,9},{8,1... | collective-permute-start | bytes 786440 | tf_op jit(solution)/shard_map/ppermute | solution.py:204
  32.0 4.3 %collective-permute-start.8 = (bf16[128,256]{1,0:T(8,128)(2,1)S(1)}, bf16[128,256]{1,0:T(8,128)(2,1)S(1)}, u32[]{:S(2)}, u32[]{:S(2)}) collective-permute-start(bf16[128,256]{1,0:T(8,128)(2,1)S(1)} %pad_maximum_fusion.1.refs_0_), channel_id=1, source_target_pairs={{4,0},{5,1},{6,2},{7,3},{0,4},{1,5},{2,6},{3,7},{12,8},{13,9},{14,... | collective-permute-start | bytes 196616 | tf_op jit(solution)/shard_map/ppermute | solution.py:204
  36.3 2.7 %copy-start.8 = (bf16[2,1,256,512]{3,2,1,0:T(8,128)(2,1)S(1)}, bf16[2,1,256,512]{3,2,1,0:T(8,128)(2,1)}, u32[]{:S(2)}) copy-start(bf16[2,1,256,512]{3,2,1,0:T(8,128)(2,1)} %slice.7) | copy-start | bytes 1572868
  36.6 1.3 %collective-permute-start.9 = (f32[64,256]{1,0:T(8,128)S(1)}, f32[64,256]{1,0:T(8,128)S(1)}, u32[]{:S(2)}, u32[]{:S(2)}) collective-permute-start(f32[64,256]{1,0:T(8,128)S(1)} %shard_map.71), channel_id=1, source_target_pairs={{1,0},{0,1},{3,2},{2,3},{5,4},{4,5},{7,6},{6,7},{9,8},{8,9},{11,10... | collective-permute-start | bytes 196616 | tf_op jit(solution)/shard_map/ppermute | solution.py:204
  37.9 5.2 %collective-permute-start.11 = (bf16[64,256]{1,0:T(8,128)(2,1)S(1)}, bf16[64,256]{1,0:T(8,128)(2,1)S(1)}, u32[]{:S(2)}, u32[]{:S(2)}) collective-permute-start(bf16[64,256]{1,0:T(8,128)(2,1)S(1)} %add_convert_fusion.2), channel_id=1, source_target_pairs={{25,0},{24,1},{27,2},{26,3},{29,4},{28,5},{31,6},{30,7},{17,8},{16... | collective-permute-start | bytes 98312 | tf_op jit(solution)/shard_map/ppermute | solution.py:204
  38.6 5.6 %collective-permute-start.10 = (bf16[64,256]{1,0:T(8,128)(2,1)S(1)}, bf16[64,256]{1,0:T(8,128)(2,1)S(1)}, u32[]{:S(2)}, u32[]{:S(2)}) collective-permute-start(bf16[64,256]{1,0:T(8,128)(2,1)S(1)} %add_convert_fusion.2), channel_id=1, source_target_pairs={{16,0},{8,1},{18,2},{10,3},{20,4},{12,5},{22,6},{14,7},{1,8},{25,9... | collective-permute-start | bytes 98312 | tf_op jit(solution)/shard_map/ppermute | solution.py:204
  39.0 14.0 %collective-permute-start.15 = (bf16[2,1,256,512]{3,2,1,0:T(8,128)(2,1)S(1)}, bf16[2,1,256,512]{3,2,1,0:T(8,128)(2,1)S(1)}, u32[]{:S(2)}, u32[]{:S(2)}) collective-permute-start(bf16[2,1,256,512]{3,2,1,0:T(8,128)(2,1)S(1)} %copy-done.8), channel_id=1, source_target_pairs={{2,0},{3,1},{0,2},{1,3},{6,4},{7,5},{4,6},{5,7},{10,8},{11,9},{8,1... | collective-permute-start | bytes 1572872 | tf_op jit(solution)/shard_map/ppermute | solution.py:204
  44.2 4.8 %collective-permute-start.12 = (bf16[128,256]{1,0:T(8,128)(2,1)S(1)}, bf16[128,256]{1,0:T(8,128)(2,1)S(1)}, u32[]{:S(2)}, u32[]{:S(2)}) collective-permute-start(bf16[128,256]{1,0:T(8,128)(2,1)S(1)} %pad_maximum_fusion.2.refs_0_), channel_id=1, source_target_pairs={{4,0},{5,1},{6,2},{7,3},{0,4},{1,5},{2,6},{3,7},{12,8},{13,9},{14,... | collective-permute-start | bytes 196616 | tf_op jit(solution)/shard_map/ppermute | solution.py:204
  49.3 1.3 %collective-permute-start.13 = (f32[64,256]{1,0:T(8,128)S(1)}, f32[64,256]{1,0:T(8,128)S(1)}, u32[]{:S(2)}, u32[]{:S(2)}) collective-permute-start(f32[64,256]{1,0:T(8,128)S(1)} %shard_map.73), channel_id=1, source_target_pairs={{1,0},{0,1},{3,2},{2,3},{5,4},{4,5},{7,6},{6,7},{9,8},{8,9},{11,10... | collective-permute-start | bytes 196616 | tf_op jit(solution)/shard_map/ppermute | solution.py:204
  53.0 5.2 %collective-permute-start.17 = (bf16[64,256]{1,0:T(8,128)(2,1)S(1)}, bf16[64,256]{1,0:T(8,128)(2,1)S(1)}, u32[]{:S(2)}, u32[]{:S(2)}) collective-permute-start(bf16[64,256]{1,0:T(8,128)(2,1)S(1)} %add_convert_fusion.1), channel_id=1, source_target_pairs={{25,0},{24,1},{27,2},{26,3},{29,4},{28,5},{31,6},{30,7},{17,8},{16... | collective-permute-start | bytes 98312 | tf_op jit(solution)/shard_map/ppermute | solution.py:204
  54.9 4.8 %collective-permute-start.16 = (bf16[64,256]{1,0:T(8,128)(2,1)S(1)}, bf16[64,256]{1,0:T(8,128)(2,1)S(1)}, u32[]{:S(2)}, u32[]{:S(2)}) collective-permute-start(bf16[64,256]{1,0:T(8,128)(2,1)S(1)} %add_convert_fusion.1), channel_id=1, source_target_pairs={{16,0},{8,1},{18,2},{10,3},{20,4},{12,5},{22,6},{14,7},{1,8},{25,9... | collective-permute-start | bytes 98312 | tf_op jit(solution)/shard_map/ppermute | solution.py:204
  56.2 7.7 %collective-permute-start.14 = (bf16[128,256]{1,0:T(8,128)(2,1)S(1)}, bf16[128,256]{1,0:T(8,128)(2,1)S(1)}, u32[]{:S(2)}, u32[]{:S(2)}) collective-permute-start(bf16[128,256]{1,0:T(8,128)(2,1)S(1)} %pad_maximum_fusion.3.refs_0_), channel_id=1, source_target_pairs={{2,0},{3,1},{0,2},{1,3},{6,4},{7,5},{4,6},{5,7},{10,8},{11,9},{8,1... | collective-permute-start | bytes 196616 | tf_op jit(solution)/shard_map/ppermute | solution.py:204
  59.8 4.5 %collective-permute-start.18 = (bf16[128,256]{1,0:T(8,128)(2,1)S(1)}, bf16[128,256]{1,0:T(8,128)(2,1)S(1)}, u32[]{:S(2)}, u32[]{:S(2)}) collective-permute-start(bf16[128,256]{1,0:T(8,128)(2,1)S(1)} %pad_maximum_fusion.4.refs_0_), channel_id=1, source_target_pairs={{4,0},{5,1},{6,2},{7,3},{0,4},{1,5},{2,6},{3,7},{12,8},{13,9},{14,... | collective-permute-start | bytes 196616 | tf_op jit(solution)/shard_map/ppermute | solution.py:204
  64.6 1.3 %collective-permute-start.19 = (f32[64,256]{1,0:T(8,128)S(1)}, f32[64,256]{1,0:T(8,128)S(1)}, u32[]{:S(2)}, u32[]{:S(2)}) collective-permute-start(f32[64,256]{1,0:T(8,128)S(1)} %shard_map.78), channel_id=1, source_target_pairs={{1,0},{0,1},{3,2},{2,3},{5,4},{4,5},{7,6},{6,7},{9,8},{8,9},{11,10... | collective-permute-start | bytes 196616 | tf_op jit(solution)/shard_map/ppermute | solution.py:204
  65.9 4.0 %collective-permute-start.20 = (bf16[64,256]{1,0:T(8,128)(2,1)S(1)}, bf16[64,256]{1,0:T(8,128)(2,1)S(1)}, u32[]{:S(2)}, u32[]{:S(2)}) collective-permute-start(bf16[64,256]{1,0:T(8,128)(2,1)S(1)} %add_convert_fusion.refs_0_), channel_id=1, source_target_pairs={{2,0},{3,1},{0,2},{1,3},{6,4},{7,5},{4,6},{5,7},{10,8},{11,9},{8,1... | collective-permute-start | bytes 98312 | tf_op jit(solution)/shard_map/ppermute | solution.py:204

commit v8 on v7

--- a/solution.py
+++ b/solution.py
@@ -347,11 +347,11 @@
                 value = step(value, [(fetched[earlier], backward[pair_index(level, earlier)])])
             for later in reversed(range(level + 1, levels)):
                 value = step(value, [(back[later], upward[later, level])])
+            if level == 1:
+                value = after(value, *high_rest)
             solved[level] = settle(value)
             if level > 0:
                 found = solved[level]
-                if level == 1:
-                    found = after(found, *high_rest)
                 stack = deep(found)
                 back[level] = wide(stack)
                 for later in range(level, levels):

time: 71.3 us -> 70.2 us (0.985)
  starting transfers between devices: 26.5 us -> 24 us
    ppermute x21, starting transfers between devices: 26.5 us -> 24 us  [send(): return lax.ppermute(value, ('prow', 'pcol'), pairs)]
  transfers between devices with their start and end apart: 21 -> 21, of which waited for: 16 -> 15; matrix products, arithmetic and copies ran while one was open for 4% -> 4% of each run, Pallas kernels for 19% -> 19%
where the time goes in v8:
time: 70.2 us; the launch traced here: 69.9 us
  waiting for transfers between devices  24.8 us (35%)
  starting transfers between devices  24 us (34%)
  Pallas kernels  16.5 us (24%)
  local copies, waits for them, and re-layouts  4.24 us (6%)
    ppermute x21, waiting for transfers between devices, send(): return lax.ppermute(value, ('prow', 'pcol'), pairs)  24.8 us
    ppermute x21, starting transfers between devices, send(): return lax.ppermute(value, ('prow', 'pcol'), pairs)  24 us
    pallas_call x16, Pallas kernels, call(): pl.pallas_call(kernel, grid=(1,), out_shape=shapes, in_specs=specs, out_s...  16.5 us
    slice x2, local copies, waits for them, and re-layouts, body(): parts = (upper_blocks[last_pair:], upper_blocks[:last_pair])  2.49 us
  transfers between devices with their start and end apart: 21, of which 15 were waited for; matrix products, arithmetic and copies ran while one was open for 4% of the time, Pallas kernels for 19%

profile of v8, /device:TPU:0, one launch (start us, length us, event | category | flops | bytes accessed | tf_op | source)
XLA Modules:
  0.0 69.9 jit_solution(18307460818632085359)
XLA Ops:
  0.0 2.9 %collective-permute-start.3 = (bf16[3,1,256,512]{3,2,1,0:T(8,128)(2,1)}, bf16[3,1,256,512]{3,2,1,0:T(8,128)(2,1)S(1)}, u32[]{:S(2)}, u32[]{:S(2)}) collective-permute-start(bf16[3,1,256,512]{3,2,1,0:T(8,128)(2,1)} %refs_2_.3), channel_id=1, source_target_pairs={{2,0},{3,1},{0,2},{1,3},{6,4},{7,5},{4,6},{5,7},{10,8},{11,9},{8,1... | collective-permute-start | bytes 2359304 | tf_op jit(solution)/shard_map/ppermute | solution.py:204
  2.9 0.6 stack.23.spot
  3.5 1.8 %shard_map.64.first = bf16[64,256]{1,0:T(8,128)(2,1)} custom-call(s32[5]{0:T(128)} %stack.23.spot, bf16[3,1,256,128]{3,2,1,0:T(8,128)(2,1)} %rhs.3, bf16[3,1,256,256]{3,2,1,0:T(8,128)(2,1)} %refs_1_.6), custom_call_target="tpu_custom_call" | custom-call | tf_op jit(solution)/shard_map/pallas_call | solution.py:49
  5.3 2.8 %collective-permute-start.1 = (bf16[64,256]{1,0:T(8,128)(2,1)}, bf16[64,256]{1,0:T(8,128)(2,1)S(1)}, u32[]{:S(2)}, u32[]{:S(2)}) collective-permute-start(bf16[64,256]{1,0:T(8,128)(2,1)} %shard_map.64.first), channel_id=1, source_target_pairs={{25,0},{24,1},{27,2},{26,3},{29,4},{28,5},{31,6},{30,7},{17,8},{16... | collective-permute-start | bytes 98312 | tf_op jit(solution)/shard_map/ppermute | solution.py:204
  8.1 0.0 collective-permute-start
  8.1 1.7 %slice.6 = bf16[1,1,256,512]{3,2,1,0:T(8,128)(2,1)} slice(bf16[3,1,256,512]{3,2,1,0:T(8,128)(2,1)} %refs_1_.9), slice={[2:3], [0:1], [0:256], [0:512]} | slice | bytes 524288 | tf_op jit(solution)/shard_map/slice | solution.py:291
  9.8 0.0 copy-start.6
  9.8 0.8 %slice.7 = bf16[2,1,256,512]{3,2,1,0:T(8,128)(2,1)} slice(bf16[3,1,256,512]{3,2,1,0:T(8,128)(2,1)S(1)} %copy-done.1), slice={[0:2], [0:1], [0:256], [0:512]} | slice | bytes 1048576 | tf_op jit(solution)/shard_map/slice | solution.py:291
  10.6 0.2 copy-done
  10.8 0.2 copy-done.2
  11.1 0.0 copy-done.4
  11.1 1.4 %shard_map.65 = (f32[64,256]{1,0:T(8,128)S(1)}, f32[64,256]{1,0:T(8,128)S(1)}, f32[64,256]{1,0:T(8,128)S(1)}, f32[64,256]{1,0:T(8,128)S(1)}) custom-call(s32[5]{0:T(128)S(1)} %copy-done.7, bf16[64,256]{1,0:T(8,128)(2,1)S(1)} %copy-done.6, bf16[3,1,256,128]{3,2,1,0:T(8,128)(2,1)S(1)} %copy-done.4, bf16[3,1,256,256]{3,2,1,0:T(8,128)(2,1)S(1)} %copy-done.2, ...), custom_call_target="tpu_custom_call" | custom-call | tf_op jit(solution)/shard_map/pallas_call | solution.py:49
  12.5 0.0 collective-permute-done.1
  12.5 0.6 collective-permute-done
  13.1 0.0 copy-start.5
  13.2 1.6 %collective-permute-start.2 = (bf16[128,256]{1,0:T(8,128)(2,1)S(1)}, bf16[128,256]{1,0:T(8,128)(2,1)S(1)}, u32[]{:S(2)}, u32[]{:S(2)}) collective-permute-start(bf16[128,256]{1,0:T(8,128)(2,1)S(1)} %pad_maximum_fusion.refs_2_.refs_0_), channel_id=1, source_target_pairs={{4,0},{5,1},{6,2},{7,3},{0,4},{1,5},{2,6},{3,7},{12,8},{13,9},{14,... | collective-permute-start | bytes 196616 | tf_op jit(solution)/shard_map/ppermute | solution.py:204
  14.8 2.8 %collective-permute-done.2.refs_3_.refs_1_ = bf16[128,256]{1,0:T(8,128)(2,1)S(1)} collective-permute-done((bf16[128,256]{1,0:T(8,128)(2,1)S(1)}, bf16[128,256]{1,0:T(8,128)(2,1)S(1)}, u32[]{:S(2)}, u32[]{:S(2)}) %collective-permute-start.2) | collective-permute-done | bytes 65568 | tf_op jit(solution)/shard_map/ppermute | solution.py:204
  17.6 3.1 %collective-permute-done.3.refs_1_.refs_3_ = bf16[3,1,256,512]{3,2,1,0:T(8,128)(2,1)S(1)} collective-permute-done((bf16[3,1,256,512]{3,2,1,0:T(8,128)(2,1)}, bf16[3,1,256,512]{3,2,1,0:T(8,128)(2,1)S(1)}, u32[]{:S(2)}, u32[]{:S(2)}) %collective-permute-start.3) | collective-permute-done | bytes 786464 | tf_op jit(solution)/shard_map/ppermute | solution.py:204
  20.7 1.4 %shard_map.66 = f32[64,256]{1,0:T(8,128)S(1)} custom-call(s32[5]{0:T(128)S(1)} %copy-done.7, s32[3,8,8]{2,1,0:T(8,128)S(1)} %copy-done.5, f32[64,256]{1,0:T(8,128)S(1)} %get-tuple-element.24.base, bf16[3,1,256,256]{3,2,1,0:T(8,128)(2,1)S(1)} %copy-done.2, bf16[3,1,256,512]{3,2,1,0:T(8,128)(2,1)S(1)} %copy-done.3, ...), custom_call_target="tpu_custom_call" | custom-call | tf_op jit(solution)/shard_map/pallas_call | solution.py:49
  22.1 0.1 collective-permute-start.4
  22.2 1.2 %collective-permute-done.4 = f32[64,256]{1,0:T(8,128)S(1)} collective-permute-done((f32[64,256]{1,0:T(8,128)S(1)}, f32[64,256]{1,0:T(8,128)S(1)}, u32[]{:S(2)}, u32[]{:S(2)}) %collective-permute-start.4) | collective-permute-done | bytes 65568 | tf_op jit(solution)/shard_map/ppermute | solution.py:204
  23.4 3.7 %collective-permute-start.6 = (bf16[64,256]{1,0:T(8,128)(2,1)S(1)}, bf16[64,256]{1,0:T(8,128)(2,1)S(1)}, u32[]{:S(2)}, u32[]{:S(2)}) collective-permute-start(bf16[64,256]{1,0:T(8,128)(2,1)S(1)} %add_convert_fusion.3), channel_id=1, source_target_pairs={{25,0},{24,1},{27,2},{26,3},{29,4},{28,5},{31,6},{30,7},{17,8},{16... | collective-permute-start | bytes 98312 | tf_op jit(solution)/shard_map/ppermute | solution.py:204
  27.1 0.0 collective-permute-start.5
  27.1 1.5 %collective-permute-start.7 = (bf16[1,1,256,512]{3,2,1,0:T(8,128)(2,1)S(1)}, bf16[1,1,256,512]{3,2,1,0:T(8,128)(2,1)S(1)}, u32[]{:S(2)}, u32[]{:S(2)}) collective-permute-start(bf16[1,1,256,512]{3,2,1,0:T(8,128)(2,1)S(1)} %copy-done.9), channel_id=1, source_target_pairs={{2,0},{3,1},{0,2},{1,3},{6,4},{7,5},{4,6},{5,7},{10,8},{11,9},{8,1... | collective-permute-start | bytes 786440 | tf_op jit(solution)/shard_map/ppermute | solution.py:204
  28.6 0.3 collective-permute-done.6
  28.9 3.0 %collective-permute-done.5 = bf16[64,256]{1,0:T(8,128)(2,1)S(1)} collective-permute-done((bf16[64,256]{1,0:T(8,128)(2,1)S(1)}, bf16[64,256]{1,0:T(8,128)(2,1)S(1)}, u32[]{:S(2)}, u32[]{:S(2)}) %collective-permute-start.5) | collective-permute-done | bytes 32800 | tf_op jit(solution)/shard_map/ppermute | solution.py:204
  32.0 1.6 %collective-permute-start.8 = (bf16[128,256]{1,0:T(8,128)(2,1)S(1)}, bf16[128,256]{1,0:T(8,128)(2,1)S(1)}, u32[]{:S(2)}, u32[]{:S(2)}) collective-permute-start(bf16[128,256]{1,0:T(8,128)(2,1)S(1)} %pad_maximum_fusion.1.refs_0_), channel_id=1, source_target_pairs={{4,0},{5,1},{6,2},{7,3},{0,4},{1,5},{2,6},{3,7},{12,8},{13,9},{14,... | collective-permute-start | bytes 196616 | tf_op jit(solution)/shard_map/ppermute | solution.py:204
  33.5 2.0 %shard_map.69 = (bf16[4,2,256,256]{3,2,1,0:T(8,128)(2,1)S(1)}, bf16[4,2,256,256]{3,2,1,0:T(8,128)(2,1)S(1)}) custom-call(s32[5]{0:T(128)S(1)} %copy-done.7, s32[3,8,8]{2,1,0:T(8,128)S(1)} %copy-done.5, bf16[3,1,256,256]{3,2,1,0:T(8,128)(2,1)S(1)} %copy-done, bf16[3,1,256,256]{3,2,1,0:T(8,128)(2,1)S(1)} %copy-done.2, bf16[3,1,256,512]{3,2,1,0:T(8,128)(2,1)S(1)} %copy-done.3, ...), custom_call_target="tpu_custom_call" | custom-call | tf_op jit(solution)/shard_map/pallas_call | solution.py:49
  35.6 0.3 shard_map.70.base
  35.9 0.0 collective-permute-done.7.refs_2_
  35.9 0.4 collective-permute-done.8.refs_1_
  36.3 0.3 shard_map.71
  36.6 0.1 collective-permute-start.9
  36.7 0.7 copy-done.8
  37.3 1.5 %collective-permute-start.13 = (bf16[2,1,256,512]{3,2,1,0:T(8,128)(2,1)S(1)}, bf16[2,1,256,512]{3,2,1,0:T(8,128)(2,1)S(1)}, u32[]{:S(2)}, u32[]{:S(2)}) collective-permute-start(bf16[2,1,256,512]{3,2,1,0:T(8,128)(2,1)S(1)} %copy-done.8), channel_id=1, source_target_pairs={{2,0},{3,1},{0,2},{1,3},{6,4},{7,5},{4,6},{5,7},{10,8},{11,9},{8,1... | collective-permute-start | bytes 1572872 | tf_op jit(solution)/shard_map/ppermute | solution.py:204
  38.8 0.0 collective-permute-done.9
  38.8 0.3 collective-permute-start.11
  39.2 0.5 collective-permute-start.10
  39.7 4.7 %collective-permute-done.11 = bf16[64,256]{1,0:T(8,128)(2,1)S(1)} collective-permute-done((bf16[64,256]{1,0:T(8,128)(2,1)S(1)}, bf16[64,256]{1,0:T(8,128)(2,1)S(1)}, u32[]{:S(2)}, u32[]{:S(2)}) %collective-permute-start.11) | collective-permute-done | bytes 32800 | tf_op jit(solution)/shard_map/ppermute | solution.py:204
  44.4 0.2 collective-permute-done.10
  44.6 1.6 %collective-permute-start.12 = (bf16[128,256]{1,0:T(8,128)(2,1)S(1)}, bf16[128,256]{1,0:T(8,128)(2,1)S(1)}, u32[]{:S(2)}, u32[]{:S(2)}) collective-permute-start(bf16[128,256]{1,0:T(8,128)(2,1)S(1)} %pad_maximum_fusion.2.refs_0_), channel_id=1, source_target_pairs={{4,0},{5,1},{6,2},{7,3},{0,4},{1,5},{2,6},{3,7},{12,8},{13,9},{14,... | collective-permute-start | bytes 196616 | tf_op jit(solution)/shard_map/ppermute | solution.py:204
  46.2 1.6 %shard_map.67.refs_2_ = bf16[4,2,256,256]{3,2,1,0:T(8,128)(2,1)S(1)} custom-call(s32[5]{0:T(128)S(1)} %copy-done.7, s32[3,8,8]{2,1,0:T(8,128)S(1)} %copy-done.5, bf16[3,1,256,256]{3,2,1,0:T(8,128)(2,1)S(1)} %copy-done, bf16[3,1,256,256]{3,2,1,0:T(8,128)(2,1)S(1)} %copy-done.2, bf16[3,1,256,512]{3,2,1,0:T(8,128)(2,1)S(1)} %copy-done.3, ...), custom_call_target="tpu_custom_call" | custom-call | tf_op jit(solution)/shard_map/pallas_call | solution.py:49
  47.8 0.3 shard_map.68.base
  48.1 1.3 %shard_map.72.refs_2_ = bf16[4,2,256,256]{3,2,1,0:T(8,128)(2,1)S(1)} custom-call(s32[5]{0:T(128)S(1)} %copy-done.7, s32[3,8,8]{2,1,0:T(8,128)S(1)} %copy-done.5, bf16[3,1,256,256]{3,2,1,0:T(8,128)(2,1)S(1)} %copy-done, bf16[3,1,256,512]{3,2,1,0:T(8,128)(2,1)S(1)} %copy-done.1, bf16[1,1,256,512]{3,2,1,0:T(8,128)(2,1)S(1)} %collective-permute-done.7.refs_2_), custom_call_target="tpu_custom_call" | custom-call | tf_op jit(solution)/shard_map/pallas_call | solution.py:49
  49.4 0.0 collective-permute-done.12.refs_1_
  49.4 0.3 shard_map.73
  49.7 1.3 %collective-permute-done.13.refs_2_ = bf16[2,1,256,512]{3,2,1,0:T(8,128)(2,1)S(1)} collective-permute-done((bf16[2,1,256,512]{3,2,1,0:T(8,128)(2,1)S(1)}, bf16[2,1,256,512]{3,2,1,0:T(8,128)(2,1)S(1)}, u32[]{:S(2)}, u32[]{:S(2)}) %collective-permute-start.13) | collective-permute-done | bytes 524320 | tf_op jit(solution)/shard_map/ppermute | solution.py:204
  51.0 1.3 %collective-permute-done.14 = f32[64,256]{1,0:T(8,128)S(1)} collective-permute-done((f32[64,256]{1,0:T(8,128)S(1)}, f32[64,256]{1,0:T(8,128)S(1)}, u32[]{:S(2)}, u32[]{:S(2)}) %collective-permute-start.14) | collective-permute-done | bytes 65568 | tf_op jit(solution)/shard_map/ppermute | solution.py:204
  52.3 0.9 %collective-permute-start.17 = (bf16[64,256]{1,0:T(8,128)(2,1)S(1)}, bf16[64,256]{1,0:T(8,128)(2,1)S(1)}, u32[]{:S(2)}, u32[]{:S(2)}) collective-permute-start(bf16[64,256]{1,0:T(8,128)(2,1)S(1)} %add_convert_fusion.1), channel_id=1, source_target_pairs={{25,0},{24,1},{27,2},{26,3},{29,4},{28,5},{31,6},{30,7},{17,8},{16... | collective-permute-start | bytes 98312 | tf_op jit(solution)/shard_map/ppermute | solution.py:204
  53.2 0.2 collective-permute-start.16
  53.4 1.6 %collective-permute-start.15 = (bf16[128,256]{1,0:T(8,128)(2,1)S(1)}, bf16[128,256]{1,0:T(8,128)(2,1)S(1)}, u32[]{:S(2)}, u32[]{:S(2)}) collective-permute-start(bf16[128,256]{1,0:T(8,128)(2,1)S(1)} %pad_maximum_fusion.3.refs_0_), channel_id=1, source_target_pairs={{2,0},{3,1},{0,2},{1,3},{6,4},{7,5},{4,6},{5,7},{10,8},{11,9},{8,1... | collective-permute-start | bytes 196616 | tf_op jit(solution)/shard_map/ppermute | solution.py:204
  55.0 2.5 %collective-permute-done.17 = bf16[64,256]{1,0:T(8,128)(2,1)S(1)} collective-permute-done((bf16[64,256]{1,0:T(8,128)(2,1)S(1)}, bf16[64,256]{1,0:T(8,128)(2,1)S(1)}, u32[]{:S(2)}, u32[]{:S(2)}) %collective-permute-start.17) | collective-permute-done | bytes 32800 | tf_op jit(solution)/shard_map/ppermute | solution.py:204
  57.5 1.0 %collective-permute-done.16 = bf16[64,256]{1,0:T(8,128)(2,1)S(1)} collective-permute-done((bf16[64,256]{1,0:T(8,128)(2,1)S(1)}, bf16[64,256]{1,0:T(8,128)(2,1)S(1)}, u32[]{:S(2)}, u32[]{:S(2)}) %collective-permute-start.16) | collective-permute-done | bytes 32800 | tf_op jit(solution)/shard_map/ppermute | solution.py:204
  58.6 1.6 %collective-permute-start.18 = (bf16[128,256]{1,0:T(8,128)(2,1)S(1)}, bf16[128,256]{1,0:T(8,128)(2,1)S(1)}, u32[]{:S(2)}, u32[]{:S(2)}) collective-permute-start(bf16[128,256]{1,0:T(8,128)(2,1)S(1)} %pad_maximum_fusion.4.refs_0_), channel_id=1, source_target_pairs={{4,0},{5,1},{6,2},{7,3},{0,4},{1,5},{2,6},{3,7},{12,8},{13,9},{14,... | collective-permute-start | bytes 196616 | tf_op jit(solution)/shard_map/ppermute | solution.py:204
  60.1 1.3 %shard_map.77.refs_2_ = bf16[4,2,256,256]{3,2,1,0:T(8,128)(2,1)S(1)} custom-call(s32[5]{0:T(128)S(1)} %copy-done.7, s32[3,8,8]{2,1,0:T(8,128)S(1)} %copy-done.5, bf16[3,1,256,256]{3,2,1,0:T(8,128)(2,1)S(1)} %copy-done, bf16[3,1,256,512]{3,2,1,0:T(8,128)(2,1)S(1)} %copy-done.1, bf16[2,1,256,512]{3,2,1,0:T(8,128)(2,1)S(1)} %collective-permute-done.13.refs_2_), custom_call_target="tpu_custom_call" | custom-call | tf_op jit(solution)/shard_map/pallas_call | solution.py:49
  61.4 1.3 %shard_map.75.refs_2_ = bf16[4,2,256,256]{3,2,1,0:T(8,128)(2,1)S(1)} custom-call(s32[5]{0:T(128)S(1)} %copy-done.7, s32[3,8,8]{2,1,0:T(8,128)S(1)} %copy-done.5, bf16[3,1,256,256]{3,2,1,0:T(8,128)(2,1)S(1)} %copy-done, bf16[3,1,256,512]{3,2,1,0:T(8,128)(2,1)S(1)} %copy-done.1, bf16[2,1,256,512]{3,2,1,0:T(8,128)(2,1)S(1)} %collective-permute-done.13.refs_2_), custom_call_target="tpu_custom_call" | custom-call | tf_op jit(solution)/shard_map/pallas_call | solution.py:49
  62.7 0.3 shard_map.76.base
  63.0 0.3 shard_map.78
  63.3 0.1 collective-permute-start.19
  63.4 1.2 %collective-permute-done.19 = f32[64,256]{1,0:T(8,128)S(1)} collective-permute-done((f32[64,256]{1,0:T(8,128)S(1)}, f32[64,256]{1,0:T(8,128)S(1)}, u32[]{:S(2)}, u32[]{:S(2)}) %collective-permute-start.19) | collective-permute-done | bytes 65568 | tf_op jit(solution)/shard_map/ppermute | solution.py:204
  64.7 1.6 %collective-permute-start.20 = (bf16[64,256]{1,0:T(8,128)(2,1)S(1)}, bf16[64,256]{1,0:T(8,128)(2,1)S(1)}, u32[]{:S(2)}, u32[]{:S(2)}) collective-permute-start(bf16[64,256]{1,0:T(8,128)(2,1)S(1)} %add_convert_fusion.refs_0_), channel_id=1, source_target_pairs={{2,0},{3,1},{0,2},{1,3},{6,4},{7,5},{4,6},{5,7},{10,8},{11,9},{8,1... | collective-permute-start | bytes 98312 | tf_op jit(solution)/shard_map/ppermute | solution.py:204
  66.2 1.4 %shard_map.74.whole = bf16[3,1,256,128]{3,2,1,0:T(8,128)(2,1)} custom-call(s32[5]{0:T(128)S(1)} %copy-done.7, bf16[128,256]{1,0:T(8,128)(2,1)S(1)} %pad_maximum_fusion.3.refs_0_, bf16[128,256]{1,0:T(8,128)(2,1)S(1)} %collective-permute-done.15.refs_1_), custom_call_target="tpu_custom_call" | custom-call | tf_op jit(solution)/shard_map/pallas_call | solution.py:49
  67.6 1.1 %collective-permute-done.20.refs_1_ = bf16[64,256]{1,0:T(8,128)(2,1)S(1)} collective-permute-done((bf16[64,256]{1,0:T(8,128)(2,1)S(1)}, bf16[64,256]{1,0:T(8,128)(2,1)S(1)}, u32[]{:S(2)}, u32[]{:S(2)}) %collective-permute-start.20) | collective-permute-done | bytes 32800 | tf_op jit(solution)/shard_map/ppermute | solution.py:204
  68.7 1.3 %shard_map.79 = bf16[3,1,256,128]{3,2,1,0:T(8,128)(2,1)} custom-call(s32[5]{0:T(128)S(1)} %copy-done.7, bf16[3,1,256,128]{3,2,1,0:T(8,128)(2,1)} %shard_map.74.whole, bf16[64,256]{1,0:T(8,128)(2,1)S(1)} %add_convert_fusion.refs_0_, bf16[64,256]{1,0:T(8,128)(2,1)S(1)} %collective-permute-done.20.refs_1_), custom_call_target="tpu_custom_call", output_to_operand_aliasing={{}: (1, {})} | custom-call | tf_op jit(solution)/shard_map/pallas_call | solution.py:49
  (30 shorter events, 0.1 us)
Async XLA Ops:
  0.0 9.8 %copy-start.1 = (bf16[3,1,256,512]{3,2,1,0:T(8,128)(2,1)S(1)}, bf16[3,1,256,512]{3,2,1,0:T(8,128)(2,1)}, u32[]{:S(2)}) copy-start(bf16[3,1,256,512]{3,2,1,0:T(8,128)(2,1)} %refs_1_.9) | copy-start | bytes 2359300
  0.0 20.7 %collective-permute-start.3 = (bf16[3,1,256,512]{3,2,1,0:T(8,128)(2,1)}, bf16[3,1,256,512]{3,2,1,0:T(8,128)(2,1)S(1)}, u32[]{:S(2)}, u32[]{:S(2)}) collective-permute-start(bf16[3,1,256,512]{3,2,1,0:T(8,128)(2,1)} %refs_2_.3), channel_id=1, source_target_pairs={{2,0},{3,1},{0,2},{1,3},{6,4},{7,5},{4,6},{5,7},{10,8},{11,9},{8,1... | collective-permute-start | bytes 2359304 | tf_op jit(solution)/shard_map/ppermute | solution.py:204
  5.3 7.2 %collective-permute-start.1 = (bf16[64,256]{1,0:T(8,128)(2,1)}, bf16[64,256]{1,0:T(8,128)(2,1)S(1)}, u32[]{:S(2)}, u32[]{:S(2)}) collective-permute-start(bf16[64,256]{1,0:T(8,128)(2,1)} %shard_map.64.first), channel_id=1, source_target_pairs={{25,0},{24,1},{27,2},{26,3},{29,4},{28,5},{31,6},{30,7},{17,8},{16... | collective-permute-start | bytes 98312 | tf_op jit(solution)/shard_map/ppermute | solution.py:204
  8.1 5.0 %collective-permute-start = (bf16[64,256]{1,0:T(8,128)(2,1)}, bf16[64,256]{1,0:T(8,128)(2,1)S(1)}, u32[]{:S(2)}, u32[]{:S(2)}) collective-permute-start(bf16[64,256]{1,0:T(8,128)(2,1)} %shard_map.64.first), channel_id=1, source_target_pairs={{16,0},{8,1},{18,2},{10,3},{20,4},{12,5},{22,6},{14,7},{1,8},{25,9... | collective-permute-start | bytes 98312 | tf_op jit(solution)/shard_map/ppermute | solution.py:204
  9.8 1.1 %copy-start = (bf16[3,1,256,256]{3,2,1,0:T(8,128)(2,1)S(1)}, bf16[3,1,256,256]{3,2,1,0:T(8,128)(2,1)}, u32[]{:S(2)}) copy-start(bf16[3,1,256,256]{3,2,1,0:T(8,128)(2,1)} %refs_0_.11) | copy-start | bytes 1179652
  9.8 1.3 %copy-start.2 = (bf16[3,1,256,256]{3,2,1,0:T(8,128)(2,1)S(1)}, bf16[3,1,256,256]{3,2,1,0:T(8,128)(2,1)}, u32[]{:S(2)}) copy-start(bf16[3,1,256,256]{3,2,1,0:T(8,128)(2,1)} %refs_1_.6) | copy-start | bytes 1179652
  9.8 1.3 %copy-start.4 = (bf16[3,1,256,128]{3,2,1,0:T(8,128)(2,1)S(1)}, bf16[3,1,256,128]{3,2,1,0:T(8,128)(2,1)}, u32[]{:S(2)}) copy-start(bf16[3,1,256,128]{3,2,1,0:T(8,128)(2,1)} %rhs.3) | copy-start | bytes 589828
  9.8 1.3 %copy-start.6 = (bf16[64,256]{1,0:T(8,128)(2,1)S(1)}, bf16[64,256]{1,0:T(8,128)(2,1)}, u32[]{:S(2)}) copy-start(bf16[64,256]{1,0:T(8,128)(2,1)} %shard_map.64.first) | copy-start | bytes 98308
  9.8 1.3 %copy-start.7 = (s32[5]{0:T(128)S(1)}, s32[5]{0:T(128)}, u32[]{:S(2)}) copy-start(s32[5]{0:T(128)} %stack.23.spot) | copy-start | bytes 64
  10.6 10.1 %copy-start.3 = (bf16[3,1,256,512]{3,2,1,0:T(8,128)(2,1)S(1)}, bf16[3,1,256,512]{3,2,1,0:T(8,128)(2,1)}, u32[]{:S(2)}) copy-start(bf16[3,1,256,512]{3,2,1,0:T(8,128)(2,1)} %refs_2_.3) | copy-start | bytes 2359300
  13.1 7.6 %copy-start.5 = (s32[3,8,8]{2,1,0:T(8,128)S(1)}, s32[3,8,8]{2,1,0:T(8,128)}, u32[]{:S(2)}) copy-start(s32[3,8,8]{2,1,0:T(8,128)} %pattern.11) | copy-start | bytes 2308
  13.2 14.0 %copy-start.9 = (bf16[1,1,256,512]{3,2,1,0:T(8,128)(2,1)S(1)}, bf16[1,1,256,512]{3,2,1,0:T(8,128)(2,1)}, u32[]{:S(2)}) copy-start(bf16[1,1,256,512]{3,2,1,0:T(8,128)(2,1)} %slice.6) | copy-start | bytes 786436
  13.2 4.4 %collective-permute-start.2 = (bf16[128,256]{1,0:T(8,128)(2,1)S(1)}, bf16[128,256]{1,0:T(8,128)(2,1)S(1)}, u32[]{:S(2)}, u32[]{:S(2)}) collective-permute-start(bf16[128,256]{1,0:T(8,128)(2,1)S(1)} %pad_maximum_fusion.refs_2_.refs_0_), channel_id=1, source_target_pairs={{4,0},{5,1},{6,2},{7,3},{0,4},{1,5},{2,6},{3,7},{12,8},{13,9},{14,... | collective-permute-start | bytes 196616 | tf_op jit(solution)/shard_map/ppermute | solution.py:204
  22.1 1.3 %collective-permute-start.4 = (f32[64,256]{1,0:T(8,128)S(1)}, f32[64,256]{1,0:T(8,128)S(1)}, u32[]{:S(2)}, u32[]{:S(2)}) collective-permute-start(f32[64,256]{1,0:T(8,128)S(1)} %shard_map.66), channel_id=1, source_target_pairs={{1,0},{0,1},{3,2},{2,3},{5,4},{4,5},{7,6},{6,7},{9,8},{8,9},{11,10... | collective-permute-start | bytes 196616 | tf_op jit(solution)/shard_map/ppermute | solution.py:204
  23.4 5.5 %collective-permute-start.6 = (bf16[64,256]{1,0:T(8,128)(2,1)S(1)}, bf16[64,256]{1,0:T(8,128)(2,1)S(1)}, u32[]{:S(2)}, u32[]{:S(2)}) collective-permute-start(bf16[64,256]{1,0:T(8,128)(2,1)S(1)} %add_convert_fusion.3), channel_id=1, source_target_pairs={{25,0},{24,1},{27,2},{26,3},{29,4},{28,5},{31,6},{30,7},{17,8},{16... | collective-permute-start | bytes 98312 | tf_op jit(solution)/shard_map/ppermute | solution.py:204
  27.1 4.8 %collective-permute-start.5 = (bf16[64,256]{1,0:T(8,128)(2,1)S(1)}, bf16[64,256]{1,0:T(8,128)(2,1)S(1)}, u32[]{:S(2)}, u32[]{:S(2)}) collective-permute-start(bf16[64,256]{1,0:T(8,128)(2,1)S(1)} %add_convert_fusion.3), channel_id=1, source_target_pairs={{16,0},{8,1},{18,2},{10,3},{20,4},{12,5},{22,6},{14,7},{1,8},{25,9... | collective-permute-start | bytes 98312 | tf_op jit(solution)/shard_map/ppermute | solution.py:204
  27.1 8.7 %collective-permute-start.7 = (bf16[1,1,256,512]{3,2,1,0:T(8,128)(2,1)S(1)}, bf16[1,1,256,512]{3,2,1,0:T(8,128)(2,1)S(1)}, u32[]{:S(2)}, u32[]{:S(2)}) collective-permute-start(bf16[1,1,256,512]{3,2,1,0:T(8,128)(2,1)S(1)} %copy-done.9), channel_id=1, source_target_pairs={{2,0},{3,1},{0,2},{1,3},{6,4},{7,5},{4,6},{5,7},{10,8},{11,9},{8,1... | collective-permute-start | bytes 786440 | tf_op jit(solution)/shard_map/ppermute | solution.py:204
  32.0 4.3 %collective-permute-start.8 = (bf16[128,256]{1,0:T(8,128)(2,1)S(1)}, bf16[128,256]{1,0:T(8,128)(2,1)S(1)}, u32[]{:S(2)}, u32[]{:S(2)}) collective-permute-start(bf16[128,256]{1,0:T(8,128)(2,1)S(1)} %pad_maximum_fusion.1.refs_0_), channel_id=1, source_target_pairs={{4,0},{5,1},{6,2},{7,3},{0,4},{1,5},{2,6},{3,7},{12,8},{13,9},{14,... | collective-permute-start | bytes 196616 | tf_op jit(solution)/shard_map/ppermute | solution.py:204
  36.3 1.0 %copy-start.8 = (bf16[2,1,256,512]{3,2,1,0:T(8,128)(2,1)S(1)}, bf16[2,1,256,512]{3,2,1,0:T(8,128)(2,1)}, u32[]{:S(2)}) copy-start(bf16[2,1,256,512]{3,2,1,0:T(8,128)(2,1)} %slice.7) | copy-start | bytes 1572868
  36.6 2.2 %collective-permute-start.9 = (f32[64,256]{1,0:T(8,128)S(1)}, f32[64,256]{1,0:T(8,128)S(1)}, u32[]{:S(2)}, u32[]{:S(2)}) collective-permute-start(f32[64,256]{1,0:T(8,128)S(1)} %shard_map.71), channel_id=1, source_target_pairs={{1,0},{0,1},{3,2},{2,3},{5,4},{4,5},{7,6},{6,7},{9,8},{8,9},{11,10... | collective-permute-start | bytes 196616 | tf_op jit(solution)/shard_map/ppermute | solution.py:204
  37.3 13.7 %collective-permute-start.13 = (bf16[2,1,256,512]{3,2,1,0:T(8,128)(2,1)S(1)}, bf16[2,1,256,512]{3,2,1,0:T(8,128)(2,1)S(1)}, u32[]{:S(2)}, u32[]{:S(2)}) collective-permute-start(bf16[2,1,256,512]{3,2,1,0:T(8,128)(2,1)S(1)} %copy-done.8), channel_id=1, source_target_pairs={{2,0},{3,1},{0,2},{1,3},{6,4},{7,5},{4,6},{5,7},{10,8},{11,9},{8,1... | collective-permute-start | bytes 1572872 | tf_op jit(solution)/shard_map/ppermute | solution.py:204
  38.8 5.6 %collective-permute-start.11 = (bf16[64,256]{1,0:T(8,128)(2,1)S(1)}, bf16[64,256]{1,0:T(8,128)(2,1)S(1)}, u32[]{:S(2)}, u32[]{:S(2)}) collective-permute-start(bf16[64,256]{1,0:T(8,128)(2,1)S(1)} %add_convert_fusion.2), channel_id=1, source_target_pairs={{25,0},{24,1},{27,2},{26,3},{29,4},{28,5},{31,6},{30,7},{17,8},{16... | collective-permute-start | bytes 98312 | tf_op jit(solution)/shard_map/ppermute | solution.py:204
  39.2 5.4 %collective-permute-start.10 = (bf16[64,256]{1,0:T(8,128)(2,1)S(1)}, bf16[64,256]{1,0:T(8,128)(2,1)S(1)}, u32[]{:S(2)}, u32[]{:S(2)}) collective-permute-start(bf16[64,256]{1,0:T(8,128)(2,1)S(1)} %add_convert_fusion.2), channel_id=1, source_target_pairs={{16,0},{8,1},{18,2},{10,3},{20,4},{12,5},{22,6},{14,7},{1,8},{25,9... | collective-permute-start | bytes 98312 | tf_op jit(solution)/shard_map/ppermute | solution.py:204
  44.6 4.8 %collective-permute-start.12 = (bf16[128,256]{1,0:T(8,128)(2,1)S(1)}, bf16[128,256]{1,0:T(8,128)(2,1)S(1)}, u32[]{:S(2)}, u32[]{:S(2)}) collective-permute-start(bf16[128,256]{1,0:T(8,128)(2,1)S(1)} %pad_maximum_fusion.2.refs_0_), channel_id=1, source_target_pairs={{4,0},{5,1},{6,2},{7,3},{0,4},{1,5},{2,6},{3,7},{12,8},{13,9},{14,... | collective-permute-start | bytes 196616 | tf_op jit(solution)/shard_map/ppermute | solution.py:204
  51.0 1.3 %collective-permute-start.14 = (f32[64,256]{1,0:T(8,128)S(1)}, f32[64,256]{1,0:T(8,128)S(1)}, u32[]{:S(2)}, u32[]{:S(2)}) collective-permute-start(f32[64,256]{1,0:T(8,128)S(1)} %shard_map.73), channel_id=1, source_target_pairs={{1,0},{0,1},{3,2},{2,3},{5,4},{4,5},{7,6},{6,7},{9,8},{8,9},{11,10... | collective-permute-start | bytes 196616 | tf_op jit(solution)/shard_map/ppermute | solution.py:204
  52.3 5.2 %collective-permute-start.17 = (bf16[64,256]{1,0:T(8,128)(2,1)S(1)}, bf16[64,256]{1,0:T(8,128)(2,1)S(1)}, u32[]{:S(2)}, u32[]{:S(2)}) collective-permute-start(bf16[64,256]{1,0:T(8,128)(2,1)S(1)} %add_convert_fusion.1), channel_id=1, source_target_pairs={{25,0},{24,1},{27,2},{26,3},{29,4},{28,5},{31,6},{30,7},{17,8},{16... | collective-permute-start | bytes 98312 | tf_op jit(solution)/shard_map/ppermute | solution.py:204
  53.2 5.3 %collective-permute-start.16 = (bf16[64,256]{1,0:T(8,128)(2,1)S(1)}, bf16[64,256]{1,0:T(8,128)(2,1)S(1)}, u32[]{:S(2)}, u32[]{:S(2)}) collective-permute-start(bf16[64,256]{1,0:T(8,128)(2,1)S(1)} %add_convert_fusion.1), channel_id=1, source_target_pairs={{16,0},{8,1},{18,2},{10,3},{20,4},{12,5},{22,6},{14,7},{1,8},{25,9... | collective-permute-start | bytes 98312 | tf_op jit(solution)/shard_map/ppermute | solution.py:204
  53.4 9.3 %collective-permute-start.15 = (bf16[128,256]{1,0:T(8,128)(2,1)S(1)}, bf16[128,256]{1,0:T(8,128)(2,1)S(1)}, u32[]{:S(2)}, u32[]{:S(2)}) collective-permute-start(bf16[128,256]{1,0:T(8,128)(2,1)S(1)} %pad_maximum_fusion.3.refs_0_), channel_id=1, source_target_pairs={{2,0},{3,1},{0,2},{1,3},{6,4},{7,5},{4,6},{5,7},{10,8},{11,9},{8,1... | collective-permute-start | bytes 196616 | tf_op jit(solution)/shard_map/ppermute | solution.py:204
  58.6 4.5 %collective-permute-start.18 = (bf16[128,256]{1,0:T(8,128)(2,1)S(1)}, bf16[128,256]{1,0:T(8,128)(2,1)S(1)}, u32[]{:S(2)}, u32[]{:S(2)}) collective-permute-start(bf16[128,256]{1,0:T(8,128)(2,1)S(1)} %pad_maximum_fusion.4.refs_0_), channel_id=1, source_target_pairs={{4,0},{5,1},{6,2},{7,3},{0,4},{1,5},{2,6},{3,7},{12,8},{13,9},{14,... | collective-permute-start | bytes 196616 | tf_op jit(solution)/shard_map/ppermute | solution.py:204
  63.3 1.3 %collective-permute-start.19 = (f32[64,256]{1,0:T(8,128)S(1)}, f32[64,256]{1,0:T(8,128)S(1)}, u32[]{:S(2)}, u32[]{:S(2)}) collective-permute-start(f32[64,256]{1,0:T(8,128)S(1)} %shard_map.78), channel_id=1, source_target_pairs={{1,0},{0,1},{3,2},{2,3},{5,4},{4,5},{7,6},{6,7},{9,8},{8,9},{11,10... | collective-permute-start | bytes 196616 | tf_op jit(solution)/shard_map/ppermute | solution.py:204
  64.7 4.0 %collective-permute-start.20 = (bf16[64,256]{1,0:T(8,128)(2,1)S(1)}, bf16[64,256]{1,0:T(8,128)(2,1)S(1)}, u32[]{:S(2)}, u32[]{:S(2)}) collective-permute-start(bf16[64,256]{1,0:T(8,128)(2,1)S(1)} %add_convert_fusion.refs_0_), channel_id=1, source_target_pairs={{2,0},{3,1},{0,2},{1,3},{6,4},{7,5},{4,6},{5,7},{10,8},{11,9},{8,1... | collective-permute-start | bytes 98312 | tf_op jit(solution)/shard_map/ppermute | solution.py:204
